TPU v7x, 32 devices: a whole 2x2x4 slice. The times are simulated.
32 devices in a mesh: shard: 8 (over y, x, core), group: 4 (over z).
Axes of the slice: x: 2, y: 2, z: 4, core: 2. Of those that a mesh axis runs over, the one named last changes fastest.
Arguments:
- embeddings: bfloat16 [16384, 768], P(('shard', 'group')), may hold values from -64 to 64
- row_group: int32 [16384, 1], P(('shard', 'group')), may hold values from 0 to 3; in each aligned block of 512 rows (0 to 511, 512 to 1023, ...) at most 128 rows name the same one
- row_cluster: int32 [16384], P(('shard', 'group')), may hold values from 0 to 5, as said below
Outputs:
- best_cosine: float32 [16384], P(('shard', 'group'))
Inputs may be any that keep to these rules, and one draw needn't show every extreme that they name: `row_group`: among the 512 rows of one device at most 128 name one group, and in every draw some device has exactly 128 rows for some group. `row_cluster`: exactly 4 rows carry a label of 2 or more, each a different label; every other row carries a label below 2.
All inputs are finite; a program needn't handle non-finite values.
Results may differ from a plain program's by a relative error of at most 0.00068.
Values may be sent and summed in bfloat16 or wider, within the bound.
No kernel may reach another device: no remote copies, remote signals or barrier semaphores. Data moves between devices by JAX's collectives and lax.ppermute only.
A program may use at most 128 MiB of HBM per device.

v0:
```python
import jax
import jax.numpy as jnp
from jax import lax
from jax.sharding import PartitionSpec as P


def masked_scores(left_units, left_labels, right_units, right_labels):
    scores = lax.dot_general(
        left_units, right_units, (((1,), (1,)), ((), ())), preferred_element_type=jnp.float32
    )
    same = (left_labels[:, None] == right_labels[None, :]) & (right_labels[None, :] >= 0)
    return jnp.where(same, scores, jnp.float32(-2.0))


def per_device(embeddings, row_group, row_cluster):
    rows = embeddings.shape[0]
    width = embeddings.shape[1]
    groups = lax.axis_size("group")
    capacity = rows // 4
    slot_count = groups * capacity
    feats = embeddings.astype(jnp.float32)
    squares = jnp.sum(feats * feats, axis=1, keepdims=True) + 1e-06
    units = (feats * lax.rsqrt(squares)).astype(jnp.bfloat16)
    dest = row_group[:, 0]
    onehot = (dest[:, None] == jnp.arange(groups, dtype=jnp.int32)[None, :]).astype(jnp.int32)
    within = jnp.sum(jnp.cumsum(onehot, axis=0) * onehot, axis=1) - 1
    place = dest * capacity + within
    send_units = jnp.zeros((slot_count, width), jnp.bfloat16).at[place].set(units)
    send_labels = (
        jnp.full((slot_count,), -1.0, jnp.bfloat16).at[place].set(row_cluster.astype(jnp.bfloat16))
    )
    recv_units, recv_labels = (
        lax.all_to_all(
            send_units.reshape(groups, capacity, width),
            "group",
            split_axis=0,
            concat_axis=0,
            tiled=True,
        ),
        lax.all_to_all(
            send_labels.reshape(groups, capacity), "group", split_axis=0, concat_axis=0, tiled=True
        ),
    )
    local_units = recv_units.reshape(slot_count, width)
    local_labels = recv_labels.reshape(slot_count)
    own_index = lax.axis_index("shard") * slot_count + jnp.arange(slot_count, dtype=jnp.int32)
    start_best = jnp.full((slot_count,), -1.0, jnp.float32)
    piece_units = lax.all_gather(local_units, "shard", axis=0, tiled=True)
    piece_labels = lax.all_gather(local_labels, "shard", axis=0, tiled=True)
    scores = masked_scores(local_units, local_labels, piece_units, piece_labels)
    other = jnp.arange(piece_labels.shape[0], dtype=jnp.int32)
    scores = jnp.where(own_index[:, None] == other[None, :], jnp.float32(-2.0), scores)
    best = jnp.maximum(start_best, jnp.max(scores, axis=1))
    back = lax.all_to_all(
        best.reshape(groups, capacity), "group", split_axis=0, concat_axis=0, tiled=True
    )
    return back.reshape(slot_count)[place]


def solution(mesh):
    placed = (P(("shard", "group"), None), P(("shard", "group"), None), P(("shard", "group")))
    return jax.shard_map(
        per_device, mesh=mesh, in_specs=placed, out_specs=P(("shard", "group")), check_vma=False
    )
```

profile of v0, /device:TPU:0, one launch (start us, length us, event | category | flops | bytes accessed | tf_op | source)
XLA Modules:
  0.0 116.1 jit_solution(10837822661466650869)
XLA Ops:
  6.5 0.0 all-gather.3.cloned.1.call-start
  6.5 0.7 fusion.8
  7.2 1.2 %reduce-window.6 = s32[4,4,128]{2,1,0:T(4,128)S(1)} reduce-window(s32[4,4,128]{2,1,0:T(4,128)S(1)} %fusion.8, s32[]{:T(128)} %constant.8.clone.1), window={size=1x1x128 pad=0_0x0_0x127_0}, to_apply=%region_0.0 | reduce-window | flops 260096 | bytes 16388 | tf_op jit(solution)/shard_map/reduce-window
  8.4 0.2 slice_reduce_fusion
  8.6 0.2 reduce-window.9
  8.8 0.1 add_bitcast_fusion
  8.9 0.7 fusion.7
  9.6 0.7 compare_select_fusion
  10.3 1.4 %fusion = f32[512]{0:T(512)S(1)} fusion(bf16[512,768]{1,0:T(8,128)(2,1)} %param.3), kind=kLoop, calls=%fused_computation.7 | loop fusion | flops 1179136 | bytes 788480 | tf_op jit(solution)/shard_map/reduce_sum | solution.py:22
  11.7 3.6 %scatter_custom_fusion.1 = bf16[512,768]{1,0:T(8,128)(2,1)S(1)} fusion(s32[512]{0:T(512)S(1)} %bitcast.40, bf16[512,768]{1,0:T(8,128)(2,1)} %param.3, f32[512]{0:T(512)S(1)} %add_rsqrt_fusion, bf16[]{:T(256)} %constant.10.clone.1), kind=kCustom, calls=%fused_computation.9 | custom fusion | flops 1179648 | bytes 1574914 | tf_op jit(solution)/shard_map/scatter | solution.py:28
  15.2 26.3 %all_to_all.20 = bf16[4,128,768]{2,1,0:T(8,128)(2,1)} all-to-all(bf16[4,128,768]{2,1,0:T(8,128)(2,1)S(1)} %bitcast.33), channel_id=1, replica_groups=mesh['shard'=8,'group'=4] {'group'}, dimensions={0} | all-to-all | bytes 1572864 | tf_op jit(solution)/shard_map/all_to_all | solution.py:33
  41.6 0.0 all-gather.3.cloned.1.call-update
  41.6 0.7 convert_element_type.15
  42.3 3.8 %scatter_custom_fusion = bf16[512]{0:T(512)(128)(2,1)S(1)} fusion(s32[512]{0:T(512)S(1)} %bitcast.41, bf16[512]{0:T(512)(128)(2,1)S(1)} %convert_element_type.15, bf16[]{:T(256)} %constant.6.clone.1), kind=kCustom, calls=%fused_computation.27 | custom fusion | bytes 1026 | tf_op jit(solution)/shard_map/scatter | solution.py:30
  46.1 0.6 copy.5
  46.6 3.2 %all-to-all-start = ((bf16[4,1,128]{2,1,0:T(2,128)(2,1)}), bf16[4,1,128]{2,1,0:T(2,128)(2,1)S(1)}, u32[]{:S(2)}, u32[]{:S(2)}) async-start(bf16[4,1,128]{2,1,0:T(2,128)(2,1)} %copy.5), calls=%async_computation | async-start | bytes 4096 | tf_op jit(solution)/shard_map/all_to_all | solution.py:40
  49.9 5.4 %all-to-all-done = bf16[4,1,128]{2,1,0:T(2,128)(2,1)S(1)} async-done(((bf16[4,1,128]{2,1,0:T(2,128)(2,1)}), bf16[4,1,128]{2,1,0:T(2,128)(2,1)S(1)}, u32[]{:S(2)}, u32[]{:S(2)}) %all-to-all-start) | async-done | bytes 1056 | tf_op jit(solution)/shard_map/all_to_all | solution.py:40
  55.3 8.9 %all-gather = bf16[8,1,512]{2,1,0:T(2,128)(2,1)S(1)} all-gather(bf16[1,1,512]{2,1,0:T(2,128)(2,1)S(1)} %bitcast.39), channel_id=1, replica_groups=mesh['shard'=8,'group'=4] {'shard'}, dimensions={0}, use_global_device_ids=true | all-gather | bytes 9216 | tf_op jit(solution)/shard_map/all_gather | solution.py:49
  64.3 22.1 %all-gather.3.cloned.1.call-done = bf16[4096,768]{1,0:T(8,128)(2,1)} async-done(((bf16[512,768]{1,0:T(8,128)(2,1)}), bf16[4096,768]{1,0:T(8,128)(2,1)}) %all-gather.3.cloned.1.call-update) | async-done | bytes 6291472 | tf_op jit(solution)/shard_map/all_gather | solution.py:48
  86.4 7.5 %select_reduce_fusion = f32[512]{0:T(512)S(1)} fusion(bf16[512,768]{1,0:T(8,128)(2,1)} %bitcast.32, bf16[4096,768]{1,0:T(8,128)(2,1)} %all-gather.3.cloned.1.call-done, s32[512]{0:T(512)S(1)} %iota_add_fusion, pred[4096]{0:T(1024)(128)(4,1)S(1)} %broadcast_compare_fusion, bf16[4096]{0:T(1024)(128)(2,1)S(1)} %bitcast.36, bf16[512]{0:T(512)(128)(2,1)S(1)} %bitcast.45), kind=kOutput, calls=%fused_computation.3 | convolution fusion | flops 3238002176 | bytes 7095296 | tf_op jit(solution)/shard_map/dot_general | solution.py:8
  94.0 0.6 broadcast_maximum_fusion
  94.6 4.6 %all-to-all-start.2 = ((f32[4,1,128]{2,1,0:T(1,128)}), f32[4,1,128]{2,1,0:T(1,128)S(1)}, u32[]{:S(2)}, u32[]{:S(2)}) async-start(f32[4,1,128]{2,1,0:T(1,128)} %bitcast.9), calls=%async_computation.2 | async-start | bytes 4096 | tf_op jit(solution)/shard_map/all_to_all | solution.py:54
  99.2 5.5 %all-to-all-done.2 = f32[4,1,128]{2,1,0:T(1,128)S(1)} async-done(((f32[4,1,128]{2,1,0:T(1,128)}), f32[4,1,128]{2,1,0:T(1,128)S(1)}, u32[]{:S(2)}, u32[]{:S(2)}) %all-to-all-start.2) | async-done | bytes 2080 | tf_op jit(solution)/shard_map/all_to_all | solution.py:54
  104.6 4.7 %gather_fusion = f32[512]{0:T(512)} fusion(f32[512]{0:T(512)S(1)} %bitcast.30, s32[1024]{0:T(1024)S(1)} %pad_clamp_fusion), kind=kCustom, calls=%fused_computation | custom fusion | bytes 6144 | tf_op jit(solution)/shard_map/gather | solution.py:57
  (8 shorter events, 0.1 us)
Async XLA Ops:
  6.5 79.9 %all-gather.3.cloned.1.call-start = ((), (), s32[]{:S(2)}) async-start(), calls=%async_computation.3 | async-start | bytes 7077888 | tf_op jit(solution)/shard_map/all_gather | solution.py:48
  46.6 8.7 %all-to-all-start = ((bf16[4,1,128]{2,1,0:T(2,128)(2,1)}), bf16[4,1,128]{2,1,0:T(2,128)(2,1)S(1)}, u32[]{:S(2)}, u32[]{:S(2)}) async-start(bf16[4,1,128]{2,1,0:T(2,128)(2,1)} %copy.5), calls=%async_computation | async-start | bytes 4096 | tf_op jit(solution)/shard_map/all_to_all | solution.py:40
  94.6 10.1 %all-to-all-start.2 = ((f32[4,1,128]{2,1,0:T(1,128)}), f32[4,1,128]{2,1,0:T(1,128)S(1)}, u32[]{:S(2)}, u32[]{:S(2)}) async-start(f32[4,1,128]{2,1,0:T(1,128)} %bitcast.9), calls=%async_computation.2 | async-start | bytes 4096 | tf_op jit(solution)/shard_map/all_to_all | solution.py:54
Sparse Core Ops, SparseCore 0:
  41.7 44.6 all-gather.2
where the time goes:
time: 117 us; the launch traced here: 116 us
  blocking collectives  35.2 us (30%)
  waiting for transfers between devices  33 us (28%)
  between operations  13.5 us (12%)
  other arithmetic  9.84 us (8%)
  local copies, waits for them, and re-layouts  9.22 us (8%)
  starting transfers between devices  7.83 us (7%)
  matrix products  7.55 us (6%)
    all_to_all x1, blocking collectives, per_device(): lax.all_to_all(send_units.reshape(groups, capacity, width), 'group', spli...  26.3 us
    all_gather x1, waiting for transfers between devices, per_device(): piece_units = lax.all_gather(local_units, 'shard', axis=0, tiled=True)  22.1 us
    all_gather x1, blocking collectives, per_device(): piece_labels = lax.all_gather(local_labels, 'shard', axis=0, tiled=True)  8.89 us
    dot_general x1, matrix products, masked_scores(): lax.dot_general(left_units, right_units, (((1,), (1,)), ((), ())), prefer...  7.55 us
    all_to_all x1, waiting for transfers between devices, per_device(): lax.all_to_all(best.reshape(groups, capacity), 'group', split_axis=0, con...  5.46 us
    all_to_all x1, waiting for transfers between devices, per_device(): lax.all_to_all(send_labels.reshape(groups, capacity), 'group', split_axis...  5.42 us
    gather x1, local copies, waits for them, and re-layouts, per_device(): return back.reshape(slot_count)[place]  4.65 us
    all_to_all x1, starting transfers between devices, per_device(): lax.all_to_all(best.reshape(groups, capacity), 'group', split_axis=0, con...  4.6 us
  transfers between devices with their start and end apart: 3, of which 3 were waited for; matrix products, arithmetic and copies ran while one was open for 4% of the time, Pallas kernels for 0%

commit v1 on v0

v1 whole, which is shorter than its diff:
```python
import jax
import jax.numpy as jnp
from jax import lax
from jax.experimental import pallas as pl
from jax.experimental.pallas import tpu as pltpu
from jax.sharding import PartitionSpec as P

LANES = 128
TAIL = 16
LOW = -2.0
VMEM_LIMIT = 48 * 1024 * 1024


def ring_order(size):
    if size % 2:
        return list(range(size))
    half = size // 2
    chips = [i ^ (i >> 1) for i in range(half)]
    if sorted(chips) != list(range(half)):
        chips = list(range(half))
    return [2 * chip + core for core in range(2) for chip in chips]


def offset_cover(size):
    offsets = list(dict.fromkeys([0, 1 % size, (size - 1) % size, size // 2]))

    def missing(chosen):
        have = {(a - b) % size for a in chosen for b in chosen}
        return [d for d in range(size) if d not in have]

    while missing(offsets):
        offsets.append(min(range(size), key=lambda x: len(missing(offsets + [x]))))
    pairs = []
    for diff in range(1, size // 2 + 1):
        found = [
            (a, b)
            for b in [1 % size] + offsets
            for a in offsets
            if (a - b) % size in (diff, size - diff)
        ]
        if 2 * diff == size:
            found = [(a, b) for a, b in found if b == 0] + found
        a, b = found[0]
        pairs.append((a, b, b != 0 or 2 * diff != size))
    return offsets, pairs


def column_of(row):
    size = row.shape[1]
    return jnp.transpose(jnp.broadcast_to(row, (size, size)))


def sort_kernel(axis, emb_ref, dest_ref, label_ref, *out_refs):
    *block_refs, place_ref = out_refs
    rows, width = emb_ref.shape
    groups = len(block_refs)
    capacity = (block_refs[0].shape[0] - TAIL) * LANES // width
    slots = groups * capacity
    chunks = width // LANES
    rel = dest_ref[...] ^ lax.axis_index(axis)
    lines = max(8, groups)
    onehot = lax.broadcasted_iota(jnp.int32, (lines, rows), 0) == rel
    before = lax.broadcasted_iota(jnp.int32, (rows, rows), 0) < lax.broadcasted_iota(
        jnp.int32, (rows, rows), 1
    )
    ranks = jnp.dot(
        jnp.where(onehot, 1.0, 0.0).astype(jnp.bfloat16),
        jnp.where(before, 1.0, 0.0).astype(jnp.bfloat16),
        preferred_element_type=jnp.float32,
    )
    rank = jnp.sum(jnp.where(onehot, ranks, 0.0), axis=0, keepdims=True)
    place = rel * capacity + rank.astype(jnp.int32)
    place_ref[...] = place
    move = jnp.where(
        lax.broadcasted_iota(jnp.int32, (slots, rows), 0) == place, 1.0, 0.0
    ).astype(jnp.bfloat16)
    feats = emb_ref[...].astype(jnp.float32)
    squares = jnp.sum(feats * feats, axis=1, keepdims=True) + 1e-06
    units = (feats * lax.rsqrt(squares)).astype(jnp.bfloat16)
    labels = jnp.broadcast_to(label_ref[...] + 1, (TAIL, rows)).astype(jnp.bfloat16)
    sorted_labels = (
        lax.dot_general(
            labels, move, (((1,), (1,)), ((), ())), preferred_element_type=jnp.float32
        )
        - 1.0
    ).astype(jnp.bfloat16)
    for k, block_ref in enumerate(block_refs):
        part = slice(k * capacity, (k + 1) * capacity)
        block = jnp.dot(move[part], units, preferred_element_type=jnp.float32).astype(jnp.bfloat16)
        for c in range(chunks):
            block_ref[pl.ds(c * capacity, capacity), :] = block[:, c * LANES : (c + 1) * LANES]
        block_ref[pl.ds(chunks * capacity, TAIL), :] = sorted_labels[:, part]


def score_kernel(offsets, pairs, groups, *refs):
    roles = len(offsets)
    blocks = [refs[r * groups : (r + 1) * groups] for r in range(roles)]
    out_refs = refs[roles * groups : roles * (groups + 1)]
    flat_ref, row_ref, column_ref = refs[roles * (groups + 1) :]
    height = blocks[0][0].shape[0] - TAIL
    capacity = LANES
    chunks = height // capacity
    slots = groups * capacity
    lane_labels = []
    for r in range(roles):
        for k in range(groups):
            for c in range(chunks):
                flat_ref[r, pl.ds(k * capacity, capacity), pl.ds(c * LANES, LANES)] = blocks[r][k][
                    pl.ds(c * capacity, capacity), :
                ]
        lane_labels.append(
            [b[pl.ds(height, TAIL), :][0:1].astype(jnp.float32) for b in blocks[r]]
        )
    low = jnp.float32(LOW)
    row_ref[...] = jnp.full(row_ref.shape, low)
    column_ref[...] = jnp.full(column_ref.shape, low)
    plan = [(0, 0, False)]
    plan += [(offsets.index(a), offsets.index(b), both) for a, b, both in pairs]
    for left, right, want_rows in plan:
        column_labels = jnp.concatenate(lane_labels[right], axis=1)
        for k in range(groups):
            rows = pl.ds(k * capacity, capacity)
            scores = lax.dot_general(
                flat_ref[left, rows, :],
                flat_ref[right],
                (((1,), (1,)), ((), ())),
                preferred_element_type=jnp.float32,
            )
            row_labels = jnp.concatenate([column_of(lane_labels[left][k])] * groups, axis=1)
            same = row_labels == column_labels
            if left == right:
                same = same & (
                    lax.broadcasted_iota(jnp.int32, (capacity, slots), 0) + k * capacity
                    != lax.broadcasted_iota(jnp.int32, (capacity, slots), 1)
                )
            scores = jnp.where(same, scores, low)
            if want_rows:
                best = scores[:, :LANES]
                for c in range(1, groups):
                    best = jnp.maximum(best, scores[:, c * LANES : (c + 1) * LANES])
                row_ref[left, rows, :] = jnp.maximum(row_ref[left, rows, :], best)
            best = jnp.max(scores.reshape(capacity // 8, 8, slots), axis=0)
            column_ref[right] = jnp.maximum(column_ref[right], best)
    for r in range(roles):
        best = jnp.max(column_ref[r], axis=0, keepdims=True)
        turned = jnp.concatenate(
            [
                jnp.max(
                    jnp.transpose(row_ref[r, pl.ds(k * capacity, capacity), :]),
                    axis=0,
                    keepdims=True,
                )
                for k in range(groups)
            ],
            axis=1,
        )
        out_refs[r][...] = jnp.maximum(best, turned)


def merge_kernel(roles, *refs):
    best = refs[0][...]
    for r in range(1, roles):
        best = jnp.maximum(best, refs[r][...])
    best = jnp.maximum(best, jnp.float32(-1.0))
    for k, out_ref in enumerate(refs[roles:]):
        out_ref[...] = best[:, k * LANES : (k + 1) * LANES]


def place_kernel(groups, *refs):
    place = refs[groups][...]
    rows = place.shape[1]
    best = jnp.full((1, rows), jnp.float32(LOW))
    for k in range(groups):
        values = jnp.concatenate([column_of(refs[k][...])] * (rows // LANES), axis=1)
        here = lax.broadcasted_iota(jnp.int32, (LANES, rows), 0) + k * LANES == place
        best = jnp.maximum(
            best, jnp.max(jnp.where(here, values, jnp.float32(LOW)), axis=0, keepdims=True)
        )
    refs[groups + 1][...] = best


def in_vmem(count):
    return [pl.BlockSpec(memory_space=pltpu.VMEM)] * count


def call(kernel, out_shape, scratch, args, flops, bytes_accessed):
    return pl.pallas_call(
        kernel,
        out_shape=out_shape,
        in_specs=in_vmem(len(args)),
        out_specs=in_vmem(len(out_shape)),
        scratch_shapes=scratch,
        compiler_params=pltpu.CompilerParams(vmem_limit_bytes=VMEM_LIMIT),
        cost_estimate=pl.CostEstimate(
            flops=flops, bytes_accessed=bytes_accessed, transcendentals=0
        ),
    )(*args)


def per_device(embeddings, row_group, row_cluster):
    rows, width = embeddings.shape
    groups = lax.axis_size("group")
    shards = lax.axis_size("shard")
    capacity = rows // 4
    slots = groups * capacity
    ring = ring_order(shards)
    offsets, pairs = offset_cover(shards)
    roles = len(offsets)
    height = width * capacity // LANES + TAIL

    def from_offset(x, offset):
        perm = [(ring[(e + offset) % shards], ring[e]) for e in range(shards)]
        return lax.ppermute(x, "shard", perm)

    def across(x, k):
        return lax.ppermute(x, "group", [(z, z ^ k) for z in range(groups)])

    *send, place = call(
        lambda *refs: sort_kernel("group", *refs),
        [jax.ShapeDtypeStruct((height, LANES), jnp.bfloat16)] * groups
        + [jax.ShapeDtypeStruct((1, rows), jnp.int32)],
        [],
        (embeddings, row_group.reshape(1, rows), row_cluster.reshape(1, rows)),
        2 * rows * slots * width,
        4 * rows * width,
    )
    own = [send[0]] + [across(send[k], k) for k in range(1, groups)]
    held = [own] + [[None] * groups for _ in offsets[1:]]
    for k in range(groups):
        for r in range(1, roles):
            held[r][k] = from_offset(own[k], offsets[r])
    partial = call(
        lambda *refs: score_kernel(offsets, pairs, groups, *refs),
        [jax.ShapeDtypeStruct((1, slots), jnp.float32)] * roles,
        [
            pltpu.VMEM((roles, slots, width), jnp.bfloat16),
            pltpu.VMEM((roles, slots, LANES), jnp.float32),
            pltpu.VMEM((roles, 8, slots), jnp.float32),
        ],
        [block for role in held for block in role],
        2 * slots * slots * width * (len(pairs) + 1),
        2 * roles * slots * width,
    )
    others = [from_offset(partial[r], -offsets[r]) for r in range(1, roles)]
    best = call(
        lambda *refs: merge_kernel(roles, *refs),
        [jax.ShapeDtypeStruct((1, capacity), jnp.float32)] * groups,
        [],
        [partial[0]] + others,
        roles * slots,
        4 * roles * slots,
    )
    back = [best[0]] + [across(best[k], k) for k in range(1, groups)]
    (result,) = call(
        lambda *refs: place_kernel(groups, *refs),
        [jax.ShapeDtypeStruct((1, rows), jnp.float32)],
        [],
        back + [place],
        rows * slots,
        4 * slots,
    )
    return result.reshape(rows)


def solution(mesh):
    placed = (P(("shard", "group"), None), P(("shard", "group"), None), P(("shard", "group")))
    return jax.shard_map(
        per_device, mesh=mesh, in_specs=placed, out_specs=P(("shard", "group")), check_vma=False
    )
```

time: 117 us -> 61.3 us (0.52)
  blocking collectives: 35.2 us -> 0 us
  between operations: 13.5 us -> 0.04 us
  starting transfers between devices: 7.83 us -> 20.8 us
  other arithmetic: 9.84 us -> 0 us
  matrix products: 7.55 us -> 0 us
  Pallas kernels: 0 us -> 7.17 us
  local copies, waits for them, and re-layouts: 9.22 us -> 2.49 us
  waiting for transfers between devices: 33 us -> 30.6 us
    ppermute x0 -> x21, waiting for transfers between devices: none -> 30.6 us  [the longest x6 17.1 us: across(): return lax.ppermute(x, 'group', [(z, z ^ k) for z in range(groups)])]
    all_to_all x1 -> x0, blocking collectives: 26.3 us -> none  [per_device(): lax.all_to_all(send_units.reshape(groups, capacity, width), 'group', spli...]
    all_gather x1 -> x0, waiting for transfers between devices: 22.1 us -> none  [per_device(): piece_units = lax.all_gather(local_units, 'shard', axis=0, tiled=True)]
    ppermute x0 -> x21, starting transfers between devices: none -> 20.8 us  [the longest x15 10.5 us: from_offset(): return lax.ppermute(x, 'shard', perm)]
    all_to_all x2 -> x0, waiting for transfers between devices: 10.9 us -> none  [the longest x1 5.46 us: per_device(): lax.all_to_all(best.reshape(groups, capacity), 'group', split_axis=0, con...]
    all_gather x1 -> x0, blocking collectives: 8.89 us -> none  [per_device(): piece_labels = lax.all_gather(local_labels, 'shard', axis=0, tiled=True)]
    all_to_all x2 -> x0, starting transfers between devices: 7.83 us -> none  [the longest x1 4.6 us: per_device(): lax.all_to_all(best.reshape(groups, capacity), 'group', split_axis=0, con...]
    dot_general x1 -> x0, matrix products: 7.55 us -> none  [masked_scores(): lax.dot_general(left_units, right_units, (((1,), (1,)), ((), ())), prefer...]
  transfers between devices with their start and end apart: 3 -> 21, of which waited for: 3 -> 11; matrix products, arithmetic and copies ran while one was open for 4% -> 0% of each run, Pallas kernels for 0% -> 0%
where the time goes in v1:
time: 61.3 us; the launch traced here: 61.1 us
  waiting for transfers between devices  30.6 us (50%)
  starting transfers between devices  20.8 us (34%)
  Pallas kernels  7.17 us (12%)
  local copies, waits for them, and re-layouts  2.49 us (4%)
    ppermute x6, waiting for transfers between devices, across(): return lax.ppermute(x, 'group', [(z, z ^ k) for z in range(groups)])  17.1 us
    ppermute x15, waiting for transfers between devices, from_offset(): return lax.ppermute(x, 'shard', perm)  13.6 us
    ppermute x15, starting transfers between devices, from_offset(): return lax.ppermute(x, 'shard', perm)  10.5 us
    ppermute x6, starting transfers between devices, across(): return lax.ppermute(x, 'group', [(z, z ^ k) for z in range(groups)])  10.3 us
    pallas_call x4, Pallas kernels, call(): pl.pallas_call(kernel, out_shape=out_shape, in_specs=in_vmem(len(args)),...  7.17 us
    unnamed x6, local copies, waits for them, and re-layouts  2.49 us
  transfers between devices with their start and end apart: 21, of which 11 were waited for; matrix products, arithmetic and copies ran while one was open for 0% of the time, Pallas kernels for 0%

profile of v1, /device:TPU:0, one launch (start us, length us, event | category | flops | bytes accessed | tf_op | source)
XLA Modules:
  0.0 61.1 jit_solution(13619184267782889062)
XLA Ops:
  0.0 0.7 %copy-done.1 = s32[512,1]{0,1:T(1,128)S(1)} copy-done((s32[512,1]{0,1:T(1,128)S(1)}, s32[512,1]{0,1:T(1,128)}, u32[]{:S(2)}) %copy-start.1) | copy-done | bytes 2072
  0.7 1.1 %copy-done = bf16[512,768]{1,0:T(8,128)(2,1)S(1)} copy-done((bf16[512,768]{1,0:T(8,128)(2,1)S(1)}, bf16[512,768]{1,0:T(8,128)(2,1)}, u32[]{:S(2)}) %copy-start) | copy-done | bytes 786456
  1.8 0.7 %copy-done.2 = s32[512]{0:T(512)S(1)} copy-done((s32[512]{0:T(512)S(1)}, s32[512]{0:T(512)}, u32[]{:S(2)}) %copy-start.2) | copy-done | bytes 2072
  2.5 1.1 %shard_map.37 = (bf16[784,128]{1,0:T(8,128)(2,1)S(1)}, bf16[784,128]{1,0:T(8,128)(2,1)S(1)}, bf16[784,128]{1,0:T(8,128)(2,1)S(1)}, bf16[784,128]{1,0:T(8,128)(2,1)S(1)}, s32[1,512]{1,0:T(1,128)S(1)}) custom-call(bf16[512,768]{1,0:T(8,128)(2,1)S(1)} %copy-done, s32[1,512]{1,0:T(1,128)S(1)} %bitcast.3, s32[1,512]{1,0:T(1,128)S(1)} %bitcast.4), custom_call_target="tpu_custom_call" | custom-call | flops 402653184 | bytes 1572864 | tf_op jit(solution)/shard_map/pallas_call | solution.py:187
  3.6 3.1 %collective-permute-start = (bf16[784,128]{1,0:T(8,128)(2,1)S(1)}, bf16[784,128]{1,0:T(8,128)(2,1)S(1)}, u32[]{:S(2)}, u32[]{:S(2)}) collective-permute-start(bf16[784,128]{1,0:T(8,128)(2,1)S(1)} %get-tuple-element.19), channel_id=1, source_target_pairs={{0,1},{1,0},{2,3},{3,2},{4,5},{5,4},{6,7},{7,6},{8,9},{9,8},{10,11... | collective-permute-start | bytes 602120 | tf_op jit(solution)/shard_map/ppermute | solution.py:216
  6.7 2.6 %collective-permute-start.1 = (bf16[784,128]{1,0:T(8,128)(2,1)S(1)}, bf16[784,128]{1,0:T(8,128)(2,1)S(1)}, u32[]{:S(2)}, u32[]{:S(2)}) collective-permute-start(bf16[784,128]{1,0:T(8,128)(2,1)S(1)} %get-tuple-element.20), channel_id=1, source_target_pairs={{0,2},{1,3},{2,0},{3,1},{4,6},{5,7},{6,4},{7,5},{8,10},{9,11},{10,... | collective-permute-start | bytes 602120 | tf_op jit(solution)/shard_map/ppermute | solution.py:216
  9.2 0.0 collective-permute-start.2
  9.2 0.0 collective-permute-start.11
  9.2 1.7 %collective-permute-start.7 = (bf16[784,128]{1,0:T(8,128)(2,1)S(1)}, bf16[784,128]{1,0:T(8,128)(2,1)S(1)}, u32[]{:S(2)}, u32[]{:S(2)}) collective-permute-start(bf16[784,128]{1,0:T(8,128)(2,1)S(1)} %get-tuple-element.18.refs_0_), channel_id=1, source_target_pairs={{20,0},{0,8},{8,24},{24,16},{16,4},{4,12},{12,28},{28,20},{21,1},{... | collective-permute-start | bytes 602120 | tf_op jit(solution)/shard_map/ppermute | solution.py:213
  11.0 4.2 %collective-permute-done.refs_1_ = bf16[784,128]{1,0:T(8,128)(2,1)S(1)} collective-permute-done((bf16[784,128]{1,0:T(8,128)(2,1)S(1)}, bf16[784,128]{1,0:T(8,128)(2,1)S(1)}, u32[]{:S(2)}, u32[]{:S(2)}) %collective-permute-start) | collective-permute-done | bytes 200736 | tf_op jit(solution)/shard_map/ppermute | solution.py:216
  15.2 0.0 collective-permute-start.3
  15.2 8.9 %collective-permute-done.1.refs_2_ = bf16[784,128]{1,0:T(8,128)(2,1)S(1)} collective-permute-done((bf16[784,128]{1,0:T(8,128)(2,1)S(1)}, bf16[784,128]{1,0:T(8,128)(2,1)S(1)}, u32[]{:S(2)}, u32[]{:S(2)}) %collective-permute-start.1) | collective-permute-done | bytes 200736 | tf_op jit(solution)/shard_map/ppermute | solution.py:216
  24.1 0.0 collective-permute-start.12
  24.1 0.0 collective-permute-done.2.refs_3_
  24.1 1.5 %collective-permute-start.8 = (bf16[784,128]{1,0:T(8,128)(2,1)S(1)}, bf16[784,128]{1,0:T(8,128)(2,1)S(1)}, u32[]{:S(2)}, u32[]{:S(2)}) collective-permute-start(bf16[784,128]{1,0:T(8,128)(2,1)S(1)} %collective-permute-done.refs_1_), channel_id=1, source_target_pairs={{20,0},{0,8},{8,24},{24,16},{16,4},{4,12},{12,28},{28,20},{21,1},{... | collective-permute-start | bytes 602120 | tf_op jit(solution)/shard_map/ppermute | solution.py:213
  25.6 0.0 collective-permute-done.11.refs_12_
  25.6 0.3 collective-permute-start.4
  25.8 0.0 collective-permute-done.7.refs_8_
  25.8 0.5 collective-permute-start.13
  26.3 0.0 collective-permute-done.3.refs_4_
  26.3 1.3 %collective-permute-start.9 = (bf16[784,128]{1,0:T(8,128)(2,1)S(1)}, bf16[784,128]{1,0:T(8,128)(2,1)S(1)}, u32[]{:S(2)}, u32[]{:S(2)}) collective-permute-start(bf16[784,128]{1,0:T(8,128)(2,1)S(1)} %collective-permute-done.1.refs_2_), channel_id=1, source_target_pairs={{20,0},{0,8},{8,24},{24,16},{16,4},{4,12},{12,28},{28,20},{21,1},{... | collective-permute-start | bytes 602120 | tf_op jit(solution)/shard_map/ppermute | solution.py:213
  27.7 0.0 collective-permute-done.12.refs_13_
  27.7 0.4 collective-permute-start.5
  28.1 2.8 %collective-permute-done.8.refs_9_ = bf16[784,128]{1,0:T(8,128)(2,1)S(1)} collective-permute-done((bf16[784,128]{1,0:T(8,128)(2,1)S(1)}, bf16[784,128]{1,0:T(8,128)(2,1)S(1)}, u32[]{:S(2)}, u32[]{:S(2)}) %collective-permute-start.8) | collective-permute-done | bytes 200736 | tf_op jit(solution)/shard_map/ppermute | solution.py:213
  30.9 1.3 %collective-permute-start.14 = (bf16[784,128]{1,0:T(8,128)(2,1)S(1)}, bf16[784,128]{1,0:T(8,128)(2,1)S(1)}, u32[]{:S(2)}, u32[]{:S(2)}) collective-permute-start(bf16[784,128]{1,0:T(8,128)(2,1)S(1)} %collective-permute-done.2.refs_3_), channel_id=1, source_target_pairs={{4,0},{12,8},{28,24},{20,16},{0,4},{8,12},{24,28},{16,20},{5,1},{1... | collective-permute-start | bytes 602120 | tf_op jit(solution)/shard_map/ppermute | solution.py:213
  32.1 1.3 %collective-permute-done.4.refs_5_ = bf16[784,128]{1,0:T(8,128)(2,1)S(1)} collective-permute-done((bf16[784,128]{1,0:T(8,128)(2,1)S(1)}, bf16[784,128]{1,0:T(8,128)(2,1)S(1)}, u32[]{:S(2)}, u32[]{:S(2)}) %collective-permute-start.4) | collective-permute-done | bytes 200736 | tf_op jit(solution)/shard_map/ppermute | solution.py:213
  33.4 1.5 %collective-permute-start.10 = (bf16[784,128]{1,0:T(8,128)(2,1)S(1)}, bf16[784,128]{1,0:T(8,128)(2,1)S(1)}, u32[]{:S(2)}, u32[]{:S(2)}) collective-permute-start(bf16[784,128]{1,0:T(8,128)(2,1)S(1)} %collective-permute-done.2.refs_3_), channel_id=1, source_target_pairs={{20,0},{0,8},{8,24},{24,16},{16,4},{4,12},{12,28},{28,20},{21,1},{... | collective-permute-start | bytes 602120 | tf_op jit(solution)/shard_map/ppermute | solution.py:213
  34.9 0.0 collective-permute-done.13.refs_14_
  34.9 0.2 collective-permute-start.6
  35.1 0.0 collective-permute-done.9.refs_10_
  35.2 2.5 %collective-permute-done.5.refs_6_ = bf16[784,128]{1,0:T(8,128)(2,1)S(1)} collective-permute-done((bf16[784,128]{1,0:T(8,128)(2,1)S(1)}, bf16[784,128]{1,0:T(8,128)(2,1)S(1)}, u32[]{:S(2)}, u32[]{:S(2)}) %collective-permute-start.5) | collective-permute-done | bytes 200736 | tf_op jit(solution)/shard_map/ppermute | solution.py:213
  37.7 0.0 collective-permute-done.14.refs_15_
  37.7 2.3 %collective-permute-done.10.refs_11_ = bf16[784,128]{1,0:T(8,128)(2,1)S(1)} collective-permute-done((bf16[784,128]{1,0:T(8,128)(2,1)S(1)}, bf16[784,128]{1,0:T(8,128)(2,1)S(1)}, u32[]{:S(2)}, u32[]{:S(2)}) %collective-permute-start.10) | collective-permute-done | bytes 200736 | tf_op jit(solution)/shard_map/ppermute | solution.py:213
  40.0 1.3 %collective-permute-done.6.refs_7_ = bf16[784,128]{1,0:T(8,128)(2,1)S(1)} collective-permute-done((bf16[784,128]{1,0:T(8,128)(2,1)S(1)}, bf16[784,128]{1,0:T(8,128)(2,1)S(1)}, u32[]{:S(2)}, u32[]{:S(2)}) %collective-permute-start.6) | collective-permute-done | bytes 200736 | tf_op jit(solution)/shard_map/ppermute | solution.py:213
  41.3 5.3 %shard_map.38 = (f32[1,512]{1,0:T(1,128)S(1)}, f32[1,512]{1,0:T(1,128)S(1)}, f32[1,512]{1,0:T(1,128)S(1)}, f32[1,512]{1,0:T(1,128)S(1)}) custom-call(bf16[784,128]{1,0:T(8,128)(2,1)S(1)} %get-tuple-element.18.refs_0_, bf16[784,128]{1,0:T(8,128)(2,1)S(1)} %collective-permute-done.refs_1_, bf16[784,128]{1,0:T(8,128)(2,1)S(1)} %collective-permute-done.1.refs_2_, ...), custom_call_target="tpu_custom_call" | custom-call | flops 2013265920 | bytes 3145728 | tf_op jit(solution)/shard_map/pallas_call | solution.py:187
  46.6 1.6 %collective-permute-start.15 = (f32[1,512]{1,0:T(1,128)S(1)}, f32[1,512]{1,0:T(1,128)S(1)}, u32[]{:S(2)}, u32[]{:S(2)}) collective-permute-start(f32[1,512]{1,0:T(1,128)S(1)} %get-tuple-element.23), channel_id=1, source_target_pairs={{20,0},{0,8},{8,24},{24,16},{16,4},{4,12},{12,28},{28,20},{21,1},{... | collective-permute-start | bytes 6152 | tf_op jit(solution)/shard_map/ppermute | solution.py:213
  48.2 0.2 collective-permute-start.16
  48.4 0.0 collective-permute-start.17
  48.4 1.3 %collective-permute-done.15.refs_1_ = f32[1,512]{1,0:T(1,128)S(1)} collective-permute-done((f32[1,512]{1,0:T(1,128)S(1)}, f32[1,512]{1,0:T(1,128)S(1)}, u32[]{:S(2)}, u32[]{:S(2)}) %collective-permute-start.15) | collective-permute-done | bytes 2080 | tf_op jit(solution)/shard_map/ppermute | solution.py:213
  49.7 2.1 %collective-permute-done.16.refs_2_ = f32[1,512]{1,0:T(1,128)S(1)} collective-permute-done((f32[1,512]{1,0:T(1,128)S(1)}, f32[1,512]{1,0:T(1,128)S(1)}, u32[]{:S(2)}, u32[]{:S(2)}) %collective-permute-start.16) | collective-permute-done | bytes 2080 | tf_op jit(solution)/shard_map/ppermute | solution.py:213
  51.8 0.0 collective-permute-done.17.refs_3_
  51.8 2.1 %collective-permute-start.18 = (f32[1,128]{1,0:T(1,128)S(1)}, f32[1,128]{1,0:T(1,128)S(1)}, u32[]{:S(2)}, u32[]{:S(2)}) collective-permute-start(f32[1,128]{1,0:T(1,128)S(1)} %get-tuple-element.27), channel_id=1, source_target_pairs={{0,1},{1,0},{2,3},{3,2},{4,5},{5,4},{6,7},{7,6},{8,9},{9,8},{10,11... | collective-permute-start | bytes 1544 | tf_op jit(solution)/shard_map/ppermute | solution.py:216
  53.9 1.1 %collective-permute-start.19 = (f32[1,128]{1,0:T(1,128)S(1)}, f32[1,128]{1,0:T(1,128)S(1)}, u32[]{:S(2)}, u32[]{:S(2)}) collective-permute-start(f32[1,128]{1,0:T(1,128)S(1)} %get-tuple-element.28), channel_id=1, source_target_pairs={{0,2},{1,3},{2,0},{3,1},{4,6},{5,7},{6,4},{7,5},{8,10},{9,11},{10,... | collective-permute-start | bytes 1544 | tf_op jit(solution)/shard_map/ppermute | solution.py:216
  55.0 1.4 %collective-permute-start.20 = (f32[1,128]{1,0:T(1,128)S(1)}, f32[1,128]{1,0:T(1,128)S(1)}, u32[]{:S(2)}, u32[]{:S(2)}) collective-permute-start(f32[1,128]{1,0:T(1,128)S(1)} %get-tuple-element.29), channel_id=1, source_target_pairs={{0,3},{1,2},{2,1},{3,0},{4,7},{5,6},{6,5},{7,4},{8,11},{9,10},{10,... | collective-permute-start | bytes 1544 | tf_op jit(solution)/shard_map/ppermute | solution.py:216
  56.4 0.0 collective-permute-done.18.refs_1_
  56.4 2.0 %collective-permute-done.19.refs_2_ = f32[1,128]{1,0:T(1,128)S(1)} collective-permute-done((f32[1,128]{1,0:T(1,128)S(1)}, f32[1,128]{1,0:T(1,128)S(1)}, u32[]{:S(2)}, u32[]{:S(2)}) %collective-permute-start.19) | collective-permute-done | bytes 544 | tf_op jit(solution)/shard_map/ppermute | solution.py:216
  58.3 2.0 %collective-permute-done.20.refs_3_ = f32[1,128]{1,0:T(1,128)S(1)} collective-permute-done((f32[1,128]{1,0:T(1,128)S(1)}, f32[1,128]{1,0:T(1,128)S(1)}, u32[]{:S(2)}, u32[]{:S(2)}) %collective-permute-start.20) | collective-permute-done | bytes 544 | tf_op jit(solution)/shard_map/ppermute | solution.py:216
  60.3 0.8 %shard_map.40 = f32[1,512]{1,0:T(1,128)} custom-call(f32[1,128]{1,0:T(1,128)S(1)} %get-tuple-element.26.refs_0_, f32[1,128]{1,0:T(1,128)S(1)} %collective-permute-done.18.refs_1_, f32[1,128]{1,0:T(1,128)S(1)} %collective-permute-done.19.refs_2_, f32[1,128]{1,0:T(1,128)S(1)} %collective-permute-done.20.refs_3_, s32[1,512]{1,0:T(1,128)S(1)} %get-tuple-element.30.refs_4_), custom_call_target="tpu_custom_call" | custom-call | flops 262144 | bytes 2048 | tf_op jit(solution)/shard_map/pallas_call | solution.py:187
  (4 shorter events, 0.0 us)
Async XLA Ops:
  0.0 0.7 %copy-start.1 = (s32[512,1]{0,1:T(1,128)S(1)}, s32[512,1]{0,1:T(1,128)}, u32[]{:S(2)}) copy-start(s32[512,1]{0,1:T(1,128)} %param.4) | copy-start | bytes 6148
  0.7 1.1 %copy-start = (bf16[512,768]{1,0:T(8,128)(2,1)S(1)}, bf16[512,768]{1,0:T(8,128)(2,1)}, u32[]{:S(2)}) copy-start(bf16[512,768]{1,0:T(8,128)(2,1)} %refs_0_.1) | copy-start | bytes 2359300
  1.8 0.7 %copy-start.2 = (s32[512]{0:T(512)S(1)}, s32[512]{0:T(512)}, u32[]{:S(2)}) copy-start(s32[512]{0:T(512)} %param.5) | copy-start | bytes 6148
  3.6 11.6 %collective-permute-start = (bf16[784,128]{1,0:T(8,128)(2,1)S(1)}, bf16[784,128]{1,0:T(8,128)(2,1)S(1)}, u32[]{:S(2)}, u32[]{:S(2)}) collective-permute-start(bf16[784,128]{1,0:T(8,128)(2,1)S(1)} %get-tuple-element.19), channel_id=1, source_target_pairs={{0,1},{1,0},{2,3},{3,2},{4,5},{5,4},{6,7},{7,6},{8,9},{9,8},{10,11... | collective-permute-start | bytes 602120 | tf_op jit(solution)/shard_map/ppermute | solution.py:216
  6.7 17.4 %collective-permute-start.1 = (bf16[784,128]{1,0:T(8,128)(2,1)S(1)}, bf16[784,128]{1,0:T(8,128)(2,1)S(1)}, u32[]{:S(2)}, u32[]{:S(2)}) collective-permute-start(bf16[784,128]{1,0:T(8,128)(2,1)S(1)} %get-tuple-element.20), channel_id=1, source_target_pairs={{0,2},{1,3},{2,0},{3,1},{4,6},{5,7},{6,4},{7,5},{8,10},{9,11},{10,... | collective-permute-start | bytes 602120 | tf_op jit(solution)/shard_map/ppermute | solution.py:216
  9.2 14.8 %collective-permute-start.2 = (bf16[784,128]{1,0:T(8,128)(2,1)S(1)}, bf16[784,128]{1,0:T(8,128)(2,1)S(1)}, u32[]{:S(2)}, u32[]{:S(2)}) collective-permute-start(bf16[784,128]{1,0:T(8,128)(2,1)S(1)} %get-tuple-element.21), channel_id=1, source_target_pairs={{0,3},{1,2},{2,1},{3,0},{4,7},{5,6},{6,5},{7,4},{8,11},{9,10},{10,... | collective-permute-start | bytes 602120 | tf_op jit(solution)/shard_map/ppermute | solution.py:216
  9.2 16.3 %collective-permute-start.11 = (bf16[784,128]{1,0:T(8,128)(2,1)S(1)}, bf16[784,128]{1,0:T(8,128)(2,1)S(1)}, u32[]{:S(2)}, u32[]{:S(2)}) collective-permute-start(bf16[784,128]{1,0:T(8,128)(2,1)S(1)} %get-tuple-element.18.refs_0_), channel_id=1, source_target_pairs={{4,0},{12,8},{28,24},{20,16},{0,4},{8,12},{24,28},{16,20},{5,1},{1... | collective-permute-start | bytes 602120 | tf_op jit(solution)/shard_map/ppermute | solution.py:213
  9.2 16.6 %collective-permute-start.7 = (bf16[784,128]{1,0:T(8,128)(2,1)S(1)}, bf16[784,128]{1,0:T(8,128)(2,1)S(1)}, u32[]{:S(2)}, u32[]{:S(2)}) collective-permute-start(bf16[784,128]{1,0:T(8,128)(2,1)S(1)} %get-tuple-element.18.refs_0_), channel_id=1, source_target_pairs={{20,0},{0,8},{8,24},{24,16},{16,4},{4,12},{12,28},{28,20},{21,1},{... | collective-permute-start | bytes 602120 | tf_op jit(solution)/shard_map/ppermute | solution.py:213
  15.2 11.2 %collective-permute-start.3 = (bf16[784,128]{1,0:T(8,128)(2,1)S(1)}, bf16[784,128]{1,0:T(8,128)(2,1)S(1)}, u32[]{:S(2)}, u32[]{:S(2)}) collective-permute-start(bf16[784,128]{1,0:T(8,128)(2,1)S(1)} %get-tuple-element.18.refs_0_), channel_id=1, source_target_pairs={{8,0},{24,8},{16,24},{4,16},{12,4},{28,12},{20,28},{0,20},{9,1},{2... | collective-permute-start | bytes 602120 | tf_op jit(solution)/shard_map/ppermute | solution.py:213
  24.1 3.6 %collective-permute-start.12 = (bf16[784,128]{1,0:T(8,128)(2,1)S(1)}, bf16[784,128]{1,0:T(8,128)(2,1)S(1)}, u32[]{:S(2)}, u32[]{:S(2)}) collective-permute-start(bf16[784,128]{1,0:T(8,128)(2,1)S(1)} %collective-permute-done.refs_1_), channel_id=1, source_target_pairs={{4,0},{12,8},{28,24},{20,16},{0,4},{8,12},{24,28},{16,20},{5,1},{1... | collective-permute-start | bytes 602120 | tf_op jit(solution)/shard_map/ppermute | solution.py:213
  24.1 6.8 %collective-permute-start.8 = (bf16[784,128]{1,0:T(8,128)(2,1)S(1)}, bf16[784,128]{1,0:T(8,128)(2,1)S(1)}, u32[]{:S(2)}, u32[]{:S(2)}) collective-permute-start(bf16[784,128]{1,0:T(8,128)(2,1)S(1)} %collective-permute-done.refs_1_), channel_id=1, source_target_pairs={{20,0},{0,8},{8,24},{24,16},{16,4},{4,12},{12,28},{28,20},{21,1},{... | collective-permute-start | bytes 602120 | tf_op jit(solution)/shard_map/ppermute | solution.py:213
  25.6 7.8 %collective-permute-start.4 = (bf16[784,128]{1,0:T(8,128)(2,1)S(1)}, bf16[784,128]{1,0:T(8,128)(2,1)S(1)}, u32[]{:S(2)}, u32[]{:S(2)}) collective-permute-start(bf16[784,128]{1,0:T(8,128)(2,1)S(1)} %collective-permute-done.refs_1_), channel_id=1, source_target_pairs={{8,0},{24,8},{16,24},{4,16},{12,4},{28,12},{20,28},{0,20},{9,1},{2... | collective-permute-start | bytes 602120 | tf_op jit(solution)/shard_map/ppermute | solution.py:213
  25.8 9.1 %collective-permute-start.13 = (bf16[784,128]{1,0:T(8,128)(2,1)S(1)}, bf16[784,128]{1,0:T(8,128)(2,1)S(1)}, u32[]{:S(2)}, u32[]{:S(2)}) collective-permute-start(bf16[784,128]{1,0:T(8,128)(2,1)S(1)} %collective-permute-done.1.refs_2_), channel_id=1, source_target_pairs={{4,0},{12,8},{28,24},{20,16},{0,4},{8,12},{24,28},{16,20},{5,1},{1... | collective-permute-start | bytes 602120 | tf_op jit(solution)/shard_map/ppermute | solution.py:213
  26.3 8.8 %collective-permute-start.9 = (bf16[784,128]{1,0:T(8,128)(2,1)S(1)}, bf16[784,128]{1,0:T(8,128)(2,1)S(1)}, u32[]{:S(2)}, u32[]{:S(2)}) collective-permute-start(bf16[784,128]{1,0:T(8,128)(2,1)S(1)} %collective-permute-done.1.refs_2_), channel_id=1, source_target_pairs={{20,0},{0,8},{8,24},{24,16},{16,4},{4,12},{12,28},{28,20},{21,1},{... | collective-permute-start | bytes 602120 | tf_op jit(solution)/shard_map/ppermute | solution.py:213
  27.7 10.0 %collective-permute-start.5 = (bf16[784,128]{1,0:T(8,128)(2,1)S(1)}, bf16[784,128]{1,0:T(8,128)(2,1)S(1)}, u32[]{:S(2)}, u32[]{:S(2)}) collective-permute-start(bf16[784,128]{1,0:T(8,128)(2,1)S(1)} %collective-permute-done.1.refs_2_), channel_id=1, source_target_pairs={{8,0},{24,8},{16,24},{4,16},{12,4},{28,12},{20,28},{0,20},{9,1},{2... | collective-permute-start | bytes 602120 | tf_op jit(solution)/shard_map/ppermute | solution.py:213
  30.9 6.8 %collective-permute-start.14 = (bf16[784,128]{1,0:T(8,128)(2,1)S(1)}, bf16[784,128]{1,0:T(8,128)(2,1)S(1)}, u32[]{:S(2)}, u32[]{:S(2)}) collective-permute-start(bf16[784,128]{1,0:T(8,128)(2,1)S(1)} %collective-permute-done.2.refs_3_), channel_id=1, source_target_pairs={{4,0},{12,8},{28,24},{20,16},{0,4},{8,12},{24,28},{16,20},{5,1},{1... | collective-permute-start | bytes 602120 | tf_op jit(solution)/shard_map/ppermute | solution.py:213
  33.4 6.6 %collective-permute-start.10 = (bf16[784,128]{1,0:T(8,128)(2,1)S(1)}, bf16[784,128]{1,0:T(8,128)(2,1)S(1)}, u32[]{:S(2)}, u32[]{:S(2)}) collective-permute-start(bf16[784,128]{1,0:T(8,128)(2,1)S(1)} %collective-permute-done.2.refs_3_), channel_id=1, source_target_pairs={{20,0},{0,8},{8,24},{24,16},{16,4},{4,12},{12,28},{28,20},{21,1},{... | collective-permute-start | bytes 602120 | tf_op jit(solution)/shard_map/ppermute | solution.py:213
  34.9 6.4 %collective-permute-start.6 = (bf16[784,128]{1,0:T(8,128)(2,1)S(1)}, bf16[784,128]{1,0:T(8,128)(2,1)S(1)}, u32[]{:S(2)}, u32[]{:S(2)}) collective-permute-start(bf16[784,128]{1,0:T(8,128)(2,1)S(1)} %collective-permute-done.2.refs_3_), channel_id=1, source_target_pairs={{8,0},{24,8},{16,24},{4,16},{12,4},{28,12},{20,28},{0,20},{9,1},{2... | collective-permute-start | bytes 602120 | tf_op jit(solution)/shard_map/ppermute | solution.py:213
  46.6 3.1 %collective-permute-start.15 = (f32[1,512]{1,0:T(1,128)S(1)}, f32[1,512]{1,0:T(1,128)S(1)}, u32[]{:S(2)}, u32[]{:S(2)}) collective-permute-start(f32[1,512]{1,0:T(1,128)S(1)} %get-tuple-element.23), channel_id=1, source_target_pairs={{20,0},{0,8},{8,24},{24,16},{16,4},{4,12},{12,28},{28,20},{21,1},{... | collective-permute-start | bytes 6152 | tf_op jit(solution)/shard_map/ppermute | solution.py:213
  48.2 3.6 %collective-permute-start.16 = (f32[1,512]{1,0:T(1,128)S(1)}, f32[1,512]{1,0:T(1,128)S(1)}, u32[]{:S(2)}, u32[]{:S(2)}) collective-permute-start(f32[1,512]{1,0:T(1,128)S(1)} %get-tuple-element.24), channel_id=1, source_target_pairs={{8,0},{24,8},{16,24},{4,16},{12,4},{28,12},{20,28},{0,20},{9,1},{2... | collective-permute-start | bytes 6152 | tf_op jit(solution)/shard_map/ppermute | solution.py:213
  48.4 3.4 %collective-permute-start.17 = (f32[1,512]{1,0:T(1,128)S(1)}, f32[1,512]{1,0:T(1,128)S(1)}, u32[]{:S(2)}, u32[]{:S(2)}) collective-permute-start(f32[1,512]{1,0:T(1,128)S(1)} %get-tuple-element.25), channel_id=1, source_target_pairs={{4,0},{12,8},{28,24},{20,16},{0,4},{8,12},{24,28},{16,20},{5,1},{1... | collective-permute-start | bytes 6152 | tf_op jit(solution)/shard_map/ppermute | solution.py:213
  51.8 4.6 %collective-permute-start.18 = (f32[1,128]{1,0:T(1,128)S(1)}, f32[1,128]{1,0:T(1,128)S(1)}, u32[]{:S(2)}, u32[]{:S(2)}) collective-permute-start(f32[1,128]{1,0:T(1,128)S(1)} %get-tuple-element.27), channel_id=1, source_target_pairs={{0,1},{1,0},{2,3},{3,2},{4,5},{5,4},{6,7},{7,6},{8,9},{9,8},{10,11... | collective-permute-start | bytes 1544 | tf_op jit(solution)/shard_map/ppermute | solution.py:216
  53.9 4.4 %collective-permute-start.19 = (f32[1,128]{1,0:T(1,128)S(1)}, f32[1,128]{1,0:T(1,128)S(1)}, u32[]{:S(2)}, u32[]{:S(2)}) collective-permute-start(f32[1,128]{1,0:T(1,128)S(1)} %get-tuple-element.28), channel_id=1, source_target_pairs={{0,2},{1,3},{2,0},{3,1},{4,6},{5,7},{6,4},{7,5},{8,10},{9,11},{10,... | collective-permute-start | bytes 1544 | tf_op jit(solution)/shard_map/ppermute | solution.py:216
  55.0 5.3 %collective-permute-start.20 = (f32[1,128]{1,0:T(1,128)S(1)}, f32[1,128]{1,0:T(1,128)S(1)}, u32[]{:S(2)}, u32[]{:S(2)}) collective-permute-start(f32[1,128]{1,0:T(1,128)S(1)} %get-tuple-element.29), channel_id=1, source_target_pairs={{0,3},{1,2},{2,1},{3,0},{4,7},{5,6},{6,5},{7,4},{8,11},{9,10},{10,... | collective-permute-start | bytes 1544 | tf_op jit(solution)/shard_map/ppermute | solution.py:216

commit v2 on v1

--- a/solution.py
+++ b/solution.py
@@ -92,11 +92,23 @@
         block_ref[pl.ds(chunks * capacity, TAIL), :] = sorted_labels[:, part]
 
 
+def stack_kernel(*refs):
+    for k, ref in enumerate(refs[:-1]):
+        refs[-1][k] = ref[...]
+
+
 def score_kernel(offsets, pairs, groups, *refs):
     roles = len(offsets)
-    blocks = [refs[r * groups : (r + 1) * groups] for r in range(roles)]
-    out_refs = refs[roles * groups : roles * (groups + 1)]
-    flat_ref, row_ref, column_ref = refs[roles * (groups + 1) :]
+    *refs, flat_ref, row_ref, column_ref = refs
+    refs, out_refs = refs[:-roles], refs[-roles:]
+    blocks = []
+    while refs:
+        if len(refs[0].shape) == 3:
+            blocks.append([refs[0].at[k] for k in range(groups)])
+            refs = refs[1:]
+        else:
+            blocks.append(refs[:groups])
+            refs = refs[groups:]
     height = blocks[0][0].shape[0] - TAIL
     capacity = LANES
     chunks = height // capacity
@@ -224,11 +236,30 @@
         2 * rows * slots * width,
         4 * rows * width,
     )
-    own = [send[0]] + [across(send[k], k) for k in range(1, groups)]
+    def after(x, *earlier):
+        return lax.optimization_barrier((x, *earlier))[0]
+
+    own = [send[0]] + [None] * (groups - 1)
     held = [own] + [[None] * groups for _ in offsets[1:]]
-    for k in range(groups):
-        for r in range(1, roles):
-            held[r][k] = from_offset(own[k], offsets[r])
+    near = [r for r in range(1, roles) if 2 * offsets[r] != shards]
+    for r in near:
+        held[r][0] = from_offset(own[0], offsets[r])
+    for k in range(1, groups):
+        own[k] = across(after(send[k], held[near[-1]][0]) if k > 2 and near else send[k], k)
+    for k in range(1, groups):
+        for r in near:
+            held[r][k] = from_offset(after(own[k], held[r][k - 1]), offsets[r])
+    for r in range(1, roles):
+        if r not in near:
+            (stack,) = call(
+                stack_kernel,
+                [jax.ShapeDtypeStruct((groups, height, LANES), jnp.bfloat16)],
+                [],
+                [after(x, *[held[q][groups - 2] for q in near]) for x in own],
+                0,
+                4 * groups * height * LANES,
+            )
+            held[r] = [from_offset(stack, offsets[r])]
     partial = call(
         lambda *refs: score_kernel(offsets, pairs, groups, *refs),
         [jax.ShapeDtypeStruct((1, slots), jnp.float32)] * roles,

time: 61.3 us -> 60.4 us (0.985)
  waiting for transfers between devices: 30.6 us -> 27.9 us
  starting transfers between devices: 20.8 us -> 22.5 us
    ppermute x6, waiting for transfers between devices: 17.1 us -> 11.2 us  [across(): return lax.ppermute(x, 'group', [(z, z ^ k) for z in range(groups)])]
    ppermute x15 -> x12, waiting for transfers between devices: 13.6 us -> 16.6 us  [from_offset(): return lax.ppermute(x, 'shard', perm)]
    ppermute x15 -> x12, starting transfers between devices: 10.5 us -> 11.4 us  [from_offset(): return lax.ppermute(x, 'shard', perm)]
    ppermute x6, starting transfers between devices: 10.3 us -> 11.1 us  [across(): return lax.ppermute(x, 'group', [(z, z ^ k) for z in range(groups)])]
    pallas_call x4 -> x5, Pallas kernels: 7.17 us -> 7.24 us  [call(): pl.pallas_call(kernel, out_shape=out_shape, in_specs=in_vmem(len(args)),...]
  transfers between devices with their start and end apart: 21 -> 18, of which waited for: 11 -> 13; matrix products, arithmetic and copies ran while one was open for 0% -> 0% of each run, Pallas kernels for 0% -> 0%
where the time goes in v2:
time: 60.4 us; the launch traced here: 60.2 us
  waiting for transfers between devices  27.9 us (46%)
  starting transfers between devices  22.5 us (37%)
  Pallas kernels  7.24 us (12%)
  local copies, waits for them, and re-layouts  2.49 us (4%)
    ppermute x12, waiting for transfers between devices, from_offset(): return lax.ppermute(x, 'shard', perm)  16.6 us
    ppermute x12, starting transfers between devices, from_offset(): return lax.ppermute(x, 'shard', perm)  11.4 us
    ppermute x6, waiting for transfers between devices, across(): return lax.ppermute(x, 'group', [(z, z ^ k) for z in range(groups)])  11.2 us
    ppermute x6, starting transfers between devices, across(): return lax.ppermute(x, 'group', [(z, z ^ k) for z in range(groups)])  11.1 us
    pallas_call x5, Pallas kernels, call(): pl.pallas_call(kernel, out_shape=out_shape, in_specs=in_vmem(len(args)),...  7.24 us
    unnamed x6, local copies, waits for them, and re-layouts  2.49 us
  transfers between devices with their start and end apart: 18, of which 13 were waited for; matrix products, arithmetic and copies ran while one was open for 0% of the time, Pallas kernels for 0%

profile of v2, /device:TPU:0, one launch (start us, length us, event | category | flops | bytes accessed | tf_op | source)
XLA Modules:
  0.0 60.2 jit_solution(16593803121837034457)
XLA Ops:
  0.0 0.0 copy-start.1
  0.0 0.7 %copy-done.1 = s32[512,1]{0,1:T(1,128)S(1)} copy-done((s32[512,1]{0,1:T(1,128)S(1)}, s32[512,1]{0,1:T(1,128)}, u32[]{:S(2)}) %copy-start.1) | copy-done | bytes 2072
  0.7 0.0 copy-start
  0.7 1.1 %copy-done = bf16[512,768]{1,0:T(8,128)(2,1)S(1)} copy-done((bf16[512,768]{1,0:T(8,128)(2,1)S(1)}, bf16[512,768]{1,0:T(8,128)(2,1)}, u32[]{:S(2)}) %copy-start) | copy-done | bytes 786456
  1.8 0.0 copy-start.2
  1.8 0.7 %copy-done.2 = s32[512]{0:T(512)S(1)} copy-done((s32[512]{0:T(512)S(1)}, s32[512]{0:T(512)}, u32[]{:S(2)}) %copy-start.2) | copy-done | bytes 2072
  2.5 1.1 %shard_map.37 = (bf16[784,128]{1,0:T(8,128)(2,1)S(1)}, bf16[784,128]{1,0:T(8,128)(2,1)S(1)}, bf16[784,128]{1,0:T(8,128)(2,1)S(1)}, bf16[784,128]{1,0:T(8,128)(2,1)S(1)}, s32[1,512]{1,0:T(1,128)S(1)}) custom-call(bf16[512,768]{1,0:T(8,128)(2,1)S(1)} %copy-done, s32[1,512]{1,0:T(1,128)S(1)} %bitcast.3, s32[1,512]{1,0:T(1,128)S(1)} %bitcast.4), custom_call_target="tpu_custom_call" | custom-call | flops 402653184 | bytes 1572864 | tf_op jit(solution)/shard_map/pallas_call | solution.py:199
  3.6 3.0 %collective-permute-start.2 = (bf16[784,128]{1,0:T(8,128)(2,1)S(1)}, bf16[784,128]{1,0:T(8,128)(2,1)S(1)}, u32[]{:S(2)}, u32[]{:S(2)}) collective-permute-start(bf16[784,128]{1,0:T(8,128)(2,1)S(1)} %get-tuple-element.40.refs_0_), channel_id=1, source_target_pairs={{20,0},{0,8},{8,24},{24,16},{16,4},{4,12},{12,28},{28,20},{21,1},{... | collective-permute-start | bytes 602120 | tf_op jit(solution)/shard_map/ppermute | solution.py:225
  6.6 1.6 %collective-permute-start = (bf16[784,128]{1,0:T(8,128)(2,1)S(1)}, bf16[784,128]{1,0:T(8,128)(2,1)S(1)}, u32[]{:S(2)}, u32[]{:S(2)}) collective-permute-start(bf16[784,128]{1,0:T(8,128)(2,1)S(1)} %get-tuple-element.30), channel_id=1, source_target_pairs={{0,1},{1,0},{2,3},{3,2},{4,5},{5,4},{6,7},{7,6},{8,9},{9,8},{10,11... | collective-permute-start | bytes 602120 | tf_op jit(solution)/shard_map/ppermute | solution.py:228
  8.1 0.0 collective-permute-start.4
  8.1 2.6 %collective-permute-start.1 = (bf16[784,128]{1,0:T(8,128)(2,1)S(1)}, bf16[784,128]{1,0:T(8,128)(2,1)S(1)}, u32[]{:S(2)}, u32[]{:S(2)}) collective-permute-start(bf16[784,128]{1,0:T(8,128)(2,1)S(1)} %get-tuple-element.31), channel_id=1, source_target_pairs={{0,2},{1,3},{2,0},{3,1},{4,6},{5,7},{6,4},{7,5},{8,10},{9,11},{10,... | collective-permute-start | bytes 602120 | tf_op jit(solution)/shard_map/ppermute | solution.py:228
  10.7 0.1 collective-permute-done.2.refs_8_
  10.8 5.0 %collective-permute-done.refs_1_ = bf16[784,128]{1,0:T(8,128)(2,1)S(1)} collective-permute-done((bf16[784,128]{1,0:T(8,128)(2,1)S(1)}, bf16[784,128]{1,0:T(8,128)(2,1)S(1)}, u32[]{:S(2)}, u32[]{:S(2)}) %collective-permute-start) | collective-permute-done | bytes 200736 | tf_op jit(solution)/shard_map/ppermute | solution.py:228
  15.8 2.7 %collective-permute-start.8 = (bf16[784,128]{1,0:T(8,128)(2,1)S(1)}, bf16[784,128]{1,0:T(8,128)(2,1)S(1)}, u32[]{:S(2)}, u32[]{:S(2)}) collective-permute-start(bf16[784,128]{1,0:T(8,128)(2,1)S(1)} %collective-permute-done.refs_1_), channel_id=1, source_target_pairs={{20,0},{0,8},{8,24},{24,16},{16,4},{4,12},{12,28},{28,20},{21,1},{... | collective-permute-start | bytes 602120 | tf_op jit(solution)/shard_map/ppermute | solution.py:225
  18.5 0.0 collective-permute-done.4.refs_4_
  18.5 0.0 collective-permute-start.5
  18.5 2.5 %collective-permute-start.3 = (bf16[784,128]{1,0:T(8,128)(2,1)S(1)}, bf16[784,128]{1,0:T(8,128)(2,1)S(1)}, u32[]{:S(2)}, u32[]{:S(2)}) collective-permute-start(bf16[784,128]{1,0:T(8,128)(2,1)S(1)} %get-tuple-element.33), channel_id=1, source_target_pairs={{0,3},{1,2},{2,1},{3,0},{4,7},{5,6},{6,5},{7,4},{8,11},{9,10},{10,... | collective-permute-start | bytes 602120 | tf_op jit(solution)/shard_map/ppermute | solution.py:228
  21.0 0.2 collective-permute-done.1.refs_2_
  21.2 1.6 %collective-permute-done.8.refs_9_ = bf16[784,128]{1,0:T(8,128)(2,1)S(1)} collective-permute-done((bf16[784,128]{1,0:T(8,128)(2,1)S(1)}, bf16[784,128]{1,0:T(8,128)(2,1)S(1)}, u32[]{:S(2)}, u32[]{:S(2)}) %collective-permute-start.8) | collective-permute-done | bytes 200736 | tf_op jit(solution)/shard_map/ppermute | solution.py:225
  22.9 1.3 %collective-permute-start.9 = (bf16[784,128]{1,0:T(8,128)(2,1)S(1)}, bf16[784,128]{1,0:T(8,128)(2,1)S(1)}, u32[]{:S(2)}, u32[]{:S(2)}) collective-permute-start(bf16[784,128]{1,0:T(8,128)(2,1)S(1)} %collective-permute-done.1.refs_2_), channel_id=1, source_target_pairs={{20,0},{0,8},{8,24},{24,16},{16,4},{4,12},{12,28},{28,20},{21,1},{... | collective-permute-start | bytes 602120 | tf_op jit(solution)/shard_map/ppermute | solution.py:225
  24.2 0.0 collective-permute-done.5.refs_5_
  24.2 0.4 collective-permute-start.6
  24.6 1.8 %collective-permute-done.3.refs_3_ = bf16[784,128]{1,0:T(8,128)(2,1)S(1)} collective-permute-done((bf16[784,128]{1,0:T(8,128)(2,1)S(1)}, bf16[784,128]{1,0:T(8,128)(2,1)S(1)}, u32[]{:S(2)}, u32[]{:S(2)}) %collective-permute-start.3) | collective-permute-done | bytes 200736 | tf_op jit(solution)/shard_map/ppermute | solution.py:228
  26.4 3.3 %collective-permute-done.9.refs_10_ = bf16[784,128]{1,0:T(8,128)(2,1)S(1)} collective-permute-done((bf16[784,128]{1,0:T(8,128)(2,1)S(1)}, bf16[784,128]{1,0:T(8,128)(2,1)S(1)}, u32[]{:S(2)}, u32[]{:S(2)}) %collective-permute-start.9) | collective-permute-done | bytes 200736 | tf_op jit(solution)/shard_map/ppermute | solution.py:225
  29.7 2.4 %collective-permute-done.6.refs_6_ = bf16[784,128]{1,0:T(8,128)(2,1)S(1)} collective-permute-done((bf16[784,128]{1,0:T(8,128)(2,1)S(1)}, bf16[784,128]{1,0:T(8,128)(2,1)S(1)}, u32[]{:S(2)}, u32[]{:S(2)}) %collective-permute-start.6) | collective-permute-done | bytes 200736 | tf_op jit(solution)/shard_map/ppermute | solution.py:225
  32.1 0.1 shard_map.38
  32.1 0.1 collective-permute-start.11
  32.2 2.1 %collective-permute-start.10 = (bf16[784,128]{1,0:T(8,128)(2,1)S(1)}, bf16[784,128]{1,0:T(8,128)(2,1)S(1)}, u32[]{:S(2)}, u32[]{:S(2)}) collective-permute-start(bf16[784,128]{1,0:T(8,128)(2,1)S(1)} %collective-permute-done.3.refs_3_), channel_id=1, source_target_pairs={{20,0},{0,8},{8,24},{24,16},{16,4},{4,12},{12,28},{28,20},{21,1},{... | collective-permute-start | bytes 602120 | tf_op jit(solution)/shard_map/ppermute | solution.py:225
  34.3 0.0 collective-permute-start.7
  34.3 4.8 %collective-permute-done.10.refs_11_ = bf16[784,128]{1,0:T(8,128)(2,1)S(1)} collective-permute-done((bf16[784,128]{1,0:T(8,128)(2,1)S(1)}, bf16[784,128]{1,0:T(8,128)(2,1)S(1)}, u32[]{:S(2)}, u32[]{:S(2)}) %collective-permute-start.10) | collective-permute-done | bytes 200736 | tf_op jit(solution)/shard_map/ppermute | solution.py:225
  39.2 2.2 %collective-permute-done.7.refs_7_ = bf16[784,128]{1,0:T(8,128)(2,1)S(1)} collective-permute-done((bf16[784,128]{1,0:T(8,128)(2,1)S(1)}, bf16[784,128]{1,0:T(8,128)(2,1)S(1)}, u32[]{:S(2)}, u32[]{:S(2)}) %collective-permute-start.7) | collective-permute-done | bytes 200736 | tf_op jit(solution)/shard_map/ppermute | solution.py:225
  41.4 0.0 collective-permute-done.11.refs_12_
  41.4 5.3 %shard_map.39 = (f32[1,512]{1,0:T(1,128)S(1)}, f32[1,512]{1,0:T(1,128)S(1)}, f32[1,512]{1,0:T(1,128)S(1)}, f32[1,512]{1,0:T(1,128)S(1)}) custom-call(bf16[784,128]{1,0:T(8,128)(2,1)S(1)} %get-tuple-element.40.refs_0_, bf16[784,128]{1,0:T(8,128)(2,1)S(1)} %collective-permute-done.refs_1_, bf16[784,128]{1,0:T(8,128)(2,1)S(1)} %collective-permute-done.1.refs_2_, ...), custom_call_target="tpu_custom_call" | custom-call | flops 2013265920 | bytes 3145728 | tf_op jit(solution)/shard_map/pallas_call | solution.py:199
  46.7 0.3 collective-permute-start.12
  47.0 1.5 %collective-permute-start.13 = (f32[1,512]{1,0:T(1,128)S(1)}, f32[1,512]{1,0:T(1,128)S(1)}, u32[]{:S(2)}, u32[]{:S(2)}) collective-permute-start(f32[1,512]{1,0:T(1,128)S(1)} %get-tuple-element.46), channel_id=1, source_target_pairs={{8,0},{24,8},{16,24},{4,16},{12,4},{28,12},{20,28},{0,20},{9,1},{2... | collective-permute-start | bytes 6152 | tf_op jit(solution)/shard_map/ppermute | solution.py:225
  48.5 0.0 collective-permute-start.14
  48.5 1.3 %collective-permute-done.12.refs_1_ = f32[1,512]{1,0:T(1,128)S(1)} collective-permute-done((f32[1,512]{1,0:T(1,128)S(1)}, f32[1,512]{1,0:T(1,128)S(1)}, u32[]{:S(2)}, u32[]{:S(2)}) %collective-permute-start.12) | collective-permute-done | bytes 2080 | tf_op jit(solution)/shard_map/ppermute | solution.py:225
  49.8 0.9 %collective-permute-done.13.refs_2_ = f32[1,512]{1,0:T(1,128)S(1)} collective-permute-done((f32[1,512]{1,0:T(1,128)S(1)}, f32[1,512]{1,0:T(1,128)S(1)}, u32[]{:S(2)}, u32[]{:S(2)}) %collective-permute-start.13) | collective-permute-done | bytes 2080 | tf_op jit(solution)/shard_map/ppermute | solution.py:225
  50.6 0.0 collective-permute-done.14.refs_3_
  50.6 0.1 collective-permute-start.15
  50.7 3.3 %collective-permute-start.16 = (f32[1,128]{1,0:T(1,128)S(1)}, f32[1,128]{1,0:T(1,128)S(1)}, u32[]{:S(2)}, u32[]{:S(2)}) collective-permute-start(f32[1,128]{1,0:T(1,128)S(1)} %get-tuple-element.50), channel_id=1, source_target_pairs={{0,2},{1,3},{2,0},{3,1},{4,6},{5,7},{6,4},{7,5},{8,10},{9,11},{10,... | collective-permute-start | bytes 1544 | tf_op jit(solution)/shard_map/ppermute | solution.py:228
  54.0 1.1 %collective-permute-start.17 = (f32[1,128]{1,0:T(1,128)S(1)}, f32[1,128]{1,0:T(1,128)S(1)}, u32[]{:S(2)}, u32[]{:S(2)}) collective-permute-start(f32[1,128]{1,0:T(1,128)S(1)} %get-tuple-element.51), channel_id=1, source_target_pairs={{0,3},{1,2},{2,1},{3,0},{4,7},{5,6},{6,5},{7,4},{8,11},{9,10},{10,... | collective-permute-start | bytes 1544 | tf_op jit(solution)/shard_map/ppermute | solution.py:228
  55.1 0.0 collective-permute-done.15.refs_1_
  55.1 0.4 collective-permute-done.16.refs_2_
  55.5 3.8 %collective-permute-done.17.refs_3_ = f32[1,128]{1,0:T(1,128)S(1)} collective-permute-done((f32[1,128]{1,0:T(1,128)S(1)}, f32[1,128]{1,0:T(1,128)S(1)}, u32[]{:S(2)}, u32[]{:S(2)}) %collective-permute-start.17) | collective-permute-done | bytes 544 | tf_op jit(solution)/shard_map/ppermute | solution.py:228
  59.4 0.8 %shard_map.41 = f32[1,512]{1,0:T(1,128)} custom-call(f32[1,128]{1,0:T(1,128)S(1)} %get-tuple-element.48.refs_0_, f32[1,128]{1,0:T(1,128)S(1)} %collective-permute-done.15.refs_1_, f32[1,128]{1,0:T(1,128)S(1)} %collective-permute-done.16.refs_2_, f32[1,128]{1,0:T(1,128)S(1)} %collective-permute-done.17.refs_3_, s32[1,512]{1,0:T(1,128)S(1)} %get-tuple-element.52.refs_4_), custom_call_target="tpu_custom_call" | custom-call | flops 262144 | bytes 2048 | tf_op jit(solution)/shard_map/pallas_call | solution.py:199
  (1 shorter events, 0.0 us)
Async XLA Ops:
  0.0 0.7 %copy-start.1 = (s32[512,1]{0,1:T(1,128)S(1)}, s32[512,1]{0,1:T(1,128)}, u32[]{:S(2)}) copy-start(s32[512,1]{0,1:T(1,128)} %param.4) | copy-start | bytes 6148
  0.7 1.1 %copy-start = (bf16[512,768]{1,0:T(8,128)(2,1)S(1)}, bf16[512,768]{1,0:T(8,128)(2,1)}, u32[]{:S(2)}) copy-start(bf16[512,768]{1,0:T(8,128)(2,1)} %refs_0_.1) | copy-start | bytes 2359300
  1.8 0.7 %copy-start.2 = (s32[512]{0:T(512)S(1)}, s32[512]{0:T(512)}, u32[]{:S(2)}) copy-start(s32[512]{0:T(512)} %param.5) | copy-start | bytes 6148
  3.6 7.2 %collective-permute-start.2 = (bf16[784,128]{1,0:T(8,128)(2,1)S(1)}, bf16[784,128]{1,0:T(8,128)(2,1)S(1)}, u32[]{:S(2)}, u32[]{:S(2)}) collective-permute-start(bf16[784,128]{1,0:T(8,128)(2,1)S(1)} %get-tuple-element.40.refs_0_), channel_id=1, source_target_pairs={{20,0},{0,8},{8,24},{24,16},{16,4},{4,12},{12,28},{28,20},{21,1},{... | collective-permute-start | bytes 602120 | tf_op jit(solution)/shard_map/ppermute | solution.py:225
  6.6 9.2 %collective-permute-start = (bf16[784,128]{1,0:T(8,128)(2,1)S(1)}, bf16[784,128]{1,0:T(8,128)(2,1)S(1)}, u32[]{:S(2)}, u32[]{:S(2)}) collective-permute-start(bf16[784,128]{1,0:T(8,128)(2,1)S(1)} %get-tuple-element.30), channel_id=1, source_target_pairs={{0,1},{1,0},{2,3},{3,2},{4,5},{5,4},{6,7},{7,6},{8,9},{9,8},{10,11... | collective-permute-start | bytes 602120 | tf_op jit(solution)/shard_map/ppermute | solution.py:228
  8.1 10.4 %collective-permute-start.4 = (bf16[784,128]{1,0:T(8,128)(2,1)S(1)}, bf16[784,128]{1,0:T(8,128)(2,1)S(1)}, u32[]{:S(2)}, u32[]{:S(2)}) collective-permute-start(bf16[784,128]{1,0:T(8,128)(2,1)S(1)} %get-tuple-element.40.refs_0_), channel_id=1, source_target_pairs={{8,0},{24,8},{16,24},{4,16},{12,4},{28,12},{20,28},{0,20},{9,1},{2... | collective-permute-start | bytes 602120 | tf_op jit(solution)/shard_map/ppermute | solution.py:225
  8.1 13.1 %collective-permute-start.1 = (bf16[784,128]{1,0:T(8,128)(2,1)S(1)}, bf16[784,128]{1,0:T(8,128)(2,1)S(1)}, u32[]{:S(2)}, u32[]{:S(2)}) collective-permute-start(bf16[784,128]{1,0:T(8,128)(2,1)S(1)} %get-tuple-element.31), channel_id=1, source_target_pairs={{0,2},{1,3},{2,0},{3,1},{4,6},{5,7},{6,4},{7,5},{8,10},{9,11},{10,... | collective-permute-start | bytes 602120 | tf_op jit(solution)/shard_map/ppermute | solution.py:228
  15.8 7.1 %collective-permute-start.8 = (bf16[784,128]{1,0:T(8,128)(2,1)S(1)}, bf16[784,128]{1,0:T(8,128)(2,1)S(1)}, u32[]{:S(2)}, u32[]{:S(2)}) collective-permute-start(bf16[784,128]{1,0:T(8,128)(2,1)S(1)} %collective-permute-done.refs_1_), channel_id=1, source_target_pairs={{20,0},{0,8},{8,24},{24,16},{16,4},{4,12},{12,28},{28,20},{21,1},{... | collective-permute-start | bytes 602120 | tf_op jit(solution)/shard_map/ppermute | solution.py:225
  18.5 5.7 %collective-permute-start.5 = (bf16[784,128]{1,0:T(8,128)(2,1)S(1)}, bf16[784,128]{1,0:T(8,128)(2,1)S(1)}, u32[]{:S(2)}, u32[]{:S(2)}) collective-permute-start(bf16[784,128]{1,0:T(8,128)(2,1)S(1)} %collective-permute-done.refs_1_), channel_id=1, source_target_pairs={{8,0},{24,8},{16,24},{4,16},{12,4},{28,12},{20,28},{0,20},{9,1},{2... | collective-permute-start | bytes 602120 | tf_op jit(solution)/shard_map/ppermute | solution.py:225
  18.5 7.9 %collective-permute-start.3 = (bf16[784,128]{1,0:T(8,128)(2,1)S(1)}, bf16[784,128]{1,0:T(8,128)(2,1)S(1)}, u32[]{:S(2)}, u32[]{:S(2)}) collective-permute-start(bf16[784,128]{1,0:T(8,128)(2,1)S(1)} %get-tuple-element.33), channel_id=1, source_target_pairs={{0,3},{1,2},{2,1},{3,0},{4,7},{5,6},{6,5},{7,4},{8,11},{9,10},{10,... | collective-permute-start | bytes 602120 | tf_op jit(solution)/shard_map/ppermute | solution.py:228
  22.9 6.9 %collective-permute-start.9 = (bf16[784,128]{1,0:T(8,128)(2,1)S(1)}, bf16[784,128]{1,0:T(8,128)(2,1)S(1)}, u32[]{:S(2)}, u32[]{:S(2)}) collective-permute-start(bf16[784,128]{1,0:T(8,128)(2,1)S(1)} %collective-permute-done.1.refs_2_), channel_id=1, source_target_pairs={{20,0},{0,8},{8,24},{24,16},{16,4},{4,12},{12,28},{28,20},{21,1},{... | collective-permute-start | bytes 602120 | tf_op jit(solution)/shard_map/ppermute | solution.py:225
  24.2 7.9 %collective-permute-start.6 = (bf16[784,128]{1,0:T(8,128)(2,1)S(1)}, bf16[784,128]{1,0:T(8,128)(2,1)S(1)}, u32[]{:S(2)}, u32[]{:S(2)}) collective-permute-start(bf16[784,128]{1,0:T(8,128)(2,1)S(1)} %collective-permute-done.1.refs_2_), channel_id=1, source_target_pairs={{8,0},{24,8},{16,24},{4,16},{12,4},{28,12},{20,28},{0,20},{9,1},{2... | collective-permute-start | bytes 602120 | tf_op jit(solution)/shard_map/ppermute | solution.py:225
  32.1 9.2 %collective-permute-start.11 = (bf16[4,784,128]{2,1,0:T(8,128)(2,1)S(1)}, bf16[4,784,128]{2,1,0:T(8,128)(2,1)S(1)}, u32[]{:S(2)}, u32[]{:S(2)}) collective-permute-start(bf16[4,784,128]{2,1,0:T(8,128)(2,1)S(1)} %shard_map.38), channel_id=1, source_target_pairs={{4,0},{12,8},{28,24},{20,16},{0,4},{8,12},{24,28},{16,20},{5,1},{1... | collective-permute-start | bytes 2408456 | tf_op jit(solution)/shard_map/ppermute | solution.py:225
  32.2 6.9 %collective-permute-start.10 = (bf16[784,128]{1,0:T(8,128)(2,1)S(1)}, bf16[784,128]{1,0:T(8,128)(2,1)S(1)}, u32[]{:S(2)}, u32[]{:S(2)}) collective-permute-start(bf16[784,128]{1,0:T(8,128)(2,1)S(1)} %collective-permute-done.3.refs_3_), channel_id=1, source_target_pairs={{20,0},{0,8},{8,24},{24,16},{16,4},{4,12},{12,28},{28,20},{21,1},{... | collective-permute-start | bytes 602120 | tf_op jit(solution)/shard_map/ppermute | solution.py:225
  34.3 7.1 %collective-permute-start.7 = (bf16[784,128]{1,0:T(8,128)(2,1)S(1)}, bf16[784,128]{1,0:T(8,128)(2,1)S(1)}, u32[]{:S(2)}, u32[]{:S(2)}) collective-permute-start(bf16[784,128]{1,0:T(8,128)(2,1)S(1)} %collective-permute-done.3.refs_3_), channel_id=1, source_target_pairs={{8,0},{24,8},{16,24},{4,16},{12,4},{28,12},{20,28},{0,20},{9,1},{2... | collective-permute-start | bytes 602120 | tf_op jit(solution)/shard_map/ppermute | solution.py:225
  46.7 3.1 %collective-permute-start.12 = (f32[1,512]{1,0:T(1,128)S(1)}, f32[1,512]{1,0:T(1,128)S(1)}, u32[]{:S(2)}, u32[]{:S(2)}) collective-permute-start(f32[1,512]{1,0:T(1,128)S(1)} %get-tuple-element.45), channel_id=1, source_target_pairs={{20,0},{0,8},{8,24},{24,16},{16,4},{4,12},{12,28},{28,20},{21,1},{... | collective-permute-start | bytes 6152 | tf_op jit(solution)/shard_map/ppermute | solution.py:225
  47.0 3.6 %collective-permute-start.13 = (f32[1,512]{1,0:T(1,128)S(1)}, f32[1,512]{1,0:T(1,128)S(1)}, u32[]{:S(2)}, u32[]{:S(2)}) collective-permute-start(f32[1,512]{1,0:T(1,128)S(1)} %get-tuple-element.46), channel_id=1, source_target_pairs={{8,0},{24,8},{16,24},{4,16},{12,4},{28,12},{20,28},{0,20},{9,1},{2... | collective-permute-start | bytes 6152 | tf_op jit(solution)/shard_map/ppermute | solution.py:225
  48.5 2.1 %collective-permute-start.14 = (f32[1,512]{1,0:T(1,128)S(1)}, f32[1,512]{1,0:T(1,128)S(1)}, u32[]{:S(2)}, u32[]{:S(2)}) collective-permute-start(f32[1,512]{1,0:T(1,128)S(1)} %get-tuple-element.47), channel_id=1, source_target_pairs={{4,0},{12,8},{28,24},{20,16},{0,4},{8,12},{24,28},{16,20},{5,1},{1... | collective-permute-start | bytes 6152 | tf_op jit(solution)/shard_map/ppermute | solution.py:225
  50.6 4.5 %collective-permute-start.15 = (f32[1,128]{1,0:T(1,128)S(1)}, f32[1,128]{1,0:T(1,128)S(1)}, u32[]{:S(2)}, u32[]{:S(2)}) collective-permute-start(f32[1,128]{1,0:T(1,128)S(1)} %get-tuple-element.49), channel_id=1, source_target_pairs={{0,1},{1,0},{2,3},{3,2},{4,5},{5,4},{6,7},{7,6},{8,9},{9,8},{10,11... | collective-permute-start | bytes 1544 | tf_op jit(solution)/shard_map/ppermute | solution.py:228
  50.7 4.8 %collective-permute-start.16 = (f32[1,128]{1,0:T(1,128)S(1)}, f32[1,128]{1,0:T(1,128)S(1)}, u32[]{:S(2)}, u32[]{:S(2)}) collective-permute-start(f32[1,128]{1,0:T(1,128)S(1)} %get-tuple-element.50), channel_id=1, source_target_pairs={{0,2},{1,3},{2,0},{3,1},{4,6},{5,7},{6,4},{7,5},{8,10},{9,11},{10,... | collective-permute-start | bytes 1544 | tf_op jit(solution)/shard_map/ppermute | solution.py:228
  54.0 5.3 %collective-permute-start.17 = (f32[1,128]{1,0:T(1,128)S(1)}, f32[1,128]{1,0:T(1,128)S(1)}, u32[]{:S(2)}, u32[]{:S(2)}) collective-permute-start(f32[1,128]{1,0:T(1,128)S(1)} %get-tuple-element.51), channel_id=1, source_target_pairs={{0,3},{1,2},{2,1},{3,0},{4,7},{5,6},{6,5},{7,4},{8,11},{9,10},{10,... | collective-permute-start | bytes 1544 | tf_op jit(solution)/shard_map/ppermute | solution.py:228

commit v3 on v1

v3 whole, which is shorter than its diff:
```python
import jax
import jax.numpy as jnp
from jax import lax
from jax.experimental import pallas as pl
from jax.experimental.pallas import tpu as pltpu
from jax.sharding import PartitionSpec as P

LANES = 128
TAIL = 16
LOW = -2.0
MIB = 1024 * 1024
WAIT = 2 * 10**10


def ring_order(size):
    if size % 2:
        return list(range(size))
    half = size // 2
    chips = [i ^ (i >> 1) for i in range(half)]
    if sorted(chips) != list(range(half)):
        chips = list(range(half))
    return [2 * chip + core for core in range(2) for chip in chips]


def offset_cover(size):
    offsets = list(dict.fromkeys([0, 1 % size, (size - 1) % size, size // 2]))

    def missing(chosen):
        have = {(a - b) % size for a in chosen for b in chosen}
        return [d for d in range(size) if d not in have]

    while missing(offsets):
        offsets.append(min(range(size), key=lambda x: len(missing(offsets + [x]))))
    pairs = []
    for diff in range(1, size // 2 + 1):
        found = [
            (a, b)
            for b in [1 % size] + offsets
            for a in offsets
            if (a - b) % size in (diff, size - diff)
        ]
        if 2 * diff == size:
            found = [(a, b) for a, b in found if b == 0] + found
        a, b = found[0]
        pairs.append((a, b, b != 0 or 2 * diff != size))
    return offsets, pairs


def column_of(row):
    size = row.shape[1]
    return jnp.transpose(jnp.broadcast_to(row, (size, size)))


def sort_kernel(axis, far_ref, code_ref, *refs):
    *block_refs, place_ref, near_ref, unit_ref, sems = refs
    rows, width = near_ref.shape
    groups = len(block_refs)
    capacity = (block_refs[0].shape[0] - TAIL) * LANES // width
    slots = groups * capacity
    chunks = width // LANES
    parts = sems.shape[0]
    size = rows // parts
    copies = [
        pltpu.make_async_copy(
            far_ref.at[pl.ds(i * size, size), :], near_ref.at[pl.ds(i * size, size), :], sems.at[i]
        )
        for i in range(parts)
    ]
    for copy in copies:
        copy.start()
    code = code_ref[...]
    rel = (code & (groups - 1)) ^ lax.axis_index(axis)
    label = code >> (groups.bit_length() - 1)
    lines = max(8, groups)
    onehot = lax.broadcasted_iota(jnp.int32, (lines, rows), 0) == rel
    before = lax.broadcasted_iota(jnp.int32, (rows, rows), 0) < lax.broadcasted_iota(
        jnp.int32, (rows, rows), 1
    )
    ranks = jnp.dot(
        jnp.where(onehot, 1.0, 0.0).astype(jnp.bfloat16),
        jnp.where(before, 1.0, 0.0).astype(jnp.bfloat16),
        preferred_element_type=jnp.float32,
    )
    rank = jnp.sum(jnp.where(onehot, ranks, 0.0), axis=0, keepdims=True)
    place = rel * capacity + rank.astype(jnp.int32)
    place_ref[...] = place
    move = jnp.where(
        lax.broadcasted_iota(jnp.int32, (slots, rows), 0) == place, 1.0, 0.0
    ).astype(jnp.bfloat16)
    labels = jnp.broadcast_to(label + 1, (TAIL, rows)).astype(jnp.bfloat16)
    sorted_labels = (
        lax.dot_general(
            labels, move, (((1,), (1,)), ((), ())), preferred_element_type=jnp.float32
        )
        - 1.0
    ).astype(jnp.bfloat16)
    for i, copy in enumerate(copies):
        copy.wait()
        feats = near_ref[pl.ds(i * size, size), :].astype(jnp.float32)
        squares = jnp.sum(feats * feats, axis=1, keepdims=True) + 1e-06
        unit_ref[pl.ds(i * size, size), :] = (feats * lax.rsqrt(squares)).astype(jnp.bfloat16)
    for k, block_ref in enumerate(block_refs):
        part = slice(k * capacity, (k + 1) * capacity)
        block = jnp.dot(
            move[part], unit_ref[...], preferred_element_type=jnp.float32
        ).astype(jnp.bfloat16)
        for c in range(chunks):
            block_ref[pl.ds(c * capacity, capacity), :] = block[:, c * LANES : (c + 1) * LANES]
        block_ref[pl.ds(chunks * capacity, TAIL), :] = sorted_labels[:, part]


def stack_kernel(*refs):
    for k, ref in enumerate(refs[:-1]):
        refs[-1][k] = ref[...]


def score_kernel(sources, tasks, groups, roles, first, last, *refs):
    *refs, flat_ref, side_ref = refs
    outs = 2 + (roles if last else 0)
    inputs, (row_ref, column_ref, *out_refs) = refs[:-outs], refs[-outs:]
    capacity = LANES
    slots = groups * capacity
    low = jnp.float32(LOW)
    if first:
        row_ref[...] = jnp.full(row_ref.shape, low)
        column_ref[...] = jnp.full(column_ref.shape, low)
    else:
        *inputs, old_rows, old_columns = inputs
        row_ref[...] = old_rows[...]
        column_ref[...] = old_columns[...]
    tops = {}
    for (role, k), (index, part) in sources.items():
        ref = inputs[index] if part is None else inputs[index].at[part]
        height = ref.shape[0] - TAIL
        rows = pl.ds(k * capacity, capacity)
        for c in range(height // capacity):
            flat_ref[role, rows, pl.ds(c * LANES, LANES)] = ref[pl.ds(c * capacity, capacity), :]
        tops[role, k] = ref[pl.ds(height, TAIL), :][0:1].astype(jnp.float32)
    for role, k in sorted({(left, k) for left, ks, _, _, _ in tasks for k in ks}):
        side_ref[role, pl.ds(k * capacity, capacity), :] = column_of(tops[role, k])
    for left, left_ks, right, right_ks, want_rows in tasks:
        start, count = left_ks[0] * capacity, len(left_ks) * capacity
        rows = pl.ds(start, count)
        for i in range(0, len(right_ks), 2):
            some = right_ks[i : i + 2]
            width = len(some) * capacity
            columns = pl.ds(some[0] * capacity, width)
            scores = lax.dot_general(
                flat_ref[left, rows, :],
                flat_ref[right, columns, :],
                (((1,), (1,)), ((), ())),
                preferred_element_type=jnp.float32,
            )
            top = jnp.concatenate([tops[right, k] for k in some], axis=1)
            same = jnp.concatenate([side_ref[left, rows, :]] * len(some), axis=1) == top
            if left == right:
                same = same & (
                    lax.broadcasted_iota(jnp.int32, (count, width), 0) + start
                    != lax.broadcasted_iota(jnp.int32, (count, width), 1) + some[0] * capacity
                )
            scores = jnp.where(same, scores, low)
            if want_rows:
                best = row_ref[left, rows, :]
                for c in range(len(some)):
                    best = jnp.maximum(best, scores[:, c * LANES : (c + 1) * LANES])
                row_ref[left, rows, :] = best
            best = jnp.max(scores.reshape(count // 8, 8, width), axis=0)
            column_ref[right, :, columns] = jnp.maximum(column_ref[right, :, columns], best)
    for role, out_ref in enumerate(out_refs):
        best = jnp.max(column_ref[role], axis=0, keepdims=True)
        turned = [
            jnp.max(
                jnp.transpose(row_ref[role, pl.ds(k * capacity, capacity), :]),
                axis=0,
                keepdims=True,
            )
            for k in range(groups)
        ]
        out_ref[...] = jnp.maximum(best, jnp.concatenate(turned, axis=1))


def merge_kernel(roles, *refs):
    best = refs[0][...]
    for r in range(1, roles):
        best = jnp.maximum(best, refs[r][...])
    best = jnp.maximum(best, jnp.float32(-1.0))
    for k, out_ref in enumerate(refs[roles:]):
        out_ref[...] = best[:, k * LANES : (k + 1) * LANES]


def place_kernel(groups, *refs):
    place = refs[groups][...]
    rows = place.shape[1]
    best = jnp.full((1, rows), jnp.float32(LOW))
    for k in range(groups):
        values = jnp.concatenate([column_of(refs[k][...])] * (rows // LANES), axis=1)
        here = lax.broadcasted_iota(jnp.int32, (LANES, rows), 0) + k * LANES == place
        best = jnp.maximum(
            best, jnp.max(jnp.where(here, values, jnp.float32(LOW)), axis=0, keepdims=True)
        )
    refs[groups + 1][...] = best


def in_vmem(count):
    return [pl.BlockSpec(memory_space=pltpu.VMEM)] * count


def call(
    kernel, out_shape, scratch, args, flops, bytes_accessed, in_specs=None, limit=48 * MIB, aliases=None
):
    return pl.pallas_call(
        kernel,
        out_shape=out_shape,
        in_specs=in_specs or in_vmem(len(args)),
        out_specs=in_vmem(len(out_shape)),
        scratch_shapes=scratch,
        input_output_aliases=aliases or {},
        compiler_params=pltpu.CompilerParams(vmem_limit_bytes=limit),
        cost_estimate=pl.CostEstimate(
            flops=flops, bytes_accessed=bytes_accessed, transcendentals=0
        ),
    )(*args)


def after(x, *earlier):
    return lax.optimization_barrier((x, *earlier))[0]


def stack(parts, wait):
    return call(
        stack_kernel,
        [jax.ShapeDtypeStruct((len(parts), *parts[0].shape), parts[0].dtype)],
        [],
        parts,
        wait,
        4 * len(parts) * parts[0].size,
    )[0]


def score(held, tasks, acc, last, slots, width):
    roles, groups = len(held), len(held[0])
    used = sorted(
        {(left, k) for left, ks, _, _, _ in tasks for k in ks}
        | {(right, k) for _, _, right, ks, _ in tasks for k in ks}
    )
    arrays, sources = [], {}
    for role, k in used:
        array, part = held[role][k]
        index = next((i for i, x in enumerate(arrays) if x is array), len(arrays))
        if index == len(arrays):
            arrays.append(array)
        sources[role, k] = (index, part)
    states = [
        jax.ShapeDtypeStruct((roles, slots, LANES), jnp.float32),
        jax.ShapeDtypeStruct((roles, 8, slots), jnp.float32),
    ]
    ends = [jax.ShapeDtypeStruct((1, slots), jnp.float32)] * roles if last else []
    tiles = sum(len(task[1]) * len(task[3]) for task in tasks)
    count = len(arrays)
    got = call(
        lambda *refs: score_kernel(sources, tasks, groups, roles, not acc, last, *refs),
        states + ends,
        [
            pltpu.VMEM((roles, slots, width), jnp.bfloat16),
            pltpu.VMEM((roles, slots, LANES), jnp.float32),
        ],
        arrays + list(acc),
        2 * tiles * LANES * LANES * width,
        2 * len(used) * LANES * width,
        aliases={count: 0, count + 1: 1} if acc else {},
    )
    return got[:2], got[2:]


def per_device(embeddings, row_group, row_cluster):
    rows, width = embeddings.shape
    groups = lax.axis_size("group")
    shards = lax.axis_size("shard")
    capacity = rows // 4
    slots = groups * capacity
    ring = ring_order(shards)
    offsets, pairs = offset_cover(shards)
    roles = len(offsets)
    height = width * capacity // LANES + TAIL

    def from_offset(x, offset):
        perm = [(ring[(e + offset) % shards], ring[e]) for e in range(shards)]
        return lax.ppermute(x, "shard", perm)

    def across(x, k):
        return lax.ppermute(x, "group", [(z, z ^ k) for z in range(groups)])

    code = row_cluster * groups + row_group[:, 0]
    *send, place = call(
        lambda *refs: sort_kernel("group", *refs),
        [jax.ShapeDtypeStruct((height, LANES), jnp.bfloat16)] * groups
        + [jax.ShapeDtypeStruct((1, rows), jnp.int32)],
        [
            pltpu.VMEM((rows, width), embeddings.dtype),
            pltpu.VMEM((rows, width), jnp.bfloat16),
            pltpu.SemaphoreType.DMA((4,)),
        ],
        (embeddings, code.reshape(1, rows)),
        2 * rows * slots * width,
        4 * rows * width,
        [pl.BlockSpec(memory_space=pltpu.HBM), pl.BlockSpec(memory_space=pltpu.VMEM)],
        53 * MIB,
    )

    early = list(range(min(2, groups)))
    late = list(range(len(early), groups))
    near = [r for r in range(1, roles) if 2 * offsets[r] != shards]
    far = [r for r in range(1, roles) if r not in near]
    own = [send[0]] + [across(send[k], k) for k in range(1, groups)]
    held = [[None] * groups for _ in offsets]
    packs = [stack([own[k] for k in ks], wait) for ks, wait in ((early, 0), (late, WAIT)) if ks]
    sent = {}
    for pack, ks in zip(packs, (early, late)):
        for r in near + far:
            if ks is late and r in near:
                pack_now = after(pack, sent[r])
            else:
                pack_now = pack
            sent[r] = from_offset(pack_now, offsets[r])
            for i, k in enumerate(ks):
                held[r][k] = (sent[r], i)
    held[0] = [(x, None) for x in own]

    everything = [(0, 0, False)]
    everything += [(offsets.index(a), offsets.index(b), both) for a, b, both in pairs]
    steps = [[], [], []]
    for left, right, both in everything:
        for left_ks in (early, late):
            for right_ks in (early, late):
                if left_ks and right_ks:
                    step = 0
                    if left_ks is late:
                        step = 1 if left == 0 else 2
                    if right_ks is late:
                        step = max(step, 1 if right == 0 else 2)
                    steps[step].append((left, left_ks, right, right_ks, both))
    steps = [tasks for tasks in steps if tasks]
    acc = []
    for i, tasks in enumerate(steps):
        acc, partial = score(held, tasks, acc, i == len(steps) - 1, slots, width)

    others = [from_offset(partial[r], -offsets[r]) for r in range(1, roles)]
    best = call(
        lambda *refs: merge_kernel(roles, *refs),
        [jax.ShapeDtypeStruct((1, capacity), jnp.float32)] * groups,
        [],
        [partial[0]] + others,
        roles * slots,
        4 * roles * slots,
    )
    back = [best[0]] + [across(best[k], k) for k in range(1, groups)]
    (result,) = call(
        lambda *refs: place_kernel(groups, *refs),
        [jax.ShapeDtypeStruct((1, rows), jnp.float32)],
        [],
        back + [place],
        rows * slots,
        4 * slots,
    )
    return result.reshape(rows)


def solution(mesh):
    placed = (P(("shard", "group"), None), P(("shard", "group"), None), P(("shard", "group")))
    return jax.shard_map(
        per_device, mesh=mesh, in_specs=placed, out_specs=P(("shard", "group")), check_vma=False
    )
```

time: 61.3 us -> 55.4 us (0.904)
  starting transfers between devices: 20.8 us -> 16.2 us
  local copies, waits for them, and re-layouts: 2.49 us -> 0 us
  waiting for transfers between devices: 30.6 us -> 31.8 us
  other arithmetic: 0 us -> 0.7 us
  Pallas kernels: 7.17 us -> 6.53 us
    ppermute x15 -> x9, starting transfers between devices: 10.5 us -> 6.02 us  [from_offset(): return lax.ppermute(x, 'shard', perm)]
    unnamed x6 -> x0, local copies, waits for them, and re-layouts: 2.49 us -> none
    ppermute x15 -> x9, waiting for transfers between devices: 13.6 us -> 14.3 us  [from_offset(): return lax.ppermute(x, 'shard', perm)]
    add x0 -> x1, other arithmetic: none -> 0.7 us  [per_device(): code = row_cluster * groups + row_group[:, 0]]
    pallas_call x4 -> x8, Pallas kernels: 7.17 us -> 6.53 us  [call(): pl.pallas_call(kernel, out_shape=out_shape, in_specs=in_specs or in_vmem(...]
  transfers between devices with their start and end apart: 21 -> 15, of which waited for: 11 -> 9; matrix products, arithmetic and copies ran while one was open for 0% -> 0% of each run, Pallas kernels for 0% -> 3%
where the time goes in v3:
time: 55.4 us; the launch traced here: 55.3 us
  waiting for transfers between devices  31.8 us (57%)
  starting transfers between devices  16.2 us (29%)
  Pallas kernels  6.53 us (12%)
  other arithmetic  0.7 us (1%)
    ppermute x6, waiting for transfers between devices, across(): return lax.ppermute(x, 'group', [(z, z ^ k) for z in range(groups)])  17.5 us
    ppermute x9, waiting for transfers between devices, from_offset(): return lax.ppermute(x, 'shard', perm)  14.3 us
    ppermute x6, starting transfers between devices, across(): return lax.ppermute(x, 'group', [(z, z ^ k) for z in range(groups)])  10.1 us
    pallas_call x8, Pallas kernels, call(): pl.pallas_call(kernel, out_shape=out_shape, in_specs=in_specs or in_vmem(...  6.53 us
    ppermute x9, starting transfers between devices, from_offset(): return lax.ppermute(x, 'shard', perm)  6.02 us
  transfers between devices with their start and end apart: 15, of which 9 were waited for; matrix products, arithmetic and copies ran while one was open for 0% of the time, Pallas kernels for 3%

profile of v3, /device:TPU:0, one launch (start us, length us, event | category | flops | bytes accessed | tf_op | source)
XLA Modules:
  0.0 55.3 jit_solution(10239533517898107495)
XLA Ops:
  0.0 0.7 %multiply_add_fusion = s32[512]{0:T(512)S(1)} fusion(s32[512]{0:T(512)} %bitcast.4, s32[512]{0:T(512)} %param.5), kind=kLoop, calls=%fused_computation | loop fusion | flops 1024 | bytes 6144 | tf_op jit(solution)/shard_map/add | solution.py:293
  0.7 2.2 %shard_map.37 = (bf16[784,128]{1,0:T(8,128)(2,1)S(1)}, bf16[784,128]{1,0:T(8,128)(2,1)S(1)}, bf16[784,128]{1,0:T(8,128)(2,1)S(1)}, bf16[784,128]{1,0:T(8,128)(2,1)S(1)}, s32[1,512]{1,0:T(1,128)S(1)}) custom-call(bf16[512,768]{1,0:T(8,128)(2,1)} %refs_0_.1, s32[1,512]{1,0:T(1,128)S(1)} %bitcast.3), custom_call_target="tpu_custom_call" | custom-call | flops 402653184 | bytes 1572864 | tf_op jit(solution)/shard_map/pallas_call | solution.py:211
  2.9 3.1 %collective-permute-start = (bf16[784,128]{1,0:T(8,128)(2,1)S(1)}, bf16[784,128]{1,0:T(8,128)(2,1)S(1)}, u32[]{:S(2)}, u32[]{:S(2)}) collective-permute-start(bf16[784,128]{1,0:T(8,128)(2,1)S(1)} %get-tuple-element.25), channel_id=1, source_target_pairs={{0,1},{1,0},{2,3},{3,2},{4,5},{5,4},{6,7},{7,6},{8,9},{9,8},{10,11... | collective-permute-start | bytes 602120 | tf_op jit(solution)/shard_map/ppermute | solution.py:291
  6.0 2.6 %collective-permute-start.1 = (bf16[784,128]{1,0:T(8,128)(2,1)S(1)}, bf16[784,128]{1,0:T(8,128)(2,1)S(1)}, u32[]{:S(2)}, u32[]{:S(2)}) collective-permute-start(bf16[784,128]{1,0:T(8,128)(2,1)S(1)} %get-tuple-element.26), channel_id=1, source_target_pairs={{0,2},{1,3},{2,0},{3,1},{4,6},{5,7},{6,4},{7,5},{8,10},{9,11},{10,... | collective-permute-start | bytes 602120 | tf_op jit(solution)/shard_map/ppermute | solution.py:291
  8.6 0.0 collective-permute-start.2
  8.6 5.9 %collective-permute-done.refs_1_ = bf16[784,128]{1,0:T(8,128)(2,1)S(1)} collective-permute-done((bf16[784,128]{1,0:T(8,128)(2,1)S(1)}, bf16[784,128]{1,0:T(8,128)(2,1)S(1)}, u32[]{:S(2)}, u32[]{:S(2)}) %collective-permute-start) | collective-permute-done | bytes 200736 | tf_op jit(solution)/shard_map/ppermute | solution.py:291
  14.6 0.1 collective-permute-start.7
  14.7 1.7 %collective-permute-start.5 = (bf16[2,784,128]{2,1,0:T(8,128)(2,1)S(1)}, bf16[2,784,128]{2,1,0:T(8,128)(2,1)S(1)}, u32[]{:S(2)}, u32[]{:S(2)}) collective-permute-start(bf16[2,784,128]{2,1,0:T(8,128)(2,1)S(1)} %shard_map.38), channel_id=1, source_target_pairs={{20,0},{0,8},{8,24},{24,16},{16,4},{4,12},{12,28},{28,20},{21,1},{... | collective-permute-start | bytes 1204232 | tf_op jit(solution)/shard_map/ppermute | solution.py:288
  16.4 0.1 collective-permute-start.3
  16.5 7.0 %collective-permute-done.1.refs_0_.refs_2_ = bf16[784,128]{1,0:T(8,128)(2,1)S(1)} collective-permute-done((bf16[784,128]{1,0:T(8,128)(2,1)S(1)}, bf16[784,128]{1,0:T(8,128)(2,1)S(1)}, u32[]{:S(2)}, u32[]{:S(2)}) %collective-permute-start.1) | collective-permute-done | bytes 200736 | tf_op jit(solution)/shard_map/ppermute | solution.py:291
  23.4 0.0 collective-permute-done.2.refs_1_.refs_3_
  23.5 0.1 collective-permute-start.8
  23.6 2.2 %collective-permute-done.5.refs_3_.refs_6_ = bf16[2,784,128]{2,1,0:T(8,128)(2,1)S(1)} collective-permute-done((bf16[2,784,128]{2,1,0:T(8,128)(2,1)S(1)}, bf16[2,784,128]{2,1,0:T(8,128)(2,1)S(1)}, u32[]{:S(2)}, u32[]{:S(2)}) %collective-permute-start.5) | collective-permute-done | bytes 401440 | tf_op jit(solution)/shard_map/ppermute | solution.py:288
  25.7 2.3 %collective-permute-start.6 = (bf16[2,784,128]{2,1,0:T(8,128)(2,1)S(1)}, bf16[2,784,128]{2,1,0:T(8,128)(2,1)S(1)}, u32[]{:S(2)}, u32[]{:S(2)}) collective-permute-start(bf16[2,784,128]{2,1,0:T(8,128)(2,1)S(1)} %shard_map.39), channel_id=1, source_target_pairs={{20,0},{0,8},{8,24},{24,16},{16,4},{4,12},{12,28},{28,20},{21,1},{... | collective-permute-start | bytes 1204232 | tf_op jit(solution)/shard_map/ppermute | solution.py:288
  28.0 0.0 collective-permute-done.3.refs_2_.refs_4_
  28.0 0.0 collective-permute-start.4
  28.0 0.0 collective-permute-done.7.refs_4_.refs_5_.refs_8_
  28.0 0.8 %shard_map.40 = (f32[4,512,128]{2,1,0:T(8,128)S(1)}, f32[4,8,512]{2,1,0:T(8,128)S(1)}) custom-call(bf16[784,128]{1,0:T(8,128)(2,1)S(1)} %get-tuple-element.24.refs_0_, bf16[784,128]{1,0:T(8,128)(2,1)S(1)} %collective-permute-done.refs_1_, bf16[2,784,128]{2,1,0:T(8,128)(2,1)S(1)} %collective-permute-done.3.refs_2_.refs_4_, ...), custom_call_target="tpu_custom_call" | custom-call | flops 503316480 | bytes 1572864 | tf_op jit(solution)/shard_map/pallas_call | solution.py:211
  28.9 0.9 %shard_map.41 = (f32[4,512,128]{2,1,0:T(8,128)S(1)}, f32[4,8,512]{2,1,0:T(8,128)S(1)}) custom-call(bf16[784,128]{1,0:T(8,128)(2,1)S(1)} %get-tuple-element.24.refs_0_, bf16[784,128]{1,0:T(8,128)(2,1)S(1)} %collective-permute-done.refs_1_, bf16[784,128]{1,0:T(8,128)(2,1)S(1)} %collective-permute-done.1.refs_0_.refs_2_, ...), custom_call_target="tpu_custom_call", output_to_operand_aliasing={{0}: (6, {}), {1}: (7, {})} | custom-call | flops 503316480 | bytes 1572864 | tf_op jit(solution)/shard_map/pallas_call | solution.py:211
  29.8 0.0 collective-permute-done.8.refs_9_
  29.8 6.7 %collective-permute-done.6.refs_7_ = bf16[2,784,128]{2,1,0:T(8,128)(2,1)S(1)} collective-permute-done((bf16[2,784,128]{2,1,0:T(8,128)(2,1)S(1)}, bf16[2,784,128]{2,1,0:T(8,128)(2,1)S(1)}, u32[]{:S(2)}, u32[]{:S(2)}) %collective-permute-start.6) | collective-permute-done | bytes 401440 | tf_op jit(solution)/shard_map/ppermute | solution.py:288
  36.5 2.1 %collective-permute-done.4.refs_5_ = bf16[2,784,128]{2,1,0:T(8,128)(2,1)S(1)} collective-permute-done((bf16[2,784,128]{2,1,0:T(8,128)(2,1)S(1)}, bf16[2,784,128]{2,1,0:T(8,128)(2,1)S(1)}, u32[]{:S(2)}, u32[]{:S(2)}) %collective-permute-start.4) | collective-permute-done | bytes 401440 | tf_op jit(solution)/shard_map/ppermute | solution.py:288
  38.6 1.7 %shard_map.42 = (f32[4,512,128]{2,1,0:T(8,128)S(1)}, f32[4,8,512]{2,1,0:T(8,128)S(1)}, f32[1,512]{1,0:T(1,128)S(1)}, f32[1,512]{1,0:T(1,128)S(1)}, f32[1,512]{1,0:T(1,128)S(1)}, /*index=5*/f32[1,512]{1,0:T(1,128)S(1)}) custom-call(bf16[784,128]{1,0:T(8,128)(2,1)S(1)} %get-tuple-element.24.refs_0_, ...), custom_call_target="tpu_custom_call", output_to_operand_aliasing={{0}: (10, {}), {1}: (11, {})} | custom-call | flops 1006632960 | bytes 3145728 | tf_op jit(solution)/shard_map/pallas_call | solution.py:211
  40.3 1.6 %collective-permute-start.9 = (f32[1,512]{1,0:T(1,128)S(1)}, f32[1,512]{1,0:T(1,128)S(1)}, u32[]{:S(2)}, u32[]{:S(2)}) collective-permute-start(f32[1,512]{1,0:T(1,128)S(1)} %get-tuple-element.35), channel_id=1, source_target_pairs={{20,0},{0,8},{8,24},{24,16},{16,4},{4,12},{12,28},{28,20},{21,1},{... | collective-permute-start | bytes 6152 | tf_op jit(solution)/shard_map/ppermute | solution.py:288
  41.9 0.2 collective-permute-start.10
  42.1 0.0 collective-permute-start.11
  42.1 1.3 %collective-permute-done.9.refs_1_ = f32[1,512]{1,0:T(1,128)S(1)} collective-permute-done((f32[1,512]{1,0:T(1,128)S(1)}, f32[1,512]{1,0:T(1,128)S(1)}, u32[]{:S(2)}, u32[]{:S(2)}) %collective-permute-start.9) | collective-permute-done | bytes 2080 | tf_op jit(solution)/shard_map/ppermute | solution.py:288
  43.4 2.1 %collective-permute-done.10.refs_2_ = f32[1,512]{1,0:T(1,128)S(1)} collective-permute-done((f32[1,512]{1,0:T(1,128)S(1)}, f32[1,512]{1,0:T(1,128)S(1)}, u32[]{:S(2)}, u32[]{:S(2)}) %collective-permute-start.10) | collective-permute-done | bytes 2080 | tf_op jit(solution)/shard_map/ppermute | solution.py:288
  45.4 0.0 collective-permute-done.11.refs_3_
  45.5 1.4 %collective-permute-start.12 = (f32[1,128]{1,0:T(1,128)S(1)}, f32[1,128]{1,0:T(1,128)S(1)}, u32[]{:S(2)}, u32[]{:S(2)}) collective-permute-start(f32[1,128]{1,0:T(1,128)S(1)} %get-tuple-element.39), channel_id=1, source_target_pairs={{0,1},{1,0},{2,3},{3,2},{4,5},{5,4},{6,7},{7,6},{8,9},{9,8},{10,11... | collective-permute-start | bytes 1544 | tf_op jit(solution)/shard_map/ppermute | solution.py:291
  46.9 2.2 %collective-permute-start.13 = (f32[1,128]{1,0:T(1,128)S(1)}, f32[1,128]{1,0:T(1,128)S(1)}, u32[]{:S(2)}, u32[]{:S(2)}) collective-permute-start(f32[1,128]{1,0:T(1,128)S(1)} %get-tuple-element.40), channel_id=1, source_target_pairs={{0,2},{1,3},{2,0},{3,1},{4,6},{5,7},{6,4},{7,5},{8,10},{9,11},{10,... | collective-permute-start | bytes 1544 | tf_op jit(solution)/shard_map/ppermute | solution.py:291
  49.1 0.8 %collective-permute-start.14 = (f32[1,128]{1,0:T(1,128)S(1)}, f32[1,128]{1,0:T(1,128)S(1)}, u32[]{:S(2)}, u32[]{:S(2)}) collective-permute-start(f32[1,128]{1,0:T(1,128)S(1)} %get-tuple-element.41), channel_id=1, source_target_pairs={{0,3},{1,2},{2,1},{3,0},{4,7},{5,6},{6,5},{7,4},{8,11},{9,10},{10,... | collective-permute-start | bytes 1544 | tf_op jit(solution)/shard_map/ppermute | solution.py:291
  49.9 0.0 collective-permute-done.12.refs_1_
  49.9 1.4 %collective-permute-done.13.refs_2_ = f32[1,128]{1,0:T(1,128)S(1)} collective-permute-done((f32[1,128]{1,0:T(1,128)S(1)}, f32[1,128]{1,0:T(1,128)S(1)}, u32[]{:S(2)}, u32[]{:S(2)}) %collective-permute-start.13) | collective-permute-done | bytes 544 | tf_op jit(solution)/shard_map/ppermute | solution.py:291
  51.3 3.1 %collective-permute-done.14.refs_3_ = f32[1,128]{1,0:T(1,128)S(1)} collective-permute-done((f32[1,128]{1,0:T(1,128)S(1)}, f32[1,128]{1,0:T(1,128)S(1)}, u32[]{:S(2)}, u32[]{:S(2)}) %collective-permute-start.14) | collective-permute-done | bytes 544 | tf_op jit(solution)/shard_map/ppermute | solution.py:291
  54.5 0.8 %shard_map.44 = f32[1,512]{1,0:T(1,128)} custom-call(f32[1,128]{1,0:T(1,128)S(1)} %get-tuple-element.38.refs_0_, f32[1,128]{1,0:T(1,128)S(1)} %collective-permute-done.12.refs_1_, f32[1,128]{1,0:T(1,128)S(1)} %collective-permute-done.13.refs_2_, f32[1,128]{1,0:T(1,128)S(1)} %collective-permute-done.14.refs_3_, s32[1,512]{1,0:T(1,128)S(1)} %get-tuple-element.42.refs_4_), custom_call_target="tpu_custom_call" | custom-call | flops 262144 | bytes 2048 | tf_op jit(solution)/shard_map/pallas_call | solution.py:211
  (3 shorter events, 0.1 us)
Async XLA Ops:
  2.9 11.6 %collective-permute-start = (bf16[784,128]{1,0:T(8,128)(2,1)S(1)}, bf16[784,128]{1,0:T(8,128)(2,1)S(1)}, u32[]{:S(2)}, u32[]{:S(2)}) collective-permute-start(bf16[784,128]{1,0:T(8,128)(2,1)S(1)} %get-tuple-element.25), channel_id=1, source_target_pairs={{0,1},{1,0},{2,3},{3,2},{4,5},{5,4},{6,7},{7,6},{8,9},{9,8},{10,11... | collective-permute-start | bytes 602120 | tf_op jit(solution)/shard_map/ppermute | solution.py:291
  6.0 17.4 %collective-permute-start.1 = (bf16[784,128]{1,0:T(8,128)(2,1)S(1)}, bf16[784,128]{1,0:T(8,128)(2,1)S(1)}, u32[]{:S(2)}, u32[]{:S(2)}) collective-permute-start(bf16[784,128]{1,0:T(8,128)(2,1)S(1)} %get-tuple-element.26), channel_id=1, source_target_pairs={{0,2},{1,3},{2,0},{3,1},{4,6},{5,7},{6,4},{7,5},{8,10},{9,11},{10,... | collective-permute-start | bytes 602120 | tf_op jit(solution)/shard_map/ppermute | solution.py:291
  8.6 14.8 %collective-permute-start.2 = (bf16[784,128]{1,0:T(8,128)(2,1)S(1)}, bf16[784,128]{1,0:T(8,128)(2,1)S(1)}, u32[]{:S(2)}, u32[]{:S(2)}) collective-permute-start(bf16[784,128]{1,0:T(8,128)(2,1)S(1)} %get-tuple-element.27), channel_id=1, source_target_pairs={{0,3},{1,2},{2,1},{3,0},{4,7},{5,6},{6,5},{7,4},{8,11},{9,10},{10,... | collective-permute-start | bytes 602120 | tf_op jit(solution)/shard_map/ppermute | solution.py:291
  14.6 13.4 %collective-permute-start.7 = (bf16[2,784,128]{2,1,0:T(8,128)(2,1)S(1)}, bf16[2,784,128]{2,1,0:T(8,128)(2,1)S(1)}, u32[]{:S(2)}, u32[]{:S(2)}) collective-permute-start(bf16[2,784,128]{2,1,0:T(8,128)(2,1)S(1)} %shard_map.38), channel_id=1, source_target_pairs={{4,0},{12,8},{28,24},{20,16},{0,4},{8,12},{24,28},{16,20},{5,1},{1... | collective-permute-start | bytes 1204232 | tf_op jit(solution)/shard_map/ppermute | solution.py:288
  14.7 11.1 %collective-permute-start.5 = (bf16[2,784,128]{2,1,0:T(8,128)(2,1)S(1)}, bf16[2,784,128]{2,1,0:T(8,128)(2,1)S(1)}, u32[]{:S(2)}, u32[]{:S(2)}) collective-permute-start(bf16[2,784,128]{2,1,0:T(8,128)(2,1)S(1)} %shard_map.38), channel_id=1, source_target_pairs={{20,0},{0,8},{8,24},{24,16},{16,4},{4,12},{12,28},{28,20},{21,1},{... | collective-permute-start | bytes 1204232 | tf_op jit(solution)/shard_map/ppermute | solution.py:288
  16.4 11.6 %collective-permute-start.3 = (bf16[2,784,128]{2,1,0:T(8,128)(2,1)S(1)}, bf16[2,784,128]{2,1,0:T(8,128)(2,1)S(1)}, u32[]{:S(2)}, u32[]{:S(2)}) collective-permute-start(bf16[2,784,128]{2,1,0:T(8,128)(2,1)S(1)} %shard_map.38), channel_id=1, source_target_pairs={{8,0},{24,8},{16,24},{4,16},{12,4},{28,12},{20,28},{0,20},{9,1},{2... | collective-permute-start | bytes 1204232 | tf_op jit(solution)/shard_map/ppermute | solution.py:288
  23.5 6.3 %collective-permute-start.8 = (bf16[2,784,128]{2,1,0:T(8,128)(2,1)S(1)}, bf16[2,784,128]{2,1,0:T(8,128)(2,1)S(1)}, u32[]{:S(2)}, u32[]{:S(2)}) collective-permute-start(bf16[2,784,128]{2,1,0:T(8,128)(2,1)S(1)} %shard_map.39), channel_id=1, source_target_pairs={{4,0},{12,8},{28,24},{20,16},{0,4},{8,12},{24,28},{16,20},{5,1},{1... | collective-permute-start | bytes 1204232 | tf_op jit(solution)/shard_map/ppermute | solution.py:288
  25.7 10.8 %collective-permute-start.6 = (bf16[2,784,128]{2,1,0:T(8,128)(2,1)S(1)}, bf16[2,784,128]{2,1,0:T(8,128)(2,1)S(1)}, u32[]{:S(2)}, u32[]{:S(2)}) collective-permute-start(bf16[2,784,128]{2,1,0:T(8,128)(2,1)S(1)} %shard_map.39), channel_id=1, source_target_pairs={{20,0},{0,8},{8,24},{24,16},{16,4},{4,12},{12,28},{28,20},{21,1},{... | collective-permute-start | bytes 1204232 | tf_op jit(solution)/shard_map/ppermute | solution.py:288
  28.0 10.6 %collective-permute-start.4 = (bf16[2,784,128]{2,1,0:T(8,128)(2,1)S(1)}, bf16[2,784,128]{2,1,0:T(8,128)(2,1)S(1)}, u32[]{:S(2)}, u32[]{:S(2)}) collective-permute-start(bf16[2,784,128]{2,1,0:T(8,128)(2,1)S(1)} %shard_map.39), channel_id=1, source_target_pairs={{8,0},{24,8},{16,24},{4,16},{12,4},{28,12},{20,28},{0,20},{9,1},{2... | collective-permute-start | bytes 1204232 | tf_op jit(solution)/shard_map/ppermute | solution.py:288
  40.3 3.1 %collective-permute-start.9 = (f32[1,512]{1,0:T(1,128)S(1)}, f32[1,512]{1,0:T(1,128)S(1)}, u32[]{:S(2)}, u32[]{:S(2)}) collective-permute-start(f32[1,512]{1,0:T(1,128)S(1)} %get-tuple-element.35), channel_id=1, source_target_pairs={{20,0},{0,8},{8,24},{24,16},{16,4},{4,12},{12,28},{28,20},{21,1},{... | collective-permute-start | bytes 6152 | tf_op jit(solution)/shard_map/ppermute | solution.py:288
  41.9 3.6 %collective-permute-start.10 = (f32[1,512]{1,0:T(1,128)S(1)}, f32[1,512]{1,0:T(1,128)S(1)}, u32[]{:S(2)}, u32[]{:S(2)}) collective-permute-start(f32[1,512]{1,0:T(1,128)S(1)} %get-tuple-element.36), channel_id=1, source_target_pairs={{8,0},{24,8},{16,24},{4,16},{12,4},{28,12},{20,28},{0,20},{9,1},{2... | collective-permute-start | bytes 6152 | tf_op jit(solution)/shard_map/ppermute | solution.py:288
  42.1 3.4 %collective-permute-start.11 = (f32[1,512]{1,0:T(1,128)S(1)}, f32[1,512]{1,0:T(1,128)S(1)}, u32[]{:S(2)}, u32[]{:S(2)}) collective-permute-start(f32[1,512]{1,0:T(1,128)S(1)} %get-tuple-element.37), channel_id=1, source_target_pairs={{4,0},{12,8},{28,24},{20,16},{0,4},{8,12},{24,28},{16,20},{5,1},{1... | collective-permute-start | bytes 6152 | tf_op jit(solution)/shard_map/ppermute | solution.py:288
  45.5 4.5 %collective-permute-start.12 = (f32[1,128]{1,0:T(1,128)S(1)}, f32[1,128]{1,0:T(1,128)S(1)}, u32[]{:S(2)}, u32[]{:S(2)}) collective-permute-start(f32[1,128]{1,0:T(1,128)S(1)} %get-tuple-element.39), channel_id=1, source_target_pairs={{0,1},{1,0},{2,3},{3,2},{4,5},{5,4},{6,7},{7,6},{8,9},{9,8},{10,11... | collective-permute-start | bytes 1544 | tf_op jit(solution)/shard_map/ppermute | solution.py:291
  46.9 4.4 %collective-permute-start.13 = (f32[1,128]{1,0:T(1,128)S(1)}, f32[1,128]{1,0:T(1,128)S(1)}, u32[]{:S(2)}, u32[]{:S(2)}) collective-permute-start(f32[1,128]{1,0:T(1,128)S(1)} %get-tuple-element.40), channel_id=1, source_target_pairs={{0,2},{1,3},{2,0},{3,1},{4,6},{5,7},{6,4},{7,5},{8,10},{9,11},{10,... | collective-permute-start | bytes 1544 | tf_op jit(solution)/shard_map/ppermute | solution.py:291
  49.1 5.3 %collective-permute-start.14 = (f32[1,128]{1,0:T(1,128)S(1)}, f32[1,128]{1,0:T(1,128)S(1)}, u32[]{:S(2)}, u32[]{:S(2)}) collective-permute-start(f32[1,128]{1,0:T(1,128)S(1)} %get-tuple-element.41), channel_id=1, source_target_pairs={{0,3},{1,2},{2,1},{3,0},{4,7},{5,6},{6,5},{7,4},{8,11},{9,10},{10,... | collective-permute-start | bytes 1544 | tf_op jit(solution)/shard_map/ppermute | solution.py:291

commit v4 on v3

--- a/solution.py
+++ b/solution.py
@@ -23,7 +23,7 @@
 
 
 def offset_cover(size):
-    offsets = list(dict.fromkeys([0, 1 % size, (size - 1) % size, size // 2]))
+    offsets = list(dict.fromkeys([0, size // 2, 1 % size, (size - 1) % size]))
 
     def missing(chosen):
         have = {(a - b) % size for a in chosen for b in chosen}
@@ -193,7 +193,7 @@
     rows = place.shape[1]
     best = jnp.full((1, rows), jnp.float32(LOW))
     for k in range(groups):
-        values = jnp.concatenate([column_of(refs[k][...])] * (rows // LANES), axis=1)
+        values = jnp.concatenate([column_of(refs[groups - 1 - k][...])] * (rows // LANES), axis=1)
         here = lax.broadcasted_iota(jnp.int32, (LANES, rows), 0) + k * LANES == place
         best = jnp.maximum(
             best, jnp.max(jnp.where(here, values, jnp.float32(LOW)), axis=0, keepdims=True)
@@ -241,7 +241,8 @@
     roles, groups = len(held), len(held[0])
     used = sorted(
         {(left, k) for left, ks, _, _, _ in tasks for k in ks}
-        | {(right, k) for _, _, right, ks, _ in tasks for k in ks}
+        | {(right, k) for _, _, right, ks, _ in tasks for k in ks},
+        key=lambda x: (x[0], -x[1]),
     )
     arrays, sources = [], {}
     for role, k in used:
@@ -287,8 +288,12 @@
         perm = [(ring[(e + offset) % shards], ring[e]) for e in range(shards)]
         return lax.ppermute(x, "shard", perm)
 
-    def across(x, k):
-        return lax.ppermute(x, "group", [(z, z ^ k) for z in range(groups)])
+    def exchange(blocks, stagger=False):
+        got = list(blocks)
+        for k in range(1, groups):
+            block = after(blocks[k], got[1]) if k > 2 and stagger else blocks[k]
+            got[k] = lax.ppermute(block, "group", [(z, z ^ k) for z in range(groups)])
+        return got
 
     code = row_cluster * groups + row_group[:, 0]
     *send, place = call(
@@ -307,25 +312,22 @@
         53 * MIB,
     )
 
-    early = list(range(min(2, groups)))
-    late = list(range(len(early), groups))
+    late = [groups - 1] if groups > 1 else []
+    early = list(range(groups - len(late)))
     near = [r for r in range(1, roles) if 2 * offsets[r] != shards]
     far = [r for r in range(1, roles) if r not in near]
-    own = [send[0]] + [across(send[k], k) for k in range(1, groups)]
+    own = exchange(send, True)
     held = [[None] * groups for _ in offsets]
-    packs = [stack([own[k] for k in ks], wait) for ks, wait in ((early, 0), (late, WAIT)) if ks]
-    sent = {}
-    for pack, ks in zip(packs, (early, late)):
-        for r in near + far:
-            if ks is late and r in near:
-                pack_now = after(pack, sent[r])
-            else:
-                pack_now = pack
-            sent[r] = from_offset(pack_now, offsets[r])
-            for i, k in enumerate(ks):
-                held[r][k] = (sent[r], i)
     held[0] = [(x, None) for x in own]
-
+    for k in range(groups):
+        block = own[k]
+        if k > 1:
+            passed = [held[r][k - 2][0] for r in near]
+            block = stack([after(block, *passed)], WAIT)
+        for r in near:
+            ready = after(block, held[near[0]][0][0]) if k == 1 else block
+            held[r][k] = (from_offset(ready, offsets[r]), 0 if k > 1 else None)
+    got = {r: from_offset(stack(own, 0), offsets[r]) for r in far}
     everything = [(0, 0, False)]
     everything += [(offsets.index(a), offsets.index(b), both) for a, b, both in pairs]
     steps = [[], [], []]
@@ -334,14 +336,18 @@
             for right_ks in (early, late):
                 if left_ks and right_ks:
                     step = 0
-                    if left_ks is late:
-                        step = 1 if left == 0 else 2
-                    if right_ks is late:
-                        step = max(step, 1 if right == 0 else 2)
+                    for role, ks in ((left, left_ks), (right, right_ks)):
+                        if role in far:
+                            step = max(step, 1)
+                        elif ks is late:
+                            step = max(step, 2 if role else 1)
                     steps[step].append((left, left_ks, right, right_ks, both))
     steps = [tasks for tasks in steps if tasks]
     acc = []
     for i, tasks in enumerate(steps):
+        if i == 1:
+            for r in far:
+                held[r] = [(got[r], k) for k in range(groups)]
         acc, partial = score(held, tasks, acc, i == len(steps) - 1, slots, width)
 
     others = [from_offset(partial[r], -offsets[r]) for r in range(1, roles)]
@@ -353,12 +359,12 @@
         roles * slots,
         4 * roles * slots,
     )
-    back = [best[0]] + [across(best[k], k) for k in range(1, groups)]
+    back = exchange(best)
     (result,) = call(
         lambda *refs: place_kernel(groups, *refs),
         [jax.ShapeDtypeStruct((1, rows), jnp.float32)],
         [],
-        back + [place],
+        back[::-1] + [place],
         rows * slots,
         4 * slots,
     )

time: 55.4 us -> 48.6 us (0.88)
  waiting for transfers between devices: 31.8 us -> 13 us
  starting transfers between devices: 16.2 us -> 26.9 us
  Pallas kernels: 6.53 us -> 7.7 us
    ppermute x6, waiting for transfers between devices: 17.5 us -> 5.81 us  [exchange(): got[k] = lax.ppermute(block, 'group', [(z, z ^ k) for z in range(groups)])]
    ppermute x9 -> x12, starting transfers between devices: 6.02 us -> 14.3 us  [from_offset(): return lax.ppermute(x, 'shard', perm)]
    ppermute x9 -> x12, waiting for transfers between devices: 14.3 us -> 7.24 us  [from_offset(): return lax.ppermute(x, 'shard', perm)]
    ppermute x6, starting transfers between devices: 10.1 us -> 12.5 us  [exchange(): got[k] = lax.ppermute(block, 'group', [(z, z ^ k) for z in range(groups)])]
    pallas_call x8 -> x9, Pallas kernels: 6.53 us -> 7.7 us  [call(): pl.pallas_call(kernel, out_shape=out_shape, in_specs=in_specs or in_vmem(...]
  transfers between devices with their start and end apart: 15 -> 18, of which waited for: 9 -> 10; matrix products, arithmetic and copies ran while one was open for 0% -> 0% of each run, Pallas kernels for 3% -> 7%
where the time goes in v4:
time: 48.6 us; the launch traced here: 48.4 us
  starting transfers between devices  26.9 us (55%)
  waiting for transfers between devices  13 us (27%)
  Pallas kernels  7.7 us (16%)
  other arithmetic  0.7 us (1%)
    ppermute x12, starting transfers between devices, from_offset(): return lax.ppermute(x, 'shard', perm)  14.3 us
    ppermute x6, starting transfers between devices, exchange(): got[k] = lax.ppermute(block, 'group', [(z, z ^ k) for z in range(groups)])  12.5 us
    pallas_call x9, Pallas kernels, call(): pl.pallas_call(kernel, out_shape=out_shape, in_specs=in_specs or in_vmem(...  7.7 us
    ppermute x12, waiting for transfers between devices, from_offset(): return lax.ppermute(x, 'shard', perm)  7.24 us
    ppermute x6, waiting for transfers between devices, exchange(): got[k] = lax.ppermute(block, 'group', [(z, z ^ k) for z in range(groups)])  5.81 us
  transfers between devices with their start and end apart: 18, of which 10 were waited for; matrix products, arithmetic and copies ran while one was open for 0% of the time, Pallas kernels for 7%

profile of v4, /device:TPU:0, one launch (start us, length us, event | category | flops | bytes accessed | tf_op | source)
XLA Modules:
  0.0 48.4 jit_solution(1268388855679836306)
XLA Ops:
  0.0 0.7 %multiply_add_fusion = s32[512]{0:T(512)S(1)} fusion(s32[512]{0:T(512)} %bitcast.4, s32[512]{0:T(512)} %param.5), kind=kLoop, calls=%fused_computation | loop fusion | flops 1024 | bytes 6144 | tf_op jit(solution)/shard_map/add | solution.py:298
  0.7 2.2 %shard_map.37 = (bf16[784,128]{1,0:T(8,128)(2,1)S(1)}, bf16[784,128]{1,0:T(8,128)(2,1)S(1)}, bf16[784,128]{1,0:T(8,128)(2,1)S(1)}, bf16[784,128]{1,0:T(8,128)(2,1)S(1)}, s32[1,512]{1,0:T(1,128)S(1)}) custom-call(bf16[512,768]{1,0:T(8,128)(2,1)} %refs_0_.1, s32[1,512]{1,0:T(1,128)S(1)} %bitcast.3), custom_call_target="tpu_custom_call" | custom-call | flops 402653184 | bytes 1572864 | tf_op jit(solution)/shard_map/pallas_call | solution.py:211
  2.9 3.1 %collective-permute-start = (bf16[784,128]{1,0:T(8,128)(2,1)S(1)}, bf16[784,128]{1,0:T(8,128)(2,1)S(1)}, u32[]{:S(2)}, u32[]{:S(2)}) collective-permute-start(bf16[784,128]{1,0:T(8,128)(2,1)S(1)} %get-tuple-element.27), channel_id=1, source_target_pairs={{0,1},{1,0},{2,3},{3,2},{4,5},{5,4},{6,7},{7,6},{8,9},{9,8},{10,11... | collective-permute-start | bytes 602120 | tf_op jit(solution)/shard_map/ppermute | solution.py:295
  6.0 0.7 %collective-permute-start.4 = (bf16[784,128]{1,0:T(8,128)(2,1)S(1)}, bf16[784,128]{1,0:T(8,128)(2,1)S(1)}, u32[]{:S(2)}, u32[]{:S(2)}) collective-permute-start(bf16[784,128]{1,0:T(8,128)(2,1)S(1)} %get-tuple-element.30.refs_0_.refs_2_.refs_3_), channel_id=1, source_target_pairs={{8,0},{24,8},{16,24},{4,16},{12,4},{28,12},{20,28},{0,20},{9,1},{2... | collective-permute-start | bytes 602120 | tf_op jit(solution)/shard_map/ppermute | solution.py:289
  6.7 2.6 %collective-permute-start.2 = (bf16[784,128]{1,0:T(8,128)(2,1)S(1)}, bf16[784,128]{1,0:T(8,128)(2,1)S(1)}, u32[]{:S(2)}, u32[]{:S(2)}) collective-permute-start(bf16[784,128]{1,0:T(8,128)(2,1)S(1)} %get-tuple-element.29), channel_id=1, source_target_pairs={{0,2},{1,3},{2,0},{3,1},{4,6},{5,7},{6,4},{7,5},{8,10},{9,11},{10,... | collective-permute-start | bytes 602120 | tf_op jit(solution)/shard_map/ppermute | solution.py:295
  9.3 1.3 %collective-permute-start.8 = (bf16[784,128]{1,0:T(8,128)(2,1)S(1)}, bf16[784,128]{1,0:T(8,128)(2,1)S(1)}, u32[]{:S(2)}, u32[]{:S(2)}) collective-permute-start(bf16[784,128]{1,0:T(8,128)(2,1)S(1)} %get-tuple-element.30.refs_0_.refs_2_.refs_3_), channel_id=1, source_target_pairs={{20,0},{0,8},{8,24},{24,16},{16,4},{4,12},{12,28},{28,20},{21,1},{... | collective-permute-start | bytes 602120 | tf_op jit(solution)/shard_map/ppermute | solution.py:289
  10.6 0.4 collective-permute-done.refs_1_.refs_2_
  11.0 1.5 %collective-permute-done.4.refs_5_.refs_7_.refs_8_ = bf16[784,128]{1,0:T(8,128)(2,1)S(1)} collective-permute-done((bf16[784,128]{1,0:T(8,128)(2,1)S(1)}, bf16[784,128]{1,0:T(8,128)(2,1)S(1)}, u32[]{:S(2)}, u32[]{:S(2)}) %collective-permute-start.4) | collective-permute-done | bytes 200736 | tf_op jit(solution)/shard_map/ppermute | solution.py:289
  12.5 4.1 %collective-permute-start.6 = (bf16[784,128]{1,0:T(8,128)(2,1)S(1)}, bf16[784,128]{1,0:T(8,128)(2,1)S(1)}, u32[]{:S(2)}, u32[]{:S(2)}) collective-permute-start(bf16[784,128]{1,0:T(8,128)(2,1)S(1)} %collective-permute-done.refs_1_.refs_2_), channel_id=1, source_target_pairs={{20,0},{0,8},{8,24},{24,16},{16,4},{4,12},{12,28},{28,20},{21,1},{... | collective-permute-start | bytes 602120 | tf_op jit(solution)/shard_map/ppermute | solution.py:289
  16.6 0.0 collective-permute-start.5
  16.6 2.5 %collective-permute-start.1 = (bf16[784,128]{1,0:T(8,128)(2,1)S(1)}, bf16[784,128]{1,0:T(8,128)(2,1)S(1)}, u32[]{:S(2)}, u32[]{:S(2)}) collective-permute-start(bf16[784,128]{1,0:T(8,128)(2,1)S(1)} %get-tuple-element.28), channel_id=1, source_target_pairs={{0,3},{1,2},{2,1},{3,0},{4,7},{5,6},{6,5},{7,4},{8,11},{9,10},{10,... | collective-permute-start | bytes 602120 | tf_op jit(solution)/shard_map/ppermute | solution.py:295
  19.1 0.7 %collective-permute-done.2.refs_2_.refs_0_.refs_1_ = bf16[784,128]{1,0:T(8,128)(2,1)S(1)} collective-permute-done((bf16[784,128]{1,0:T(8,128)(2,1)S(1)}, bf16[784,128]{1,0:T(8,128)(2,1)S(1)}, u32[]{:S(2)}, u32[]{:S(2)}) %collective-permute-start.2) | collective-permute-done | bytes 200736 | tf_op jit(solution)/shard_map/ppermute | solution.py:295
  19.8 0.0 collective-permute-done.8.refs_8_.refs_12_
  19.8 1.4 %collective-permute-start.11 = (bf16[1,784,128]{2,1,0:T(8,128)(2,1)S(1)}, bf16[1,784,128]{2,1,0:T(8,128)(2,1)S(1)}, u32[]{:S(2)}, u32[]{:S(2)}) collective-permute-start(bf16[1,784,128]{2,1,0:T(8,128)(2,1)S(1)} %shard_map.40), channel_id=1, source_target_pairs={{20,0},{0,8},{8,24},{24,16},{16,4},{4,12},{12,28},{28,20},{21,1},{... | collective-permute-start | bytes 602120 | tf_op jit(solution)/shard_map/ppermute | solution.py:289
  21.2 0.4 collective-permute-start.9
  21.6 2.6 %collective-permute-done.1.refs_3_.refs_0_ = bf16[784,128]{1,0:T(8,128)(2,1)S(1)} collective-permute-done((bf16[784,128]{1,0:T(8,128)(2,1)S(1)}, bf16[784,128]{1,0:T(8,128)(2,1)S(1)}, u32[]{:S(2)}, u32[]{:S(2)}) %collective-permute-start.1) | collective-permute-done | bytes 200736 | tf_op jit(solution)/shard_map/ppermute | solution.py:295
  24.2 0.0 collective-permute-done.6.refs_7_.refs_11_
  24.2 0.0 collective-permute-done.5.refs_4_.refs_6_.refs_7_
  24.2 0.1 shard_map.38
  24.3 2.0 %collective-permute-start.3 = (bf16[4,784,128]{2,1,0:T(8,128)(2,1)S(1)}, bf16[4,784,128]{2,1,0:T(8,128)(2,1)S(1)}, u32[]{:S(2)}, u32[]{:S(2)}) collective-permute-start(bf16[4,784,128]{2,1,0:T(8,128)(2,1)S(1)} %shard_map.38), channel_id=1, source_target_pairs={{4,0},{12,8},{28,24},{20,16},{0,4},{8,12},{24,28},{16,20},{5,1},{1... | collective-permute-start | bytes 2408456 | tf_op jit(solution)/shard_map/ppermute | solution.py:289
  26.2 0.2 collective-permute-start.10
  26.5 1.8 %collective-permute-start.7 = (bf16[1,784,128]{2,1,0:T(8,128)(2,1)S(1)}, bf16[1,784,128]{2,1,0:T(8,128)(2,1)S(1)}, u32[]{:S(2)}, u32[]{:S(2)}) collective-permute-start(bf16[1,784,128]{2,1,0:T(8,128)(2,1)S(1)} %shard_map.39), channel_id=1, source_target_pairs={{8,0},{24,8},{16,24},{4,16},{12,4},{28,12},{20,28},{0,20},{9,1},{2... | collective-permute-start | bytes 602120 | tf_op jit(solution)/shard_map/ppermute | solution.py:289
  28.3 0.0 collective-permute-done.11.refs_6_.refs_10_
  28.3 0.0 collective-permute-done.9.refs_3_.refs_5_.refs_6_
  28.3 1.2 %shard_map.41 = (f32[4,512,128]{2,1,0:T(8,128)S(1)}, f32[4,8,512]{2,1,0:T(8,128)S(1)}) custom-call(bf16[784,128]{1,0:T(8,128)(2,1)S(1)} %collective-permute-done.2.refs_2_.refs_0_.refs_1_, bf16[784,128]{1,0:T(8,128)(2,1)S(1)} %collective-permute-done.refs_1_.refs_2_, bf16[784,128]{1,0:T(8,128)(2,1)S(1)} %get-tuple-element.30.refs_0_.refs_2_.refs_3_, ...), custom_call_target="tpu_custom_call" | custom-call | flops 679477248 | bytes 1769472 | tf_op jit(solution)/shard_map/pallas_call | solution.py:211
  29.5 0.0 collective-permute-done.3.refs_4_
  29.5 2.0 %shard_map.42 = (f32[4,512,128]{2,1,0:T(8,128)S(1)}, f32[4,8,512]{2,1,0:T(8,128)S(1)}) custom-call(bf16[784,128]{1,0:T(8,128)(2,1)S(1)} %collective-permute-done.1.refs_3_.refs_0_, bf16[784,128]{1,0:T(8,128)(2,1)S(1)} %collective-permute-done.2.refs_2_.refs_0_.refs_1_, ...), custom_call_target="tpu_custom_call", output_to_operand_aliasing={{0}: (8, {}), {1}: (9, {})} | custom-call | flops 956301312 | bytes 2162688 | tf_op jit(solution)/shard_map/pallas_call | solution.py:211
  31.6 2.2 %collective-permute-done.10.refs_9_ = bf16[1,784,128]{2,1,0:T(8,128)(2,1)S(1)} collective-permute-done((bf16[1,784,128]{2,1,0:T(8,128)(2,1)S(1)}, bf16[1,784,128]{2,1,0:T(8,128)(2,1)S(1)}, u32[]{:S(2)}, u32[]{:S(2)}) %collective-permute-start.10) | collective-permute-done | bytes 200736 | tf_op jit(solution)/shard_map/ppermute | solution.py:289
  33.8 0.0 collective-permute-done.7.refs_5_
  33.8 1.4 %shard_map.43 = (f32[4,512,128]{2,1,0:T(8,128)S(1)}, f32[4,8,512]{2,1,0:T(8,128)S(1)}, f32[1,512]{1,0:T(1,128)S(1)}, f32[1,512]{1,0:T(1,128)S(1)}, f32[1,512]{1,0:T(1,128)S(1)}, /*index=5*/f32[1,512]{1,0:T(1,128)S(1)}) custom-call(bf16[784,128]{1,0:T(8,128)(2,1)S(1)} %collective-permute-done.1.refs_3_.refs_0_, ...), custom_call_target="tpu_custom_call", output_to_operand_aliasing={{0}: (13, {}), {1}: (14, {})} | custom-call | flops 377487360 | bytes 3145728 | tf_op jit(solution)/shard_map/pallas_call | solution.py:211
  35.2 0.2 collective-permute-start.12
  35.4 2.1 %collective-permute-start.13 = (f32[1,512]{1,0:T(1,128)S(1)}, f32[1,512]{1,0:T(1,128)S(1)}, u32[]{:S(2)}, u32[]{:S(2)}) collective-permute-start(f32[1,512]{1,0:T(1,128)S(1)} %get-tuple-element.40), channel_id=1, source_target_pairs={{20,0},{0,8},{8,24},{24,16},{16,4},{4,12},{12,28},{28,20},{21,1},{... | collective-permute-start | bytes 6152 | tf_op jit(solution)/shard_map/ppermute | solution.py:289
  37.5 0.0 collective-permute-start.14
  37.5 0.0 collective-permute-done.12.refs_1_
  37.5 1.3 %collective-permute-done.13.refs_2_ = f32[1,512]{1,0:T(1,128)S(1)} collective-permute-done((f32[1,512]{1,0:T(1,128)S(1)}, f32[1,512]{1,0:T(1,128)S(1)}, u32[]{:S(2)}, u32[]{:S(2)}) %collective-permute-start.13) | collective-permute-done | bytes 2080 | tf_op jit(solution)/shard_map/ppermute | solution.py:289
  38.8 2.3 %collective-permute-done.14.refs_3_ = f32[1,512]{1,0:T(1,128)S(1)} collective-permute-done((f32[1,512]{1,0:T(1,128)S(1)}, f32[1,512]{1,0:T(1,128)S(1)}, u32[]{:S(2)}, u32[]{:S(2)}) %collective-permute-start.14) | collective-permute-done | bytes 2080 | tf_op jit(solution)/shard_map/ppermute | solution.py:289
  41.0 1.6 %collective-permute-start.15 = (f32[1,128]{1,0:T(1,128)S(1)}, f32[1,128]{1,0:T(1,128)S(1)}, u32[]{:S(2)}, u32[]{:S(2)}) collective-permute-start(f32[1,128]{1,0:T(1,128)S(1)} %get-tuple-element.42), channel_id=1, source_target_pairs={{0,3},{1,2},{2,1},{3,0},{4,7},{5,6},{6,5},{7,4},{8,11},{9,10},{10,... | collective-permute-start | bytes 1544 | tf_op jit(solution)/shard_map/ppermute | solution.py:295
  42.7 1.4 %collective-permute-start.16 = (f32[1,128]{1,0:T(1,128)S(1)}, f32[1,128]{1,0:T(1,128)S(1)}, u32[]{:S(2)}, u32[]{:S(2)}) collective-permute-start(f32[1,128]{1,0:T(1,128)S(1)} %get-tuple-element.43), channel_id=1, source_target_pairs={{0,2},{1,3},{2,0},{3,1},{4,6},{5,7},{6,4},{7,5},{8,10},{9,11},{10,... | collective-permute-start | bytes 1544 | tf_op jit(solution)/shard_map/ppermute | solution.py:295
  44.1 1.4 %collective-permute-start.17 = (f32[1,128]{1,0:T(1,128)S(1)}, f32[1,128]{1,0:T(1,128)S(1)}, u32[]{:S(2)}, u32[]{:S(2)}) collective-permute-start(f32[1,128]{1,0:T(1,128)S(1)} %get-tuple-element.44), channel_id=1, source_target_pairs={{0,1},{1,0},{2,3},{3,2},{4,5},{5,4},{6,7},{7,6},{8,9},{9,8},{10,11... | collective-permute-start | bytes 1544 | tf_op jit(solution)/shard_map/ppermute | solution.py:295
  45.4 0.9 %collective-permute-done.15.refs_0_ = f32[1,128]{1,0:T(1,128)S(1)} collective-permute-done((f32[1,128]{1,0:T(1,128)S(1)}, f32[1,128]{1,0:T(1,128)S(1)}, u32[]{:S(2)}, u32[]{:S(2)}) %collective-permute-start.15) | collective-permute-done | bytes 544 | tf_op jit(solution)/shard_map/ppermute | solution.py:295
  46.4 0.7 %collective-permute-done.16.refs_1_ = f32[1,128]{1,0:T(1,128)S(1)} collective-permute-done((f32[1,128]{1,0:T(1,128)S(1)}, f32[1,128]{1,0:T(1,128)S(1)}, u32[]{:S(2)}, u32[]{:S(2)}) %collective-permute-start.16) | collective-permute-done | bytes 544 | tf_op jit(solution)/shard_map/ppermute | solution.py:295
  47.1 0.5 collective-permute-done.17.refs_2_
  47.6 0.8 %shard_map.45 = f32[1,512]{1,0:T(1,128)} custom-call(f32[1,128]{1,0:T(1,128)S(1)} %collective-permute-done.15.refs_0_, f32[1,128]{1,0:T(1,128)S(1)} %collective-permute-done.16.refs_1_, f32[1,128]{1,0:T(1,128)S(1)} %collective-permute-done.17.refs_2_, f32[1,128]{1,0:T(1,128)S(1)} %get-tuple-element.45.refs_3_, s32[1,512]{1,0:T(1,128)S(1)} %get-tuple-element.46.refs_4_), custom_call_target="tpu_custom_call" | custom-call | flops 262144 | bytes 2048 | tf_op jit(solution)/shard_map/pallas_call | solution.py:211
  (3 shorter events, 0.0 us)
Async XLA Ops:
  2.9 8.1 %collective-permute-start = (bf16[784,128]{1,0:T(8,128)(2,1)S(1)}, bf16[784,128]{1,0:T(8,128)(2,1)S(1)}, u32[]{:S(2)}, u32[]{:S(2)}) collective-permute-start(bf16[784,128]{1,0:T(8,128)(2,1)S(1)} %get-tuple-element.27), channel_id=1, source_target_pairs={{0,1},{1,0},{2,3},{3,2},{4,5},{5,4},{6,7},{7,6},{8,9},{9,8},{10,11... | collective-permute-start | bytes 602120 | tf_op jit(solution)/shard_map/ppermute | solution.py:295
  6.0 6.4 %collective-permute-start.4 = (bf16[784,128]{1,0:T(8,128)(2,1)S(1)}, bf16[784,128]{1,0:T(8,128)(2,1)S(1)}, u32[]{:S(2)}, u32[]{:S(2)}) collective-permute-start(bf16[784,128]{1,0:T(8,128)(2,1)S(1)} %get-tuple-element.30.refs_0_.refs_2_.refs_3_), channel_id=1, source_target_pairs={{8,0},{24,8},{16,24},{4,16},{12,4},{28,12},{20,28},{0,20},{9,1},{2... | collective-permute-start | bytes 602120 | tf_op jit(solution)/shard_map/ppermute | solution.py:289
  6.7 13.1 %collective-permute-start.2 = (bf16[784,128]{1,0:T(8,128)(2,1)S(1)}, bf16[784,128]{1,0:T(8,128)(2,1)S(1)}, u32[]{:S(2)}, u32[]{:S(2)}) collective-permute-start(bf16[784,128]{1,0:T(8,128)(2,1)S(1)} %get-tuple-element.29), channel_id=1, source_target_pairs={{0,2},{1,3},{2,0},{3,1},{4,6},{5,7},{6,4},{7,5},{8,10},{9,11},{10,... | collective-permute-start | bytes 602120 | tf_op jit(solution)/shard_map/ppermute | solution.py:295
  9.3 10.5 %collective-permute-start.8 = (bf16[784,128]{1,0:T(8,128)(2,1)S(1)}, bf16[784,128]{1,0:T(8,128)(2,1)S(1)}, u32[]{:S(2)}, u32[]{:S(2)}) collective-permute-start(bf16[784,128]{1,0:T(8,128)(2,1)S(1)} %get-tuple-element.30.refs_0_.refs_2_.refs_3_), channel_id=1, source_target_pairs={{20,0},{0,8},{8,24},{24,16},{16,4},{4,12},{12,28},{28,20},{21,1},{... | collective-permute-start | bytes 602120 | tf_op jit(solution)/shard_map/ppermute | solution.py:289
  12.5 11.7 %collective-permute-start.6 = (bf16[784,128]{1,0:T(8,128)(2,1)S(1)}, bf16[784,128]{1,0:T(8,128)(2,1)S(1)}, u32[]{:S(2)}, u32[]{:S(2)}) collective-permute-start(bf16[784,128]{1,0:T(8,128)(2,1)S(1)} %collective-permute-done.refs_1_.refs_2_), channel_id=1, source_target_pairs={{20,0},{0,8},{8,24},{24,16},{16,4},{4,12},{12,28},{28,20},{21,1},{... | collective-permute-start | bytes 602120 | tf_op jit(solution)/shard_map/ppermute | solution.py:289
  16.6 7.6 %collective-permute-start.5 = (bf16[784,128]{1,0:T(8,128)(2,1)S(1)}, bf16[784,128]{1,0:T(8,128)(2,1)S(1)}, u32[]{:S(2)}, u32[]{:S(2)}) collective-permute-start(bf16[784,128]{1,0:T(8,128)(2,1)S(1)} %collective-permute-done.refs_1_.refs_2_), channel_id=1, source_target_pairs={{8,0},{24,8},{16,24},{4,16},{12,4},{28,12},{20,28},{0,20},{9,1},{2... | collective-permute-start | bytes 602120 | tf_op jit(solution)/shard_map/ppermute | solution.py:289
  16.6 7.6 %collective-permute-start.1 = (bf16[784,128]{1,0:T(8,128)(2,1)S(1)}, bf16[784,128]{1,0:T(8,128)(2,1)S(1)}, u32[]{:S(2)}, u32[]{:S(2)}) collective-permute-start(bf16[784,128]{1,0:T(8,128)(2,1)S(1)} %get-tuple-element.28), channel_id=1, source_target_pairs={{0,3},{1,2},{2,1},{3,0},{4,7},{5,6},{6,5},{7,4},{8,11},{9,10},{10,... | collective-permute-start | bytes 602120 | tf_op jit(solution)/shard_map/ppermute | solution.py:295
  19.8 8.5 %collective-permute-start.11 = (bf16[1,784,128]{2,1,0:T(8,128)(2,1)S(1)}, bf16[1,784,128]{2,1,0:T(8,128)(2,1)S(1)}, u32[]{:S(2)}, u32[]{:S(2)}) collective-permute-start(bf16[1,784,128]{2,1,0:T(8,128)(2,1)S(1)} %shard_map.40), channel_id=1, source_target_pairs={{20,0},{0,8},{8,24},{24,16},{16,4},{4,12},{12,28},{28,20},{21,1},{... | collective-permute-start | bytes 602120 | tf_op jit(solution)/shard_map/ppermute | solution.py:289
  21.2 7.1 %collective-permute-start.9 = (bf16[1,784,128]{2,1,0:T(8,128)(2,1)S(1)}, bf16[1,784,128]{2,1,0:T(8,128)(2,1)S(1)}, u32[]{:S(2)}, u32[]{:S(2)}) collective-permute-start(bf16[1,784,128]{2,1,0:T(8,128)(2,1)S(1)} %shard_map.40), channel_id=1, source_target_pairs={{8,0},{24,8},{16,24},{4,16},{12,4},{28,12},{20,28},{0,20},{9,1},{2... | collective-permute-start | bytes 602120 | tf_op jit(solution)/shard_map/ppermute | solution.py:289
  24.3 5.3 %collective-permute-start.3 = (bf16[4,784,128]{2,1,0:T(8,128)(2,1)S(1)}, bf16[4,784,128]{2,1,0:T(8,128)(2,1)S(1)}, u32[]{:S(2)}, u32[]{:S(2)}) collective-permute-start(bf16[4,784,128]{2,1,0:T(8,128)(2,1)S(1)} %shard_map.38), channel_id=1, source_target_pairs={{4,0},{12,8},{28,24},{20,16},{0,4},{8,12},{24,28},{16,20},{5,1},{1... | collective-permute-start | bytes 2408456 | tf_op jit(solution)/shard_map/ppermute | solution.py:289
  26.2 7.5 %collective-permute-start.10 = (bf16[1,784,128]{2,1,0:T(8,128)(2,1)S(1)}, bf16[1,784,128]{2,1,0:T(8,128)(2,1)S(1)}, u32[]{:S(2)}, u32[]{:S(2)}) collective-permute-start(bf16[1,784,128]{2,1,0:T(8,128)(2,1)S(1)} %shard_map.39), channel_id=1, source_target_pairs={{20,0},{0,8},{8,24},{24,16},{16,4},{4,12},{12,28},{28,20},{21,1},{... | collective-permute-start | bytes 602120 | tf_op jit(solution)/shard_map/ppermute | solution.py:289
  26.5 7.3 %collective-permute-start.7 = (bf16[1,784,128]{2,1,0:T(8,128)(2,1)S(1)}, bf16[1,784,128]{2,1,0:T(8,128)(2,1)S(1)}, u32[]{:S(2)}, u32[]{:S(2)}) collective-permute-start(bf16[1,784,128]{2,1,0:T(8,128)(2,1)S(1)} %shard_map.39), channel_id=1, source_target_pairs={{8,0},{24,8},{16,24},{4,16},{12,4},{28,12},{20,28},{0,20},{9,1},{2... | collective-permute-start | bytes 602120 | tf_op jit(solution)/shard_map/ppermute | solution.py:289
  35.2 2.3 %collective-permute-start.12 = (f32[1,512]{1,0:T(1,128)S(1)}, f32[1,512]{1,0:T(1,128)S(1)}, u32[]{:S(2)}, u32[]{:S(2)}) collective-permute-start(f32[1,512]{1,0:T(1,128)S(1)} %get-tuple-element.39), channel_id=1, source_target_pairs={{4,0},{12,8},{28,24},{20,16},{0,4},{8,12},{24,28},{16,20},{5,1},{1... | collective-permute-start | bytes 6152 | tf_op jit(solution)/shard_map/ppermute | solution.py:289
  35.4 3.4 %collective-permute-start.13 = (f32[1,512]{1,0:T(1,128)S(1)}, f32[1,512]{1,0:T(1,128)S(1)}, u32[]{:S(2)}, u32[]{:S(2)}) collective-permute-start(f32[1,512]{1,0:T(1,128)S(1)} %get-tuple-element.40), channel_id=1, source_target_pairs={{20,0},{0,8},{8,24},{24,16},{16,4},{4,12},{12,28},{28,20},{21,1},{... | collective-permute-start | bytes 6152 | tf_op jit(solution)/shard_map/ppermute | solution.py:289
  37.5 3.6 %collective-permute-start.14 = (f32[1,512]{1,0:T(1,128)S(1)}, f32[1,512]{1,0:T(1,128)S(1)}, u32[]{:S(2)}, u32[]{:S(2)}) collective-permute-start(f32[1,512]{1,0:T(1,128)S(1)} %get-tuple-element.41), channel_id=1, source_target_pairs={{8,0},{24,8},{16,24},{4,16},{12,4},{28,12},{20,28},{0,20},{9,1},{2... | collective-permute-start | bytes 6152 | tf_op jit(solution)/shard_map/ppermute | solution.py:289
  41.0 5.3 %collective-permute-start.15 = (f32[1,128]{1,0:T(1,128)S(1)}, f32[1,128]{1,0:T(1,128)S(1)}, u32[]{:S(2)}, u32[]{:S(2)}) collective-permute-start(f32[1,128]{1,0:T(1,128)S(1)} %get-tuple-element.42), channel_id=1, source_target_pairs={{0,3},{1,2},{2,1},{3,0},{4,7},{5,6},{6,5},{7,4},{8,11},{9,10},{10,... | collective-permute-start | bytes 1544 | tf_op jit(solution)/shard_map/ppermute | solution.py:295
  42.7 4.4 %collective-permute-start.16 = (f32[1,128]{1,0:T(1,128)S(1)}, f32[1,128]{1,0:T(1,128)S(1)}, u32[]{:S(2)}, u32[]{:S(2)}) collective-permute-start(f32[1,128]{1,0:T(1,128)S(1)} %get-tuple-element.43), channel_id=1, source_target_pairs={{0,2},{1,3},{2,0},{3,1},{4,6},{5,7},{6,4},{7,5},{8,10},{9,11},{10,... | collective-permute-start | bytes 1544 | tf_op jit(solution)/shard_map/ppermute | solution.py:295
  44.1 3.5 %collective-permute-start.17 = (f32[1,128]{1,0:T(1,128)S(1)}, f32[1,128]{1,0:T(1,128)S(1)}, u32[]{:S(2)}, u32[]{:S(2)}) collective-permute-start(f32[1,128]{1,0:T(1,128)S(1)} %get-tuple-element.44), channel_id=1, source_target_pairs={{0,1},{1,0},{2,3},{3,2},{4,5},{5,4},{6,7},{7,6},{8,9},{9,8},{10,11... | collective-permute-start | bytes 1544 | tf_op jit(solution)/shard_map/ppermute | solution.py:295

commit v5 on v4

--- a/solution.py
+++ b/solution.py
@@ -288,10 +288,10 @@
         perm = [(ring[(e + offset) % shards], ring[e]) for e in range(shards)]
         return lax.ppermute(x, "shard", perm)
 
-    def exchange(blocks, stagger=False):
+    def exchange(blocks, last=()):
         got = list(blocks)
         for k in range(1, groups):
-            block = after(blocks[k], got[1]) if k > 2 and stagger else blocks[k]
+            block = after(blocks[k], *last) if k == groups - 1 else blocks[k]
             got[k] = lax.ppermute(block, "group", [(z, z ^ k) for z in range(groups)])
         return got
 
@@ -316,17 +316,20 @@
     early = list(range(groups - len(late)))
     near = [r for r in range(1, roles) if 2 * offsets[r] != shards]
     far = [r for r in range(1, roles) if r not in near]
-    own = exchange(send, True)
+    first = {r: from_offset(send[0], offsets[r]) for r in near}
+    own = exchange(send, [first[r] for r in near[:1]])
     held = [[None] * groups for _ in offsets]
     held[0] = [(x, None) for x in own]
-    for k in range(groups):
-        block = own[k]
-        if k > 1:
-            passed = [held[r][k - 2][0] for r in near]
-            block = stack([after(block, *passed)], WAIT)
-        for r in near:
-            ready = after(block, held[near[0]][0][0]) if k == 1 else block
-            held[r][k] = (from_offset(ready, offsets[r]), 0 if k > 1 else None)
+    for r in near:
+        held[r][0] = (first[r], None)
+    for ks, wait in ((early[1:], WAIT), (late, WAIT)):
+        if ks:
+            passed = []
+            block = stack([after(own[k], *passed) for k in ks], wait)
+            for r in near:
+                got = from_offset(block, offsets[r])
+                for i, k in enumerate(ks):
+                    held[r][k] = (got, i)
     got = {r: from_offset(stack(own, 0), offsets[r]) for r in far}
     everything = [(0, 0, False)]
     everything += [(offsets.index(a), offsets.index(b), both) for a, b, both in pairs]

time: 48.6 us -> 50.8 us (1.045)
  waiting for transfers between devices: 13 us -> 18.5 us
  starting transfers between devices: 26.9 us -> 23.7 us
    ppermute x12 -> x10, starting transfers between devices: 14.3 us -> 11.3 us  [from_offset(): return lax.ppermute(x, 'shard', perm)]
    ppermute x12 -> x10, waiting for transfers between devices: 7.24 us -> 9.95 us  [from_offset(): return lax.ppermute(x, 'shard', perm)]
    ppermute x6, waiting for transfers between devices: 5.81 us -> 8.51 us  [exchange(): got[k] = lax.ppermute(block, 'group', [(z, z ^ k) for z in range(groups)])]
  transfers between devices with their start and end apart: 18 -> 16, of which waited for: 10 -> 9; matrix products, arithmetic and copies ran while one was open for 0% -> 0% of each run, Pallas kernels for 7% -> 7%
where the time goes in v5:
time: 50.8 us; the launch traced here: 50.6 us
  starting transfers between devices  23.7 us (47%)
  waiting for transfers between devices  18.5 us (36%)
  Pallas kernels  7.72 us (15%)
  other arithmetic  0.7 us (1%)
    ppermute x6, starting transfers between devices, exchange(): got[k] = lax.ppermute(block, 'group', [(z, z ^ k) for z in range(groups)])  12.4 us
    ppermute x10, starting transfers between devices, from_offset(): return lax.ppermute(x, 'shard', perm)  11.3 us
    ppermute x10, waiting for transfers between devices, from_offset(): return lax.ppermute(x, 'shard', perm)  9.95 us
    ppermute x6, waiting for transfers between devices, exchange(): got[k] = lax.ppermute(block, 'group', [(z, z ^ k) for z in range(groups)])  8.51 us
    pallas_call x9, Pallas kernels, call(): pl.pallas_call(kernel, out_shape=out_shape, in_specs=in_specs or in_vmem(...  7.72 us
  transfers between devices with their start and end apart: 16, of which 9 were waited for; matrix products, arithmetic and copies ran while one was open for 0% of the time, Pallas kernels for 7%

profile of v5, /device:TPU:0, one launch (start us, length us, event | category | flops | bytes accessed | tf_op | source)
XLA Modules:
  0.0 50.6 jit_solution(13067658306095750888)
XLA Ops:
  0.0 0.7 %multiply_add_fusion = s32[512]{0:T(512)S(1)} fusion(s32[512]{0:T(512)} %bitcast.4, s32[512]{0:T(512)} %param.5), kind=kLoop, calls=%fused_computation | loop fusion | flops 1024 | bytes 6144 | tf_op jit(solution)/shard_map/add | solution.py:298
  0.7 2.2 %shard_map.37 = (bf16[784,128]{1,0:T(8,128)(2,1)S(1)}, bf16[784,128]{1,0:T(8,128)(2,1)S(1)}, bf16[784,128]{1,0:T(8,128)(2,1)S(1)}, bf16[784,128]{1,0:T(8,128)(2,1)S(1)}, s32[1,512]{1,0:T(1,128)S(1)}) custom-call(bf16[512,768]{1,0:T(8,128)(2,1)} %refs_0_.1, s32[1,512]{1,0:T(1,128)S(1)} %bitcast.3), custom_call_target="tpu_custom_call" | custom-call | flops 402653184 | bytes 1572864 | tf_op jit(solution)/shard_map/pallas_call | solution.py:211
  2.9 2.5 %collective-permute-start = (bf16[784,128]{1,0:T(8,128)(2,1)S(1)}, bf16[784,128]{1,0:T(8,128)(2,1)S(1)}, u32[]{:S(2)}, u32[]{:S(2)}) collective-permute-start(bf16[784,128]{1,0:T(8,128)(2,1)S(1)} %get-tuple-element.24.refs_0_.refs_2_.refs_3_), channel_id=1, source_target_pairs={{8,0},{24,8},{16,24},{4,16},{12,4},{28,12},{20,28},{0,20},{9,1},{2... | collective-permute-start | bytes 602120 | tf_op jit(solution)/shard_map/ppermute | solution.py:289
  5.4 2.6 %collective-permute-start.2 = (bf16[784,128]{1,0:T(8,128)(2,1)S(1)}, bf16[784,128]{1,0:T(8,128)(2,1)S(1)}, u32[]{:S(2)}, u32[]{:S(2)}) collective-permute-start(bf16[784,128]{1,0:T(8,128)(2,1)S(1)} %get-tuple-element.26), channel_id=1, source_target_pairs={{0,2},{1,3},{2,0},{3,1},{4,6},{5,7},{6,4},{7,5},{8,10},{9,11},{10,... | collective-permute-start | bytes 602120 | tf_op jit(solution)/shard_map/ppermute | solution.py:295
  8.0 1.6 %collective-permute-start.3 = (bf16[784,128]{1,0:T(8,128)(2,1)S(1)}, bf16[784,128]{1,0:T(8,128)(2,1)S(1)}, u32[]{:S(2)}, u32[]{:S(2)}) collective-permute-start(bf16[784,128]{1,0:T(8,128)(2,1)S(1)} %get-tuple-element.27), channel_id=1, source_target_pairs={{0,1},{1,0},{2,3},{3,2},{4,5},{5,4},{6,7},{7,6},{8,9},{9,8},{10,11... | collective-permute-start | bytes 602120 | tf_op jit(solution)/shard_map/ppermute | solution.py:295
  9.6 1.1 %collective-permute-start.9 = (bf16[784,128]{1,0:T(8,128)(2,1)S(1)}, bf16[784,128]{1,0:T(8,128)(2,1)S(1)}, u32[]{:S(2)}, u32[]{:S(2)}) collective-permute-start(bf16[784,128]{1,0:T(8,128)(2,1)S(1)} %get-tuple-element.24.refs_0_.refs_2_.refs_3_), channel_id=1, source_target_pairs={{20,0},{0,8},{8,24},{24,16},{16,4},{4,12},{12,28},{28,20},{21,1},{... | collective-permute-start | bytes 602120 | tf_op jit(solution)/shard_map/ppermute | solution.py:289
  10.6 0.3 collective-permute-done.refs_4_.refs_6_.refs_7_
  10.9 3.8 %collective-permute-start.1 = (bf16[784,128]{1,0:T(8,128)(2,1)S(1)}, bf16[784,128]{1,0:T(8,128)(2,1)S(1)}, u32[]{:S(2)}, u32[]{:S(2)}) collective-permute-start(bf16[784,128]{1,0:T(8,128)(2,1)S(1)} %get-tuple-element.25), channel_id=1, source_target_pairs={{0,3},{1,2},{2,1},{3,0},{4,7},{5,6},{6,5},{7,4},{8,11},{9,10},{10,... | collective-permute-start | bytes 602120 | tf_op jit(solution)/shard_map/ppermute | solution.py:295
  14.8 3.7 %collective-permute-done.2.refs_2_.refs_1_.refs_0_ = bf16[784,128]{1,0:T(8,128)(2,1)S(1)} collective-permute-done((bf16[784,128]{1,0:T(8,128)(2,1)S(1)}, bf16[784,128]{1,0:T(8,128)(2,1)S(1)}, u32[]{:S(2)}, u32[]{:S(2)}) %collective-permute-start.2) | collective-permute-done | bytes 200736 | tf_op jit(solution)/shard_map/ppermute | solution.py:295
  18.5 0.0 collective-permute-done.3.refs_1_.refs_0_.refs_2_
  18.5 2.2 %collective-permute-start.8 = (bf16[2,784,128]{2,1,0:T(8,128)(2,1)S(1)}, bf16[2,784,128]{2,1,0:T(8,128)(2,1)S(1)}, u32[]{:S(2)}, u32[]{:S(2)}) collective-permute-start(bf16[2,784,128]{2,1,0:T(8,128)(2,1)S(1)} %shard_map.40), channel_id=1, source_target_pairs={{20,0},{0,8},{8,24},{24,16},{16,4},{4,12},{12,28},{28,20},{21,1},{... | collective-permute-start | bytes 1204232 | tf_op jit(solution)/shard_map/ppermute | solution.py:289
  20.7 0.0 collective-permute-start.6
  20.7 2.9 %collective-permute-done.1.refs_3_.refs_0_ = bf16[784,128]{1,0:T(8,128)(2,1)S(1)} collective-permute-done((bf16[784,128]{1,0:T(8,128)(2,1)S(1)}, bf16[784,128]{1,0:T(8,128)(2,1)S(1)}, u32[]{:S(2)}, u32[]{:S(2)}) %collective-permute-start.1) | collective-permute-done | bytes 200736 | tf_op jit(solution)/shard_map/ppermute | solution.py:295
  23.6 0.1 shard_map.38
  23.7 1.3 %collective-permute-start.4 = (bf16[4,784,128]{2,1,0:T(8,128)(2,1)S(1)}, bf16[4,784,128]{2,1,0:T(8,128)(2,1)S(1)}, u32[]{:S(2)}, u32[]{:S(2)}) collective-permute-start(bf16[4,784,128]{2,1,0:T(8,128)(2,1)S(1)} %shard_map.38), channel_id=1, source_target_pairs={{4,0},{12,8},{28,24},{20,16},{0,4},{8,12},{24,28},{16,20},{5,1},{1... | collective-permute-start | bytes 2408456 | tf_op jit(solution)/shard_map/ppermute | solution.py:289
  25.0 0.4 collective-permute-start.7
  25.4 0.0 collective-permute-done.9.refs_6_.refs_10_
  25.4 1.7 %collective-permute-start.5 = (bf16[1,784,128]{2,1,0:T(8,128)(2,1)S(1)}, bf16[1,784,128]{2,1,0:T(8,128)(2,1)S(1)}, u32[]{:S(2)}, u32[]{:S(2)}) collective-permute-start(bf16[1,784,128]{2,1,0:T(8,128)(2,1)S(1)} %shard_map.39), channel_id=1, source_target_pairs={{8,0},{24,8},{16,24},{4,16},{12,4},{28,12},{20,28},{0,20},{9,1},{2... | collective-permute-start | bytes 602120 | tf_op jit(solution)/shard_map/ppermute | solution.py:289
  27.1 1.1 %collective-permute-done.8.refs_5_.refs_9_ = bf16[2,784,128]{2,1,0:T(8,128)(2,1)S(1)} collective-permute-done((bf16[2,784,128]{2,1,0:T(8,128)(2,1)S(1)}, bf16[2,784,128]{2,1,0:T(8,128)(2,1)S(1)}, u32[]{:S(2)}, u32[]{:S(2)}) %collective-permute-start.8) | collective-permute-done | bytes 401440 | tf_op jit(solution)/shard_map/ppermute | solution.py:289
  28.2 5.0 %collective-permute-done.6.refs_3_.refs_5_.refs_6_ = bf16[2,784,128]{2,1,0:T(8,128)(2,1)S(1)} collective-permute-done((bf16[2,784,128]{2,1,0:T(8,128)(2,1)S(1)}, bf16[2,784,128]{2,1,0:T(8,128)(2,1)S(1)}, u32[]{:S(2)}, u32[]{:S(2)}) %collective-permute-start.6) | collective-permute-done | bytes 401440 | tf_op jit(solution)/shard_map/ppermute | solution.py:289
  33.2 1.2 %shard_map.41 = (f32[4,512,128]{2,1,0:T(8,128)S(1)}, f32[4,8,512]{2,1,0:T(8,128)S(1)}) custom-call(bf16[784,128]{1,0:T(8,128)(2,1)S(1)} %collective-permute-done.2.refs_2_.refs_1_.refs_0_, bf16[784,128]{1,0:T(8,128)(2,1)S(1)} %collective-permute-done.3.refs_1_.refs_0_.refs_2_, bf16[784,128]{1,0:T(8,128)(2,1)S(1)} %get-tuple-element.24.refs_0_.refs_2_.refs_3_, ...), custom_call_target="tpu_custom_call" | custom-call | flops 679477248 | bytes 1769472 | tf_op jit(solution)/shard_map/pallas_call | solution.py:211
  34.3 0.0 collective-permute-done.4.refs_4_
  34.3 2.0 %shard_map.42 = (f32[4,512,128]{2,1,0:T(8,128)S(1)}, f32[4,8,512]{2,1,0:T(8,128)S(1)}) custom-call(bf16[784,128]{1,0:T(8,128)(2,1)S(1)} %collective-permute-done.1.refs_3_.refs_0_, bf16[784,128]{1,0:T(8,128)(2,1)S(1)} %collective-permute-done.2.refs_2_.refs_1_.refs_0_, ...), custom_call_target="tpu_custom_call", output_to_operand_aliasing={{0}: (7, {}), {1}: (8, {})} | custom-call | flops 956301312 | bytes 2162688 | tf_op jit(solution)/shard_map/pallas_call | solution.py:211
  36.4 0.0 collective-permute-done.7.refs_8_
  36.4 0.0 collective-permute-done.5.refs_5_
  36.4 1.4 %shard_map.43 = (f32[4,512,128]{2,1,0:T(8,128)S(1)}, f32[4,8,512]{2,1,0:T(8,128)S(1)}, f32[1,512]{1,0:T(1,128)S(1)}, f32[1,512]{1,0:T(1,128)S(1)}, f32[1,512]{1,0:T(1,128)S(1)}, /*index=5*/f32[1,512]{1,0:T(1,128)S(1)}) custom-call(bf16[784,128]{1,0:T(8,128)(2,1)S(1)} %collective-permute-done.1.refs_3_.refs_0_, ...), custom_call_target="tpu_custom_call", output_to_operand_aliasing={{0}: (11, {}), {1}: (12, {})} | custom-call | flops 377487360 | bytes 3145728 | tf_op jit(solution)/shard_map/pallas_call | solution.py:211
  37.8 0.1 collective-permute-start.10
  37.9 2.1 %collective-permute-start.11 = (f32[1,512]{1,0:T(1,128)S(1)}, f32[1,512]{1,0:T(1,128)S(1)}, u32[]{:S(2)}, u32[]{:S(2)}) collective-permute-start(f32[1,512]{1,0:T(1,128)S(1)} %get-tuple-element.34), channel_id=1, source_target_pairs={{20,0},{0,8},{8,24},{24,16},{16,4},{4,12},{12,28},{28,20},{21,1},{... | collective-permute-start | bytes 6152 | tf_op jit(solution)/shard_map/ppermute | solution.py:289
  40.0 0.0 collective-permute-start.12
  40.0 0.0 collective-permute-done.10.refs_1_
  40.0 1.3 %collective-permute-done.11.refs_2_ = f32[1,512]{1,0:T(1,128)S(1)} collective-permute-done((f32[1,512]{1,0:T(1,128)S(1)}, f32[1,512]{1,0:T(1,128)S(1)}, u32[]{:S(2)}, u32[]{:S(2)}) %collective-permute-start.11) | collective-permute-done | bytes 2080 | tf_op jit(solution)/shard_map/ppermute | solution.py:289
  41.3 2.3 %collective-permute-done.12.refs_3_ = f32[1,512]{1,0:T(1,128)S(1)} collective-permute-done((f32[1,512]{1,0:T(1,128)S(1)}, f32[1,512]{1,0:T(1,128)S(1)}, u32[]{:S(2)}, u32[]{:S(2)}) %collective-permute-start.12) | collective-permute-done | bytes 2080 | tf_op jit(solution)/shard_map/ppermute | solution.py:289
  43.6 1.8 %collective-permute-start.13 = (f32[1,128]{1,0:T(1,128)S(1)}, f32[1,128]{1,0:T(1,128)S(1)}, u32[]{:S(2)}, u32[]{:S(2)}) collective-permute-start(f32[1,128]{1,0:T(1,128)S(1)} %get-tuple-element.36), channel_id=1, source_target_pairs={{0,3},{1,2},{2,1},{3,0},{4,7},{5,6},{6,5},{7,4},{8,11},{9,10},{10,... | collective-permute-start | bytes 1544 | tf_op jit(solution)/shard_map/ppermute | solution.py:295
  45.4 0.0 collective-permute-start.14
  45.4 2.6 %collective-permute-start.15 = (f32[1,128]{1,0:T(1,128)S(1)}, f32[1,128]{1,0:T(1,128)S(1)}, u32[]{:S(2)}, u32[]{:S(2)}) collective-permute-start(f32[1,128]{1,0:T(1,128)S(1)} %get-tuple-element.38), channel_id=1, source_target_pairs={{0,1},{1,0},{2,3},{3,2},{4,5},{5,4},{6,7},{7,6},{8,9},{9,8},{10,11... | collective-permute-start | bytes 1544 | tf_op jit(solution)/shard_map/ppermute | solution.py:295
  48.0 0.9 %collective-permute-done.13.refs_0_ = f32[1,128]{1,0:T(1,128)S(1)} collective-permute-done((f32[1,128]{1,0:T(1,128)S(1)}, f32[1,128]{1,0:T(1,128)S(1)}, u32[]{:S(2)}, u32[]{:S(2)}) %collective-permute-start.13) | collective-permute-done | bytes 544 | tf_op jit(solution)/shard_map/ppermute | solution.py:295
  48.9 0.9 %collective-permute-done.14.refs_1_ = f32[1,128]{1,0:T(1,128)S(1)} collective-permute-done((f32[1,128]{1,0:T(1,128)S(1)}, f32[1,128]{1,0:T(1,128)S(1)}, u32[]{:S(2)}, u32[]{:S(2)}) %collective-permute-start.14) | collective-permute-done | bytes 544 | tf_op jit(solution)/shard_map/ppermute | solution.py:295
  49.8 0.0 collective-permute-done.15.refs_2_
  49.8 0.8 %shard_map.45 = f32[1,512]{1,0:T(1,128)} custom-call(f32[1,128]{1,0:T(1,128)S(1)} %collective-permute-done.13.refs_0_, f32[1,128]{1,0:T(1,128)S(1)} %collective-permute-done.14.refs_1_, f32[1,128]{1,0:T(1,128)S(1)} %collective-permute-done.15.refs_2_, f32[1,128]{1,0:T(1,128)S(1)} %get-tuple-element.39.refs_3_, s32[1,512]{1,0:T(1,128)S(1)} %get-tuple-element.40.refs_4_), custom_call_target="tpu_custom_call" | custom-call | flops 262144 | bytes 2048 | tf_op jit(solution)/shard_map/pallas_call | solution.py:211
  (3 shorter events, 0.0 us)
Async XLA Ops:
  2.9 8.0 %collective-permute-start = (bf16[784,128]{1,0:T(8,128)(2,1)S(1)}, bf16[784,128]{1,0:T(8,128)(2,1)S(1)}, u32[]{:S(2)}, u32[]{:S(2)}) collective-permute-start(bf16[784,128]{1,0:T(8,128)(2,1)S(1)} %get-tuple-element.24.refs_0_.refs_2_.refs_3_), channel_id=1, source_target_pairs={{8,0},{24,8},{16,24},{4,16},{12,4},{28,12},{20,28},{0,20},{9,1},{2... | collective-permute-start | bytes 602120 | tf_op jit(solution)/shard_map/ppermute | solution.py:289
  5.4 13.1 %collective-permute-start.2 = (bf16[784,128]{1,0:T(8,128)(2,1)S(1)}, bf16[784,128]{1,0:T(8,128)(2,1)S(1)}, u32[]{:S(2)}, u32[]{:S(2)}) collective-permute-start(bf16[784,128]{1,0:T(8,128)(2,1)S(1)} %get-tuple-element.26), channel_id=1, source_target_pairs={{0,2},{1,3},{2,0},{3,1},{4,6},{5,7},{6,4},{7,5},{8,10},{9,11},{10,... | collective-permute-start | bytes 602120 | tf_op jit(solution)/shard_map/ppermute | solution.py:295
  8.0 10.5 %collective-permute-start.3 = (bf16[784,128]{1,0:T(8,128)(2,1)S(1)}, bf16[784,128]{1,0:T(8,128)(2,1)S(1)}, u32[]{:S(2)}, u32[]{:S(2)}) collective-permute-start(bf16[784,128]{1,0:T(8,128)(2,1)S(1)} %get-tuple-element.27), channel_id=1, source_target_pairs={{0,1},{1,0},{2,3},{3,2},{4,5},{5,4},{6,7},{7,6},{8,9},{9,8},{10,11... | collective-permute-start | bytes 602120 | tf_op jit(solution)/shard_map/ppermute | solution.py:295
  9.6 15.8 %collective-permute-start.9 = (bf16[784,128]{1,0:T(8,128)(2,1)S(1)}, bf16[784,128]{1,0:T(8,128)(2,1)S(1)}, u32[]{:S(2)}, u32[]{:S(2)}) collective-permute-start(bf16[784,128]{1,0:T(8,128)(2,1)S(1)} %get-tuple-element.24.refs_0_.refs_2_.refs_3_), channel_id=1, source_target_pairs={{20,0},{0,8},{8,24},{24,16},{16,4},{4,12},{12,28},{28,20},{21,1},{... | collective-permute-start | bytes 602120 | tf_op jit(solution)/shard_map/ppermute | solution.py:289
  10.9 12.7 %collective-permute-start.1 = (bf16[784,128]{1,0:T(8,128)(2,1)S(1)}, bf16[784,128]{1,0:T(8,128)(2,1)S(1)}, u32[]{:S(2)}, u32[]{:S(2)}) collective-permute-start(bf16[784,128]{1,0:T(8,128)(2,1)S(1)} %get-tuple-element.25), channel_id=1, source_target_pairs={{0,3},{1,2},{2,1},{3,0},{4,7},{5,6},{6,5},{7,4},{8,11},{9,10},{10,... | collective-permute-start | bytes 602120 | tf_op jit(solution)/shard_map/ppermute | solution.py:295
  18.5 9.7 %collective-permute-start.8 = (bf16[2,784,128]{2,1,0:T(8,128)(2,1)S(1)}, bf16[2,784,128]{2,1,0:T(8,128)(2,1)S(1)}, u32[]{:S(2)}, u32[]{:S(2)}) collective-permute-start(bf16[2,784,128]{2,1,0:T(8,128)(2,1)S(1)} %shard_map.40), channel_id=1, source_target_pairs={{20,0},{0,8},{8,24},{24,16},{16,4},{4,12},{12,28},{28,20},{21,1},{... | collective-permute-start | bytes 1204232 | tf_op jit(solution)/shard_map/ppermute | solution.py:289
  20.7 12.4 %collective-permute-start.6 = (bf16[2,784,128]{2,1,0:T(8,128)(2,1)S(1)}, bf16[2,784,128]{2,1,0:T(8,128)(2,1)S(1)}, u32[]{:S(2)}, u32[]{:S(2)}) collective-permute-start(bf16[2,784,128]{2,1,0:T(8,128)(2,1)S(1)} %shard_map.40), channel_id=1, source_target_pairs={{8,0},{24,8},{16,24},{4,16},{12,4},{28,12},{20,28},{0,20},{9,1},{2... | collective-permute-start | bytes 1204232 | tf_op jit(solution)/shard_map/ppermute | solution.py:289
  23.7 10.6 %collective-permute-start.4 = (bf16[4,784,128]{2,1,0:T(8,128)(2,1)S(1)}, bf16[4,784,128]{2,1,0:T(8,128)(2,1)S(1)}, u32[]{:S(2)}, u32[]{:S(2)}) collective-permute-start(bf16[4,784,128]{2,1,0:T(8,128)(2,1)S(1)} %shard_map.38), channel_id=1, source_target_pairs={{4,0},{12,8},{28,24},{20,16},{0,4},{8,12},{24,28},{16,20},{5,1},{1... | collective-permute-start | bytes 2408456 | tf_op jit(solution)/shard_map/ppermute | solution.py:289
  25.0 11.4 %collective-permute-start.7 = (bf16[1,784,128]{2,1,0:T(8,128)(2,1)S(1)}, bf16[1,784,128]{2,1,0:T(8,128)(2,1)S(1)}, u32[]{:S(2)}, u32[]{:S(2)}) collective-permute-start(bf16[1,784,128]{2,1,0:T(8,128)(2,1)S(1)} %shard_map.39), channel_id=1, source_target_pairs={{20,0},{0,8},{8,24},{24,16},{16,4},{4,12},{12,28},{28,20},{21,1},{... | collective-permute-start | bytes 602120 | tf_op jit(solution)/shard_map/ppermute | solution.py:289
  25.4 11.0 %collective-permute-start.5 = (bf16[1,784,128]{2,1,0:T(8,128)(2,1)S(1)}, bf16[1,784,128]{2,1,0:T(8,128)(2,1)S(1)}, u32[]{:S(2)}, u32[]{:S(2)}) collective-permute-start(bf16[1,784,128]{2,1,0:T(8,128)(2,1)S(1)} %shard_map.39), channel_id=1, source_target_pairs={{8,0},{24,8},{16,24},{4,16},{12,4},{28,12},{20,28},{0,20},{9,1},{2... | collective-permute-start | bytes 602120 | tf_op jit(solution)/shard_map/ppermute | solution.py:289
  37.8 2.2 %collective-permute-start.10 = (f32[1,512]{1,0:T(1,128)S(1)}, f32[1,512]{1,0:T(1,128)S(1)}, u32[]{:S(2)}, u32[]{:S(2)}) collective-permute-start(f32[1,512]{1,0:T(1,128)S(1)} %get-tuple-element.33), channel_id=1, source_target_pairs={{4,0},{12,8},{28,24},{20,16},{0,4},{8,12},{24,28},{16,20},{5,1},{1... | collective-permute-start | bytes 6152 | tf_op jit(solution)/shard_map/ppermute | solution.py:289
  37.9 3.4 %collective-permute-start.11 = (f32[1,512]{1,0:T(1,128)S(1)}, f32[1,512]{1,0:T(1,128)S(1)}, u32[]{:S(2)}, u32[]{:S(2)}) collective-permute-start(f32[1,512]{1,0:T(1,128)S(1)} %get-tuple-element.34), channel_id=1, source_target_pairs={{20,0},{0,8},{8,24},{24,16},{16,4},{4,12},{12,28},{28,20},{21,1},{... | collective-permute-start | bytes 6152 | tf_op jit(solution)/shard_map/ppermute | solution.py:289
  40.0 3.6 %collective-permute-start.12 = (f32[1,512]{1,0:T(1,128)S(1)}, f32[1,512]{1,0:T(1,128)S(1)}, u32[]{:S(2)}, u32[]{:S(2)}) collective-permute-start(f32[1,512]{1,0:T(1,128)S(1)} %get-tuple-element.35), channel_id=1, source_target_pairs={{8,0},{24,8},{16,24},{4,16},{12,4},{28,12},{20,28},{0,20},{9,1},{2... | collective-permute-start | bytes 6152 | tf_op jit(solution)/shard_map/ppermute | solution.py:289
  43.6 5.3 %collective-permute-start.13 = (f32[1,128]{1,0:T(1,128)S(1)}, f32[1,128]{1,0:T(1,128)S(1)}, u32[]{:S(2)}, u32[]{:S(2)}) collective-permute-start(f32[1,128]{1,0:T(1,128)S(1)} %get-tuple-element.36), channel_id=1, source_target_pairs={{0,3},{1,2},{2,1},{3,0},{4,7},{5,6},{6,5},{7,4},{8,11},{9,10},{10,... | collective-permute-start | bytes 1544 | tf_op jit(solution)/shard_map/ppermute | solution.py:295
  45.4 4.4 %collective-permute-start.14 = (f32[1,128]{1,0:T(1,128)S(1)}, f32[1,128]{1,0:T(1,128)S(1)}, u32[]{:S(2)}, u32[]{:S(2)}) collective-permute-start(f32[1,128]{1,0:T(1,128)S(1)} %get-tuple-element.37), channel_id=1, source_target_pairs={{0,2},{1,3},{2,0},{3,1},{4,6},{5,7},{6,4},{7,5},{8,10},{9,11},{10,... | collective-permute-start | bytes 1544 | tf_op jit(solution)/shard_map/ppermute | solution.py:295
  45.4 4.4 %collective-permute-start.15 = (f32[1,128]{1,0:T(1,128)S(1)}, f32[1,128]{1,0:T(1,128)S(1)}, u32[]{:S(2)}, u32[]{:S(2)}) collective-permute-start(f32[1,128]{1,0:T(1,128)S(1)} %get-tuple-element.38), channel_id=1, source_target_pairs={{0,1},{1,0},{2,3},{3,2},{4,5},{5,4},{6,7},{7,6},{8,9},{9,8},{10,11... | collective-permute-start | bytes 1544 | tf_op jit(solution)/shard_map/ppermute | solution.py:295

commit v6 on v4

--- a/solution.py
+++ b/solution.py
@@ -323,7 +323,7 @@
         block = own[k]
         if k > 1:
             passed = [held[r][k - 2][0] for r in near]
-            block = stack([after(block, *passed)], WAIT)
+            block = stack([after(block, *passed)], WAIT if k == groups - 1 else WAIT // 20)
         for r in near:
             ready = after(block, held[near[0]][0][0]) if k == 1 else block
             held[r][k] = (from_offset(ready, offsets[r]), 0 if k > 1 else None)

time: 48.6 us -> 49.8 us (1.025)
  waiting for transfers between devices: 13 us -> 13.8 us
  starting transfers between devices: 26.9 us -> 27.4 us
    ppermute x6, waiting for transfers between devices: 5.81 us -> 8.26 us  [exchange(): got[k] = lax.ppermute(block, 'group', [(z, z ^ k) for z in range(groups)])]
    ppermute x6, starting transfers between devices: 12.5 us -> 14.9 us  [exchange(): got[k] = lax.ppermute(block, 'group', [(z, z ^ k) for z in range(groups)])]
    ppermute x12, starting transfers between devices: 14.3 us -> 12.5 us  [from_offset(): return lax.ppermute(x, 'shard', perm)]
    ppermute x12, waiting for transfers between devices: 7.24 us -> 5.49 us  [from_offset(): return lax.ppermute(x, 'shard', perm)]
where the time goes in v6:
time: 49.8 us; the launch traced here: 49.6 us
  starting transfers between devices  27.4 us (55%)
  waiting for transfers between devices  13.8 us (28%)
  Pallas kernels  7.71 us (15%)
  other arithmetic  0.7 us (1%)
    ppermute x6, starting transfers between devices, exchange(): got[k] = lax.ppermute(block, 'group', [(z, z ^ k) for z in range(groups)])  14.9 us
    ppermute x12, starting transfers between devices, from_offset(): return lax.ppermute(x, 'shard', perm)  12.5 us
    ppermute x6, waiting for transfers between devices, exchange(): got[k] = lax.ppermute(block, 'group', [(z, z ^ k) for z in range(groups)])  8.26 us
    pallas_call x9, Pallas kernels, call(): pl.pallas_call(kernel, out_shape=out_shape, in_specs=in_specs or in_vmem(...  7.71 us
    ppermute x12, waiting for transfers between devices, from_offset(): return lax.ppermute(x, 'shard', perm)  5.49 us
  transfers between devices with their start and end apart: 18, of which 10 were waited for; matrix products, arithmetic and copies ran while one was open for 0% of the time, Pallas kernels for 7%

profile of v6, /device:TPU:0, one launch (start us, length us, event | category | flops | bytes accessed | tf_op | source)
XLA Modules:
  0.0 49.6 jit_solution(714589494888495385)
XLA Ops:
  0.0 0.7 %multiply_add_fusion = s32[512]{0:T(512)S(1)} fusion(s32[512]{0:T(512)} %bitcast.4, s32[512]{0:T(512)} %param.5), kind=kLoop, calls=%fused_computation | loop fusion | flops 1024 | bytes 6144 | tf_op jit(solution)/shard_map/add | solution.py:298
  0.7 2.2 %shard_map.37 = (bf16[784,128]{1,0:T(8,128)(2,1)S(1)}, bf16[784,128]{1,0:T(8,128)(2,1)S(1)}, bf16[784,128]{1,0:T(8,128)(2,1)S(1)}, bf16[784,128]{1,0:T(8,128)(2,1)S(1)}, s32[1,512]{1,0:T(1,128)S(1)}) custom-call(bf16[512,768]{1,0:T(8,128)(2,1)} %refs_0_.1, s32[1,512]{1,0:T(1,128)S(1)} %bitcast.3), custom_call_target="tpu_custom_call" | custom-call | flops 402653184 | bytes 1572864 | tf_op jit(solution)/shard_map/pallas_call | solution.py:211
  2.9 3.1 %collective-permute-start = (bf16[784,128]{1,0:T(8,128)(2,1)S(1)}, bf16[784,128]{1,0:T(8,128)(2,1)S(1)}, u32[]{:S(2)}, u32[]{:S(2)}) collective-permute-start(bf16[784,128]{1,0:T(8,128)(2,1)S(1)} %get-tuple-element.27), channel_id=1, source_target_pairs={{0,1},{1,0},{2,3},{3,2},{4,5},{5,4},{6,7},{7,6},{8,9},{9,8},{10,11... | collective-permute-start | bytes 602120 | tf_op jit(solution)/shard_map/ppermute | solution.py:295
  6.0 0.7 %collective-permute-start.4 = (bf16[784,128]{1,0:T(8,128)(2,1)S(1)}, bf16[784,128]{1,0:T(8,128)(2,1)S(1)}, u32[]{:S(2)}, u32[]{:S(2)}) collective-permute-start(bf16[784,128]{1,0:T(8,128)(2,1)S(1)} %get-tuple-element.30.refs_0_.refs_2_.refs_3_), channel_id=1, source_target_pairs={{8,0},{24,8},{16,24},{4,16},{12,4},{28,12},{20,28},{0,20},{9,1},{2... | collective-permute-start | bytes 602120 | tf_op jit(solution)/shard_map/ppermute | solution.py:289
  6.7 2.6 %collective-permute-start.2 = (bf16[784,128]{1,0:T(8,128)(2,1)S(1)}, bf16[784,128]{1,0:T(8,128)(2,1)S(1)}, u32[]{:S(2)}, u32[]{:S(2)}) collective-permute-start(bf16[784,128]{1,0:T(8,128)(2,1)S(1)} %get-tuple-element.29), channel_id=1, source_target_pairs={{0,2},{1,3},{2,0},{3,1},{4,6},{5,7},{6,4},{7,5},{8,10},{9,11},{10,... | collective-permute-start | bytes 602120 | tf_op jit(solution)/shard_map/ppermute | solution.py:295
  9.3 1.3 %collective-permute-start.8 = (bf16[784,128]{1,0:T(8,128)(2,1)S(1)}, bf16[784,128]{1,0:T(8,128)(2,1)S(1)}, u32[]{:S(2)}, u32[]{:S(2)}) collective-permute-start(bf16[784,128]{1,0:T(8,128)(2,1)S(1)} %get-tuple-element.30.refs_0_.refs_2_.refs_3_), channel_id=1, source_target_pairs={{20,0},{0,8},{8,24},{24,16},{16,4},{4,12},{12,28},{28,20},{21,1},{... | collective-permute-start | bytes 602120 | tf_op jit(solution)/shard_map/ppermute | solution.py:289
  10.6 0.4 collective-permute-done.refs_1_.refs_2_
  11.0 4.8 %collective-permute-start.1 = (bf16[784,128]{1,0:T(8,128)(2,1)S(1)}, bf16[784,128]{1,0:T(8,128)(2,1)S(1)}, u32[]{:S(2)}, u32[]{:S(2)}) collective-permute-start(bf16[784,128]{1,0:T(8,128)(2,1)S(1)} %get-tuple-element.28), channel_id=1, source_target_pairs={{0,3},{1,2},{2,1},{3,0},{4,7},{5,6},{6,5},{7,4},{8,11},{9,10},{10,... | collective-permute-start | bytes 602120 | tf_op jit(solution)/shard_map/ppermute | solution.py:295
  15.8 0.0 collective-permute-done.4.refs_5_.refs_7_.refs_8_
  15.9 3.2 %collective-permute-start.6 = (bf16[784,128]{1,0:T(8,128)(2,1)S(1)}, bf16[784,128]{1,0:T(8,128)(2,1)S(1)}, u32[]{:S(2)}, u32[]{:S(2)}) collective-permute-start(bf16[784,128]{1,0:T(8,128)(2,1)S(1)} %collective-permute-done.refs_1_.refs_2_), channel_id=1, source_target_pairs={{20,0},{0,8},{8,24},{24,16},{16,4},{4,12},{12,28},{28,20},{21,1},{... | collective-permute-start | bytes 602120 | tf_op jit(solution)/shard_map/ppermute | solution.py:289
  19.1 0.0 collective-permute-start.5
  19.1 5.0 %collective-permute-done.2.refs_2_.refs_0_.refs_1_ = bf16[784,128]{1,0:T(8,128)(2,1)S(1)} collective-permute-done((bf16[784,128]{1,0:T(8,128)(2,1)S(1)}, bf16[784,128]{1,0:T(8,128)(2,1)S(1)}, u32[]{:S(2)}, u32[]{:S(2)}) %collective-permute-start.2) | collective-permute-done | bytes 200736 | tf_op jit(solution)/shard_map/ppermute | solution.py:295
  24.1 0.0 collective-permute-done.8.refs_8_.refs_12_
  24.1 0.1 collective-permute-start.11
  24.2 1.7 %collective-permute-start.9 = (bf16[1,784,128]{2,1,0:T(8,128)(2,1)S(1)}, bf16[1,784,128]{2,1,0:T(8,128)(2,1)S(1)}, u32[]{:S(2)}, u32[]{:S(2)}) collective-permute-start(bf16[1,784,128]{2,1,0:T(8,128)(2,1)S(1)} %shard_map.40), channel_id=1, source_target_pairs={{8,0},{24,8},{16,24},{4,16},{12,4},{28,12},{20,28},{0,20},{9,1},{2... | collective-permute-start | bytes 602120 | tf_op jit(solution)/shard_map/ppermute | solution.py:289
  25.9 0.0 collective-permute-done.1.refs_3_.refs_0_
  25.9 0.0 collective-permute-done.6.refs_7_.refs_11_
  25.9 0.0 collective-permute-done.5.refs_4_.refs_6_.refs_7_
  25.9 0.1 shard_map.38
  26.0 0.7 %collective-permute-start.3 = (bf16[4,784,128]{2,1,0:T(8,128)(2,1)S(1)}, bf16[4,784,128]{2,1,0:T(8,128)(2,1)S(1)}, u32[]{:S(2)}, u32[]{:S(2)}) collective-permute-start(bf16[4,784,128]{2,1,0:T(8,128)(2,1)S(1)} %shard_map.38), channel_id=1, source_target_pairs={{4,0},{12,8},{28,24},{20,16},{0,4},{8,12},{24,28},{16,20},{5,1},{1... | collective-permute-start | bytes 2408456 | tf_op jit(solution)/shard_map/ppermute | solution.py:289
  26.7 1.6 %collective-permute-start.10 = (bf16[1,784,128]{2,1,0:T(8,128)(2,1)S(1)}, bf16[1,784,128]{2,1,0:T(8,128)(2,1)S(1)}, u32[]{:S(2)}, u32[]{:S(2)}) collective-permute-start(bf16[1,784,128]{2,1,0:T(8,128)(2,1)S(1)} %shard_map.39), channel_id=1, source_target_pairs={{20,0},{0,8},{8,24},{24,16},{16,4},{4,12},{12,28},{28,20},{21,1},{... | collective-permute-start | bytes 602120 | tf_op jit(solution)/shard_map/ppermute | solution.py:289
  28.3 0.5 %collective-permute-start.7 = (bf16[1,784,128]{2,1,0:T(8,128)(2,1)S(1)}, bf16[1,784,128]{2,1,0:T(8,128)(2,1)S(1)}, u32[]{:S(2)}, u32[]{:S(2)}) collective-permute-start(bf16[1,784,128]{2,1,0:T(8,128)(2,1)S(1)} %shard_map.39), channel_id=1, source_target_pairs={{8,0},{24,8},{16,24},{4,16},{12,4},{28,12},{20,28},{0,20},{9,1},{2... | collective-permute-start | bytes 602120 | tf_op jit(solution)/shard_map/ppermute | solution.py:289
  28.8 1.9 %collective-permute-done.11.refs_6_.refs_10_ = bf16[1,784,128]{2,1,0:T(8,128)(2,1)S(1)} collective-permute-done((bf16[1,784,128]{2,1,0:T(8,128)(2,1)S(1)}, bf16[1,784,128]{2,1,0:T(8,128)(2,1)S(1)}, u32[]{:S(2)}, u32[]{:S(2)}) %collective-permute-start.11) | collective-permute-done | bytes 200736 | tf_op jit(solution)/shard_map/ppermute | solution.py:289
  30.7 0.6 %collective-permute-done.9.refs_3_.refs_5_.refs_6_ = bf16[1,784,128]{2,1,0:T(8,128)(2,1)S(1)} collective-permute-done((bf16[1,784,128]{2,1,0:T(8,128)(2,1)S(1)}, bf16[1,784,128]{2,1,0:T(8,128)(2,1)S(1)}, u32[]{:S(2)}, u32[]{:S(2)}) %collective-permute-start.9) | collective-permute-done | bytes 200736 | tf_op jit(solution)/shard_map/ppermute | solution.py:289
  31.3 1.2 %shard_map.41 = (f32[4,512,128]{2,1,0:T(8,128)S(1)}, f32[4,8,512]{2,1,0:T(8,128)S(1)}) custom-call(bf16[784,128]{1,0:T(8,128)(2,1)S(1)} %collective-permute-done.2.refs_2_.refs_0_.refs_1_, bf16[784,128]{1,0:T(8,128)(2,1)S(1)} %collective-permute-done.refs_1_.refs_2_, bf16[784,128]{1,0:T(8,128)(2,1)S(1)} %get-tuple-element.30.refs_0_.refs_2_.refs_3_, ...), custom_call_target="tpu_custom_call" | custom-call | flops 679477248 | bytes 1769472 | tf_op jit(solution)/shard_map/pallas_call | solution.py:211
  32.5 0.0 collective-permute-done.3.refs_4_
  32.5 2.0 %shard_map.42 = (f32[4,512,128]{2,1,0:T(8,128)S(1)}, f32[4,8,512]{2,1,0:T(8,128)S(1)}) custom-call(bf16[784,128]{1,0:T(8,128)(2,1)S(1)} %collective-permute-done.1.refs_3_.refs_0_, bf16[784,128]{1,0:T(8,128)(2,1)S(1)} %collective-permute-done.2.refs_2_.refs_0_.refs_1_, ...), custom_call_target="tpu_custom_call", output_to_operand_aliasing={{0}: (8, {}), {1}: (9, {})} | custom-call | flops 956301312 | bytes 2162688 | tf_op jit(solution)/shard_map/pallas_call | solution.py:211
  34.5 0.5 collective-permute-done.10.refs_9_
  35.0 0.6 %collective-permute-done.7.refs_5_ = bf16[1,784,128]{2,1,0:T(8,128)(2,1)S(1)} collective-permute-done((bf16[1,784,128]{2,1,0:T(8,128)(2,1)S(1)}, bf16[1,784,128]{2,1,0:T(8,128)(2,1)S(1)}, u32[]{:S(2)}, u32[]{:S(2)}) %collective-permute-start.7) | collective-permute-done | bytes 200736 | tf_op jit(solution)/shard_map/ppermute | solution.py:289
  35.6 1.4 %shard_map.43 = (f32[4,512,128]{2,1,0:T(8,128)S(1)}, f32[4,8,512]{2,1,0:T(8,128)S(1)}, f32[1,512]{1,0:T(1,128)S(1)}, f32[1,512]{1,0:T(1,128)S(1)}, f32[1,512]{1,0:T(1,128)S(1)}, /*index=5*/f32[1,512]{1,0:T(1,128)S(1)}) custom-call(bf16[784,128]{1,0:T(8,128)(2,1)S(1)} %collective-permute-done.1.refs_3_.refs_0_, ...), custom_call_target="tpu_custom_call", output_to_operand_aliasing={{0}: (13, {}), {1}: (14, {})} | custom-call | flops 377487360 | bytes 3145728 | tf_op jit(solution)/shard_map/pallas_call | solution.py:211
  37.0 0.1 collective-permute-start.12
  37.1 0.8 %collective-permute-start.13 = (f32[1,512]{1,0:T(1,128)S(1)}, f32[1,512]{1,0:T(1,128)S(1)}, u32[]{:S(2)}, u32[]{:S(2)}) collective-permute-start(f32[1,512]{1,0:T(1,128)S(1)} %get-tuple-element.40), channel_id=1, source_target_pairs={{20,0},{0,8},{8,24},{24,16},{16,4},{4,12},{12,28},{28,20},{21,1},{... | collective-permute-start | bytes 6152 | tf_op jit(solution)/shard_map/ppermute | solution.py:289
  37.9 1.7 %collective-permute-start.14 = (f32[1,512]{1,0:T(1,128)S(1)}, f32[1,512]{1,0:T(1,128)S(1)}, u32[]{:S(2)}, u32[]{:S(2)}) collective-permute-start(f32[1,512]{1,0:T(1,128)S(1)} %get-tuple-element.41), channel_id=1, source_target_pairs={{8,0},{24,8},{16,24},{4,16},{12,4},{28,12},{20,28},{0,20},{9,1},{2... | collective-permute-start | bytes 6152 | tf_op jit(solution)/shard_map/ppermute | solution.py:289
  39.6 0.0 collective-permute-done.12.refs_1_
  39.6 1.3 %collective-permute-done.13.refs_2_ = f32[1,512]{1,0:T(1,128)S(1)} collective-permute-done((f32[1,512]{1,0:T(1,128)S(1)}, f32[1,512]{1,0:T(1,128)S(1)}, u32[]{:S(2)}, u32[]{:S(2)}) %collective-permute-start.13) | collective-permute-done | bytes 2080 | tf_op jit(solution)/shard_map/ppermute | solution.py:289
  40.8 0.7 %collective-permute-done.14.refs_3_ = f32[1,512]{1,0:T(1,128)S(1)} collective-permute-done((f32[1,512]{1,0:T(1,128)S(1)}, f32[1,512]{1,0:T(1,128)S(1)}, u32[]{:S(2)}, u32[]{:S(2)}) %collective-permute-start.14) | collective-permute-done | bytes 2080 | tf_op jit(solution)/shard_map/ppermute | solution.py:289
  41.5 2.9 %collective-permute-start.15 = (f32[1,128]{1,0:T(1,128)S(1)}, f32[1,128]{1,0:T(1,128)S(1)}, u32[]{:S(2)}, u32[]{:S(2)}) collective-permute-start(f32[1,128]{1,0:T(1,128)S(1)} %get-tuple-element.42), channel_id=1, source_target_pairs={{0,3},{1,2},{2,1},{3,0},{4,7},{5,6},{6,5},{7,4},{8,11},{9,10},{10,... | collective-permute-start | bytes 1544 | tf_op jit(solution)/shard_map/ppermute | solution.py:295
  44.4 0.0 collective-permute-start.16
  44.4 1.5 %collective-permute-start.17 = (f32[1,128]{1,0:T(1,128)S(1)}, f32[1,128]{1,0:T(1,128)S(1)}, u32[]{:S(2)}, u32[]{:S(2)}) collective-permute-start(f32[1,128]{1,0:T(1,128)S(1)} %get-tuple-element.44), channel_id=1, source_target_pairs={{0,1},{1,0},{2,3},{3,2},{4,5},{5,4},{6,7},{7,6},{8,9},{9,8},{10,11... | collective-permute-start | bytes 1544 | tf_op jit(solution)/shard_map/ppermute | solution.py:295
  45.9 0.9 %collective-permute-done.15.refs_0_ = f32[1,128]{1,0:T(1,128)S(1)} collective-permute-done((f32[1,128]{1,0:T(1,128)S(1)}, f32[1,128]{1,0:T(1,128)S(1)}, u32[]{:S(2)}, u32[]{:S(2)}) %collective-permute-start.15) | collective-permute-done | bytes 544 | tf_op jit(solution)/shard_map/ppermute | solution.py:295
  46.9 2.0 %collective-permute-done.16.refs_1_ = f32[1,128]{1,0:T(1,128)S(1)} collective-permute-done((f32[1,128]{1,0:T(1,128)S(1)}, f32[1,128]{1,0:T(1,128)S(1)}, u32[]{:S(2)}, u32[]{:S(2)}) %collective-permute-start.16) | collective-permute-done | bytes 544 | tf_op jit(solution)/shard_map/ppermute | solution.py:295
  48.8 0.0 collective-permute-done.17.refs_2_
  48.8 0.8 %shard_map.45 = f32[1,512]{1,0:T(1,128)} custom-call(f32[1,128]{1,0:T(1,128)S(1)} %collective-permute-done.15.refs_0_, f32[1,128]{1,0:T(1,128)S(1)} %collective-permute-done.16.refs_1_, f32[1,128]{1,0:T(1,128)S(1)} %collective-permute-done.17.refs_2_, f32[1,128]{1,0:T(1,128)S(1)} %get-tuple-element.45.refs_3_, s32[1,512]{1,0:T(1,128)S(1)} %get-tuple-element.46.refs_4_), custom_call_target="tpu_custom_call" | custom-call | flops 262144 | bytes 2048 | tf_op jit(solution)/shard_map/pallas_call | solution.py:211
  (3 shorter events, 0.0 us)
Async XLA Ops:
  2.9 8.1 %collective-permute-start = (bf16[784,128]{1,0:T(8,128)(2,1)S(1)}, bf16[784,128]{1,0:T(8,128)(2,1)S(1)}, u32[]{:S(2)}, u32[]{:S(2)}) collective-permute-start(bf16[784,128]{1,0:T(8,128)(2,1)S(1)} %get-tuple-element.27), channel_id=1, source_target_pairs={{0,1},{1,0},{2,3},{3,2},{4,5},{5,4},{6,7},{7,6},{8,9},{9,8},{10,11... | collective-permute-start | bytes 602120 | tf_op jit(solution)/shard_map/ppermute | solution.py:295
  6.0 9.8 %collective-permute-start.4 = (bf16[784,128]{1,0:T(8,128)(2,1)S(1)}, bf16[784,128]{1,0:T(8,128)(2,1)S(1)}, u32[]{:S(2)}, u32[]{:S(2)}) collective-permute-start(bf16[784,128]{1,0:T(8,128)(2,1)S(1)} %get-tuple-element.30.refs_0_.refs_2_.refs_3_), channel_id=1, source_target_pairs={{8,0},{24,8},{16,24},{4,16},{12,4},{28,12},{20,28},{0,20},{9,1},{2... | collective-permute-start | bytes 602120 | tf_op jit(solution)/shard_map/ppermute | solution.py:289
  6.7 17.4 %collective-permute-start.2 = (bf16[784,128]{1,0:T(8,128)(2,1)S(1)}, bf16[784,128]{1,0:T(8,128)(2,1)S(1)}, u32[]{:S(2)}, u32[]{:S(2)}) collective-permute-start(bf16[784,128]{1,0:T(8,128)(2,1)S(1)} %get-tuple-element.29), channel_id=1, source_target_pairs={{0,2},{1,3},{2,0},{3,1},{4,6},{5,7},{6,4},{7,5},{8,10},{9,11},{10,... | collective-permute-start | bytes 602120 | tf_op jit(solution)/shard_map/ppermute | solution.py:295
  9.3 14.8 %collective-permute-start.8 = (bf16[784,128]{1,0:T(8,128)(2,1)S(1)}, bf16[784,128]{1,0:T(8,128)(2,1)S(1)}, u32[]{:S(2)}, u32[]{:S(2)}) collective-permute-start(bf16[784,128]{1,0:T(8,128)(2,1)S(1)} %get-tuple-element.30.refs_0_.refs_2_.refs_3_), channel_id=1, source_target_pairs={{20,0},{0,8},{8,24},{24,16},{16,4},{4,12},{12,28},{28,20},{21,1},{... | collective-permute-start | bytes 602120 | tf_op jit(solution)/shard_map/ppermute | solution.py:289
  11.0 14.9 %collective-permute-start.1 = (bf16[784,128]{1,0:T(8,128)(2,1)S(1)}, bf16[784,128]{1,0:T(8,128)(2,1)S(1)}, u32[]{:S(2)}, u32[]{:S(2)}) collective-permute-start(bf16[784,128]{1,0:T(8,128)(2,1)S(1)} %get-tuple-element.28), channel_id=1, source_target_pairs={{0,3},{1,2},{2,1},{3,0},{4,7},{5,6},{6,5},{7,4},{8,11},{9,10},{10,... | collective-permute-start | bytes 602120 | tf_op jit(solution)/shard_map/ppermute | solution.py:295
  15.9 10.1 %collective-permute-start.6 = (bf16[784,128]{1,0:T(8,128)(2,1)S(1)}, bf16[784,128]{1,0:T(8,128)(2,1)S(1)}, u32[]{:S(2)}, u32[]{:S(2)}) collective-permute-start(bf16[784,128]{1,0:T(8,128)(2,1)S(1)} %collective-permute-done.refs_1_.refs_2_), channel_id=1, source_target_pairs={{20,0},{0,8},{8,24},{24,16},{16,4},{4,12},{12,28},{28,20},{21,1},{... | collective-permute-start | bytes 602120 | tf_op jit(solution)/shard_map/ppermute | solution.py:289
  19.1 6.8 %collective-permute-start.5 = (bf16[784,128]{1,0:T(8,128)(2,1)S(1)}, bf16[784,128]{1,0:T(8,128)(2,1)S(1)}, u32[]{:S(2)}, u32[]{:S(2)}) collective-permute-start(bf16[784,128]{1,0:T(8,128)(2,1)S(1)} %collective-permute-done.refs_1_.refs_2_), channel_id=1, source_target_pairs={{8,0},{24,8},{16,24},{4,16},{12,4},{28,12},{20,28},{0,20},{9,1},{2... | collective-permute-start | bytes 602120 | tf_op jit(solution)/shard_map/ppermute | solution.py:289
  24.1 6.6 %collective-permute-start.11 = (bf16[1,784,128]{2,1,0:T(8,128)(2,1)S(1)}, bf16[1,784,128]{2,1,0:T(8,128)(2,1)S(1)}, u32[]{:S(2)}, u32[]{:S(2)}) collective-permute-start(bf16[1,784,128]{2,1,0:T(8,128)(2,1)S(1)} %shard_map.40), channel_id=1, source_target_pairs={{20,0},{0,8},{8,24},{24,16},{16,4},{4,12},{12,28},{28,20},{21,1},{... | collective-permute-start | bytes 602120 | tf_op jit(solution)/shard_map/ppermute | solution.py:289
  24.2 7.1 %collective-permute-start.9 = (bf16[1,784,128]{2,1,0:T(8,128)(2,1)S(1)}, bf16[1,784,128]{2,1,0:T(8,128)(2,1)S(1)}, u32[]{:S(2)}, u32[]{:S(2)}) collective-permute-start(bf16[1,784,128]{2,1,0:T(8,128)(2,1)S(1)} %shard_map.40), channel_id=1, source_target_pairs={{8,0},{24,8},{16,24},{4,16},{12,4},{28,12},{20,28},{0,20},{9,1},{2... | collective-permute-start | bytes 602120 | tf_op jit(solution)/shard_map/ppermute | solution.py:289
  26.0 6.5 %collective-permute-start.3 = (bf16[4,784,128]{2,1,0:T(8,128)(2,1)S(1)}, bf16[4,784,128]{2,1,0:T(8,128)(2,1)S(1)}, u32[]{:S(2)}, u32[]{:S(2)}) collective-permute-start(bf16[4,784,128]{2,1,0:T(8,128)(2,1)S(1)} %shard_map.38), channel_id=1, source_target_pairs={{4,0},{12,8},{28,24},{20,16},{0,4},{8,12},{24,28},{16,20},{5,1},{1... | collective-permute-start | bytes 2408456 | tf_op jit(solution)/shard_map/ppermute | solution.py:289
  26.7 8.3 %collective-permute-start.10 = (bf16[1,784,128]{2,1,0:T(8,128)(2,1)S(1)}, bf16[1,784,128]{2,1,0:T(8,128)(2,1)S(1)}, u32[]{:S(2)}, u32[]{:S(2)}) collective-permute-start(bf16[1,784,128]{2,1,0:T(8,128)(2,1)S(1)} %shard_map.39), channel_id=1, source_target_pairs={{20,0},{0,8},{8,24},{24,16},{16,4},{4,12},{12,28},{28,20},{21,1},{... | collective-permute-start | bytes 602120 | tf_op jit(solution)/shard_map/ppermute | solution.py:289
  28.3 7.3 %collective-permute-start.7 = (bf16[1,784,128]{2,1,0:T(8,128)(2,1)S(1)}, bf16[1,784,128]{2,1,0:T(8,128)(2,1)S(1)}, u32[]{:S(2)}, u32[]{:S(2)}) collective-permute-start(bf16[1,784,128]{2,1,0:T(8,128)(2,1)S(1)} %shard_map.39), channel_id=1, source_target_pairs={{8,0},{24,8},{16,24},{4,16},{12,4},{28,12},{20,28},{0,20},{9,1},{2... | collective-permute-start | bytes 602120 | tf_op jit(solution)/shard_map/ppermute | solution.py:289
  37.0 2.6 %collective-permute-start.12 = (f32[1,512]{1,0:T(1,128)S(1)}, f32[1,512]{1,0:T(1,128)S(1)}, u32[]{:S(2)}, u32[]{:S(2)}) collective-permute-start(f32[1,512]{1,0:T(1,128)S(1)} %get-tuple-element.39), channel_id=1, source_target_pairs={{4,0},{12,8},{28,24},{20,16},{0,4},{8,12},{24,28},{16,20},{5,1},{1... | collective-permute-start | bytes 6152 | tf_op jit(solution)/shard_map/ppermute | solution.py:289
  37.1 3.7 %collective-permute-start.13 = (f32[1,512]{1,0:T(1,128)S(1)}, f32[1,512]{1,0:T(1,128)S(1)}, u32[]{:S(2)}, u32[]{:S(2)}) collective-permute-start(f32[1,512]{1,0:T(1,128)S(1)} %get-tuple-element.40), channel_id=1, source_target_pairs={{20,0},{0,8},{8,24},{24,16},{16,4},{4,12},{12,28},{28,20},{21,1},{... | collective-permute-start | bytes 6152 | tf_op jit(solution)/shard_map/ppermute | solution.py:289
  37.9 3.6 %collective-permute-start.14 = (f32[1,512]{1,0:T(1,128)S(1)}, f32[1,512]{1,0:T(1,128)S(1)}, u32[]{:S(2)}, u32[]{:S(2)}) collective-permute-start(f32[1,512]{1,0:T(1,128)S(1)} %get-tuple-element.41), channel_id=1, source_target_pairs={{8,0},{24,8},{16,24},{4,16},{12,4},{28,12},{20,28},{0,20},{9,1},{2... | collective-permute-start | bytes 6152 | tf_op jit(solution)/shard_map/ppermute | solution.py:289
  41.5 5.3 %collective-permute-start.15 = (f32[1,128]{1,0:T(1,128)S(1)}, f32[1,128]{1,0:T(1,128)S(1)}, u32[]{:S(2)}, u32[]{:S(2)}) collective-permute-start(f32[1,128]{1,0:T(1,128)S(1)} %get-tuple-element.42), channel_id=1, source_target_pairs={{0,3},{1,2},{2,1},{3,0},{4,7},{5,6},{6,5},{7,4},{8,11},{9,10},{10,... | collective-permute-start | bytes 1544 | tf_op jit(solution)/shard_map/ppermute | solution.py:295
  44.4 4.4 %collective-permute-start.16 = (f32[1,128]{1,0:T(1,128)S(1)}, f32[1,128]{1,0:T(1,128)S(1)}, u32[]{:S(2)}, u32[]{:S(2)}) collective-permute-start(f32[1,128]{1,0:T(1,128)S(1)} %get-tuple-element.43), channel_id=1, source_target_pairs={{0,2},{1,3},{2,0},{3,1},{4,6},{5,7},{6,4},{7,5},{8,10},{9,11},{10,... | collective-permute-start | bytes 1544 | tf_op jit(solution)/shard_map/ppermute | solution.py:295
  44.4 4.4 %collective-permute-start.17 = (f32[1,128]{1,0:T(1,128)S(1)}, f32[1,128]{1,0:T(1,128)S(1)}, u32[]{:S(2)}, u32[]{:S(2)}) collective-permute-start(f32[1,128]{1,0:T(1,128)S(1)} %get-tuple-element.44), channel_id=1, source_target_pairs={{0,1},{1,0},{2,3},{3,2},{4,5},{5,4},{6,7},{7,6},{8,9},{9,8},{10,11... | collective-permute-start | bytes 1544 | tf_op jit(solution)/shard_map/ppermute | solution.py:295

commit v7 on v5

--- a/solution.py
+++ b/solution.py
@@ -291,7 +291,7 @@
     def exchange(blocks, last=()):
         got = list(blocks)
         for k in range(1, groups):
-            block = after(blocks[k], *last) if k == groups - 1 else blocks[k]
+            block = after(blocks[k], got[2]) if k > 2 and last else blocks[k]
             got[k] = lax.ppermute(block, "group", [(z, z ^ k) for z in range(groups)])
         return got
 
@@ -317,7 +317,7 @@
     near = [r for r in range(1, roles) if 2 * offsets[r] != shards]
     far = [r for r in range(1, roles) if r not in near]
     first = {r: from_offset(send[0], offsets[r]) for r in near}
-    own = exchange(send, [first[r] for r in near[:1]])
+    own = exchange(send, True)
     held = [[None] * groups for _ in offsets]
     held[0] = [(x, None) for x in own]
     for r in near:

time: 50.8 us -> 50.4 us (level)
  starting transfers between devices: 23.7 us -> 20.8 us
  waiting for transfers between devices: 18.5 us -> 21 us
    ppermute x10, starting transfers between devices: 11.3 us -> 7.31 us  [from_offset(): return lax.ppermute(x, 'shard', perm)]
    ppermute x6, waiting for transfers between devices: 8.51 us -> 11 us  [exchange(): got[k] = lax.ppermute(block, 'group', [(z, z ^ k) for z in range(groups)])]
    ppermute x6, starting transfers between devices: 12.4 us -> 13.5 us  [exchange(): got[k] = lax.ppermute(block, 'group', [(z, z ^ k) for z in range(groups)])]
  transfers between devices with their start and end apart: 16 -> 16, of which waited for: 9 -> 8; matrix products, arithmetic and copies ran while one was open for 0% -> 0% of each run, Pallas kernels for 7% -> 7%
where the time goes in v7:
time: 50.4 us; the launch traced here: 50.3 us
  waiting for transfers between devices  21 us (42%)
  starting transfers between devices  20.8 us (41%)
  Pallas kernels  7.71 us (15%)
  other arithmetic  0.7 us (1%)
    ppermute x6, starting transfers between devices, exchange(): got[k] = lax.ppermute(block, 'group', [(z, z ^ k) for z in range(groups)])  13.5 us
    ppermute x6, waiting for transfers between devices, exchange(): got[k] = lax.ppermute(block, 'group', [(z, z ^ k) for z in range(groups)])  11 us
    ppermute x10, waiting for transfers between devices, from_offset(): return lax.ppermute(x, 'shard', perm)  9.93 us
    pallas_call x9, Pallas kernels, call(): pl.pallas_call(kernel, out_shape=out_shape, in_specs=in_specs or in_vmem(...  7.71 us
    ppermute x10, starting transfers between devices, from_offset(): return lax.ppermute(x, 'shard', perm)  7.31 us
  transfers between devices with their start and end apart: 16, of which 8 were waited for; matrix products, arithmetic and copies ran while one was open for 0% of the time, Pallas kernels for 7%

profile of v7, /device:TPU:0, one launch (start us, length us, event | category | flops | bytes accessed | tf_op | source)
XLA Modules:
  0.0 50.3 jit_solution(16350093531726594163)
XLA Ops:
  0.0 0.7 %multiply_add_fusion = s32[512]{0:T(512)S(1)} fusion(s32[512]{0:T(512)} %bitcast.4, s32[512]{0:T(512)} %param.5), kind=kLoop, calls=%fused_computation | loop fusion | flops 1024 | bytes 6144 | tf_op jit(solution)/shard_map/add | solution.py:298
  0.7 2.2 %shard_map.37 = (bf16[784,128]{1,0:T(8,128)(2,1)S(1)}, bf16[784,128]{1,0:T(8,128)(2,1)S(1)}, bf16[784,128]{1,0:T(8,128)(2,1)S(1)}, bf16[784,128]{1,0:T(8,128)(2,1)S(1)}, s32[1,512]{1,0:T(1,128)S(1)}) custom-call(bf16[512,768]{1,0:T(8,128)(2,1)} %refs_0_.1, s32[1,512]{1,0:T(1,128)S(1)} %bitcast.3), custom_call_target="tpu_custom_call" | custom-call | flops 402653184 | bytes 1572864 | tf_op jit(solution)/shard_map/pallas_call | solution.py:211
  2.9 4.1 %collective-permute-start = (bf16[784,128]{1,0:T(8,128)(2,1)S(1)}, bf16[784,128]{1,0:T(8,128)(2,1)S(1)}, u32[]{:S(2)}, u32[]{:S(2)}) collective-permute-start(bf16[784,128]{1,0:T(8,128)(2,1)S(1)} %get-tuple-element.24), channel_id=1, source_target_pairs={{0,2},{1,3},{2,0},{3,1},{4,6},{5,7},{6,4},{7,5},{8,10},{9,11},{10,... | collective-permute-start | bytes 602120 | tf_op jit(solution)/shard_map/ppermute | solution.py:295
  7.0 1.6 %collective-permute-start.2 = (bf16[784,128]{1,0:T(8,128)(2,1)S(1)}, bf16[784,128]{1,0:T(8,128)(2,1)S(1)}, u32[]{:S(2)}, u32[]{:S(2)}) collective-permute-start(bf16[784,128]{1,0:T(8,128)(2,1)S(1)} %get-tuple-element.26), channel_id=1, source_target_pairs={{0,1},{1,0},{2,3},{3,2},{4,5},{5,4},{6,7},{7,6},{8,9},{9,8},{10,11... | collective-permute-start | bytes 602120 | tf_op jit(solution)/shard_map/ppermute | solution.py:295
  8.6 1.5 %collective-permute-start.9 = (bf16[784,128]{1,0:T(8,128)(2,1)S(1)}, bf16[784,128]{1,0:T(8,128)(2,1)S(1)}, u32[]{:S(2)}, u32[]{:S(2)}) collective-permute-start(bf16[784,128]{1,0:T(8,128)(2,1)S(1)} %get-tuple-element.27.refs_0_.refs_2_.refs_3_), channel_id=1, source_target_pairs={{20,0},{0,8},{8,24},{24,16},{16,4},{4,12},{12,28},{28,20},{21,1},{... | collective-permute-start | bytes 602120 | tf_op jit(solution)/shard_map/ppermute | solution.py:289
  10.1 0.3 collective-permute-start.6
  10.4 6.1 %collective-permute-done.refs_2_.refs_1_.refs_0_ = bf16[784,128]{1,0:T(8,128)(2,1)S(1)} collective-permute-done((bf16[784,128]{1,0:T(8,128)(2,1)S(1)}, bf16[784,128]{1,0:T(8,128)(2,1)S(1)}, u32[]{:S(2)}, u32[]{:S(2)}) %collective-permute-start) | collective-permute-done | bytes 200736 | tf_op jit(solution)/shard_map/ppermute | solution.py:295
  16.4 3.4 %collective-permute-start.1 = (bf16[784,128]{1,0:T(8,128)(2,1)S(1)}, bf16[784,128]{1,0:T(8,128)(2,1)S(1)}, u32[]{:S(2)}, u32[]{:S(2)}) collective-permute-start(bf16[784,128]{1,0:T(8,128)(2,1)S(1)} %get-tuple-element.25), channel_id=1, source_target_pairs={{0,3},{1,2},{2,1},{3,0},{4,7},{5,6},{6,5},{7,4},{8,11},{9,10},{10,... | collective-permute-start | bytes 602120 | tf_op jit(solution)/shard_map/ppermute | solution.py:295
  19.9 0.0 collective-permute-done.2.refs_1_.refs_0_.refs_2_
  19.9 1.6 %collective-permute-start.8 = (bf16[2,784,128]{2,1,0:T(8,128)(2,1)S(1)}, bf16[2,784,128]{2,1,0:T(8,128)(2,1)S(1)}, u32[]{:S(2)}, u32[]{:S(2)}) collective-permute-start(bf16[2,784,128]{2,1,0:T(8,128)(2,1)S(1)} %shard_map.40), channel_id=1, source_target_pairs={{20,0},{0,8},{8,24},{24,16},{16,4},{4,12},{12,28},{28,20},{21,1},{... | collective-permute-start | bytes 1204232 | tf_op jit(solution)/shard_map/ppermute | solution.py:289
  21.5 0.3 collective-permute-start.5
  21.7 3.4 %collective-permute-done.1.refs_3_.refs_0_ = bf16[784,128]{1,0:T(8,128)(2,1)S(1)} collective-permute-done((bf16[784,128]{1,0:T(8,128)(2,1)S(1)}, bf16[784,128]{1,0:T(8,128)(2,1)S(1)}, u32[]{:S(2)}, u32[]{:S(2)}) %collective-permute-start.1) | collective-permute-done | bytes 200736 | tf_op jit(solution)/shard_map/ppermute | solution.py:295
  25.1 0.1 shard_map.38
  25.2 0.1 collective-permute-start.3
  25.3 0.0 collective-permute-done.9.refs_6_.refs_10_
  25.3 1.6 %collective-permute-start.7 = (bf16[1,784,128]{2,1,0:T(8,128)(2,1)S(1)}, bf16[1,784,128]{2,1,0:T(8,128)(2,1)S(1)}, u32[]{:S(2)}, u32[]{:S(2)}) collective-permute-start(bf16[1,784,128]{2,1,0:T(8,128)(2,1)S(1)} %shard_map.39), channel_id=1, source_target_pairs={{20,0},{0,8},{8,24},{24,16},{16,4},{4,12},{12,28},{28,20},{21,1},{... | collective-permute-start | bytes 602120 | tf_op jit(solution)/shard_map/ppermute | solution.py:289
  26.9 0.0 collective-permute-done.6.refs_4_.refs_6_.refs_7_
  26.9 0.3 collective-permute-start.4
  27.1 4.4 %collective-permute-done.8.refs_5_.refs_9_ = bf16[2,784,128]{2,1,0:T(8,128)(2,1)S(1)} collective-permute-done((bf16[2,784,128]{2,1,0:T(8,128)(2,1)S(1)}, bf16[2,784,128]{2,1,0:T(8,128)(2,1)S(1)}, u32[]{:S(2)}, u32[]{:S(2)}) %collective-permute-start.8) | collective-permute-done | bytes 401440 | tf_op jit(solution)/shard_map/ppermute | solution.py:289
  31.5 2.2 %collective-permute-done.5.refs_3_.refs_5_.refs_6_ = bf16[2,784,128]{2,1,0:T(8,128)(2,1)S(1)} collective-permute-done((bf16[2,784,128]{2,1,0:T(8,128)(2,1)S(1)}, bf16[2,784,128]{2,1,0:T(8,128)(2,1)S(1)}, u32[]{:S(2)}, u32[]{:S(2)}) %collective-permute-start.5) | collective-permute-done | bytes 401440 | tf_op jit(solution)/shard_map/ppermute | solution.py:289
  33.7 1.2 %shard_map.41 = (f32[4,512,128]{2,1,0:T(8,128)S(1)}, f32[4,8,512]{2,1,0:T(8,128)S(1)}) custom-call(bf16[784,128]{1,0:T(8,128)(2,1)S(1)} %collective-permute-done.refs_2_.refs_1_.refs_0_, bf16[784,128]{1,0:T(8,128)(2,1)S(1)} %collective-permute-done.2.refs_1_.refs_0_.refs_2_, bf16[784,128]{1,0:T(8,128)(2,1)S(1)} %get-tuple-element.27.refs_0_.refs_2_.refs_3_, ...), custom_call_target="tpu_custom_call" | custom-call | flops 679477248 | bytes 1769472 | tf_op jit(solution)/shard_map/pallas_call | solution.py:211
  34.9 0.0 collective-permute-done.3.refs_4_
  34.9 2.0 %shard_map.42 = (f32[4,512,128]{2,1,0:T(8,128)S(1)}, f32[4,8,512]{2,1,0:T(8,128)S(1)}) custom-call(bf16[784,128]{1,0:T(8,128)(2,1)S(1)} %collective-permute-done.1.refs_3_.refs_0_, bf16[784,128]{1,0:T(8,128)(2,1)S(1)} %collective-permute-done.refs_2_.refs_1_.refs_0_, ...), custom_call_target="tpu_custom_call", output_to_operand_aliasing={{0}: (7, {}), {1}: (8, {})} | custom-call | flops 956301312 | bytes 2162688 | tf_op jit(solution)/shard_map/pallas_call | solution.py:211
  36.9 0.0 collective-permute-done.7.refs_8_
  36.9 0.0 collective-permute-done.4.refs_5_
  36.9 1.4 %shard_map.43 = (f32[4,512,128]{2,1,0:T(8,128)S(1)}, f32[4,8,512]{2,1,0:T(8,128)S(1)}, f32[1,512]{1,0:T(1,128)S(1)}, f32[1,512]{1,0:T(1,128)S(1)}, f32[1,512]{1,0:T(1,128)S(1)}, /*index=5*/f32[1,512]{1,0:T(1,128)S(1)}) custom-call(bf16[784,128]{1,0:T(8,128)(2,1)S(1)} %collective-permute-done.1.refs_3_.refs_0_, ...), custom_call_target="tpu_custom_call", output_to_operand_aliasing={{0}: (11, {}), {1}: (12, {})} | custom-call | flops 377487360 | bytes 3145728 | tf_op jit(solution)/shard_map/pallas_call | solution.py:211
  38.3 0.1 collective-permute-start.10
  38.4 1.6 %collective-permute-start.11 = (f32[1,512]{1,0:T(1,128)S(1)}, f32[1,512]{1,0:T(1,128)S(1)}, u32[]{:S(2)}, u32[]{:S(2)}) collective-permute-start(f32[1,512]{1,0:T(1,128)S(1)} %get-tuple-element.34), channel_id=1, source_target_pairs={{20,0},{0,8},{8,24},{24,16},{16,4},{4,12},{12,28},{28,20},{21,1},{... | collective-permute-start | bytes 6152 | tf_op jit(solution)/shard_map/ppermute | solution.py:289
  40.0 0.2 collective-permute-start.12
  40.2 0.0 collective-permute-done.10.refs_1_
  40.2 1.3 %collective-permute-done.11.refs_2_ = f32[1,512]{1,0:T(1,128)S(1)} collective-permute-done((f32[1,512]{1,0:T(1,128)S(1)}, f32[1,512]{1,0:T(1,128)S(1)}, u32[]{:S(2)}, u32[]{:S(2)}) %collective-permute-start.11) | collective-permute-done | bytes 2080 | tf_op jit(solution)/shard_map/ppermute | solution.py:289
  41.5 2.1 %collective-permute-done.12.refs_3_ = f32[1,512]{1,0:T(1,128)S(1)} collective-permute-done((f32[1,512]{1,0:T(1,128)S(1)}, f32[1,512]{1,0:T(1,128)S(1)}, u32[]{:S(2)}, u32[]{:S(2)}) %collective-permute-start.12) | collective-permute-done | bytes 2080 | tf_op jit(solution)/shard_map/ppermute | solution.py:289
  43.6 0.6 %collective-permute-start.13 = (f32[1,128]{1,0:T(1,128)S(1)}, f32[1,128]{1,0:T(1,128)S(1)}, u32[]{:S(2)}, u32[]{:S(2)}) collective-permute-start(f32[1,128]{1,0:T(1,128)S(1)} %get-tuple-element.36), channel_id=1, source_target_pairs={{0,3},{1,2},{2,1},{3,0},{4,7},{5,6},{6,5},{7,4},{8,11},{9,10},{10,... | collective-permute-start | bytes 1544 | tf_op jit(solution)/shard_map/ppermute | solution.py:295
  44.2 1.0 %collective-permute-start.14 = (f32[1,128]{1,0:T(1,128)S(1)}, f32[1,128]{1,0:T(1,128)S(1)}, u32[]{:S(2)}, u32[]{:S(2)}) collective-permute-start(f32[1,128]{1,0:T(1,128)S(1)} %get-tuple-element.37), channel_id=1, source_target_pairs={{0,2},{1,3},{2,0},{3,1},{4,6},{5,7},{6,4},{7,5},{8,10},{9,11},{10,... | collective-permute-start | bytes 1544 | tf_op jit(solution)/shard_map/ppermute | solution.py:295
  45.2 2.8 %collective-permute-start.15 = (f32[1,128]{1,0:T(1,128)S(1)}, f32[1,128]{1,0:T(1,128)S(1)}, u32[]{:S(2)}, u32[]{:S(2)}) collective-permute-start(f32[1,128]{1,0:T(1,128)S(1)} %get-tuple-element.38), channel_id=1, source_target_pairs={{0,1},{1,0},{2,3},{3,2},{4,5},{5,4},{6,7},{7,6},{8,9},{9,8},{10,11... | collective-permute-start | bytes 1544 | tf_op jit(solution)/shard_map/ppermute | solution.py:295
  48.0 0.9 %collective-permute-done.13.refs_0_ = f32[1,128]{1,0:T(1,128)S(1)} collective-permute-done((f32[1,128]{1,0:T(1,128)S(1)}, f32[1,128]{1,0:T(1,128)S(1)}, u32[]{:S(2)}, u32[]{:S(2)}) %collective-permute-start.13) | collective-permute-done | bytes 544 | tf_op jit(solution)/shard_map/ppermute | solution.py:295
  48.9 0.0 collective-permute-done.14.refs_1_
  48.9 0.6 %collective-permute-done.15.refs_2_ = f32[1,128]{1,0:T(1,128)S(1)} collective-permute-done((f32[1,128]{1,0:T(1,128)S(1)}, f32[1,128]{1,0:T(1,128)S(1)}, u32[]{:S(2)}, u32[]{:S(2)}) %collective-permute-start.15) | collective-permute-done | bytes 544 | tf_op jit(solution)/shard_map/ppermute | solution.py:295
  49.5 0.8 %shard_map.45 = f32[1,512]{1,0:T(1,128)} custom-call(f32[1,128]{1,0:T(1,128)S(1)} %collective-permute-done.13.refs_0_, f32[1,128]{1,0:T(1,128)S(1)} %collective-permute-done.14.refs_1_, f32[1,128]{1,0:T(1,128)S(1)} %collective-permute-done.15.refs_2_, f32[1,128]{1,0:T(1,128)S(1)} %get-tuple-element.39.refs_3_, s32[1,512]{1,0:T(1,128)S(1)} %get-tuple-element.40.refs_4_), custom_call_target="tpu_custom_call" | custom-call | flops 262144 | bytes 2048 | tf_op jit(solution)/shard_map/pallas_call | solution.py:211
  (3 shorter events, 0.1 us)
Async XLA Ops:
  2.9 13.5 %collective-permute-start = (bf16[784,128]{1,0:T(8,128)(2,1)S(1)}, bf16[784,128]{1,0:T(8,128)(2,1)S(1)}, u32[]{:S(2)}, u32[]{:S(2)}) collective-permute-start(bf16[784,128]{1,0:T(8,128)(2,1)S(1)} %get-tuple-element.24), channel_id=1, source_target_pairs={{0,2},{1,3},{2,0},{3,1},{4,6},{5,7},{6,4},{7,5},{8,10},{9,11},{10,... | collective-permute-start | bytes 602120 | tf_op jit(solution)/shard_map/ppermute | solution.py:295
  7.0 12.8 %collective-permute-start.2 = (bf16[784,128]{1,0:T(8,128)(2,1)S(1)}, bf16[784,128]{1,0:T(8,128)(2,1)S(1)}, u32[]{:S(2)}, u32[]{:S(2)}) collective-permute-start(bf16[784,128]{1,0:T(8,128)(2,1)S(1)} %get-tuple-element.26), channel_id=1, source_target_pairs={{0,1},{1,0},{2,3},{3,2},{4,5},{5,4},{6,7},{7,6},{8,9},{9,8},{10,11... | collective-permute-start | bytes 602120 | tf_op jit(solution)/shard_map/ppermute | solution.py:295
  8.6 16.7 %collective-permute-start.9 = (bf16[784,128]{1,0:T(8,128)(2,1)S(1)}, bf16[784,128]{1,0:T(8,128)(2,1)S(1)}, u32[]{:S(2)}, u32[]{:S(2)}) collective-permute-start(bf16[784,128]{1,0:T(8,128)(2,1)S(1)} %get-tuple-element.27.refs_0_.refs_2_.refs_3_), channel_id=1, source_target_pairs={{20,0},{0,8},{8,24},{24,16},{16,4},{4,12},{12,28},{28,20},{21,1},{... | collective-permute-start | bytes 602120 | tf_op jit(solution)/shard_map/ppermute | solution.py:289
  10.1 16.8 %collective-permute-start.6 = (bf16[784,128]{1,0:T(8,128)(2,1)S(1)}, bf16[784,128]{1,0:T(8,128)(2,1)S(1)}, u32[]{:S(2)}, u32[]{:S(2)}) collective-permute-start(bf16[784,128]{1,0:T(8,128)(2,1)S(1)} %get-tuple-element.27.refs_0_.refs_2_.refs_3_), channel_id=1, source_target_pairs={{8,0},{24,8},{16,24},{4,16},{12,4},{28,12},{20,28},{0,20},{9,1},{2... | collective-permute-start | bytes 602120 | tf_op jit(solution)/shard_map/ppermute | solution.py:289
  16.4 8.7 %collective-permute-start.1 = (bf16[784,128]{1,0:T(8,128)(2,1)S(1)}, bf16[784,128]{1,0:T(8,128)(2,1)S(1)}, u32[]{:S(2)}, u32[]{:S(2)}) collective-permute-start(bf16[784,128]{1,0:T(8,128)(2,1)S(1)} %get-tuple-element.25), channel_id=1, source_target_pairs={{0,3},{1,2},{2,1},{3,0},{4,7},{5,6},{6,5},{7,4},{8,11},{9,10},{10,... | collective-permute-start | bytes 602120 | tf_op jit(solution)/shard_map/ppermute | solution.py:295
  19.9 11.6 %collective-permute-start.8 = (bf16[2,784,128]{2,1,0:T(8,128)(2,1)S(1)}, bf16[2,784,128]{2,1,0:T(8,128)(2,1)S(1)}, u32[]{:S(2)}, u32[]{:S(2)}) collective-permute-start(bf16[2,784,128]{2,1,0:T(8,128)(2,1)S(1)} %shard_map.40), channel_id=1, source_target_pairs={{20,0},{0,8},{8,24},{24,16},{16,4},{4,12},{12,28},{28,20},{21,1},{... | collective-permute-start | bytes 1204232 | tf_op jit(solution)/shard_map/ppermute | solution.py:289
  21.5 12.2 %collective-permute-start.5 = (bf16[2,784,128]{2,1,0:T(8,128)(2,1)S(1)}, bf16[2,784,128]{2,1,0:T(8,128)(2,1)S(1)}, u32[]{:S(2)}, u32[]{:S(2)}) collective-permute-start(bf16[2,784,128]{2,1,0:T(8,128)(2,1)S(1)} %shard_map.40), channel_id=1, source_target_pairs={{8,0},{24,8},{16,24},{4,16},{12,4},{28,12},{20,28},{0,20},{9,1},{2... | collective-permute-start | bytes 1204232 | tf_op jit(solution)/shard_map/ppermute | solution.py:289
  25.2 9.7 %collective-permute-start.3 = (bf16[4,784,128]{2,1,0:T(8,128)(2,1)S(1)}, bf16[4,784,128]{2,1,0:T(8,128)(2,1)S(1)}, u32[]{:S(2)}, u32[]{:S(2)}) collective-permute-start(bf16[4,784,128]{2,1,0:T(8,128)(2,1)S(1)} %shard_map.38), channel_id=1, source_target_pairs={{4,0},{12,8},{28,24},{20,16},{0,4},{8,12},{24,28},{16,20},{5,1},{1... | collective-permute-start | bytes 2408456 | tf_op jit(solution)/shard_map/ppermute | solution.py:289
  25.3 11.6 %collective-permute-start.7 = (bf16[1,784,128]{2,1,0:T(8,128)(2,1)S(1)}, bf16[1,784,128]{2,1,0:T(8,128)(2,1)S(1)}, u32[]{:S(2)}, u32[]{:S(2)}) collective-permute-start(bf16[1,784,128]{2,1,0:T(8,128)(2,1)S(1)} %shard_map.39), channel_id=1, source_target_pairs={{20,0},{0,8},{8,24},{24,16},{16,4},{4,12},{12,28},{28,20},{21,1},{... | collective-permute-start | bytes 602120 | tf_op jit(solution)/shard_map/ppermute | solution.py:289
  26.9 10.0 %collective-permute-start.4 = (bf16[1,784,128]{2,1,0:T(8,128)(2,1)S(1)}, bf16[1,784,128]{2,1,0:T(8,128)(2,1)S(1)}, u32[]{:S(2)}, u32[]{:S(2)}) collective-permute-start(bf16[1,784,128]{2,1,0:T(8,128)(2,1)S(1)} %shard_map.39), channel_id=1, source_target_pairs={{8,0},{24,8},{16,24},{4,16},{12,4},{28,12},{20,28},{0,20},{9,1},{2... | collective-permute-start | bytes 602120 | tf_op jit(solution)/shard_map/ppermute | solution.py:289
  38.3 1.9 %collective-permute-start.10 = (f32[1,512]{1,0:T(1,128)S(1)}, f32[1,512]{1,0:T(1,128)S(1)}, u32[]{:S(2)}, u32[]{:S(2)}) collective-permute-start(f32[1,512]{1,0:T(1,128)S(1)} %get-tuple-element.33), channel_id=1, source_target_pairs={{4,0},{12,8},{28,24},{20,16},{0,4},{8,12},{24,28},{16,20},{5,1},{1... | collective-permute-start | bytes 6152 | tf_op jit(solution)/shard_map/ppermute | solution.py:289
  38.4 3.1 %collective-permute-start.11 = (f32[1,512]{1,0:T(1,128)S(1)}, f32[1,512]{1,0:T(1,128)S(1)}, u32[]{:S(2)}, u32[]{:S(2)}) collective-permute-start(f32[1,512]{1,0:T(1,128)S(1)} %get-tuple-element.34), channel_id=1, source_target_pairs={{20,0},{0,8},{8,24},{24,16},{16,4},{4,12},{12,28},{28,20},{21,1},{... | collective-permute-start | bytes 6152 | tf_op jit(solution)/shard_map/ppermute | solution.py:289
  40.0 3.6 %collective-permute-start.12 = (f32[1,512]{1,0:T(1,128)S(1)}, f32[1,512]{1,0:T(1,128)S(1)}, u32[]{:S(2)}, u32[]{:S(2)}) collective-permute-start(f32[1,512]{1,0:T(1,128)S(1)} %get-tuple-element.35), channel_id=1, source_target_pairs={{8,0},{24,8},{16,24},{4,16},{12,4},{28,12},{20,28},{0,20},{9,1},{2... | collective-permute-start | bytes 6152 | tf_op jit(solution)/shard_map/ppermute | solution.py:289
  43.6 5.3 %collective-permute-start.13 = (f32[1,128]{1,0:T(1,128)S(1)}, f32[1,128]{1,0:T(1,128)S(1)}, u32[]{:S(2)}, u32[]{:S(2)}) collective-permute-start(f32[1,128]{1,0:T(1,128)S(1)} %get-tuple-element.36), channel_id=1, source_target_pairs={{0,3},{1,2},{2,1},{3,0},{4,7},{5,6},{6,5},{7,4},{8,11},{9,10},{10,... | collective-permute-start | bytes 1544 | tf_op jit(solution)/shard_map/ppermute | solution.py:295
  44.2 4.8 %collective-permute-start.14 = (f32[1,128]{1,0:T(1,128)S(1)}, f32[1,128]{1,0:T(1,128)S(1)}, u32[]{:S(2)}, u32[]{:S(2)}) collective-permute-start(f32[1,128]{1,0:T(1,128)S(1)} %get-tuple-element.37), channel_id=1, source_target_pairs={{0,2},{1,3},{2,0},{3,1},{4,6},{5,7},{6,4},{7,5},{8,10},{9,11},{10,... | collective-permute-start | bytes 1544 | tf_op jit(solution)/shard_map/ppermute | solution.py:295
  45.2 4.3 %collective-permute-start.15 = (f32[1,128]{1,0:T(1,128)S(1)}, f32[1,128]{1,0:T(1,128)S(1)}, u32[]{:S(2)}, u32[]{:S(2)}) collective-permute-start(f32[1,128]{1,0:T(1,128)S(1)} %get-tuple-element.38), channel_id=1, source_target_pairs={{0,1},{1,0},{2,3},{3,2},{4,5},{5,4},{6,7},{7,6},{8,9},{9,8},{10,11... | collective-permute-start | bytes 1544 | tf_op jit(solution)/shard_map/ppermute | solution.py:295

commit v8 on v7

--- a/solution.py
+++ b/solution.py
@@ -35,7 +35,7 @@
     for diff in range(1, size // 2 + 1):
         found = [
             (a, b)
-            for b in [1 % size] + offsets
+            for b in [(size - 1) % size] + offsets
             for a in offsets
             if (a - b) % size in (diff, size - diff)
         ]
@@ -69,7 +69,8 @@
     for copy in copies:
         copy.start()
     code = code_ref[...]
-    rel = (code & (groups - 1)) ^ lax.axis_index(axis)
+    shift = (code - lax.axis_index(axis)) & (groups - 1)
+    rel = jnp.maximum(jnp.where(2 * shift > groups, 2 * (groups - shift), 2 * shift - 1), 0)
     label = code >> (groups.bit_length() - 1)
     lines = max(8, groups)
     onehot = lax.broadcasted_iota(jnp.int32, (lines, rows), 0) == rel
@@ -114,9 +115,9 @@
         refs[-1][k] = ref[...]
 
 
-def score_kernel(sources, tasks, groups, roles, first, last, *refs):
+def score_kernel(sources, tasks, groups, done, first, *refs):
     *refs, flat_ref, side_ref = refs
-    outs = 2 + (roles if last else 0)
+    outs = 2 + len(done)
     inputs, (row_ref, column_ref, *out_refs) = refs[:-outs], refs[-outs:]
     capacity = LANES
     slots = groups * capacity
@@ -166,7 +167,7 @@
                 row_ref[left, rows, :] = best
             best = jnp.max(scores.reshape(count // 8, 8, width), axis=0)
             column_ref[right, :, columns] = jnp.maximum(column_ref[right, :, columns], best)
-    for role, out_ref in enumerate(out_refs):
+    for role, out_ref in zip(done, out_refs):
         best = jnp.max(column_ref[role], axis=0, keepdims=True)
         turned = [
             jnp.max(
@@ -237,7 +238,7 @@
     )[0]
 
 
-def score(held, tasks, acc, last, slots, width):
+def score(held, tasks, acc, done, slots, width):
     roles, groups = len(held), len(held[0])
     used = sorted(
         {(left, k) for left, ks, _, _, _ in tasks for k in ks}
@@ -255,11 +256,11 @@
         jax.ShapeDtypeStruct((roles, slots, LANES), jnp.float32),
         jax.ShapeDtypeStruct((roles, 8, slots), jnp.float32),
     ]
-    ends = [jax.ShapeDtypeStruct((1, slots), jnp.float32)] * roles if last else []
+    ends = [jax.ShapeDtypeStruct((1, slots), jnp.float32)] * len(done)
     tiles = sum(len(task[1]) * len(task[3]) for task in tasks)
     count = len(arrays)
     got = call(
-        lambda *refs: score_kernel(sources, tasks, groups, roles, not acc, last, *refs),
+        lambda *refs: score_kernel(sources, tasks, groups, done, not acc, *refs),
         states + ends,
         [
             pltpu.VMEM((roles, slots, width), jnp.bfloat16),
@@ -288,11 +289,12 @@
         perm = [(ring[(e + offset) % shards], ring[e]) for e in range(shards)]
         return lax.ppermute(x, "shard", perm)
 
-    def exchange(blocks, last=()):
+    def exchange(blocks, way, last=()):
         got = list(blocks)
         for k in range(1, groups):
-            block = after(blocks[k], got[2]) if k > 2 and last else blocks[k]
-            got[k] = lax.ppermute(block, "group", [(z, z ^ k) for z in range(groups)])
+            shift = way * ((k + 1) // 2 if k % 2 else -(k // 2))
+            block = after(blocks[k], got[1]) if last and k > 2 else blocks[k]
+            got[k] = lax.ppermute(block, "group", [(z, (z + shift) % groups) for z in range(groups)])
         return got
 
     code = row_cluster * groups + row_group[:, 0]
@@ -317,7 +319,7 @@
     near = [r for r in range(1, roles) if 2 * offsets[r] != shards]
     far = [r for r in range(1, roles) if r not in near]
     first = {r: from_offset(send[0], offsets[r]) for r in near}
-    own = exchange(send, True)
+    own = exchange(send, 1, True)
     held = [[None] * groups for _ in offsets]
     held[0] = [(x, None) for x in own]
     for r in near:
@@ -333,7 +335,8 @@
     got = {r: from_offset(stack(own, 0), offsets[r]) for r in far}
     everything = [(0, 0, False)]
     everything += [(offsets.index(a), offsets.index(b), both) for a, b, both in pairs]
-    steps = [[], [], []]
+    steps = [[] for _ in range(4)]
+    final = [0] * roles
     for left, right, both in everything:
         for left_ks in (early, late):
             for right_ks in (early, late):
@@ -343,15 +346,21 @@
                         if role in far:
                             step = max(step, 1)
                         elif ks is late:
-                            step = max(step, 2 if role else 1)
+                            step = max(step, (3 if role == near[0] else 2) if role else 1)
                     steps[step].append((left, left_ks, right, right_ks, both))
-    steps = [tasks for tasks in steps if tasks]
-    acc = []
-    for i, tasks in enumerate(steps):
-        if i == 1:
-            for r in far:
-                held[r] = [(got[r], k) for k in range(groups)]
-        acc, partial = score(held, tasks, acc, i == len(steps) - 1, slots, width)
+                    final[right] = max(final[right], step)
+                    if both:
+                        final[left] = max(final[left], step)
+    acc, partial = [], [None] * roles
+    for step, tasks in enumerate(steps):
+        if tasks:
+            if step == 1:
+                for r in far:
+                    held[r] = [(got[r], k) for k in range(groups)]
+            done = [r for r in range(roles) if final[r] == step]
+            acc, ends = score(held, tasks, acc, done, slots, width)
+            for r, end in zip(done, ends):
+                partial[r] = end
 
     others = [from_offset(partial[r], -offsets[r]) for r in range(1, roles)]
     best = call(
@@ -362,7 +371,7 @@
         roles * slots,
         4 * roles * slots,
     )
-    back = exchange(best)
+    back = exchange(best, -1)
     (result,) = call(
         lambda *refs: place_kernel(groups, *refs),
         [jax.ShapeDtypeStruct((1, rows), jnp.float32)],

time: 50.4 us -> 48.6 us (0.964)
  waiting for transfers between devices: 21 us -> 16.6 us
  starting transfers between devices: 20.8 us -> 22.8 us
  Pallas kernels: 7.71 us -> 8.31 us
    ppermute x10, waiting for transfers between devices: 9.93 us -> 7.1 us  [from_offset(): return lax.ppermute(x, 'shard', perm)]
    ppermute x6, starting transfers between devices: 13.5 us -> 15.3 us  [exchange(): lax.ppermute(block, 'group', [(z, (z + shift) % groups) for z in range(gr...]
    ppermute x6, waiting for transfers between devices: 11 us -> 9.45 us  [exchange(): lax.ppermute(block, 'group', [(z, (z + shift) % groups) for z in range(gr...]
    pallas_call x9 -> x10, Pallas kernels: 7.71 us -> 8.31 us  [call(): pl.pallas_call(kernel, out_shape=out_shape, in_specs=in_specs or in_vmem(...]
  transfers between devices with their start and end apart: 16 -> 16, of which waited for: 8 -> 8; matrix products, arithmetic and copies ran while one was open for 0% -> 0% of each run, Pallas kernels for 7% -> 11%
where the time goes in v8:
time: 48.6 us; the launch traced here: 48.4 us
  starting transfers between devices  22.8 us (47%)
  waiting for transfers between devices  16.6 us (34%)
  Pallas kernels  8.31 us (17%)
  other arithmetic  0.7 us (1%)
    ppermute x6, starting transfers between devices, exchange(): lax.ppermute(block, 'group', [(z, (z + shift) % groups) for z in range(gr...  15.3 us
    ppermute x6, waiting for transfers between devices, exchange(): lax.ppermute(block, 'group', [(z, (z + shift) % groups) for z in range(gr...  9.45 us
    pallas_call x10, Pallas kernels, call(): pl.pallas_call(kernel, out_shape=out_shape, in_specs=in_specs or in_vmem(...  8.31 us
    ppermute x10, starting transfers between devices, from_offset(): return lax.ppermute(x, 'shard', perm)  7.41 us
    ppermute x10, waiting for transfers between devices, from_offset(): return lax.ppermute(x, 'shard', perm)  7.1 us
  transfers between devices with their start and end apart: 16, of which 8 were waited for; matrix products, arithmetic and copies ran while one was open for 0% of the time, Pallas kernels for 11%

profile of v8, /device:TPU:0, one launch (start us, length us, event | category | flops | bytes accessed | tf_op | source)
XLA Modules:
  0.0 48.4 jit_solution(2452894159287600850)
XLA Ops:
  0.0 0.7 %multiply_add_fusion = s32[512]{0:T(512)S(1)} fusion(s32[512]{0:T(512)} %bitcast.4, s32[512]{0:T(512)} %param.5), kind=kLoop, calls=%fused_computation | loop fusion | flops 1024 | bytes 6144 | tf_op jit(solution)/shard_map/add | solution.py:300
  0.7 2.2 %shard_map.37 = (bf16[784,128]{1,0:T(8,128)(2,1)S(1)}, bf16[784,128]{1,0:T(8,128)(2,1)S(1)}, bf16[784,128]{1,0:T(8,128)(2,1)S(1)}, bf16[784,128]{1,0:T(8,128)(2,1)S(1)}, s32[1,512]{1,0:T(1,128)S(1)}) custom-call(bf16[512,768]{1,0:T(8,128)(2,1)} %refs_0_.1, s32[1,512]{1,0:T(1,128)S(1)} %bitcast.3), custom_call_target="tpu_custom_call" | custom-call | flops 402653184 | bytes 1572864 | tf_op jit(solution)/shard_map/pallas_call | solution.py:212
  2.9 3.1 %collective-permute-start = (bf16[784,128]{1,0:T(8,128)(2,1)S(1)}, bf16[784,128]{1,0:T(8,128)(2,1)S(1)}, u32[]{:S(2)}, u32[]{:S(2)}) collective-permute-start(bf16[784,128]{1,0:T(8,128)(2,1)S(1)} %get-tuple-element.26), channel_id=1, source_target_pairs={{0,1},{1,2},{2,3},{3,0},{4,5},{5,6},{6,7},{7,4},{8,9},{9,10},{10,1... | collective-permute-start | bytes 602120 | tf_op jit(solution)/shard_map/ppermute | solution.py:297
  6.0 2.1 %collective-permute-start.2 = (bf16[784,128]{1,0:T(8,128)(2,1)S(1)}, bf16[784,128]{1,0:T(8,128)(2,1)S(1)}, u32[]{:S(2)}, u32[]{:S(2)}) collective-permute-start(bf16[784,128]{1,0:T(8,128)(2,1)S(1)} %get-tuple-element.28), channel_id=1, source_target_pairs={{0,3},{1,0},{2,1},{3,2},{4,7},{5,4},{6,5},{7,6},{8,11},{9,8},{10,9... | collective-permute-start | bytes 602120 | tf_op jit(solution)/shard_map/ppermute | solution.py:297
  8.1 1.6 %collective-permute-start.8 = (bf16[784,128]{1,0:T(8,128)(2,1)S(1)}, bf16[784,128]{1,0:T(8,128)(2,1)S(1)}, u32[]{:S(2)}, u32[]{:S(2)}) collective-permute-start(bf16[784,128]{1,0:T(8,128)(2,1)S(1)} %get-tuple-element.29.refs_0_.refs_2_.refs_3_), channel_id=1, source_target_pairs={{20,0},{0,8},{8,24},{24,16},{16,4},{4,12},{12,28},{28,20},{21,1},{... | collective-permute-start | bytes 602120 | tf_op jit(solution)/shard_map/ppermute | solution.py:290
  9.8 0.1 collective-permute-start.5
  9.9 4.1 %collective-permute-done.refs_1_.refs_0_.refs_2_ = bf16[784,128]{1,0:T(8,128)(2,1)S(1)} collective-permute-done((bf16[784,128]{1,0:T(8,128)(2,1)S(1)}, bf16[784,128]{1,0:T(8,128)(2,1)S(1)}, u32[]{:S(2)}, u32[]{:S(2)}) %collective-permute-start) | collective-permute-done | bytes 200736 | tf_op jit(solution)/shard_map/ppermute | solution.py:297
  13.9 6.3 %collective-permute-start.1 = (bf16[784,128]{1,0:T(8,128)(2,1)S(1)}, bf16[784,128]{1,0:T(8,128)(2,1)S(1)}, u32[]{:S(2)}, u32[]{:S(2)}) collective-permute-start(bf16[784,128]{1,0:T(8,128)(2,1)S(1)} %get-tuple-element.27), channel_id=1, source_target_pairs={{0,2},{1,3},{2,0},{3,1},{4,6},{5,7},{6,4},{7,5},{8,10},{9,11},{10,... | collective-permute-start | bytes 602120 | tf_op jit(solution)/shard_map/ppermute | solution.py:297
  20.2 0.0 collective-permute-done.2.refs_2_.refs_1_.refs_0_
  20.2 1.6 %collective-permute-start.7 = (bf16[2,784,128]{2,1,0:T(8,128)(2,1)S(1)}, bf16[2,784,128]{2,1,0:T(8,128)(2,1)S(1)}, u32[]{:S(2)}, u32[]{:S(2)}) collective-permute-start(bf16[2,784,128]{2,1,0:T(8,128)(2,1)S(1)} %shard_map.39), channel_id=1, source_target_pairs={{20,0},{0,8},{8,24},{24,16},{16,4},{4,12},{12,28},{28,20},{21,1},{... | collective-permute-start | bytes 1204232 | tf_op jit(solution)/shard_map/ppermute | solution.py:290
  21.8 0.3 collective-permute-start.4
  22.0 3.9 %collective-permute-done.1.refs_3_.refs_0_ = bf16[784,128]{1,0:T(8,128)(2,1)S(1)} collective-permute-done((bf16[784,128]{1,0:T(8,128)(2,1)S(1)}, bf16[784,128]{1,0:T(8,128)(2,1)S(1)}, u32[]{:S(2)}, u32[]{:S(2)}) %collective-permute-start.1) | collective-permute-done | bytes 200736 | tf_op jit(solution)/shard_map/ppermute | solution.py:297
  25.9 0.1 shard_map.38
  26.0 0.1 collective-permute-start.3
  26.1 0.0 collective-permute-done.8.refs_6_.refs_3_
  26.1 1.6 %collective-permute-start.6 = (bf16[1,784,128]{2,1,0:T(8,128)(2,1)S(1)}, bf16[1,784,128]{2,1,0:T(8,128)(2,1)S(1)}, u32[]{:S(2)}, u32[]{:S(2)}) collective-permute-start(bf16[1,784,128]{2,1,0:T(8,128)(2,1)S(1)} %shard_map.40), channel_id=1, source_target_pairs={{20,0},{0,8},{8,24},{24,16},{16,4},{4,12},{12,28},{28,20},{21,1},{... | collective-permute-start | bytes 602120 | tf_op jit(solution)/shard_map/ppermute | solution.py:290
  27.7 0.0 collective-permute-done.5.refs_4_.refs_6_
  27.7 0.3 collective-permute-start.10
  27.9 3.9 %collective-permute-done.7.refs_5_.refs_2_ = bf16[2,784,128]{2,1,0:T(8,128)(2,1)S(1)} collective-permute-done((bf16[2,784,128]{2,1,0:T(8,128)(2,1)S(1)}, bf16[2,784,128]{2,1,0:T(8,128)(2,1)S(1)}, u32[]{:S(2)}, u32[]{:S(2)}) %collective-permute-start.7) | collective-permute-done | bytes 401440 | tf_op jit(solution)/shard_map/ppermute | solution.py:290
  31.8 0.0 collective-permute-done.4.refs_3_.refs_5_
  31.8 1.2 %shard_map.41 = (f32[4,512,128]{2,1,0:T(8,128)S(1)}, f32[4,8,512]{2,1,0:T(8,128)S(1)}) custom-call(bf16[784,128]{1,0:T(8,128)(2,1)S(1)} %collective-permute-done.2.refs_2_.refs_1_.refs_0_, bf16[784,128]{1,0:T(8,128)(2,1)S(1)} %collective-permute-done.refs_1_.refs_0_.refs_2_, bf16[784,128]{1,0:T(8,128)(2,1)S(1)} %get-tuple-element.29.refs_0_.refs_2_.refs_3_, ...), custom_call_target="tpu_custom_call" | custom-call | flops 679477248 | bytes 1769472 | tf_op jit(solution)/shard_map/pallas_call | solution.py:212
  33.0 0.0 collective-permute-done.3.refs_4_
  33.0 2.1 %shard_map.42 = (f32[4,512,128]{2,1,0:T(8,128)S(1)}, f32[4,8,512]{2,1,0:T(8,128)S(1)}) custom-call(bf16[784,128]{1,0:T(8,128)(2,1)S(1)} %collective-permute-done.1.refs_3_.refs_0_, bf16[784,128]{1,0:T(8,128)(2,1)S(1)} %collective-permute-done.2.refs_2_.refs_1_.refs_0_, ...), custom_call_target="tpu_custom_call", output_to_operand_aliasing={{0}: (7, {}), {1}: (8, {})} | custom-call | flops 956301312 | bytes 2162688 | tf_op jit(solution)/shard_map/pallas_call | solution.py:212
  35.1 1.0 %collective-permute-done.6.refs_7_.refs_1_ = bf16[1,784,128]{2,1,0:T(8,128)(2,1)S(1)} collective-permute-done((bf16[1,784,128]{2,1,0:T(8,128)(2,1)S(1)}, bf16[1,784,128]{2,1,0:T(8,128)(2,1)S(1)}, u32[]{:S(2)}, u32[]{:S(2)}) %collective-permute-start.6) | collective-permute-done | bytes 200736 | tf_op jit(solution)/shard_map/ppermute | solution.py:290
  36.1 1.1 %shard_map.43 = (f32[4,512,128]{2,1,0:T(8,128)S(1)}, f32[4,8,512]{2,1,0:T(8,128)S(1)}, f32[1,512]{1,0:T(1,128)S(1)}, f32[1,512]{1,0:T(1,128)S(1)}) custom-call(bf16[784,128]{1,0:T(8,128)(2,1)S(1)} %collective-permute-done.1.refs_3_.refs_0_, ...), custom_call_target="tpu_custom_call", output_to_operand_aliasing={{0}: (8, {}), {1}: (9, {})} | custom-call | flops 276824064 | bytes 2359296 | tf_op jit(solution)/shard_map/pallas_call | solution.py:212
  37.2 0.2 collective-permute-start.9
  37.4 0.0 collective-permute-done.10.refs_0_
  37.4 0.8 %shard_map.44 = (f32[4,512,128]{2,1,0:T(8,128)S(1)}, f32[4,8,512]{2,1,0:T(8,128)S(1)}, f32[1,512]{1,0:T(1,128)S(1)}, f32[1,512]{1,0:T(1,128)S(1)}) custom-call(bf16[1,784,128]{2,1,0:T(8,128)(2,1)S(1)} %collective-permute-done.10.refs_0_, ...), custom_call_target="tpu_custom_call", output_to_operand_aliasing={{0}: (4, {}), {1}: (5, {})} | custom-call | flops 100663296 | bytes 983040 | tf_op jit(solution)/shard_map/pallas_call | solution.py:212
  38.3 0.1 collective-permute-start.11
  38.3 1.7 %collective-permute-start.12 = (f32[1,512]{1,0:T(1,128)S(1)}, f32[1,512]{1,0:T(1,128)S(1)}, u32[]{:S(2)}, u32[]{:S(2)}) collective-permute-start(f32[1,512]{1,0:T(1,128)S(1)} %get-tuple-element.39), channel_id=1, source_target_pairs={{8,0},{24,8},{16,24},{4,16},{12,4},{28,12},{20,28},{0,20},{9,1},{2... | collective-permute-start | bytes 6152 | tf_op jit(solution)/shard_map/ppermute | solution.py:290
  40.1 0.0 collective-permute-done.9.refs_1_
  40.1 1.3 %collective-permute-done.11.refs_2_ = f32[1,512]{1,0:T(1,128)S(1)} collective-permute-done((f32[1,512]{1,0:T(1,128)S(1)}, f32[1,512]{1,0:T(1,128)S(1)}, u32[]{:S(2)}, u32[]{:S(2)}) %collective-permute-start.11) | collective-permute-done | bytes 2080 | tf_op jit(solution)/shard_map/ppermute | solution.py:290
  41.3 0.9 %collective-permute-done.12.refs_3_ = f32[1,512]{1,0:T(1,128)S(1)} collective-permute-done((f32[1,512]{1,0:T(1,128)S(1)}, f32[1,512]{1,0:T(1,128)S(1)}, u32[]{:S(2)}, u32[]{:S(2)}) %collective-permute-start.12) | collective-permute-done | bytes 2080 | tf_op jit(solution)/shard_map/ppermute | solution.py:290
  42.2 0.0 collective-permute-start.13
  42.2 1.2 %collective-permute-start.14 = (f32[1,128]{1,0:T(1,128)S(1)}, f32[1,128]{1,0:T(1,128)S(1)}, u32[]{:S(2)}, u32[]{:S(2)}) collective-permute-start(f32[1,128]{1,0:T(1,128)S(1)} %get-tuple-element.41), channel_id=1, source_target_pairs={{0,1},{1,2},{2,3},{3,0},{4,5},{5,6},{6,7},{7,4},{8,9},{9,10},{10,1... | collective-permute-start | bytes 1544 | tf_op jit(solution)/shard_map/ppermute | solution.py:297
  43.4 2.7 %collective-permute-start.15 = (f32[1,128]{1,0:T(1,128)S(1)}, f32[1,128]{1,0:T(1,128)S(1)}, u32[]{:S(2)}, u32[]{:S(2)}) collective-permute-start(f32[1,128]{1,0:T(1,128)S(1)} %get-tuple-element.42), channel_id=1, source_target_pairs={{0,3},{1,0},{2,1},{3,2},{4,7},{5,4},{6,5},{7,6},{8,11},{9,8},{10,9... | collective-permute-start | bytes 1544 | tf_op jit(solution)/shard_map/ppermute | solution.py:297
  46.1 0.6 %collective-permute-done.13.refs_0_ = f32[1,128]{1,0:T(1,128)S(1)} collective-permute-done((f32[1,128]{1,0:T(1,128)S(1)}, f32[1,128]{1,0:T(1,128)S(1)}, u32[]{:S(2)}, u32[]{:S(2)}) %collective-permute-start.13) | collective-permute-done | bytes 544 | tf_op jit(solution)/shard_map/ppermute | solution.py:297
  46.7 1.0 %collective-permute-done.14.refs_1_ = f32[1,128]{1,0:T(1,128)S(1)} collective-permute-done((f32[1,128]{1,0:T(1,128)S(1)}, f32[1,128]{1,0:T(1,128)S(1)}, u32[]{:S(2)}, u32[]{:S(2)}) %collective-permute-start.14) | collective-permute-done | bytes 544 | tf_op jit(solution)/shard_map/ppermute | solution.py:297
  47.6 0.0 collective-permute-done.15.refs_2_
  47.6 0.8 %shard_map.46 = f32[1,512]{1,0:T(1,128)} custom-call(f32[1,128]{1,0:T(1,128)S(1)} %collective-permute-done.13.refs_0_, f32[1,128]{1,0:T(1,128)S(1)} %collective-permute-done.14.refs_1_, f32[1,128]{1,0:T(1,128)S(1)} %collective-permute-done.15.refs_2_, f32[1,128]{1,0:T(1,128)S(1)} %get-tuple-element.43.refs_3_, s32[1,512]{1,0:T(1,128)S(1)} %get-tuple-element.44.refs_4_), custom_call_target="tpu_custom_call" | custom-call | flops 262144 | bytes 2048 | tf_op jit(solution)/shard_map/pallas_call | solution.py:212
  (3 shorter events, 0.1 us)
Async XLA Ops:
  2.9 11.0 %collective-permute-start = (bf16[784,128]{1,0:T(8,128)(2,1)S(1)}, bf16[784,128]{1,0:T(8,128)(2,1)S(1)}, u32[]{:S(2)}, u32[]{:S(2)}) collective-permute-start(bf16[784,128]{1,0:T(8,128)(2,1)S(1)} %get-tuple-element.26), channel_id=1, source_target_pairs={{0,1},{1,2},{2,3},{3,0},{4,5},{5,6},{6,7},{7,4},{8,9},{9,10},{10,1... | collective-permute-start | bytes 602120 | tf_op jit(solution)/shard_map/ppermute | solution.py:297
  6.0 14.2 %collective-permute-start.2 = (bf16[784,128]{1,0:T(8,128)(2,1)S(1)}, bf16[784,128]{1,0:T(8,128)(2,1)S(1)}, u32[]{:S(2)}, u32[]{:S(2)}) collective-permute-start(bf16[784,128]{1,0:T(8,128)(2,1)S(1)} %get-tuple-element.28), channel_id=1, source_target_pairs={{0,3},{1,0},{2,1},{3,2},{4,7},{5,4},{6,5},{7,6},{8,11},{9,8},{10,9... | collective-permute-start | bytes 602120 | tf_op jit(solution)/shard_map/ppermute | solution.py:297
  8.1 18.0 %collective-permute-start.8 = (bf16[784,128]{1,0:T(8,128)(2,1)S(1)}, bf16[784,128]{1,0:T(8,128)(2,1)S(1)}, u32[]{:S(2)}, u32[]{:S(2)}) collective-permute-start(bf16[784,128]{1,0:T(8,128)(2,1)S(1)} %get-tuple-element.29.refs_0_.refs_2_.refs_3_), channel_id=1, source_target_pairs={{20,0},{0,8},{8,24},{24,16},{16,4},{4,12},{12,28},{28,20},{21,1},{... | collective-permute-start | bytes 602120 | tf_op jit(solution)/shard_map/ppermute | solution.py:290
  9.8 17.9 %collective-permute-start.5 = (bf16[784,128]{1,0:T(8,128)(2,1)S(1)}, bf16[784,128]{1,0:T(8,128)(2,1)S(1)}, u32[]{:S(2)}, u32[]{:S(2)}) collective-permute-start(bf16[784,128]{1,0:T(8,128)(2,1)S(1)} %get-tuple-element.29.refs_0_.refs_2_.refs_3_), channel_id=1, source_target_pairs={{8,0},{24,8},{16,24},{4,16},{12,4},{28,12},{20,28},{0,20},{9,1},{2... | collective-permute-start | bytes 602120 | tf_op jit(solution)/shard_map/ppermute | solution.py:290
  13.9 12.0 %collective-permute-start.1 = (bf16[784,128]{1,0:T(8,128)(2,1)S(1)}, bf16[784,128]{1,0:T(8,128)(2,1)S(1)}, u32[]{:S(2)}, u32[]{:S(2)}) collective-permute-start(bf16[784,128]{1,0:T(8,128)(2,1)S(1)} %get-tuple-element.27), channel_id=1, source_target_pairs={{0,2},{1,3},{2,0},{3,1},{4,6},{5,7},{6,4},{7,5},{8,10},{9,11},{10,... | collective-permute-start | bytes 602120 | tf_op jit(solution)/shard_map/ppermute | solution.py:297
  20.2 11.6 %collective-permute-start.7 = (bf16[2,784,128]{2,1,0:T(8,128)(2,1)S(1)}, bf16[2,784,128]{2,1,0:T(8,128)(2,1)S(1)}, u32[]{:S(2)}, u32[]{:S(2)}) collective-permute-start(bf16[2,784,128]{2,1,0:T(8,128)(2,1)S(1)} %shard_map.39), channel_id=1, source_target_pairs={{20,0},{0,8},{8,24},{24,16},{16,4},{4,12},{12,28},{28,20},{21,1},{... | collective-permute-start | bytes 1204232 | tf_op jit(solution)/shard_map/ppermute | solution.py:290
  21.8 10.0 %collective-permute-start.4 = (bf16[2,784,128]{2,1,0:T(8,128)(2,1)S(1)}, bf16[2,784,128]{2,1,0:T(8,128)(2,1)S(1)}, u32[]{:S(2)}, u32[]{:S(2)}) collective-permute-start(bf16[2,784,128]{2,1,0:T(8,128)(2,1)S(1)} %shard_map.39), channel_id=1, source_target_pairs={{8,0},{24,8},{16,24},{4,16},{12,4},{28,12},{20,28},{0,20},{9,1},{2... | collective-permute-start | bytes 1204232 | tf_op jit(solution)/shard_map/ppermute | solution.py:290
  26.0 7.0 %collective-permute-start.3 = (bf16[4,784,128]{2,1,0:T(8,128)(2,1)S(1)}, bf16[4,784,128]{2,1,0:T(8,128)(2,1)S(1)}, u32[]{:S(2)}, u32[]{:S(2)}) collective-permute-start(bf16[4,784,128]{2,1,0:T(8,128)(2,1)S(1)} %shard_map.38), channel_id=1, source_target_pairs={{4,0},{12,8},{28,24},{20,16},{0,4},{8,12},{24,28},{16,20},{5,1},{1... | collective-permute-start | bytes 2408456 | tf_op jit(solution)/shard_map/ppermute | solution.py:290
  26.1 10.0 %collective-permute-start.6 = (bf16[1,784,128]{2,1,0:T(8,128)(2,1)S(1)}, bf16[1,784,128]{2,1,0:T(8,128)(2,1)S(1)}, u32[]{:S(2)}, u32[]{:S(2)}) collective-permute-start(bf16[1,784,128]{2,1,0:T(8,128)(2,1)S(1)} %shard_map.40), channel_id=1, source_target_pairs={{20,0},{0,8},{8,24},{24,16},{16,4},{4,12},{12,28},{28,20},{21,1},{... | collective-permute-start | bytes 602120 | tf_op jit(solution)/shard_map/ppermute | solution.py:290
  27.7 9.8 %collective-permute-start.10 = (bf16[1,784,128]{2,1,0:T(8,128)(2,1)S(1)}, bf16[1,784,128]{2,1,0:T(8,128)(2,1)S(1)}, u32[]{:S(2)}, u32[]{:S(2)}) collective-permute-start(bf16[1,784,128]{2,1,0:T(8,128)(2,1)S(1)} %shard_map.40), channel_id=1, source_target_pairs={{8,0},{24,8},{16,24},{4,16},{12,4},{28,12},{20,28},{0,20},{9,1},{2... | collective-permute-start | bytes 602120 | tf_op jit(solution)/shard_map/ppermute | solution.py:290
  37.2 2.8 %collective-permute-start.9 = (f32[1,512]{1,0:T(1,128)S(1)}, f32[1,512]{1,0:T(1,128)S(1)}, u32[]{:S(2)}, u32[]{:S(2)}) collective-permute-start(f32[1,512]{1,0:T(1,128)S(1)} %get-tuple-element.35), channel_id=1, source_target_pairs={{4,0},{12,8},{28,24},{20,16},{0,4},{8,12},{24,28},{16,20},{5,1},{1... | collective-permute-start | bytes 6152 | tf_op jit(solution)/shard_map/ppermute | solution.py:290
  38.3 3.1 %collective-permute-start.11 = (f32[1,512]{1,0:T(1,128)S(1)}, f32[1,512]{1,0:T(1,128)S(1)}, u32[]{:S(2)}, u32[]{:S(2)}) collective-permute-start(f32[1,512]{1,0:T(1,128)S(1)} %get-tuple-element.38), channel_id=1, source_target_pairs={{20,0},{0,8},{8,24},{24,16},{16,4},{4,12},{12,28},{28,20},{21,1},{... | collective-permute-start | bytes 6152 | tf_op jit(solution)/shard_map/ppermute | solution.py:290
  38.3 3.9 %collective-permute-start.12 = (f32[1,512]{1,0:T(1,128)S(1)}, f32[1,512]{1,0:T(1,128)S(1)}, u32[]{:S(2)}, u32[]{:S(2)}) collective-permute-start(f32[1,512]{1,0:T(1,128)S(1)} %get-tuple-element.39), channel_id=1, source_target_pairs={{8,0},{24,8},{16,24},{4,16},{12,4},{28,12},{20,28},{0,20},{9,1},{2... | collective-permute-start | bytes 6152 | tf_op jit(solution)/shard_map/ppermute | solution.py:290
  42.2 4.4 %collective-permute-start.13 = (f32[1,128]{1,0:T(1,128)S(1)}, f32[1,128]{1,0:T(1,128)S(1)}, u32[]{:S(2)}, u32[]{:S(2)}) collective-permute-start(f32[1,128]{1,0:T(1,128)S(1)} %get-tuple-element.40), channel_id=1, source_target_pairs={{0,2},{1,3},{2,0},{3,1},{4,6},{5,7},{6,4},{7,5},{8,10},{9,11},{10,... | collective-permute-start | bytes 1544 | tf_op jit(solution)/shard_map/ppermute | solution.py:297
  42.2 5.4 %collective-permute-start.14 = (f32[1,128]{1,0:T(1,128)S(1)}, f32[1,128]{1,0:T(1,128)S(1)}, u32[]{:S(2)}, u32[]{:S(2)}) collective-permute-start(f32[1,128]{1,0:T(1,128)S(1)} %get-tuple-element.41), channel_id=1, source_target_pairs={{0,1},{1,2},{2,3},{3,0},{4,5},{5,6},{6,7},{7,4},{8,9},{9,10},{10,1... | collective-permute-start | bytes 1544 | tf_op jit(solution)/shard_map/ppermute | solution.py:297
  43.4 4.2 %collective-permute-start.15 = (f32[1,128]{1,0:T(1,128)S(1)}, f32[1,128]{1,0:T(1,128)S(1)}, u32[]{:S(2)}, u32[]{:S(2)}) collective-permute-start(f32[1,128]{1,0:T(1,128)S(1)} %get-tuple-element.42), channel_id=1, source_target_pairs={{0,3},{1,0},{2,1},{3,2},{4,7},{5,4},{6,5},{7,6},{8,11},{9,8},{10,9... | collective-permute-start | bytes 1544 | tf_op jit(solution)/shard_map/ppermute | solution.py:297

commit v9 on v8

--- a/solution.py
+++ b/solution.py
@@ -115,12 +115,11 @@
         refs[-1][k] = ref[...]
 
 
-def score_kernel(sources, tasks, groups, done, first, *refs):
+def score_kernel(sources, tasks, turns, done, first, *refs):
     *refs, flat_ref, side_ref = refs
     outs = 2 + len(done)
     inputs, (row_ref, column_ref, *out_refs) = refs[:-outs], refs[-outs:]
     capacity = LANES
-    slots = groups * capacity
     low = jnp.float32(LOW)
     if first:
         row_ref[...] = jnp.full(row_ref.shape, low)
@@ -167,17 +166,12 @@
                 row_ref[left, rows, :] = best
             best = jnp.max(scores.reshape(count // 8, 8, width), axis=0)
             column_ref[right, :, columns] = jnp.maximum(column_ref[right, :, columns], best)
+    for role, k in turns:
+        rows = pl.ds(k * capacity, capacity)
+        turned = jnp.transpose(row_ref[role, rows, :]).reshape(capacity // 8, 8, capacity)
+        column_ref[role, :, rows] = jnp.maximum(column_ref[role, :, rows], jnp.max(turned, axis=0))
     for role, out_ref in zip(done, out_refs):
-        best = jnp.max(column_ref[role], axis=0, keepdims=True)
-        turned = [
-            jnp.max(
-                jnp.transpose(row_ref[role, pl.ds(k * capacity, capacity), :]),
-                axis=0,
-                keepdims=True,
-            )
-            for k in range(groups)
-        ]
-        out_ref[...] = jnp.maximum(best, jnp.concatenate(turned, axis=1))
+        out_ref[...] = jnp.max(column_ref[role], axis=0, keepdims=True)
 
 
 def merge_kernel(roles, *refs):
@@ -238,8 +232,8 @@
     )[0]
 
 
-def score(held, tasks, acc, done, slots, width):
-    roles, groups = len(held), len(held[0])
+def score(held, tasks, turns, acc, done, slots, width):
+    roles = len(held)
     used = sorted(
         {(left, k) for left, ks, _, _, _ in tasks for k in ks}
         | {(right, k) for _, _, right, ks, _ in tasks for k in ks},
@@ -258,9 +252,8 @@
     ]
     ends = [jax.ShapeDtypeStruct((1, slots), jnp.float32)] * len(done)
     tiles = sum(len(task[1]) * len(task[3]) for task in tasks)
-    count = len(arrays)
     got = call(
-        lambda *refs: score_kernel(sources, tasks, groups, done, not acc, *refs),
+        lambda *refs: score_kernel(sources, tasks, turns, done, not acc, *refs),
         states + ends,
         [
             pltpu.VMEM((roles, slots, width), jnp.bfloat16),
@@ -269,9 +262,9 @@
         arrays + list(acc),
         2 * tiles * LANES * LANES * width,
         2 * len(used) * LANES * width,
-        aliases={count: 0, count + 1: 1} if acc else {},
-    )
-    return got[:2], got[2:]
+        aliases={len(arrays) + i: i for i in range(len(acc))},
+    )
+    return got[: len(states)], got[len(states) :]
 
 
 def per_device(embeddings, row_group, row_cluster):
@@ -289,11 +282,11 @@
         perm = [(ring[(e + offset) % shards], ring[e]) for e in range(shards)]
         return lax.ppermute(x, "shard", perm)
 
-    def exchange(blocks, way, last=()):
+    def exchange(blocks, way, stagger=False):
         got = list(blocks)
         for k in range(1, groups):
             shift = way * ((k + 1) // 2 if k % 2 else -(k // 2))
-            block = after(blocks[k], got[1]) if last and k > 2 else blocks[k]
+            block = after(blocks[k], got[1]) if stagger and k > 2 else blocks[k]
             got[k] = lax.ppermute(block, "group", [(z, (z + shift) % groups) for z in range(groups)])
         return got
 
@@ -316,6 +309,8 @@
 
     late = [groups - 1] if groups > 1 else []
     early = list(range(groups - len(late)))
+    late = [groups - 1] if groups > 1 else []
+    early = list(range(groups - len(late)))
     near = [r for r in range(1, roles) if 2 * offsets[r] != shards]
     far = [r for r in range(1, roles) if r not in near]
     first = {r: from_offset(send[0], offsets[r]) for r in near}
@@ -324,19 +319,19 @@
     held[0] = [(x, None) for x in own]
     for r in near:
         held[r][0] = (first[r], None)
-    for ks, wait in ((early[1:], WAIT), (late, WAIT)):
-        if ks:
-            passed = []
-            block = stack([after(own[k], *passed) for k in ks], wait)
-            for r in near:
-                got = from_offset(block, offsets[r])
-                for i, k in enumerate(ks):
-                    held[r][k] = (got, i)
+    for k in range(1, groups):
+        if k == 1:
+            block = after(own[k], first[near[0]]) if near else own[k]
+        else:
+            passed = [held[r][k - 2][0] for r in near]
+            block = stack([after(own[k], *passed)], WAIT if k in late else WAIT // 20)
+        for r in near:
+            held[r][k] = (from_offset(block, offsets[r]), 0 if k > 1 else None)
     got = {r: from_offset(stack(own, 0), offsets[r]) for r in far}
     everything = [(0, 0, False)]
     everything += [(offsets.index(a), offsets.index(b), both) for a, b, both in pairs]
     steps = [[] for _ in range(4)]
-    final = [0] * roles
+    turn, final = {}, [0] * roles
     for left, right, both in everything:
         for left_ks in (early, late):
             for right_ks in (early, late):
@@ -351,6 +346,8 @@
                     final[right] = max(final[right], step)
                     if both:
                         final[left] = max(final[left], step)
+                        for k in left_ks:
+                            turn[left, k] = max(turn.get((left, k), step), step)
     acc, partial = [], [None] * roles
     for step, tasks in enumerate(steps):
         if tasks:
@@ -358,7 +355,8 @@
                 for r in far:
                     held[r] = [(got[r], k) for k in range(groups)]
             done = [r for r in range(roles) if final[r] == step]
-            acc, ends = score(held, tasks, acc, done, slots, width)
+            turns = sorted(x for x in turn if turn[x] == step)
+            acc, ends = score(held, tasks, turns, acc, done, slots, width)
             for r, end in zip(done, ends):
                 partial[r] = end
 

time: 48.6 us -> 49.6 us (1.021)
  starting transfers between devices: 22.8 us -> 25.6 us
  waiting for transfers between devices: 16.6 us -> 14.9 us
    ppermute x10 -> x12, starting transfers between devices: 7.41 us -> 9.81 us  [from_offset(): return lax.ppermute(x, 'shard', perm)]
    ppermute x6, waiting for transfers between devices: 9.45 us -> 7.21 us  [exchange(): lax.ppermute(block, 'group', [(z, (z + shift) % groups) for z in range(gr...]
    ppermute x10 -> x12, waiting for transfers between devices: 7.1 us -> 7.74 us  [from_offset(): return lax.ppermute(x, 'shard', perm)]
  transfers between devices with their start and end apart: 16 -> 18, of which waited for: 8 -> 10; matrix products, arithmetic and copies ran while one was open for 0% -> 0% of each run, Pallas kernels for 11% -> 10%
where the time goes in v9:
time: 49.6 us; the launch traced here: 49.4 us
  starting transfers between devices  25.6 us (52%)
  waiting for transfers between devices  14.9 us (30%)
  Pallas kernels  8.06 us (16%)
  other arithmetic  0.7 us (1%)
    ppermute x6, starting transfers between devices, exchange(): lax.ppermute(block, 'group', [(z, (z + shift) % groups) for z in range(gr...  15.8 us
    ppermute x12, starting transfers between devices, from_offset(): return lax.ppermute(x, 'shard', perm)  9.81 us
    pallas_call x10, Pallas kernels, call(): pl.pallas_call(kernel, out_shape=out_shape, in_specs=in_specs or in_vmem(...  8.06 us
    ppermute x12, waiting for transfers between devices, from_offset(): return lax.ppermute(x, 'shard', perm)  7.74 us
    ppermute x6, waiting for transfers between devices, exchange(): lax.ppermute(block, 'group', [(z, (z + shift) % groups) for z in range(gr...  7.21 us
  transfers between devices with their start and end apart: 18, of which 10 were waited for; matrix products, arithmetic and copies ran while one was open for 0% of the time, Pallas kernels for 10%

profile of v9, /device:TPU:0, one launch (start us, length us, event | category | flops | bytes accessed | tf_op | source)
XLA Modules:
  0.0 49.4 jit_solution(15971511287296589767)
XLA Ops:
  0.0 0.7 %multiply_add_fusion = s32[512]{0:T(512)S(1)} fusion(s32[512]{0:T(512)} %bitcast.4, s32[512]{0:T(512)} %param.5), kind=kLoop, calls=%fused_computation | loop fusion | flops 1024 | bytes 6144 | tf_op jit(solution)/shard_map/add | solution.py:293
  0.7 2.2 %shard_map.37 = (bf16[784,128]{1,0:T(8,128)(2,1)S(1)}, bf16[784,128]{1,0:T(8,128)(2,1)S(1)}, bf16[784,128]{1,0:T(8,128)(2,1)S(1)}, bf16[784,128]{1,0:T(8,128)(2,1)S(1)}, s32[1,512]{1,0:T(1,128)S(1)}) custom-call(bf16[512,768]{1,0:T(8,128)(2,1)} %refs_0_.1, s32[1,512]{1,0:T(1,128)S(1)} %bitcast.3), custom_call_target="tpu_custom_call" | custom-call | flops 402653184 | bytes 1572864 | tf_op jit(solution)/shard_map/pallas_call | solution.py:206
  2.9 3.1 %collective-permute-start = (bf16[784,128]{1,0:T(8,128)(2,1)S(1)}, bf16[784,128]{1,0:T(8,128)(2,1)S(1)}, u32[]{:S(2)}, u32[]{:S(2)}) collective-permute-start(bf16[784,128]{1,0:T(8,128)(2,1)S(1)} %get-tuple-element.29), channel_id=1, source_target_pairs={{0,1},{1,2},{2,3},{3,0},{4,5},{5,6},{6,7},{7,4},{8,9},{9,10},{10,1... | collective-permute-start | bytes 602120 | tf_op jit(solution)/shard_map/ppermute | solution.py:290
  6.0 0.7 %collective-permute-start.4 = (bf16[784,128]{1,0:T(8,128)(2,1)S(1)}, bf16[784,128]{1,0:T(8,128)(2,1)S(1)}, u32[]{:S(2)}, u32[]{:S(2)}) collective-permute-start(bf16[784,128]{1,0:T(8,128)(2,1)S(1)} %get-tuple-element.32.refs_0_.refs_2_.refs_3_), channel_id=1, source_target_pairs={{8,0},{24,8},{16,24},{4,16},{12,4},{28,12},{20,28},{0,20},{9,1},{2... | collective-permute-start | bytes 602120 | tf_op jit(solution)/shard_map/ppermute | solution.py:283
  6.7 2.4 %collective-permute-start.2 = (bf16[784,128]{1,0:T(8,128)(2,1)S(1)}, bf16[784,128]{1,0:T(8,128)(2,1)S(1)}, u32[]{:S(2)}, u32[]{:S(2)}) collective-permute-start(bf16[784,128]{1,0:T(8,128)(2,1)S(1)} %get-tuple-element.31), channel_id=1, source_target_pairs={{0,3},{1,0},{2,1},{3,2},{4,7},{5,4},{6,5},{7,6},{8,11},{9,8},{10,9... | collective-permute-start | bytes 602120 | tf_op jit(solution)/shard_map/ppermute | solution.py:290
  9.1 1.1 %collective-permute-start.5 = (bf16[784,128]{1,0:T(8,128)(2,1)S(1)}, bf16[784,128]{1,0:T(8,128)(2,1)S(1)}, u32[]{:S(2)}, u32[]{:S(2)}) collective-permute-start(bf16[784,128]{1,0:T(8,128)(2,1)S(1)} %get-tuple-element.32.refs_0_.refs_2_.refs_3_), channel_id=1, source_target_pairs={{20,0},{0,8},{8,24},{24,16},{16,4},{4,12},{12,28},{28,20},{21,1},{... | collective-permute-start | bytes 602120 | tf_op jit(solution)/shard_map/ppermute | solution.py:283
  10.1 3.6 %collective-permute-done.refs_1_.refs_2_ = bf16[784,128]{1,0:T(8,128)(2,1)S(1)} collective-permute-done((bf16[784,128]{1,0:T(8,128)(2,1)S(1)}, bf16[784,128]{1,0:T(8,128)(2,1)S(1)}, u32[]{:S(2)}, u32[]{:S(2)}) %collective-permute-start) | collective-permute-done | bytes 200736 | tf_op jit(solution)/shard_map/ppermute | solution.py:290
  13.7 6.5 %collective-permute-start.1 = (bf16[784,128]{1,0:T(8,128)(2,1)S(1)}, bf16[784,128]{1,0:T(8,128)(2,1)S(1)}, u32[]{:S(2)}, u32[]{:S(2)}) collective-permute-start(bf16[784,128]{1,0:T(8,128)(2,1)S(1)} %get-tuple-element.30), channel_id=1, source_target_pairs={{0,2},{1,3},{2,0},{3,1},{4,6},{5,7},{6,4},{7,5},{8,10},{9,11},{10,... | collective-permute-start | bytes 602120 | tf_op jit(solution)/shard_map/ppermute | solution.py:290
  20.2 0.0 collective-permute-done.4.refs_5_.refs_7_
  20.2 1.5 %collective-permute-start.8 = (bf16[784,128]{1,0:T(8,128)(2,1)S(1)}, bf16[784,128]{1,0:T(8,128)(2,1)S(1)}, u32[]{:S(2)}, u32[]{:S(2)}) collective-permute-start(bf16[784,128]{1,0:T(8,128)(2,1)S(1)} %collective-permute-done.refs_1_.refs_2_), channel_id=1, source_target_pairs={{20,0},{0,8},{8,24},{24,16},{16,4},{4,12},{12,28},{28,20},{21,1},{... | collective-permute-start | bytes 602120 | tf_op jit(solution)/shard_map/ppermute | solution.py:283
  21.7 0.3 collective-permute-start.7
  22.0 0.0 collective-permute-done.2.refs_2_.refs_0_.refs_1_
  22.0 0.0 collective-permute-done.5.refs_8_.refs_7_.refs_4_
  22.0 1.8 %collective-permute-start.10 = (bf16[1,784,128]{2,1,0:T(8,128)(2,1)S(1)}, bf16[1,784,128]{2,1,0:T(8,128)(2,1)S(1)}, u32[]{:S(2)}, u32[]{:S(2)}) collective-permute-start(bf16[1,784,128]{2,1,0:T(8,128)(2,1)S(1)} %shard_map.39), channel_id=1, source_target_pairs={{20,0},{0,8},{8,24},{24,16},{16,4},{4,12},{12,28},{28,20},{21,1},{... | collective-permute-start | bytes 602120 | tf_op jit(solution)/shard_map/ppermute | solution.py:283
  23.8 0.0 collective-permute-start.6
  23.8 2.1 %collective-permute-done.1.refs_3_.refs_0_ = bf16[784,128]{1,0:T(8,128)(2,1)S(1)} collective-permute-done((bf16[784,128]{1,0:T(8,128)(2,1)S(1)}, bf16[784,128]{1,0:T(8,128)(2,1)S(1)}, u32[]{:S(2)}, u32[]{:S(2)}) %collective-permute-start.1) | collective-permute-done | bytes 200736 | tf_op jit(solution)/shard_map/ppermute | solution.py:290
  25.9 1.5 %collective-permute-done.8.refs_7_.refs_6_.refs_3_ = bf16[784,128]{1,0:T(8,128)(2,1)S(1)} collective-permute-done((bf16[784,128]{1,0:T(8,128)(2,1)S(1)}, bf16[784,128]{1,0:T(8,128)(2,1)S(1)}, u32[]{:S(2)}, u32[]{:S(2)}) %collective-permute-start.8) | collective-permute-done | bytes 200736 | tf_op jit(solution)/shard_map/ppermute | solution.py:283
  27.4 1.5 %collective-permute-done.7.refs_4_.refs_6_ = bf16[784,128]{1,0:T(8,128)(2,1)S(1)} collective-permute-done((bf16[784,128]{1,0:T(8,128)(2,1)S(1)}, bf16[784,128]{1,0:T(8,128)(2,1)S(1)}, u32[]{:S(2)}, u32[]{:S(2)}) %collective-permute-start.7) | collective-permute-done | bytes 200736 | tf_op jit(solution)/shard_map/ppermute | solution.py:283
  28.9 0.1 shard_map.38
  29.0 0.1 collective-permute-start.3
  29.1 0.5 %collective-permute-start.9 = (bf16[1,784,128]{2,1,0:T(8,128)(2,1)S(1)}, bf16[1,784,128]{2,1,0:T(8,128)(2,1)S(1)}, u32[]{:S(2)}, u32[]{:S(2)}) collective-permute-start(bf16[1,784,128]{2,1,0:T(8,128)(2,1)S(1)} %shard_map.40), channel_id=1, source_target_pairs={{20,0},{0,8},{8,24},{24,16},{16,4},{4,12},{12,28},{28,20},{21,1},{... | collective-permute-start | bytes 602120 | tf_op jit(solution)/shard_map/ppermute | solution.py:283
  29.6 1.3 %collective-permute-start.12 = (bf16[1,784,128]{2,1,0:T(8,128)(2,1)S(1)}, bf16[1,784,128]{2,1,0:T(8,128)(2,1)S(1)}, u32[]{:S(2)}, u32[]{:S(2)}) collective-permute-start(bf16[1,784,128]{2,1,0:T(8,128)(2,1)S(1)} %shard_map.40), channel_id=1, source_target_pairs={{8,0},{24,8},{16,24},{4,16},{12,4},{28,12},{20,28},{0,20},{9,1},{2... | collective-permute-start | bytes 602120 | tf_op jit(solution)/shard_map/ppermute | solution.py:283
  30.9 0.9 %collective-permute-done.10.refs_6_.refs_5_.refs_2_ = bf16[1,784,128]{2,1,0:T(8,128)(2,1)S(1)} collective-permute-done((bf16[1,784,128]{2,1,0:T(8,128)(2,1)S(1)}, bf16[1,784,128]{2,1,0:T(8,128)(2,1)S(1)}, u32[]{:S(2)}, u32[]{:S(2)}) %collective-permute-start.10) | collective-permute-done | bytes 200736 | tf_op jit(solution)/shard_map/ppermute | solution.py:283
  31.7 0.0 collective-permute-done.6.refs_3_.refs_5_
  31.7 1.2 %shard_map.41 = (f32[4,512,128]{2,1,0:T(8,128)S(1)}, f32[4,8,512]{2,1,0:T(8,128)S(1)}) custom-call(bf16[784,128]{1,0:T(8,128)(2,1)S(1)} %collective-permute-done.2.refs_2_.refs_0_.refs_1_, bf16[784,128]{1,0:T(8,128)(2,1)S(1)} %collective-permute-done.refs_1_.refs_2_, bf16[784,128]{1,0:T(8,128)(2,1)S(1)} %get-tuple-element.32.refs_0_.refs_2_.refs_3_, ...), custom_call_target="tpu_custom_call" | custom-call | flops 679477248 | bytes 1769472 | tf_op jit(solution)/shard_map/pallas_call | solution.py:206
  32.9 0.0 collective-permute-done.3.refs_4_
  32.9 2.1 %shard_map.42 = (f32[4,512,128]{2,1,0:T(8,128)S(1)}, f32[4,8,512]{2,1,0:T(8,128)S(1)}) custom-call(bf16[784,128]{1,0:T(8,128)(2,1)S(1)} %collective-permute-done.1.refs_3_.refs_0_, bf16[784,128]{1,0:T(8,128)(2,1)S(1)} %collective-permute-done.2.refs_2_.refs_0_.refs_1_, ...), custom_call_target="tpu_custom_call", output_to_operand_aliasing={{0}: (8, {}), {1}: (9, {})} | custom-call | flops 956301312 | bytes 2162688 | tf_op jit(solution)/shard_map/pallas_call | solution.py:206
  35.0 0.8 %collective-permute-done.9.refs_8_.refs_1_ = bf16[1,784,128]{2,1,0:T(8,128)(2,1)S(1)} collective-permute-done((bf16[1,784,128]{2,1,0:T(8,128)(2,1)S(1)}, bf16[1,784,128]{2,1,0:T(8,128)(2,1)S(1)}, u32[]{:S(2)}, u32[]{:S(2)}) %collective-permute-start.9) | collective-permute-done | bytes 200736 | tf_op jit(solution)/shard_map/ppermute | solution.py:283
  35.8 1.1 %shard_map.43 = (f32[4,512,128]{2,1,0:T(8,128)S(1)}, f32[4,8,512]{2,1,0:T(8,128)S(1)}, f32[1,512]{1,0:T(1,128)S(1)}, f32[1,512]{1,0:T(1,128)S(1)}) custom-call(bf16[784,128]{1,0:T(8,128)(2,1)S(1)} %collective-permute-done.1.refs_3_.refs_0_, ...), custom_call_target="tpu_custom_call", output_to_operand_aliasing={{0}: (9, {}), {1}: (10, {})} | custom-call | flops 276824064 | bytes 2359296 | tf_op jit(solution)/shard_map/pallas_call | solution.py:206
  36.9 0.8 %collective-permute-start.11 = (f32[1,512]{1,0:T(1,128)S(1)}, f32[1,512]{1,0:T(1,128)S(1)}, u32[]{:S(2)}, u32[]{:S(2)}) collective-permute-start(f32[1,512]{1,0:T(1,128)S(1)} %get-tuple-element.41), channel_id=1, source_target_pairs={{4,0},{12,8},{28,24},{20,16},{0,4},{8,12},{24,28},{16,20},{5,1},{1... | collective-permute-start | bytes 6152 | tf_op jit(solution)/shard_map/ppermute | solution.py:283
  37.7 0.0 collective-permute-done.12.refs_0_
  37.7 0.6 %shard_map.44 = (f32[4,512,128]{2,1,0:T(8,128)S(1)}, f32[4,8,512]{2,1,0:T(8,128)S(1)}, f32[1,512]{1,0:T(1,128)S(1)}, f32[1,512]{1,0:T(1,128)S(1)}) custom-call(bf16[1,784,128]{2,1,0:T(8,128)(2,1)S(1)} %collective-permute-done.12.refs_0_, ...), custom_call_target="tpu_custom_call", output_to_operand_aliasing={{0}: (5, {}), {1}: (6, {})} | custom-call | flops 100663296 | bytes 983040 | tf_op jit(solution)/shard_map/pallas_call | solution.py:206
  38.3 1.3 %collective-permute-start.13 = (f32[1,512]{1,0:T(1,128)S(1)}, f32[1,512]{1,0:T(1,128)S(1)}, u32[]{:S(2)}, u32[]{:S(2)}) collective-permute-start(f32[1,512]{1,0:T(1,128)S(1)} %get-tuple-element.44), channel_id=1, source_target_pairs={{20,0},{0,8},{8,24},{24,16},{16,4},{4,12},{12,28},{28,20},{21,1},{... | collective-permute-start | bytes 6152 | tf_op jit(solution)/shard_map/ppermute | solution.py:283
  39.6 0.5 collective-permute-start.14
  40.1 0.0 collective-permute-done.11.refs_1_
  40.1 1.3 %collective-permute-done.13.refs_2_ = f32[1,512]{1,0:T(1,128)S(1)} collective-permute-done((f32[1,512]{1,0:T(1,128)S(1)}, f32[1,512]{1,0:T(1,128)S(1)}, u32[]{:S(2)}, u32[]{:S(2)}) %collective-permute-start.13) | collective-permute-done | bytes 2080 | tf_op jit(solution)/shard_map/ppermute | solution.py:283
  41.4 1.8 %collective-permute-done.14.refs_3_ = f32[1,512]{1,0:T(1,128)S(1)} collective-permute-done((f32[1,512]{1,0:T(1,128)S(1)}, f32[1,512]{1,0:T(1,128)S(1)}, u32[]{:S(2)}, u32[]{:S(2)}) %collective-permute-start.14) | collective-permute-done | bytes 2080 | tf_op jit(solution)/shard_map/ppermute | solution.py:283
  43.2 0.0 collective-permute-start.15
  43.2 0.1 collective-permute-start.16
  43.3 3.8 %collective-permute-start.17 = (f32[1,128]{1,0:T(1,128)S(1)}, f32[1,128]{1,0:T(1,128)S(1)}, u32[]{:S(2)}, u32[]{:S(2)}) collective-permute-start(f32[1,128]{1,0:T(1,128)S(1)} %get-tuple-element.48), channel_id=1, source_target_pairs={{0,3},{1,0},{2,1},{3,2},{4,7},{5,4},{6,5},{7,6},{8,11},{9,8},{10,9... | collective-permute-start | bytes 1544 | tf_op jit(solution)/shard_map/ppermute | solution.py:290
  47.1 0.6 %collective-permute-done.15.refs_0_ = f32[1,128]{1,0:T(1,128)S(1)} collective-permute-done((f32[1,128]{1,0:T(1,128)S(1)}, f32[1,128]{1,0:T(1,128)S(1)}, u32[]{:S(2)}, u32[]{:S(2)}) %collective-permute-start.15) | collective-permute-done | bytes 544 | tf_op jit(solution)/shard_map/ppermute | solution.py:290
  47.7 1.0 %collective-permute-done.16.refs_1_ = f32[1,128]{1,0:T(1,128)S(1)} collective-permute-done((f32[1,128]{1,0:T(1,128)S(1)}, f32[1,128]{1,0:T(1,128)S(1)}, u32[]{:S(2)}, u32[]{:S(2)}) %collective-permute-start.16) | collective-permute-done | bytes 544 | tf_op jit(solution)/shard_map/ppermute | solution.py:290
  48.6 0.0 collective-permute-done.17.refs_2_
  48.6 0.8 %shard_map.46 = f32[1,512]{1,0:T(1,128)} custom-call(f32[1,128]{1,0:T(1,128)S(1)} %collective-permute-done.15.refs_0_, f32[1,128]{1,0:T(1,128)S(1)} %collective-permute-done.16.refs_1_, f32[1,128]{1,0:T(1,128)S(1)} %collective-permute-done.17.refs_2_, f32[1,128]{1,0:T(1,128)S(1)} %get-tuple-element.49.refs_3_, s32[1,512]{1,0:T(1,128)S(1)} %get-tuple-element.50.refs_4_), custom_call_target="tpu_custom_call" | custom-call | flops 262144 | bytes 2048 | tf_op jit(solution)/shard_map/pallas_call | solution.py:206
  (3 shorter events, 0.0 us)
Async XLA Ops:
  2.9 10.8 %collective-permute-start = (bf16[784,128]{1,0:T(8,128)(2,1)S(1)}, bf16[784,128]{1,0:T(8,128)(2,1)S(1)}, u32[]{:S(2)}, u32[]{:S(2)}) collective-permute-start(bf16[784,128]{1,0:T(8,128)(2,1)S(1)} %get-tuple-element.29), channel_id=1, source_target_pairs={{0,1},{1,2},{2,3},{3,0},{4,5},{5,6},{6,7},{7,4},{8,9},{9,10},{10,1... | collective-permute-start | bytes 602120 | tf_op jit(solution)/shard_map/ppermute | solution.py:290
  6.0 14.2 %collective-permute-start.4 = (bf16[784,128]{1,0:T(8,128)(2,1)S(1)}, bf16[784,128]{1,0:T(8,128)(2,1)S(1)}, u32[]{:S(2)}, u32[]{:S(2)}) collective-permute-start(bf16[784,128]{1,0:T(8,128)(2,1)S(1)} %get-tuple-element.32.refs_0_.refs_2_.refs_3_), channel_id=1, source_target_pairs={{8,0},{24,8},{16,24},{4,16},{12,4},{28,12},{20,28},{0,20},{9,1},{2... | collective-permute-start | bytes 602120 | tf_op jit(solution)/shard_map/ppermute | solution.py:283
  6.7 15.3 %collective-permute-start.2 = (bf16[784,128]{1,0:T(8,128)(2,1)S(1)}, bf16[784,128]{1,0:T(8,128)(2,1)S(1)}, u32[]{:S(2)}, u32[]{:S(2)}) collective-permute-start(bf16[784,128]{1,0:T(8,128)(2,1)S(1)} %get-tuple-element.31), channel_id=1, source_target_pairs={{0,3},{1,0},{2,1},{3,2},{4,7},{5,4},{6,5},{7,6},{8,11},{9,8},{10,9... | collective-permute-start | bytes 602120 | tf_op jit(solution)/shard_map/ppermute | solution.py:290
  9.1 12.9 %collective-permute-start.5 = (bf16[784,128]{1,0:T(8,128)(2,1)S(1)}, bf16[784,128]{1,0:T(8,128)(2,1)S(1)}, u32[]{:S(2)}, u32[]{:S(2)}) collective-permute-start(bf16[784,128]{1,0:T(8,128)(2,1)S(1)} %get-tuple-element.32.refs_0_.refs_2_.refs_3_), channel_id=1, source_target_pairs={{20,0},{0,8},{8,24},{24,16},{16,4},{4,12},{12,28},{28,20},{21,1},{... | collective-permute-start | bytes 602120 | tf_op jit(solution)/shard_map/ppermute | solution.py:283
  13.7 12.2 %collective-permute-start.1 = (bf16[784,128]{1,0:T(8,128)(2,1)S(1)}, bf16[784,128]{1,0:T(8,128)(2,1)S(1)}, u32[]{:S(2)}, u32[]{:S(2)}) collective-permute-start(bf16[784,128]{1,0:T(8,128)(2,1)S(1)} %get-tuple-element.30), channel_id=1, source_target_pairs={{0,2},{1,3},{2,0},{3,1},{4,6},{5,7},{6,4},{7,5},{8,10},{9,11},{10,... | collective-permute-start | bytes 602120 | tf_op jit(solution)/shard_map/ppermute | solution.py:290
  20.2 7.2 %collective-permute-start.8 = (bf16[784,128]{1,0:T(8,128)(2,1)S(1)}, bf16[784,128]{1,0:T(8,128)(2,1)S(1)}, u32[]{:S(2)}, u32[]{:S(2)}) collective-permute-start(bf16[784,128]{1,0:T(8,128)(2,1)S(1)} %collective-permute-done.refs_1_.refs_2_), channel_id=1, source_target_pairs={{20,0},{0,8},{8,24},{24,16},{16,4},{4,12},{12,28},{28,20},{21,1},{... | collective-permute-start | bytes 602120 | tf_op jit(solution)/shard_map/ppermute | solution.py:283
  21.7 7.2 %collective-permute-start.7 = (bf16[784,128]{1,0:T(8,128)(2,1)S(1)}, bf16[784,128]{1,0:T(8,128)(2,1)S(1)}, u32[]{:S(2)}, u32[]{:S(2)}) collective-permute-start(bf16[784,128]{1,0:T(8,128)(2,1)S(1)} %collective-permute-done.refs_1_.refs_2_), channel_id=1, source_target_pairs={{8,0},{24,8},{16,24},{4,16},{12,4},{28,12},{20,28},{0,20},{9,1},{2... | collective-permute-start | bytes 602120 | tf_op jit(solution)/shard_map/ppermute | solution.py:283
  22.0 9.7 %collective-permute-start.10 = (bf16[1,784,128]{2,1,0:T(8,128)(2,1)S(1)}, bf16[1,784,128]{2,1,0:T(8,128)(2,1)S(1)}, u32[]{:S(2)}, u32[]{:S(2)}) collective-permute-start(bf16[1,784,128]{2,1,0:T(8,128)(2,1)S(1)} %shard_map.39), channel_id=1, source_target_pairs={{20,0},{0,8},{8,24},{24,16},{16,4},{4,12},{12,28},{28,20},{21,1},{... | collective-permute-start | bytes 602120 | tf_op jit(solution)/shard_map/ppermute | solution.py:283
  23.8 7.9 %collective-permute-start.6 = (bf16[1,784,128]{2,1,0:T(8,128)(2,1)S(1)}, bf16[1,784,128]{2,1,0:T(8,128)(2,1)S(1)}, u32[]{:S(2)}, u32[]{:S(2)}) collective-permute-start(bf16[1,784,128]{2,1,0:T(8,128)(2,1)S(1)} %shard_map.39), channel_id=1, source_target_pairs={{8,0},{24,8},{16,24},{4,16},{12,4},{28,12},{20,28},{0,20},{9,1},{2... | collective-permute-start | bytes 602120 | tf_op jit(solution)/shard_map/ppermute | solution.py:283
  29.0 4.0 %collective-permute-start.3 = (bf16[4,784,128]{2,1,0:T(8,128)(2,1)S(1)}, bf16[4,784,128]{2,1,0:T(8,128)(2,1)S(1)}, u32[]{:S(2)}, u32[]{:S(2)}) collective-permute-start(bf16[4,784,128]{2,1,0:T(8,128)(2,1)S(1)} %shard_map.38), channel_id=1, source_target_pairs={{4,0},{12,8},{28,24},{20,16},{0,4},{8,12},{24,28},{16,20},{5,1},{1... | collective-permute-start | bytes 2408456 | tf_op jit(solution)/shard_map/ppermute | solution.py:283
  29.1 6.7 %collective-permute-start.9 = (bf16[1,784,128]{2,1,0:T(8,128)(2,1)S(1)}, bf16[1,784,128]{2,1,0:T(8,128)(2,1)S(1)}, u32[]{:S(2)}, u32[]{:S(2)}) collective-permute-start(bf16[1,784,128]{2,1,0:T(8,128)(2,1)S(1)} %shard_map.40), channel_id=1, source_target_pairs={{20,0},{0,8},{8,24},{24,16},{16,4},{4,12},{12,28},{28,20},{21,1},{... | collective-permute-start | bytes 602120 | tf_op jit(solution)/shard_map/ppermute | solution.py:283
  29.6 8.2 %collective-permute-start.12 = (bf16[1,784,128]{2,1,0:T(8,128)(2,1)S(1)}, bf16[1,784,128]{2,1,0:T(8,128)(2,1)S(1)}, u32[]{:S(2)}, u32[]{:S(2)}) collective-permute-start(bf16[1,784,128]{2,1,0:T(8,128)(2,1)S(1)} %shard_map.40), channel_id=1, source_target_pairs={{8,0},{24,8},{16,24},{4,16},{12,4},{28,12},{20,28},{0,20},{9,1},{2... | collective-permute-start | bytes 602120 | tf_op jit(solution)/shard_map/ppermute | solution.py:283
  36.9 3.2 %collective-permute-start.11 = (f32[1,512]{1,0:T(1,128)S(1)}, f32[1,512]{1,0:T(1,128)S(1)}, u32[]{:S(2)}, u32[]{:S(2)}) collective-permute-start(f32[1,512]{1,0:T(1,128)S(1)} %get-tuple-element.41), channel_id=1, source_target_pairs={{4,0},{12,8},{28,24},{20,16},{0,4},{8,12},{24,28},{16,20},{5,1},{1... | collective-permute-start | bytes 6152 | tf_op jit(solution)/shard_map/ppermute | solution.py:283
  38.3 3.1 %collective-permute-start.13 = (f32[1,512]{1,0:T(1,128)S(1)}, f32[1,512]{1,0:T(1,128)S(1)}, u32[]{:S(2)}, u32[]{:S(2)}) collective-permute-start(f32[1,512]{1,0:T(1,128)S(1)} %get-tuple-element.44), channel_id=1, source_target_pairs={{20,0},{0,8},{8,24},{24,16},{16,4},{4,12},{12,28},{28,20},{21,1},{... | collective-permute-start | bytes 6152 | tf_op jit(solution)/shard_map/ppermute | solution.py:283
  39.6 3.6 %collective-permute-start.14 = (f32[1,512]{1,0:T(1,128)S(1)}, f32[1,512]{1,0:T(1,128)S(1)}, u32[]{:S(2)}, u32[]{:S(2)}) collective-permute-start(f32[1,512]{1,0:T(1,128)S(1)} %get-tuple-element.45), channel_id=1, source_target_pairs={{8,0},{24,8},{16,24},{4,16},{12,4},{28,12},{20,28},{0,20},{9,1},{2... | collective-permute-start | bytes 6152 | tf_op jit(solution)/shard_map/ppermute | solution.py:283
  43.2 4.4 %collective-permute-start.15 = (f32[1,128]{1,0:T(1,128)S(1)}, f32[1,128]{1,0:T(1,128)S(1)}, u32[]{:S(2)}, u32[]{:S(2)}) collective-permute-start(f32[1,128]{1,0:T(1,128)S(1)} %get-tuple-element.46), channel_id=1, source_target_pairs={{0,2},{1,3},{2,0},{3,1},{4,6},{5,7},{6,4},{7,5},{8,10},{9,11},{10,... | collective-permute-start | bytes 1544 | tf_op jit(solution)/shard_map/ppermute | solution.py:290
  43.2 5.4 %collective-permute-start.16 = (f32[1,128]{1,0:T(1,128)S(1)}, f32[1,128]{1,0:T(1,128)S(1)}, u32[]{:S(2)}, u32[]{:S(2)}) collective-permute-start(f32[1,128]{1,0:T(1,128)S(1)} %get-tuple-element.47), channel_id=1, source_target_pairs={{0,1},{1,2},{2,3},{3,0},{4,5},{5,6},{6,7},{7,4},{8,9},{9,10},{10,1... | collective-permute-start | bytes 1544 | tf_op jit(solution)/shard_map/ppermute | solution.py:290
  43.3 5.3 %collective-permute-start.17 = (f32[1,128]{1,0:T(1,128)S(1)}, f32[1,128]{1,0:T(1,128)S(1)}, u32[]{:S(2)}, u32[]{:S(2)}) collective-permute-start(f32[1,128]{1,0:T(1,128)S(1)} %get-tuple-element.48), channel_id=1, source_target_pairs={{0,3},{1,0},{2,1},{3,2},{4,7},{5,4},{6,5},{7,6},{8,11},{9,8},{10,9... | collective-permute-start | bytes 1544 | tf_op jit(solution)/shard_map/ppermute | solution.py:290

commit v10 on v9

--- a/solution.py
+++ b/solution.py
@@ -84,7 +84,7 @@
     )
     rank = jnp.sum(jnp.where(onehot, ranks, 0.0), axis=0, keepdims=True)
     place = rel * capacity + rank.astype(jnp.int32)
-    place_ref[...] = place
+    place_ref[...] = (code & (groups - 1)) * capacity + rank.astype(jnp.int32)
     move = jnp.where(
         lax.broadcasted_iota(jnp.int32, (slots, rows), 0) == place, 1.0, 0.0
     ).astype(jnp.bfloat16)
@@ -174,26 +174,38 @@
         out_ref[...] = jnp.max(column_ref[role], axis=0, keepdims=True)
 
 
-def merge_kernel(roles, *refs):
-    best = refs[0][...]
-    for r in range(1, roles):
-        best = jnp.maximum(best, refs[r][...])
-    best = jnp.maximum(best, jnp.float32(-1.0))
-    for k, out_ref in enumerate(refs[roles:]):
-        out_ref[...] = best[:, k * LANES : (k + 1) * LANES]
-
-
-def place_kernel(groups, *refs):
-    place = refs[groups][...]
+def slot_shift(k):
+    return (k + 1) // 2 if k % 2 else -(k // 2)
+
+
+def spread_kernel(ring, offsets, groups, *refs):
+    *partial_refs, out_ref = refs
+    shards = len(ring)
+    out_ref[...] = jnp.full(out_ref.shape, jnp.float32(LOW))
+    shard, group = lax.axis_index("shard"), lax.axis_index("group")
+    for offset, ref in zip(offsets, partial_refs):
+        target = sum(
+            jnp.where(shard == ring[e], ring[(e + offset) % shards], 0) for e in range(shards)
+        )
+        for k in range(groups):
+            row = target * groups + ((group - slot_shift(k)) & (groups - 1))
+            out_ref[pl.ds(row, 1)] = ref[:, k * LANES : (k + 1) * LANES].reshape(1, 1, LANES)
+
+
+def place_kernel(groups, back_ref, place_ref, out_ref):
+    place = place_ref[...]
     rows = place.shape[1]
     best = jnp.full((1, rows), jnp.float32(LOW))
-    for k in range(groups):
-        values = jnp.concatenate([column_of(refs[groups - 1 - k][...])] * (rows // LANES), axis=1)
-        here = lax.broadcasted_iota(jnp.int32, (LANES, rows), 0) + k * LANES == place
+    for g in range(groups):
+        row = jnp.full((1, LANES), jnp.float32(-1.0))
+        for s in range(back_ref.shape[0] // groups):
+            row = jnp.maximum(row, back_ref[s * groups + g])
+        values = jnp.concatenate([column_of(row)] * (rows // LANES), axis=1)
+        here = lax.broadcasted_iota(jnp.int32, (LANES, rows), 0) + g * LANES == place
         best = jnp.maximum(
             best, jnp.max(jnp.where(here, values, jnp.float32(LOW)), axis=0, keepdims=True)
         )
-    refs[groups + 1][...] = best
+    out_ref[...] = best
 
 
 def in_vmem(count):
@@ -282,11 +294,11 @@
         perm = [(ring[(e + offset) % shards], ring[e]) for e in range(shards)]
         return lax.ppermute(x, "shard", perm)
 
-    def exchange(blocks, way, stagger=False):
+    def exchange(blocks):
         got = list(blocks)
         for k in range(1, groups):
-            shift = way * ((k + 1) // 2 if k % 2 else -(k // 2))
-            block = after(blocks[k], got[1]) if stagger and k > 2 else blocks[k]
+            shift = slot_shift(k)
+            block = after(blocks[k], got[1]) if k > 2 else blocks[k]
             got[k] = lax.ppermute(block, "group", [(z, (z + shift) % groups) for z in range(groups)])
         return got
 
@@ -314,19 +326,18 @@
     near = [r for r in range(1, roles) if 2 * offsets[r] != shards]
     far = [r for r in range(1, roles) if r not in near]
     first = {r: from_offset(send[0], offsets[r]) for r in near}
-    own = exchange(send, 1, True)
+    own = exchange(send)
     held = [[None] * groups for _ in offsets]
     held[0] = [(x, None) for x in own]
     for r in near:
         held[r][0] = (first[r], None)
-    for k in range(1, groups):
-        if k == 1:
-            block = after(own[k], first[near[0]]) if near else own[k]
-        else:
-            passed = [held[r][k - 2][0] for r in near]
-            block = stack([after(own[k], *passed)], WAIT if k in late else WAIT // 20)
-        for r in near:
-            held[r][k] = (from_offset(block, offsets[r]), 0 if k > 1 else None)
+    for ks, wait in ((early[1:], WAIT), (late, WAIT)):
+        if ks:
+            block = stack([own[k] for k in ks], wait)
+            for r in near:
+                moved = from_offset(block, offsets[r])
+                for i, k in enumerate(ks):
+                    held[r][k] = (moved, i)
     got = {r: from_offset(stack(own, 0), offsets[r]) for r in far}
     everything = [(0, 0, False)]
     everything += [(offsets.index(a), offsets.index(b), both) for a, b, both in pairs]
@@ -360,21 +371,20 @@
             for r, end in zip(done, ends):
                 partial[r] = end
 
-    others = [from_offset(partial[r], -offsets[r]) for r in range(1, roles)]
-    best = call(
-        lambda *refs: merge_kernel(roles, *refs),
-        [jax.ShapeDtypeStruct((1, capacity), jnp.float32)] * groups,
+    (best,) = call(
+        lambda *refs: spread_kernel(ring, offsets, groups, *refs),
+        [jax.ShapeDtypeStruct((shards * groups, 1, capacity), jnp.float32)],
         [],
-        [partial[0]] + others,
+        partial,
         roles * slots,
         4 * roles * slots,
     )
-    back = exchange(best, -1)
+    back = lax.all_to_all(best, ("shard", "group"), split_axis=0, concat_axis=0, tiled=True)
     (result,) = call(
         lambda *refs: place_kernel(groups, *refs),
         [jax.ShapeDtypeStruct((1, rows), jnp.float32)],
         [],
-        back[::-1] + [place],
+        [back, place],
         rows * slots,
         4 * slots,
     )

time: 49.6 us -> 48.1 us (0.970)
  blocking collectives: 0 us -> 9.21 us
  starting transfers between devices: 25.6 us -> 16.9 us
  waiting for transfers between devices: 14.9 us -> 12.9 us
    all_to_all x0 -> x1, blocking collectives: none -> 9.21 us  [per_device(): lax.all_to_all(best, ('shard', 'group'), split_axis=0, concat_axis=0, til...]
    ppermute x12 -> x7, starting transfers between devices: 9.81 us -> 5.43 us  [from_offset(): return lax.ppermute(x, 'shard', perm)]
    ppermute x6 -> x3, starting transfers between devices: 15.8 us -> 11.5 us  [exchange(): lax.ppermute(block, 'group', [(z, (z + shift) % groups) for z in range(gr...]
    ppermute x12 -> x7, waiting for transfers between devices: 7.74 us -> 4.95 us  [from_offset(): return lax.ppermute(x, 'shard', perm)]
    ppermute x6 -> x3, waiting for transfers between devices: 7.21 us -> 7.94 us  [exchange(): lax.ppermute(block, 'group', [(z, (z + shift) % groups) for z in range(gr...]
  transfers between devices with their start and end apart: 18 -> 10, of which waited for: 10 -> 4; matrix products, arithmetic and copies ran while one was open for 0% -> 0% of each run, Pallas kernels for 10% -> 9%
where the time goes in v10:
time: 48.1 us; the launch traced here: 47.9 us
  starting transfers between devices  16.9 us (35%)
  waiting for transfers between devices  12.9 us (27%)
  blocking collectives  9.21 us (19%)
  Pallas kernels  8.12 us (17%)
  other arithmetic  0.7 us (1%)
    ppermute x3, starting transfers between devices, exchange(): lax.ppermute(block, 'group', [(z, (z + shift) % groups) for z in range(gr...  11.5 us
    all_to_all x1, blocking collectives, per_device(): lax.all_to_all(best, ('shard', 'group'), split_axis=0, concat_axis=0, til...  9.21 us
    pallas_call x10, Pallas kernels, call(): pl.pallas_call(kernel, out_shape=out_shape, in_specs=in_specs or in_vmem(...  8.12 us
    ppermute x3, waiting for transfers between devices, exchange(): lax.ppermute(block, 'group', [(z, (z + shift) % groups) for z in range(gr...  7.94 us
    ppermute x7, starting transfers between devices, from_offset(): return lax.ppermute(x, 'shard', perm)  5.43 us
    ppermute x7, waiting for transfers between devices, from_offset(): return lax.ppermute(x, 'shard', perm)  4.95 us
  transfers between devices with their start and end apart: 10, of which 4 were waited for; matrix products, arithmetic and copies ran while one was open for 0% of the time, Pallas kernels for 9%

profile of v10, /device:TPU:0, one launch (start us, length us, event | category | flops | bytes accessed | tf_op | source)
XLA Modules:
  0.0 47.9 jit_solution(1544225827584801460)
XLA Ops:
  0.0 0.7 %multiply_add_fusion = s32[512]{0:T(512)S(1)} fusion(s32[512]{0:T(512)} %bitcast.4, s32[512]{0:T(512)} %param.5), kind=kLoop, calls=%fused_computation | loop fusion | flops 1024 | bytes 6144 | tf_op jit(solution)/shard_map/add | solution.py:305
  0.7 2.2 %shard_map.37 = (bf16[784,128]{1,0:T(8,128)(2,1)S(1)}, bf16[784,128]{1,0:T(8,128)(2,1)S(1)}, bf16[784,128]{1,0:T(8,128)(2,1)S(1)}, bf16[784,128]{1,0:T(8,128)(2,1)S(1)}, s32[1,512]{1,0:T(1,128)S(1)}) custom-call(bf16[512,768]{1,0:T(8,128)(2,1)} %refs_0_.1, s32[1,512]{1,0:T(1,128)S(1)} %bitcast.3), custom_call_target="tpu_custom_call" | custom-call | flops 402653184 | bytes 1572864 | tf_op jit(solution)/shard_map/pallas_call | solution.py:218
  2.9 3.1 %collective-permute-start = (bf16[784,128]{1,0:T(8,128)(2,1)S(1)}, bf16[784,128]{1,0:T(8,128)(2,1)S(1)}, u32[]{:S(2)}, u32[]{:S(2)}) collective-permute-start(bf16[784,128]{1,0:T(8,128)(2,1)S(1)} %get-tuple-element.22), channel_id=1, source_target_pairs={{0,1},{1,2},{2,3},{3,0},{4,5},{5,6},{6,7},{7,4},{8,9},{9,10},{10,1... | collective-permute-start | bytes 602120 | tf_op jit(solution)/shard_map/ppermute | solution.py:302
  6.0 2.1 %collective-permute-start.2 = (bf16[784,128]{1,0:T(8,128)(2,1)S(1)}, bf16[784,128]{1,0:T(8,128)(2,1)S(1)}, u32[]{:S(2)}, u32[]{:S(2)}) collective-permute-start(bf16[784,128]{1,0:T(8,128)(2,1)S(1)} %get-tuple-element.24), channel_id=1, source_target_pairs={{0,3},{1,0},{2,1},{3,2},{4,7},{5,4},{6,5},{7,6},{8,11},{9,8},{10,9... | collective-permute-start | bytes 602120 | tf_op jit(solution)/shard_map/ppermute | solution.py:302
  8.1 1.6 %collective-permute-start.8 = (bf16[784,128]{1,0:T(8,128)(2,1)S(1)}, bf16[784,128]{1,0:T(8,128)(2,1)S(1)}, u32[]{:S(2)}, u32[]{:S(2)}) collective-permute-start(bf16[784,128]{1,0:T(8,128)(2,1)S(1)} %get-tuple-element.25.refs_0_.refs_2_.refs_3_), channel_id=1, source_target_pairs={{20,0},{0,8},{8,24},{24,16},{16,4},{4,12},{12,28},{28,20},{21,1},{... | collective-permute-start | bytes 602120 | tf_op jit(solution)/shard_map/ppermute | solution.py:295
  9.8 0.1 collective-permute-start.5
  9.9 4.1 %collective-permute-done.refs_1_.refs_0_.refs_2_ = bf16[784,128]{1,0:T(8,128)(2,1)S(1)} collective-permute-done((bf16[784,128]{1,0:T(8,128)(2,1)S(1)}, bf16[784,128]{1,0:T(8,128)(2,1)S(1)}, u32[]{:S(2)}, u32[]{:S(2)}) %collective-permute-start) | collective-permute-done | bytes 200736 | tf_op jit(solution)/shard_map/ppermute | solution.py:302
  13.9 6.3 %collective-permute-start.1 = (bf16[784,128]{1,0:T(8,128)(2,1)S(1)}, bf16[784,128]{1,0:T(8,128)(2,1)S(1)}, u32[]{:S(2)}, u32[]{:S(2)}) collective-permute-start(bf16[784,128]{1,0:T(8,128)(2,1)S(1)} %get-tuple-element.23), channel_id=1, source_target_pairs={{0,2},{1,3},{2,0},{3,1},{4,6},{5,7},{6,4},{7,5},{8,10},{9,11},{10,... | collective-permute-start | bytes 602120 | tf_op jit(solution)/shard_map/ppermute | solution.py:302
  20.2 0.0 collective-permute-done.2.refs_2_.refs_1_.refs_0_
  20.2 1.6 %collective-permute-start.7 = (bf16[2,784,128]{2,1,0:T(8,128)(2,1)S(1)}, bf16[2,784,128]{2,1,0:T(8,128)(2,1)S(1)}, u32[]{:S(2)}, u32[]{:S(2)}) collective-permute-start(bf16[2,784,128]{2,1,0:T(8,128)(2,1)S(1)} %shard_map.39), channel_id=1, source_target_pairs={{20,0},{0,8},{8,24},{24,16},{16,4},{4,12},{12,28},{28,20},{21,1},{... | collective-permute-start | bytes 1204232 | tf_op jit(solution)/shard_map/ppermute | solution.py:295
  21.8 0.3 collective-permute-start.4
  22.0 3.9 %collective-permute-done.1.refs_3_.refs_0_ = bf16[784,128]{1,0:T(8,128)(2,1)S(1)} collective-permute-done((bf16[784,128]{1,0:T(8,128)(2,1)S(1)}, bf16[784,128]{1,0:T(8,128)(2,1)S(1)}, u32[]{:S(2)}, u32[]{:S(2)}) %collective-permute-start.1) | collective-permute-done | bytes 200736 | tf_op jit(solution)/shard_map/ppermute | solution.py:302
  25.9 0.1 shard_map.38
  26.0 0.1 collective-permute-start.3
  26.1 0.0 collective-permute-done.8.refs_6_.refs_3_
  26.1 1.6 %collective-permute-start.6 = (bf16[1,784,128]{2,1,0:T(8,128)(2,1)S(1)}, bf16[1,784,128]{2,1,0:T(8,128)(2,1)S(1)}, u32[]{:S(2)}, u32[]{:S(2)}) collective-permute-start(bf16[1,784,128]{2,1,0:T(8,128)(2,1)S(1)} %shard_map.40), channel_id=1, source_target_pairs={{20,0},{0,8},{8,24},{24,16},{16,4},{4,12},{12,28},{28,20},{21,1},{... | collective-permute-start | bytes 602120 | tf_op jit(solution)/shard_map/ppermute | solution.py:295
  27.7 0.0 collective-permute-done.5.refs_4_.refs_6_
  27.7 0.3 collective-permute-start.9
  27.9 3.9 %collective-permute-done.7.refs_5_.refs_2_ = bf16[2,784,128]{2,1,0:T(8,128)(2,1)S(1)} collective-permute-done((bf16[2,784,128]{2,1,0:T(8,128)(2,1)S(1)}, bf16[2,784,128]{2,1,0:T(8,128)(2,1)S(1)}, u32[]{:S(2)}, u32[]{:S(2)}) %collective-permute-start.7) | collective-permute-done | bytes 401440 | tf_op jit(solution)/shard_map/ppermute | solution.py:295
  31.8 0.0 collective-permute-done.4.refs_3_.refs_5_
  31.8 1.2 %shard_map.41 = (f32[4,512,128]{2,1,0:T(8,128)S(1)}, f32[4,8,512]{2,1,0:T(8,128)S(1)}) custom-call(bf16[784,128]{1,0:T(8,128)(2,1)S(1)} %collective-permute-done.2.refs_2_.refs_1_.refs_0_, bf16[784,128]{1,0:T(8,128)(2,1)S(1)} %collective-permute-done.refs_1_.refs_0_.refs_2_, bf16[784,128]{1,0:T(8,128)(2,1)S(1)} %get-tuple-element.25.refs_0_.refs_2_.refs_3_, ...), custom_call_target="tpu_custom_call" | custom-call | flops 679477248 | bytes 1769472 | tf_op jit(solution)/shard_map/pallas_call | solution.py:218
  33.0 0.0 collective-permute-done.3.refs_4_
  33.0 2.1 %shard_map.42 = (f32[4,512,128]{2,1,0:T(8,128)S(1)}, f32[4,8,512]{2,1,0:T(8,128)S(1)}) custom-call(bf16[784,128]{1,0:T(8,128)(2,1)S(1)} %collective-permute-done.1.refs_3_.refs_0_, bf16[784,128]{1,0:T(8,128)(2,1)S(1)} %collective-permute-done.2.refs_2_.refs_1_.refs_0_, ...), custom_call_target="tpu_custom_call", output_to_operand_aliasing={{0}: (7, {}), {1}: (8, {})} | custom-call | flops 956301312 | bytes 2162688 | tf_op jit(solution)/shard_map/pallas_call | solution.py:218
  35.1 1.0 %collective-permute-done.6.refs_7_.refs_1_ = bf16[1,784,128]{2,1,0:T(8,128)(2,1)S(1)} collective-permute-done((bf16[1,784,128]{2,1,0:T(8,128)(2,1)S(1)}, bf16[1,784,128]{2,1,0:T(8,128)(2,1)S(1)}, u32[]{:S(2)}, u32[]{:S(2)}) %collective-permute-start.6) | collective-permute-done | bytes 200736 | tf_op jit(solution)/shard_map/ppermute | solution.py:295
  36.1 1.1 %shard_map.43 = (f32[4,512,128]{2,1,0:T(8,128)S(1)}, f32[4,8,512]{2,1,0:T(8,128)S(1)}, f32[1,512]{1,0:T(1,128)S(1)}, f32[1,512]{1,0:T(1,128)S(1)}) custom-call(bf16[784,128]{1,0:T(8,128)(2,1)S(1)} %collective-permute-done.1.refs_3_.refs_0_, ...), custom_call_target="tpu_custom_call", output_to_operand_aliasing={{0}: (8, {}), {1}: (9, {})} | custom-call | flops 276824064 | bytes 2359296 | tf_op jit(solution)/shard_map/pallas_call | solution.py:218
  37.3 0.0 collective-permute-done.9.refs_0_
  37.3 0.6 %shard_map.44 = (f32[4,512,128]{2,1,0:T(8,128)S(1)}, f32[4,8,512]{2,1,0:T(8,128)S(1)}, f32[1,512]{1,0:T(1,128)S(1)}, f32[1,512]{1,0:T(1,128)S(1)}) custom-call(bf16[1,784,128]{2,1,0:T(8,128)(2,1)S(1)} %collective-permute-done.9.refs_0_, ...), custom_call_target="tpu_custom_call", output_to_operand_aliasing={{0}: (4, {}), {1}: (5, {})} | custom-call | flops 100663296 | bytes 983040 | tf_op jit(solution)/shard_map/pallas_call | solution.py:218
  37.9 0.1 shard_map.45
  37.9 9.2 %all_to_all.5.refs_0_ = f32[32,1,128]{2,1,0:T(1,128)S(1)} all-to-all(f32[32,1,128]{2,1,0:T(1,128)S(1)} %shard_map.45), channel_id=1, replica_groups=mesh['shard'=8,'group'=4] {'shard','group'}, dimensions={0} | all-to-all | bytes 32768 | tf_op jit(solution)/shard_map/all_to_all | solution.py:382
  47.1 0.8 %shard_map.46 = f32[1,512]{1,0:T(1,128)} custom-call(f32[32,1,128]{2,1,0:T(1,128)S(1)} %all_to_all.5.refs_0_, s32[1,512]{1,0:T(1,128)S(1)} %get-tuple-element.36.refs_1_), custom_call_target="tpu_custom_call" | custom-call | flops 262144 | bytes 2048 | tf_op jit(solution)/shard_map/pallas_call | solution.py:218
  (2 shorter events, 0.0 us)
Async XLA Ops:
  2.9 11.0 %collective-permute-start = (bf16[784,128]{1,0:T(8,128)(2,1)S(1)}, bf16[784,128]{1,0:T(8,128)(2,1)S(1)}, u32[]{:S(2)}, u32[]{:S(2)}) collective-permute-start(bf16[784,128]{1,0:T(8,128)(2,1)S(1)} %get-tuple-element.22), channel_id=1, source_target_pairs={{0,1},{1,2},{2,3},{3,0},{4,5},{5,6},{6,7},{7,4},{8,9},{9,10},{10,1... | collective-permute-start | bytes 602120 | tf_op jit(solution)/shard_map/ppermute | solution.py:302
  6.0 14.2 %collective-permute-start.2 = (bf16[784,128]{1,0:T(8,128)(2,1)S(1)}, bf16[784,128]{1,0:T(8,128)(2,1)S(1)}, u32[]{:S(2)}, u32[]{:S(2)}) collective-permute-start(bf16[784,128]{1,0:T(8,128)(2,1)S(1)} %get-tuple-element.24), channel_id=1, source_target_pairs={{0,3},{1,0},{2,1},{3,2},{4,7},{5,4},{6,5},{7,6},{8,11},{9,8},{10,9... | collective-permute-start | bytes 602120 | tf_op jit(solution)/shard_map/ppermute | solution.py:302
  8.1 18.0 %collective-permute-start.8 = (bf16[784,128]{1,0:T(8,128)(2,1)S(1)}, bf16[784,128]{1,0:T(8,128)(2,1)S(1)}, u32[]{:S(2)}, u32[]{:S(2)}) collective-permute-start(bf16[784,128]{1,0:T(8,128)(2,1)S(1)} %get-tuple-element.25.refs_0_.refs_2_.refs_3_), channel_id=1, source_target_pairs={{20,0},{0,8},{8,24},{24,16},{16,4},{4,12},{12,28},{28,20},{21,1},{... | collective-permute-start | bytes 602120 | tf_op jit(solution)/shard_map/ppermute | solution.py:295
  9.8 17.9 %collective-permute-start.5 = (bf16[784,128]{1,0:T(8,128)(2,1)S(1)}, bf16[784,128]{1,0:T(8,128)(2,1)S(1)}, u32[]{:S(2)}, u32[]{:S(2)}) collective-permute-start(bf16[784,128]{1,0:T(8,128)(2,1)S(1)} %get-tuple-element.25.refs_0_.refs_2_.refs_3_), channel_id=1, source_target_pairs={{8,0},{24,8},{16,24},{4,16},{12,4},{28,12},{20,28},{0,20},{9,1},{2... | collective-permute-start | bytes 602120 | tf_op jit(solution)/shard_map/ppermute | solution.py:295
  13.9 12.0 %collective-permute-start.1 = (bf16[784,128]{1,0:T(8,128)(2,1)S(1)}, bf16[784,128]{1,0:T(8,128)(2,1)S(1)}, u32[]{:S(2)}, u32[]{:S(2)}) collective-permute-start(bf16[784,128]{1,0:T(8,128)(2,1)S(1)} %get-tuple-element.23), channel_id=1, source_target_pairs={{0,2},{1,3},{2,0},{3,1},{4,6},{5,7},{6,4},{7,5},{8,10},{9,11},{10,... | collective-permute-start | bytes 602120 | tf_op jit(solution)/shard_map/ppermute | solution.py:302
  20.2 11.6 %collective-permute-start.7 = (bf16[2,784,128]{2,1,0:T(8,128)(2,1)S(1)}, bf16[2,784,128]{2,1,0:T(8,128)(2,1)S(1)}, u32[]{:S(2)}, u32[]{:S(2)}) collective-permute-start(bf16[2,784,128]{2,1,0:T(8,128)(2,1)S(1)} %shard_map.39), channel_id=1, source_target_pairs={{20,0},{0,8},{8,24},{24,16},{16,4},{4,12},{12,28},{28,20},{21,1},{... | collective-permute-start | bytes 1204232 | tf_op jit(solution)/shard_map/ppermute | solution.py:295
  21.8 10.0 %collective-permute-start.4 = (bf16[2,784,128]{2,1,0:T(8,128)(2,1)S(1)}, bf16[2,784,128]{2,1,0:T(8,128)(2,1)S(1)}, u32[]{:S(2)}, u32[]{:S(2)}) collective-permute-start(bf16[2,784,128]{2,1,0:T(8,128)(2,1)S(1)} %shard_map.39), channel_id=1, source_target_pairs={{8,0},{24,8},{16,24},{4,16},{12,4},{28,12},{20,28},{0,20},{9,1},{2... | collective-permute-start | bytes 1204232 | tf_op jit(solution)/shard_map/ppermute | solution.py:295
  26.0 7.0 %collective-permute-start.3 = (bf16[4,784,128]{2,1,0:T(8,128)(2,1)S(1)}, bf16[4,784,128]{2,1,0:T(8,128)(2,1)S(1)}, u32[]{:S(2)}, u32[]{:S(2)}) collective-permute-start(bf16[4,784,128]{2,1,0:T(8,128)(2,1)S(1)} %shard_map.38), channel_id=1, source_target_pairs={{4,0},{12,8},{28,24},{20,16},{0,4},{8,12},{24,28},{16,20},{5,1},{1... | collective-permute-start | bytes 2408456 | tf_op jit(solution)/shard_map/ppermute | solution.py:295
  26.1 10.0 %collective-permute-start.6 = (bf16[1,784,128]{2,1,0:T(8,128)(2,1)S(1)}, bf16[1,784,128]{2,1,0:T(8,128)(2,1)S(1)}, u32[]{:S(2)}, u32[]{:S(2)}) collective-permute-start(bf16[1,784,128]{2,1,0:T(8,128)(2,1)S(1)} %shard_map.40), channel_id=1, source_target_pairs={{20,0},{0,8},{8,24},{24,16},{16,4},{4,12},{12,28},{28,20},{21,1},{... | collective-permute-start | bytes 602120 | tf_op jit(solution)/shard_map/ppermute | solution.py:295
  27.7 9.6 %collective-permute-start.9 = (bf16[1,784,128]{2,1,0:T(8,128)(2,1)S(1)}, bf16[1,784,128]{2,1,0:T(8,128)(2,1)S(1)}, u32[]{:S(2)}, u32[]{:S(2)}) collective-permute-start(bf16[1,784,128]{2,1,0:T(8,128)(2,1)S(1)} %shard_map.40), channel_id=1, source_target_pairs={{8,0},{24,8},{16,24},{4,16},{12,4},{28,12},{20,28},{0,20},{9,1},{2... | collective-permute-start | bytes 602120 | tf_op jit(solution)/shard_map/ppermute | solution.py:295

commit v11 on v10

--- a/solution.py
+++ b/solution.py
@@ -51,15 +51,9 @@
     return jnp.transpose(jnp.broadcast_to(row, (size, size)))
 
 
-def sort_kernel(axis, far_ref, code_ref, *refs):
-    *block_refs, place_ref, near_ref, unit_ref, sems = refs
-    rows, width = near_ref.shape
-    groups = len(block_refs)
-    capacity = (block_refs[0].shape[0] - TAIL) * LANES // width
-    slots = groups * capacity
-    chunks = width // LANES
+def unit_kernel(far_ref, unit_ref, near_ref, sems):
     parts = sems.shape[0]
-    size = rows // parts
+    size = far_ref.shape[0] // parts
     copies = [
         pltpu.make_async_copy(
             far_ref.at[pl.ds(i * size, size), :], near_ref.at[pl.ds(i * size, size), :], sems.at[i]
@@ -68,10 +62,22 @@
     ]
     for copy in copies:
         copy.start()
-    code = code_ref[...]
-    shift = (code - lax.axis_index(axis)) & (groups - 1)
-    rel = jnp.maximum(jnp.where(2 * shift > groups, 2 * (groups - shift), 2 * shift - 1), 0)
-    label = code >> (groups.bit_length() - 1)
+    for i, copy in enumerate(copies):
+        copy.wait()
+        feats = near_ref[pl.ds(i * size, size), :].astype(jnp.float32)
+        squares = jnp.sum(feats * feats, axis=1, keepdims=True) + 1e-06
+        unit_ref[pl.ds(i * size, size), :] = (feats * lax.rsqrt(squares)).astype(jnp.bfloat16)
+
+
+def sort_kernel(axis, unit_ref, group_ref, label_ref, *out_refs):
+    *block_refs, place_ref = out_refs
+    rows, width = unit_ref.shape
+    groups = len(block_refs)
+    capacity = (block_refs[0].shape[0] - TAIL) * LANES // width
+    slots = groups * capacity
+    chunks = width // LANES
+    owner = group_ref[...]
+    rel = owner ^ lax.axis_index(axis)
     lines = max(8, groups)
     onehot = lax.broadcasted_iota(jnp.int32, (lines, rows), 0) == rel
     before = lax.broadcasted_iota(jnp.int32, (rows, rows), 0) < lax.broadcasted_iota(
@@ -82,24 +88,18 @@
         jnp.where(before, 1.0, 0.0).astype(jnp.bfloat16),
         preferred_element_type=jnp.float32,
     )
-    rank = jnp.sum(jnp.where(onehot, ranks, 0.0), axis=0, keepdims=True)
-    place = rel * capacity + rank.astype(jnp.int32)
-    place_ref[...] = (code & (groups - 1)) * capacity + rank.astype(jnp.int32)
+    rank = jnp.sum(jnp.where(onehot, ranks, 0.0), axis=0, keepdims=True).astype(jnp.int32)
+    place_ref[...] = owner * capacity + rank
     move = jnp.where(
-        lax.broadcasted_iota(jnp.int32, (slots, rows), 0) == place, 1.0, 0.0
+        lax.broadcasted_iota(jnp.int32, (slots, rows), 0) == rel * capacity + rank, 1.0, 0.0
     ).astype(jnp.bfloat16)
-    labels = jnp.broadcast_to(label + 1, (TAIL, rows)).astype(jnp.bfloat16)
+    labels = jnp.broadcast_to(label_ref[...] + 1, (TAIL, rows)).astype(jnp.bfloat16)
     sorted_labels = (
         lax.dot_general(
             labels, move, (((1,), (1,)), ((), ())), preferred_element_type=jnp.float32
         )
         - 1.0
     ).astype(jnp.bfloat16)
-    for i, copy in enumerate(copies):
-        copy.wait()
-        feats = near_ref[pl.ds(i * size, size), :].astype(jnp.float32)
-        squares = jnp.sum(feats * feats, axis=1, keepdims=True) + 1e-06
-        unit_ref[pl.ds(i * size, size), :] = (feats * lax.rsqrt(squares)).astype(jnp.bfloat16)
     for k, block_ref in enumerate(block_refs):
         part = slice(k * capacity, (k + 1) * capacity)
         block = jnp.dot(
@@ -115,19 +115,14 @@
         refs[-1][k] = ref[...]
 
 
-def score_kernel(sources, tasks, turns, done, first, *refs):
-    *refs, flat_ref, side_ref = refs
-    outs = 2 + len(done)
-    inputs, (row_ref, column_ref, *out_refs) = refs[:-outs], refs[-outs:]
+def score_kernel(sources, tasks, done, *refs):
+    *refs, flat_ref, side_ref, row_ref = refs
+    outs = 1 + len(done)
+    inputs, (best_ref, *out_refs) = refs[:-outs], refs[-outs:]
     capacity = LANES
     low = jnp.float32(LOW)
-    if first:
-        row_ref[...] = jnp.full(row_ref.shape, low)
-        column_ref[...] = jnp.full(column_ref.shape, low)
-    else:
-        *inputs, old_rows, old_columns = inputs
-        row_ref[...] = old_rows[...]
-        column_ref[...] = old_columns[...]
+    arrays = 1 + max(index for index, _ in sources.values())
+    best_ref[...] = inputs[arrays][...] if len(inputs) > arrays else jnp.full(best_ref.shape, low)
     tops = {}
     for (role, k), (index, part) in sources.items():
         ref = inputs[index] if part is None else inputs[index].at[part]
@@ -138,7 +133,10 @@
         tops[role, k] = ref[pl.ds(height, TAIL), :][0:1].astype(jnp.float32)
     for role, k in sorted({(left, k) for left, ks, _, _, _ in tasks for k in ks}):
         side_ref[role, pl.ds(k * capacity, capacity), :] = column_of(tops[role, k])
-    for left, left_ks, right, right_ks, want_rows in tasks:
+    turns = sorted({(left, k) for left, ks, _, _, both in tasks if both for k in ks})
+    for role, k in turns:
+        row_ref[role, pl.ds(k * capacity, capacity), :] = jnp.full((capacity, LANES), low)
+    for left, left_ks, right, right_ks, both in tasks:
         start, count = left_ks[0] * capacity, len(left_ks) * capacity
         rows = pl.ds(start, count)
         for i in range(0, len(right_ks), 2):
@@ -159,23 +157,19 @@
                     != lax.broadcasted_iota(jnp.int32, (count, width), 1) + some[0] * capacity
                 )
             scores = jnp.where(same, scores, low)
-            if want_rows:
+            if both:
                 best = row_ref[left, rows, :]
                 for c in range(len(some)):
                     best = jnp.maximum(best, scores[:, c * LANES : (c + 1) * LANES])
                 row_ref[left, rows, :] = best
             best = jnp.max(scores.reshape(count // 8, 8, width), axis=0)
-            column_ref[right, :, columns] = jnp.maximum(column_ref[right, :, columns], best)
+            best_ref[right, :, columns] = jnp.maximum(best_ref[right, :, columns], best)
     for role, k in turns:
         rows = pl.ds(k * capacity, capacity)
         turned = jnp.transpose(row_ref[role, rows, :]).reshape(capacity // 8, 8, capacity)
-        column_ref[role, :, rows] = jnp.maximum(column_ref[role, :, rows], jnp.max(turned, axis=0))
+        best_ref[role, :, rows] = jnp.maximum(best_ref[role, :, rows], jnp.max(turned, axis=0))
     for role, out_ref in zip(done, out_refs):
-        out_ref[...] = jnp.max(column_ref[role], axis=0, keepdims=True)
-
-
-def slot_shift(k):
-    return (k + 1) // 2 if k % 2 else -(k // 2)
+        out_ref[...] = jnp.max(best_ref[role], axis=0, keepdims=True)
 
 
 def spread_kernel(ring, offsets, groups, *refs):
@@ -188,7 +182,7 @@
             jnp.where(shard == ring[e], ring[(e + offset) % shards], 0) for e in range(shards)
         )
         for k in range(groups):
-            row = target * groups + ((group - slot_shift(k)) & (groups - 1))
+            row = target * groups + (group ^ k)
             out_ref[pl.ds(row, 1)] = ref[:, k * LANES : (k + 1) * LANES].reshape(1, 1, LANES)
 
 
@@ -213,7 +207,7 @@
 
 
 def call(
-    kernel, out_shape, scratch, args, flops, bytes_accessed, in_specs=None, limit=48 * MIB, aliases=None
+    kernel, out_shape, scratch, args, flops, bytes_accessed, in_specs=None, limit=48 * MIB
 ):
     return pl.pallas_call(
         kernel,
@@ -221,7 +215,6 @@
         in_specs=in_specs or in_vmem(len(args)),
         out_specs=in_vmem(len(out_shape)),
         scratch_shapes=scratch,
-        input_output_aliases=aliases or {},
         compiler_params=pltpu.CompilerParams(vmem_limit_bytes=limit),
         cost_estimate=pl.CostEstimate(
             flops=flops, bytes_accessed=bytes_accessed, transcendentals=0
@@ -244,7 +237,7 @@
     )[0]
 
 
-def score(held, tasks, turns, acc, done, slots, width):
+def score(held, tasks, acc, done, slots, width):
     roles = len(held)
     used = sorted(
         {(left, k) for left, ks, _, _, _ in tasks for k in ks}
@@ -258,25 +251,21 @@
         if index == len(arrays):
             arrays.append(array)
         sources[role, k] = (index, part)
-    states = [
-        jax.ShapeDtypeStruct((roles, slots, LANES), jnp.float32),
-        jax.ShapeDtypeStruct((roles, 8, slots), jnp.float32),
-    ]
     ends = [jax.ShapeDtypeStruct((1, slots), jnp.float32)] * len(done)
     tiles = sum(len(task[1]) * len(task[3]) for task in tasks)
-    got = call(
-        lambda *refs: score_kernel(sources, tasks, turns, done, not acc, *refs),
-        states + ends,
+    best, *ends = call(
+        lambda *refs: score_kernel(sources, tasks, done, *refs),
+        [jax.ShapeDtypeStruct((roles, 8, slots), jnp.float32)] + ends,
         [
             pltpu.VMEM((roles, slots, width), jnp.bfloat16),
             pltpu.VMEM((roles, slots, LANES), jnp.float32),
+            pltpu.VMEM((roles, slots, LANES), jnp.float32),
         ],
-        arrays + list(acc),
+        arrays + acc,
         2 * tiles * LANES * LANES * width,
         2 * len(used) * LANES * width,
-        aliases={len(arrays) + i: i for i in range(len(acc))},
-    )
-    return got[: len(states)], got[len(states) :]
+    )
+    return [best], ends
 
 
 def per_device(embeddings, row_group, row_cluster):
@@ -297,26 +286,28 @@
     def exchange(blocks):
         got = list(blocks)
         for k in range(1, groups):
-            shift = slot_shift(k)
             block = after(blocks[k], got[1]) if k > 2 else blocks[k]
-            got[k] = lax.ppermute(block, "group", [(z, (z + shift) % groups) for z in range(groups)])
+            got[k] = lax.ppermute(block, "group", [(z, z ^ k) for z in range(groups)])
         return got
 
-    code = row_cluster * groups + row_group[:, 0]
+    (units,) = call(
+        unit_kernel,
+        [jax.ShapeDtypeStruct((rows, width), jnp.bfloat16)],
+        [pltpu.VMEM((rows, width), embeddings.dtype), pltpu.SemaphoreType.DMA((4,))],
+        (embeddings,),
+        4 * rows * width,
+        4 * rows * width,
+        [pl.BlockSpec(memory_space=pltpu.HBM)],
+        53 * MIB,
+    )
     *send, place = call(
         lambda *refs: sort_kernel("group", *refs),
         [jax.ShapeDtypeStruct((height, LANES), jnp.bfloat16)] * groups
         + [jax.ShapeDtypeStruct((1, rows), jnp.int32)],
-        [
-            pltpu.VMEM((rows, width), embeddings.dtype),
-            pltpu.VMEM((rows, width), jnp.bfloat16),
-            pltpu.SemaphoreType.DMA((4,)),
-        ],
-        (embeddings, code.reshape(1, rows)),
+        [],
+        (units, *lax.optimization_barrier((row_group.reshape(1, rows), row_cluster.reshape(1, rows)))),
         2 * rows * slots * width,
         4 * rows * width,
-        [pl.BlockSpec(memory_space=pltpu.HBM), pl.BlockSpec(memory_space=pltpu.VMEM)],
-        53 * MIB,
     )
 
     late = [groups - 1] if groups > 1 else []
@@ -331,46 +322,43 @@
     held[0] = [(x, None) for x in own]
     for r in near:
         held[r][0] = (first[r], None)
-    for ks, wait in ((early[1:], WAIT), (late, WAIT)):
-        if ks:
-            block = stack([own[k] for k in ks], wait)
-            for r in near:
-                moved = from_offset(block, offsets[r])
-                for i, k in enumerate(ks):
-                    held[r][k] = (moved, i)
+    for k in range(1, groups):
+        if k == 1:
+            block = after(own[k], first[near[0]]) if near else own[k]
+        else:
+            passed = [held[r][k - 2][0] for r in near]
+            block = stack([after(own[k], *passed)], WAIT)
+        for r in near:
+            held[r][k] = (from_offset(block, offsets[r]), 0 if k > 1 else None)
     got = {r: from_offset(stack(own, 0), offsets[r]) for r in far}
+    for r in far:
+        held[r] = [(got[r], k) for k in range(groups)]
     everything = [(0, 0, False)]
     everything += [(offsets.index(a), offsets.index(b), both) for a, b, both in pairs]
     steps = [[] for _ in range(4)]
-    turn, final = {}, [0] * roles
+    final = [0] * roles
     for left, right, both in everything:
         for left_ks in (early, late):
             for right_ks in (early, late):
                 if left_ks and right_ks:
                     step = 0
                     for role, ks in ((left, left_ks), (right, right_ks)):
-                        if role in far:
-                            step = max(step, 1)
-                        elif ks is late:
-                            step = max(step, (3 if role == near[0] else 2) if role else 1)
-                    steps[step].append((left, left_ks, right, right_ks, both))
+                        if role in near:
+                            step = max(step, 1 if ks is early else 3 if role == near[0] else 2)
+                    task = (left, left_ks, right, right_ks, both)
+                    if both and right_ks is late:
+                        task = (right, right_ks, left, left_ks, both)
+                    steps[step].append(task)
                     final[right] = max(final[right], step)
                     if both:
                         final[left] = max(final[left], step)
-                        for k in left_ks:
-                            turn[left, k] = max(turn.get((left, k), step), step)
     acc, partial = [], [None] * roles
     for step, tasks in enumerate(steps):
         if tasks:
-            if step == 1:
-                for r in far:
-                    held[r] = [(got[r], k) for k in range(groups)]
             done = [r for r in range(roles) if final[r] == step]
-            turns = sorted(x for x in turn if turn[x] == step)
-            acc, ends = score(held, tasks, turns, acc, done, slots, width)
+            acc, ends = score(held, tasks, acc, done, slots, width)
             for r, end in zip(done, ends):
                 partial[r] = end
-
     (best,) = call(
         lambda *refs: spread_kernel(ring, offsets, groups, *refs),
         [jax.ShapeDtypeStruct((shards * groups, 1, capacity), jnp.float32)],

time: 48.1 us -> 47.9 us (level)
  waiting for transfers between devices: 12.9 us -> 8.05 us
  blocking collectives: 9.21 us -> 12.6 us
  starting transfers between devices: 16.9 us -> 18.3 us
  other arithmetic: 0.7 us -> 0 us
    ppermute x7 -> x9, starting transfers between devices: 5.43 us -> 10.2 us  [from_offset(): return lax.ppermute(x, 'shard', perm)]
    ppermute x3, waiting for transfers between devices: 7.94 us -> 3.65 us  [exchange(): got[k] = lax.ppermute(block, 'group', [(z, z ^ k) for z in range(groups)])]
    all_to_all x1, blocking collectives: 9.21 us -> 12.6 us  [per_device(): lax.all_to_all(best, ('shard', 'group'), split_axis=0, concat_axis=0, til...]
    ppermute x3, starting transfers between devices: 11.5 us -> 8.15 us  [exchange(): got[k] = lax.ppermute(block, 'group', [(z, z ^ k) for z in range(groups)])]
    add x1 -> x0, other arithmetic: 0.7 us -> none  [per_device(): code = row_cluster * groups + row_group[:, 0]]
    ppermute x7 -> x9, waiting for transfers between devices: 4.95 us -> 4.4 us  [from_offset(): return lax.ppermute(x, 'shard', perm)]
    pallas_call x10 -> x11, Pallas kernels: 8.12 us -> 8.58 us  [call(): pl.pallas_call(kernel, out_shape=out_shape, in_specs=in_specs or in_vmem(...]
  transfers between devices with their start and end apart: 10 -> 12, of which waited for: 4 -> 7; matrix products, arithmetic and copies ran while one was open for 0% -> 0% of each run, Pallas kernels for 9% -> 9%
where the time goes in v11:
time: 47.9 us; the launch traced here: 47.7 us
  starting transfers between devices  18.3 us (38%)
  blocking collectives  12.6 us (26%)
  Pallas kernels  8.58 us (18%)
  waiting for transfers between devices  8.05 us (17%)
    all_to_all x1, blocking collectives, per_device(): lax.all_to_all(best, ('shard', 'group'), split_axis=0, concat_axis=0, til...  12.6 us
    ppermute x9, starting transfers between devices, from_offset(): return lax.ppermute(x, 'shard', perm)  10.2 us
    pallas_call x11, Pallas kernels, call(): pl.pallas_call(kernel, out_shape=out_shape, in_specs=in_specs or in_vmem(...  8.58 us
    ppermute x3, starting transfers between devices, exchange(): got[k] = lax.ppermute(block, 'group', [(z, z ^ k) for z in range(groups)])  8.15 us
    ppermute x9, waiting for transfers between devices, from_offset(): return lax.ppermute(x, 'shard', perm)  4.4 us
    ppermute x3, waiting for transfers between devices, exchange(): got[k] = lax.ppermute(block, 'group', [(z, z ^ k) for z in range(groups)])  3.65 us
  transfers between devices with their start and end apart: 12, of which 7 were waited for; matrix products, arithmetic and copies ran while one was open for 0% of the time, Pallas kernels for 9%

profile of v11, /device:TPU:0, one launch (start us, length us, event | category | flops | bytes accessed | tf_op | source)
XLA Modules:
  0.0 47.7 jit_solution(6114023351380603865)
XLA Ops:
  0.0 0.0 copy-start
  0.0 0.0 copy-start.1
  0.0 1.5 %shard_map.37.refs_0_ = bf16[512,768]{1,0:T(8,128)(2,1)S(1)} custom-call(bf16[512,768]{1,0:T(8,128)(2,1)} %far_ref.1), custom_call_target="tpu_custom_call" | custom-call | flops 1572864 | bytes 1572864 | tf_op jit(solution)/shard_map/pallas_call | solution.py:212
  1.5 0.0 copy-done
  1.5 0.0 copy-done.1
  1.5 0.9 %shard_map.38 = (bf16[784,128]{1,0:T(8,128)(2,1)S(1)}, bf16[784,128]{1,0:T(8,128)(2,1)S(1)}, bf16[784,128]{1,0:T(8,128)(2,1)S(1)}, bf16[784,128]{1,0:T(8,128)(2,1)S(1)}, s32[1,512]{1,0:T(1,128)S(1)}) custom-call(bf16[512,768]{1,0:T(8,128)(2,1)S(1)} %shard_map.37.refs_0_, s32[1,512]{1,0:T(1,128)S(1)} %bitcast.3, s32[1,512]{1,0:T(1,128)S(1)} %bitcast.4), custom_call_target="tpu_custom_call" | custom-call | flops 402653184 | bytes 1572864 | tf_op jit(solution)/shard_map/pallas_call | solution.py:212
  2.5 3.1 %collective-permute-start = (bf16[784,128]{1,0:T(8,128)(2,1)S(1)}, bf16[784,128]{1,0:T(8,128)(2,1)S(1)}, u32[]{:S(2)}, u32[]{:S(2)}) collective-permute-start(bf16[784,128]{1,0:T(8,128)(2,1)S(1)} %get-tuple-element.24), channel_id=1, source_target_pairs={{0,1},{1,0},{2,3},{3,2},{4,5},{5,4},{6,7},{7,6},{8,9},{9,8},{10,11... | collective-permute-start | bytes 602120 | tf_op jit(solution)/shard_map/ppermute | solution.py:290
  5.6 0.7 %collective-permute-start.4 = (bf16[784,128]{1,0:T(8,128)(2,1)S(1)}, bf16[784,128]{1,0:T(8,128)(2,1)S(1)}, u32[]{:S(2)}, u32[]{:S(2)}) collective-permute-start(bf16[784,128]{1,0:T(8,128)(2,1)S(1)} %get-tuple-element.27.refs_0_.refs_3_), channel_id=1, source_target_pairs={{8,0},{24,8},{16,24},{4,16},{12,4},{28,12},{20,28},{0,20},{9,1},{2... | collective-permute-start | bytes 602120 | tf_op jit(solution)/shard_map/ppermute | solution.py:284
  6.2 2.6 %collective-permute-start.2 = (bf16[784,128]{1,0:T(8,128)(2,1)S(1)}, bf16[784,128]{1,0:T(8,128)(2,1)S(1)}, u32[]{:S(2)}, u32[]{:S(2)}) collective-permute-start(bf16[784,128]{1,0:T(8,128)(2,1)S(1)} %get-tuple-element.26), channel_id=1, source_target_pairs={{0,2},{1,3},{2,0},{3,1},{4,6},{5,7},{6,4},{7,5},{8,10},{9,11},{10,... | collective-permute-start | bytes 602120 | tf_op jit(solution)/shard_map/ppermute | solution.py:290
  8.8 1.3 %collective-permute-start.5 = (bf16[784,128]{1,0:T(8,128)(2,1)S(1)}, bf16[784,128]{1,0:T(8,128)(2,1)S(1)}, u32[]{:S(2)}, u32[]{:S(2)}) collective-permute-start(bf16[784,128]{1,0:T(8,128)(2,1)S(1)} %get-tuple-element.27.refs_0_.refs_3_), channel_id=1, source_target_pairs={{20,0},{0,8},{8,24},{24,16},{16,4},{4,12},{12,28},{28,20},{21,1},{... | collective-permute-start | bytes 602120 | tf_op jit(solution)/shard_map/ppermute | solution.py:284
  10.2 0.4 collective-permute-done.refs_1_.refs_2_
  10.5 1.5 %collective-permute-done.4.refs_7_ = bf16[784,128]{1,0:T(8,128)(2,1)S(1)} collective-permute-done((bf16[784,128]{1,0:T(8,128)(2,1)S(1)}, bf16[784,128]{1,0:T(8,128)(2,1)S(1)}, u32[]{:S(2)}, u32[]{:S(2)}) %collective-permute-start.4) | collective-permute-done | bytes 200736 | tf_op jit(solution)/shard_map/ppermute | solution.py:284
  12.0 1.5 %collective-permute-start.7 = (bf16[784,128]{1,0:T(8,128)(2,1)S(1)}, bf16[784,128]{1,0:T(8,128)(2,1)S(1)}, u32[]{:S(2)}, u32[]{:S(2)}) collective-permute-start(bf16[784,128]{1,0:T(8,128)(2,1)S(1)} %collective-permute-done.refs_1_.refs_2_), channel_id=1, source_target_pairs={{8,0},{24,8},{16,24},{4,16},{12,4},{28,12},{20,28},{0,20},{9,1},{2... | collective-permute-start | bytes 602120 | tf_op jit(solution)/shard_map/ppermute | solution.py:284
  13.6 2.6 %collective-permute-start.8 = (bf16[784,128]{1,0:T(8,128)(2,1)S(1)}, bf16[784,128]{1,0:T(8,128)(2,1)S(1)}, u32[]{:S(2)}, u32[]{:S(2)}) collective-permute-start(bf16[784,128]{1,0:T(8,128)(2,1)S(1)} %collective-permute-done.refs_1_.refs_2_), channel_id=1, source_target_pairs={{20,0},{0,8},{8,24},{24,16},{16,4},{4,12},{12,28},{28,20},{21,1},{... | collective-permute-start | bytes 602120 | tf_op jit(solution)/shard_map/ppermute | solution.py:284
  16.1 2.5 %collective-permute-start.1 = (bf16[784,128]{1,0:T(8,128)(2,1)S(1)}, bf16[784,128]{1,0:T(8,128)(2,1)S(1)}, u32[]{:S(2)}, u32[]{:S(2)}) collective-permute-start(bf16[784,128]{1,0:T(8,128)(2,1)S(1)} %get-tuple-element.25), channel_id=1, source_target_pairs={{0,3},{1,2},{2,1},{3,0},{4,7},{5,6},{6,5},{7,4},{8,11},{9,10},{10,... | collective-permute-start | bytes 602120 | tf_op jit(solution)/shard_map/ppermute | solution.py:290
  18.6 0.7 %collective-permute-done.2.refs_2_.refs_0_.refs_1_ = bf16[784,128]{1,0:T(8,128)(2,1)S(1)} collective-permute-done((bf16[784,128]{1,0:T(8,128)(2,1)S(1)}, bf16[784,128]{1,0:T(8,128)(2,1)S(1)}, u32[]{:S(2)}, u32[]{:S(2)}) %collective-permute-start.2) | collective-permute-done | bytes 200736 | tf_op jit(solution)/shard_map/ppermute | solution.py:290
  19.3 0.0 collective-permute-done.5.refs_10_.refs_4_
  19.3 1.4 %collective-permute-start.10 = (bf16[1,784,128]{2,1,0:T(8,128)(2,1)S(1)}, bf16[1,784,128]{2,1,0:T(8,128)(2,1)S(1)}, u32[]{:S(2)}, u32[]{:S(2)}) collective-permute-start(bf16[1,784,128]{2,1,0:T(8,128)(2,1)S(1)} %shard_map.40), channel_id=1, source_target_pairs={{20,0},{0,8},{8,24},{24,16},{16,4},{4,12},{12,28},{28,20},{21,1},{... | collective-permute-start | bytes 602120 | tf_op jit(solution)/shard_map/ppermute | solution.py:284
  20.7 0.4 collective-permute-start.6
  21.1 2.6 %collective-permute-done.1.refs_3_.refs_0_ = bf16[784,128]{1,0:T(8,128)(2,1)S(1)} collective-permute-done((bf16[784,128]{1,0:T(8,128)(2,1)S(1)}, bf16[784,128]{1,0:T(8,128)(2,1)S(1)}, u32[]{:S(2)}, u32[]{:S(2)}) %collective-permute-start.1) | collective-permute-done | bytes 200736 | tf_op jit(solution)/shard_map/ppermute | solution.py:290
  23.7 0.1 shard_map.39
  23.8 0.1 collective-permute-start.3
  23.9 0.0 collective-permute-done.7.refs_6_
  23.9 0.0 collective-permute-done.8.refs_9_.refs_3_
  23.9 2.1 %collective-permute-start.9 = (bf16[1,784,128]{2,1,0:T(8,128)(2,1)S(1)}, bf16[1,784,128]{2,1,0:T(8,128)(2,1)S(1)}, u32[]{:S(2)}, u32[]{:S(2)}) collective-permute-start(bf16[1,784,128]{2,1,0:T(8,128)(2,1)S(1)} %shard_map.41), channel_id=1, source_target_pairs={{20,0},{0,8},{8,24},{24,16},{16,4},{4,12},{12,28},{28,20},{21,1},{... | collective-permute-start | bytes 602120 | tf_op jit(solution)/shard_map/ppermute | solution.py:284
  26.0 0.0 collective-permute-start.11
  26.0 0.1 collective-permute-done.3.refs_4_
  26.2 1.6 %shard_map.42.refs_11_ = f32[4,8,512]{2,1,0:T(8,128)S(1)} custom-call(bf16[784,128]{1,0:T(8,128)(2,1)S(1)} %collective-permute-done.1.refs_3_.refs_0_, bf16[784,128]{1,0:T(8,128)(2,1)S(1)} %collective-permute-done.2.refs_2_.refs_0_.refs_1_, bf16[784,128]{1,0:T(8,128)(2,1)S(1)} %collective-permute-done.refs_1_.refs_2_, ...), custom_call_target="tpu_custom_call" | custom-call | flops 805306368 | bytes 1572864 | tf_op jit(solution)/shard_map/pallas_call | solution.py:212
  27.7 0.0 collective-permute-done.10.refs_8_.refs_2_
  27.7 0.0 collective-permute-done.6.refs_5_
  27.7 1.6 %shard_map.43.refs_9_ = f32[4,8,512]{2,1,0:T(8,128)S(1)} custom-call(bf16[784,128]{1,0:T(8,128)(2,1)S(1)} %collective-permute-done.1.refs_3_.refs_0_, bf16[784,128]{1,0:T(8,128)(2,1)S(1)} %collective-permute-done.2.refs_2_.refs_0_.refs_1_, bf16[784,128]{1,0:T(8,128)(2,1)S(1)} %collective-permute-done.refs_1_.refs_2_, ...), custom_call_target="tpu_custom_call" | custom-call | flops 830472192 | bytes 2752512 | tf_op jit(solution)/shard_map/pallas_call | solution.py:212
  29.3 1.6 %collective-permute-done.9.refs_8_.refs_1_ = bf16[1,784,128]{2,1,0:T(8,128)(2,1)S(1)} collective-permute-done((bf16[1,784,128]{2,1,0:T(8,128)(2,1)S(1)}, bf16[1,784,128]{2,1,0:T(8,128)(2,1)S(1)}, u32[]{:S(2)}, u32[]{:S(2)}) %collective-permute-start.9) | collective-permute-done | bytes 200736 | tf_op jit(solution)/shard_map/ppermute | solution.py:284
  30.9 1.0 %shard_map.44 = (f32[4,8,512]{2,1,0:T(8,128)S(1)}, f32[1,512]{1,0:T(1,128)S(1)}, f32[1,512]{1,0:T(1,128)S(1)}) custom-call(bf16[784,128]{1,0:T(8,128)(2,1)S(1)} %collective-permute-done.1.refs_3_.refs_0_, bf16[784,128]{1,0:T(8,128)(2,1)S(1)} %collective-permute-done.2.refs_2_.refs_0_.refs_1_, bf16[784,128]{1,0:T(8,128)(2,1)S(1)} %collective-permute-done.refs_1_.refs_2_, ...), custom_call_target="tpu_custom_call" | custom-call | flops 276824064 | bytes 2359296 | tf_op jit(solution)/shard_map/pallas_call | solution.py:212
  31.9 1.2 %collective-permute-done.11.refs_0_ = bf16[1,784,128]{2,1,0:T(8,128)(2,1)S(1)} collective-permute-done((bf16[1,784,128]{2,1,0:T(8,128)(2,1)S(1)}, bf16[1,784,128]{2,1,0:T(8,128)(2,1)S(1)}, u32[]{:S(2)}, u32[]{:S(2)}) %collective-permute-start.11) | collective-permute-done | bytes 200736 | tf_op jit(solution)/shard_map/ppermute | solution.py:284
  33.1 1.1 %shard_map.45 = (f32[4,8,512]{2,1,0:T(8,128)}, f32[1,512]{1,0:T(1,128)S(1)}, f32[1,512]{1,0:T(1,128)S(1)}) custom-call(bf16[1,784,128]{2,1,0:T(8,128)(2,1)S(1)} %collective-permute-done.11.refs_0_, bf16[1,784,128]{2,1,0:T(8,128)(2,1)S(1)} %collective-permute-done.9.refs_8_.refs_1_, bf16[1,784,128]{2,1,0:T(8,128)(2,1)S(1)} %collective-permute-done.10.refs_8_.refs_2_, ...), custom_call_target="tpu_custom_call" | custom-call | flops 100663296 | bytes 983040 | tf_op jit(solution)/shard_map/pallas_call | solution.py:212
  34.3 12.6 %all_to_all.5.refs_0_ = f32[32,1,128]{2,1,0:T(1,128)S(1)} all-to-all(f32[32,1,128]{2,1,0:T(1,128)S(1)} %shard_map.46), channel_id=1, replica_groups=mesh['shard'=8,'group'=4] {'shard','group'}, dimensions={0} | all-to-all | bytes 32768 | tf_op jit(solution)/shard_map/all_to_all | solution.py:370
  46.9 0.8 %shard_map.47 = f32[1,512]{1,0:T(1,128)} custom-call(f32[32,1,128]{2,1,0:T(1,128)S(1)} %all_to_all.5.refs_0_, s32[1,512]{1,0:T(1,128)S(1)} %get-tuple-element.36.refs_1_), custom_call_target="tpu_custom_call" | custom-call | flops 262144 | bytes 2048 | tf_op jit(solution)/shard_map/pallas_call | solution.py:212
  (3 shorter events, 0.1 us)
Async XLA Ops:
  0.0 1.5 %copy-start = (s32[512,1]{0,1:T(1,128)S(1)}, s32[512,1]{0,1:T(1,128)}, u32[]{:S(2)}) copy-start(s32[512,1]{0,1:T(1,128)} %param.4) | copy-start | bytes 6148
  0.0 1.5 %copy-start.1 = (s32[512]{0:T(512)S(1)}, s32[512]{0:T(512)}, u32[]{:S(2)}) copy-start(s32[512]{0:T(512)} %param.5) | copy-start | bytes 6148
  2.5 8.1 %collective-permute-start = (bf16[784,128]{1,0:T(8,128)(2,1)S(1)}, bf16[784,128]{1,0:T(8,128)(2,1)S(1)}, u32[]{:S(2)}, u32[]{:S(2)}) collective-permute-start(bf16[784,128]{1,0:T(8,128)(2,1)S(1)} %get-tuple-element.24), channel_id=1, source_target_pairs={{0,1},{1,0},{2,3},{3,2},{4,5},{5,4},{6,7},{7,6},{8,9},{9,8},{10,11... | collective-permute-start | bytes 602120 | tf_op jit(solution)/shard_map/ppermute | solution.py:290
  5.6 6.5 %collective-permute-start.4 = (bf16[784,128]{1,0:T(8,128)(2,1)S(1)}, bf16[784,128]{1,0:T(8,128)(2,1)S(1)}, u32[]{:S(2)}, u32[]{:S(2)}) collective-permute-start(bf16[784,128]{1,0:T(8,128)(2,1)S(1)} %get-tuple-element.27.refs_0_.refs_3_), channel_id=1, source_target_pairs={{8,0},{24,8},{16,24},{4,16},{12,4},{28,12},{20,28},{0,20},{9,1},{2... | collective-permute-start | bytes 602120 | tf_op jit(solution)/shard_map/ppermute | solution.py:284
  6.2 13.1 %collective-permute-start.2 = (bf16[784,128]{1,0:T(8,128)(2,1)S(1)}, bf16[784,128]{1,0:T(8,128)(2,1)S(1)}, u32[]{:S(2)}, u32[]{:S(2)}) collective-permute-start(bf16[784,128]{1,0:T(8,128)(2,1)S(1)} %get-tuple-element.26), channel_id=1, source_target_pairs={{0,2},{1,3},{2,0},{3,1},{4,6},{5,7},{6,4},{7,5},{8,10},{9,11},{10,... | collective-permute-start | bytes 602120 | tf_op jit(solution)/shard_map/ppermute | solution.py:290
  8.8 10.5 %collective-permute-start.5 = (bf16[784,128]{1,0:T(8,128)(2,1)S(1)}, bf16[784,128]{1,0:T(8,128)(2,1)S(1)}, u32[]{:S(2)}, u32[]{:S(2)}) collective-permute-start(bf16[784,128]{1,0:T(8,128)(2,1)S(1)} %get-tuple-element.27.refs_0_.refs_3_), channel_id=1, source_target_pairs={{20,0},{0,8},{8,24},{24,16},{16,4},{4,12},{12,28},{28,20},{21,1},{... | collective-permute-start | bytes 602120 | tf_op jit(solution)/shard_map/ppermute | solution.py:284
  12.0 11.9 %collective-permute-start.7 = (bf16[784,128]{1,0:T(8,128)(2,1)S(1)}, bf16[784,128]{1,0:T(8,128)(2,1)S(1)}, u32[]{:S(2)}, u32[]{:S(2)}) collective-permute-start(bf16[784,128]{1,0:T(8,128)(2,1)S(1)} %collective-permute-done.refs_1_.refs_2_), channel_id=1, source_target_pairs={{8,0},{24,8},{16,24},{4,16},{12,4},{28,12},{20,28},{0,20},{9,1},{2... | collective-permute-start | bytes 602120 | tf_op jit(solution)/shard_map/ppermute | solution.py:284
  13.6 10.3 %collective-permute-start.8 = (bf16[784,128]{1,0:T(8,128)(2,1)S(1)}, bf16[784,128]{1,0:T(8,128)(2,1)S(1)}, u32[]{:S(2)}, u32[]{:S(2)}) collective-permute-start(bf16[784,128]{1,0:T(8,128)(2,1)S(1)} %collective-permute-done.refs_1_.refs_2_), channel_id=1, source_target_pairs={{20,0},{0,8},{8,24},{24,16},{16,4},{4,12},{12,28},{28,20},{21,1},{... | collective-permute-start | bytes 602120 | tf_op jit(solution)/shard_map/ppermute | solution.py:284
  16.1 7.6 %collective-permute-start.1 = (bf16[784,128]{1,0:T(8,128)(2,1)S(1)}, bf16[784,128]{1,0:T(8,128)(2,1)S(1)}, u32[]{:S(2)}, u32[]{:S(2)}) collective-permute-start(bf16[784,128]{1,0:T(8,128)(2,1)S(1)} %get-tuple-element.25), channel_id=1, source_target_pairs={{0,3},{1,2},{2,1},{3,0},{4,7},{5,6},{6,5},{7,4},{8,11},{9,10},{10,... | collective-permute-start | bytes 602120 | tf_op jit(solution)/shard_map/ppermute | solution.py:290
  19.3 8.4 %collective-permute-start.10 = (bf16[1,784,128]{2,1,0:T(8,128)(2,1)S(1)}, bf16[1,784,128]{2,1,0:T(8,128)(2,1)S(1)}, u32[]{:S(2)}, u32[]{:S(2)}) collective-permute-start(bf16[1,784,128]{2,1,0:T(8,128)(2,1)S(1)} %shard_map.40), channel_id=1, source_target_pairs={{20,0},{0,8},{8,24},{24,16},{16,4},{4,12},{12,28},{28,20},{21,1},{... | collective-permute-start | bytes 602120 | tf_op jit(solution)/shard_map/ppermute | solution.py:284
  20.7 7.0 %collective-permute-start.6 = (bf16[1,784,128]{2,1,0:T(8,128)(2,1)S(1)}, bf16[1,784,128]{2,1,0:T(8,128)(2,1)S(1)}, u32[]{:S(2)}, u32[]{:S(2)}) collective-permute-start(bf16[1,784,128]{2,1,0:T(8,128)(2,1)S(1)} %shard_map.40), channel_id=1, source_target_pairs={{8,0},{24,8},{16,24},{4,16},{12,4},{28,12},{20,28},{0,20},{9,1},{2... | collective-permute-start | bytes 602120 | tf_op jit(solution)/shard_map/ppermute | solution.py:284
  23.8 2.4 %collective-permute-start.3 = (bf16[4,784,128]{2,1,0:T(8,128)(2,1)S(1)}, bf16[4,784,128]{2,1,0:T(8,128)(2,1)S(1)}, u32[]{:S(2)}, u32[]{:S(2)}) collective-permute-start(bf16[4,784,128]{2,1,0:T(8,128)(2,1)S(1)} %shard_map.39), channel_id=1, source_target_pairs={{4,0},{12,8},{28,24},{20,16},{0,4},{8,12},{24,28},{16,20},{5,1},{1... | collective-permute-start | bytes 2408456 | tf_op jit(solution)/shard_map/ppermute | solution.py:284
  23.9 7.0 %collective-permute-start.9 = (bf16[1,784,128]{2,1,0:T(8,128)(2,1)S(1)}, bf16[1,784,128]{2,1,0:T(8,128)(2,1)S(1)}, u32[]{:S(2)}, u32[]{:S(2)}) collective-permute-start(bf16[1,784,128]{2,1,0:T(8,128)(2,1)S(1)} %shard_map.41), channel_id=1, source_target_pairs={{20,0},{0,8},{8,24},{24,16},{16,4},{4,12},{12,28},{28,20},{21,1},{... | collective-permute-start | bytes 602120 | tf_op jit(solution)/shard_map/ppermute | solution.py:284
  26.0 7.1 %collective-permute-start.11 = (bf16[1,784,128]{2,1,0:T(8,128)(2,1)S(1)}, bf16[1,784,128]{2,1,0:T(8,128)(2,1)S(1)}, u32[]{:S(2)}, u32[]{:S(2)}) collective-permute-start(bf16[1,784,128]{2,1,0:T(8,128)(2,1)S(1)} %shard_map.41), channel_id=1, source_target_pairs={{8,0},{24,8},{16,24},{4,16},{12,4},{28,12},{20,28},{0,20},{9,1},{2... | collective-permute-start | bytes 602120 | tf_op jit(solution)/shard_map/ppermute | solution.py:284

commit v12 on v11

--- a/solution.py
+++ b/solution.py
@@ -182,7 +182,7 @@
             jnp.where(shard == ring[e], ring[(e + offset) % shards], 0) for e in range(shards)
         )
         for k in range(groups):
-            row = target * groups + (group ^ k)
+            row = (shards - target) * groups - 1 - (group ^ k)
             out_ref[pl.ds(row, 1)] = ref[:, k * LANES : (k + 1) * LANES].reshape(1, 1, LANES)
 
 
@@ -193,7 +193,7 @@
     for g in range(groups):
         row = jnp.full((1, LANES), jnp.float32(-1.0))
         for s in range(back_ref.shape[0] // groups):
-            row = jnp.maximum(row, back_ref[s * groups + g])
+            row = jnp.maximum(row, back_ref[s * groups + groups - 1 - g])
         values = jnp.concatenate([column_of(row)] * (rows // LANES), axis=1)
         here = lax.broadcasted_iota(jnp.int32, (LANES, rows), 0) + g * LANES == place
         best = jnp.maximum(
@@ -286,7 +286,7 @@
     def exchange(blocks):
         got = list(blocks)
         for k in range(1, groups):
-            block = after(blocks[k], got[1]) if k > 2 else blocks[k]
+            block = after(blocks[k], got[2]) if k > 2 else blocks[k]
             got[k] = lax.ppermute(block, "group", [(z, z ^ k) for z in range(groups)])
         return got
 
@@ -346,7 +346,7 @@
                         if role in near:
                             step = max(step, 1 if ks is early else 3 if role == near[0] else 2)
                     task = (left, left_ks, right, right_ks, both)
-                    if both and right_ks is late:
+                    if both and right_ks is late and left_ks is early:
                         task = (right, right_ks, left, left_ks, both)
                     steps[step].append(task)
                     final[right] = max(final[right], step)
@@ -367,7 +367,14 @@
         roles * slots,
         4 * roles * slots,
     )
-    back = lax.all_to_all(best, ("shard", "group"), split_axis=0, concat_axis=0, tiled=True)
+    back = lax.all_to_all(
+        best,
+        ("shard", "group"),
+        split_axis=0,
+        concat_axis=0,
+        axis_index_groups=[list(reversed(range(shards * groups)))],
+        tiled=True,
+    )
     (result,) = call(
         lambda *refs: place_kernel(groups, *refs),
         [jax.ShapeDtypeStruct((1, rows), jnp.float32)],

time: 47.9 us -> 49 us (1.023)
  waiting for transfers between devices: 8.05 us -> 11.3 us
  blocking collectives: 12.6 us -> 10.8 us
    ppermute x3, waiting for transfers between devices: 3.65 us -> 8.07 us  [exchange(): got[k] = lax.ppermute(block, 'group', [(z, z ^ k) for z in range(groups)])]
    all_to_all x1, blocking collectives: 12.6 us -> 10.8 us  [per_device(): lax.all_to_all(best, ('shard', 'group'), split_axis=0, concat_axis=0, axi...]
    ppermute x9, waiting for transfers between devices: 4.4 us -> 3.21 us  [from_offset(): return lax.ppermute(x, 'shard', perm)]
  transfers between devices with their start and end apart: 12 -> 12, of which waited for: 7 -> 6; matrix products, arithmetic and copies ran while one was open for 0% -> 0% of each run, Pallas kernels for 9% -> 9%
where the time goes in v12:
time: 49 us; the launch traced here: 48.8 us
  starting transfers between devices  18 us (37%)
  waiting for transfers between devices  11.3 us (23%)
  blocking collectives  10.8 us (22%)
  Pallas kernels  8.6 us (18%)
    all_to_all x1, blocking collectives, per_device(): lax.all_to_all(best, ('shard', 'group'), split_axis=0, concat_axis=0, axi...  10.8 us
    ppermute x9, starting transfers between devices, from_offset(): return lax.ppermute(x, 'shard', perm)  9.83 us
    pallas_call x11, Pallas kernels, call(): pl.pallas_call(kernel, out_shape=out_shape, in_specs=in_specs or in_vmem(...  8.6 us
    ppermute x3, starting transfers between devices, exchange(): got[k] = lax.ppermute(block, 'group', [(z, z ^ k) for z in range(groups)])  8.19 us
    ppermute x3, waiting for transfers between devices, exchange(): got[k] = lax.ppermute(block, 'group', [(z, z ^ k) for z in range(groups)])  8.07 us
    ppermute x9, waiting for transfers between devices, from_offset(): return lax.ppermute(x, 'shard', perm)  3.21 us
  transfers between devices with their start and end apart: 12, of which 6 were waited for; matrix products, arithmetic and copies ran while one was open for 0% of the time, Pallas kernels for 9%

profile of v12, /device:TPU:0, one launch (start us, length us, event | category | flops | bytes accessed | tf_op | source)
XLA Modules:
  0.0 48.8 jit_solution(18388371764340728369)
XLA Ops:
  0.0 0.0 copy-start
  0.0 0.0 copy-start.1
  0.0 1.5 %shard_map.37.refs_0_ = bf16[512,768]{1,0:T(8,128)(2,1)S(1)} custom-call(bf16[512,768]{1,0:T(8,128)(2,1)} %far_ref.1), custom_call_target="tpu_custom_call" | custom-call | flops 1572864 | bytes 1572864 | tf_op jit(solution)/shard_map/pallas_call | solution.py:212
  1.5 0.0 copy-done
  1.5 0.0 copy-done.1
  1.5 0.9 %shard_map.38 = (bf16[784,128]{1,0:T(8,128)(2,1)S(1)}, bf16[784,128]{1,0:T(8,128)(2,1)S(1)}, bf16[784,128]{1,0:T(8,128)(2,1)S(1)}, bf16[784,128]{1,0:T(8,128)(2,1)S(1)}, s32[1,512]{1,0:T(1,128)S(1)}) custom-call(bf16[512,768]{1,0:T(8,128)(2,1)S(1)} %shard_map.37.refs_0_, s32[1,512]{1,0:T(1,128)S(1)} %bitcast.3, s32[1,512]{1,0:T(1,128)S(1)} %bitcast.4), custom_call_target="tpu_custom_call" | custom-call | flops 402653184 | bytes 1572864 | tf_op jit(solution)/shard_map/pallas_call | solution.py:212
  2.5 3.1 %collective-permute-start.2 = (bf16[784,128]{1,0:T(8,128)(2,1)S(1)}, bf16[784,128]{1,0:T(8,128)(2,1)S(1)}, u32[]{:S(2)}, u32[]{:S(2)}) collective-permute-start(bf16[784,128]{1,0:T(8,128)(2,1)S(1)} %get-tuple-element.26), channel_id=1, source_target_pairs={{0,1},{1,0},{2,3},{3,2},{4,5},{5,4},{6,7},{7,6},{8,9},{9,8},{10,11... | collective-permute-start | bytes 602120 | tf_op jit(solution)/shard_map/ppermute | solution.py:290
  5.6 0.7 %collective-permute-start.4 = (bf16[784,128]{1,0:T(8,128)(2,1)S(1)}, bf16[784,128]{1,0:T(8,128)(2,1)S(1)}, u32[]{:S(2)}, u32[]{:S(2)}) collective-permute-start(bf16[784,128]{1,0:T(8,128)(2,1)S(1)} %get-tuple-element.27.refs_0_.refs_3_), channel_id=1, source_target_pairs={{8,0},{24,8},{16,24},{4,16},{12,4},{28,12},{20,28},{0,20},{9,1},{2... | collective-permute-start | bytes 602120 | tf_op jit(solution)/shard_map/ppermute | solution.py:284
  6.2 2.6 %collective-permute-start = (bf16[784,128]{1,0:T(8,128)(2,1)S(1)}, bf16[784,128]{1,0:T(8,128)(2,1)S(1)}, u32[]{:S(2)}, u32[]{:S(2)}) collective-permute-start(bf16[784,128]{1,0:T(8,128)(2,1)S(1)} %get-tuple-element.24), channel_id=1, source_target_pairs={{0,2},{1,3},{2,0},{3,1},{4,6},{5,7},{6,4},{7,5},{8,10},{9,11},{10,... | collective-permute-start | bytes 602120 | tf_op jit(solution)/shard_map/ppermute | solution.py:290
  8.8 1.3 %collective-permute-start.5 = (bf16[784,128]{1,0:T(8,128)(2,1)S(1)}, bf16[784,128]{1,0:T(8,128)(2,1)S(1)}, u32[]{:S(2)}, u32[]{:S(2)}) collective-permute-start(bf16[784,128]{1,0:T(8,128)(2,1)S(1)} %get-tuple-element.27.refs_0_.refs_3_), channel_id=1, source_target_pairs={{20,0},{0,8},{8,24},{24,16},{16,4},{4,12},{12,28},{28,20},{21,1},{... | collective-permute-start | bytes 602120 | tf_op jit(solution)/shard_map/ppermute | solution.py:284
  10.2 0.4 collective-permute-done.2.refs_1_.refs_2_
  10.5 1.5 %collective-permute-done.4.refs_7_ = bf16[784,128]{1,0:T(8,128)(2,1)S(1)} collective-permute-done((bf16[784,128]{1,0:T(8,128)(2,1)S(1)}, bf16[784,128]{1,0:T(8,128)(2,1)S(1)}, u32[]{:S(2)}, u32[]{:S(2)}) %collective-permute-start.4) | collective-permute-done | bytes 200736 | tf_op jit(solution)/shard_map/ppermute | solution.py:284
  12.0 1.5 %collective-permute-start.7 = (bf16[784,128]{1,0:T(8,128)(2,1)S(1)}, bf16[784,128]{1,0:T(8,128)(2,1)S(1)}, u32[]{:S(2)}, u32[]{:S(2)}) collective-permute-start(bf16[784,128]{1,0:T(8,128)(2,1)S(1)} %collective-permute-done.2.refs_1_.refs_2_), channel_id=1, source_target_pairs={{8,0},{24,8},{16,24},{4,16},{12,4},{28,12},{20,28},{0,20},{9,1},{2... | collective-permute-start | bytes 602120 | tf_op jit(solution)/shard_map/ppermute | solution.py:284
  13.6 2.6 %collective-permute-start.8 = (bf16[784,128]{1,0:T(8,128)(2,1)S(1)}, bf16[784,128]{1,0:T(8,128)(2,1)S(1)}, u32[]{:S(2)}, u32[]{:S(2)}) collective-permute-start(bf16[784,128]{1,0:T(8,128)(2,1)S(1)} %collective-permute-done.2.refs_1_.refs_2_), channel_id=1, source_target_pairs={{20,0},{0,8},{8,24},{24,16},{16,4},{4,12},{12,28},{28,20},{21,1},{... | collective-permute-start | bytes 602120 | tf_op jit(solution)/shard_map/ppermute | solution.py:284
  16.1 3.1 %collective-permute-done.refs_2_.refs_0_.refs_1_ = bf16[784,128]{1,0:T(8,128)(2,1)S(1)} collective-permute-done((bf16[784,128]{1,0:T(8,128)(2,1)S(1)}, bf16[784,128]{1,0:T(8,128)(2,1)S(1)}, u32[]{:S(2)}, u32[]{:S(2)}) %collective-permute-start) | collective-permute-done | bytes 200736 | tf_op jit(solution)/shard_map/ppermute | solution.py:290
  19.3 2.5 %collective-permute-start.1 = (bf16[784,128]{1,0:T(8,128)(2,1)S(1)}, bf16[784,128]{1,0:T(8,128)(2,1)S(1)}, u32[]{:S(2)}, u32[]{:S(2)}) collective-permute-start(bf16[784,128]{1,0:T(8,128)(2,1)S(1)} %get-tuple-element.25), channel_id=1, source_target_pairs={{0,3},{1,2},{2,1},{3,0},{4,7},{5,6},{6,5},{7,4},{8,11},{9,10},{10,... | collective-permute-start | bytes 602120 | tf_op jit(solution)/shard_map/ppermute | solution.py:290
  21.8 0.0 collective-permute-done.5.refs_10_.refs_4_
  21.8 0.1 collective-permute-start.10
  21.9 1.7 %collective-permute-start.6 = (bf16[1,784,128]{2,1,0:T(8,128)(2,1)S(1)}, bf16[1,784,128]{2,1,0:T(8,128)(2,1)S(1)}, u32[]{:S(2)}, u32[]{:S(2)}) collective-permute-start(bf16[1,784,128]{2,1,0:T(8,128)(2,1)S(1)} %shard_map.40), channel_id=1, source_target_pairs={{8,0},{24,8},{16,24},{4,16},{12,4},{28,12},{20,28},{0,20},{9,1},{2... | collective-permute-start | bytes 602120 | tf_op jit(solution)/shard_map/ppermute | solution.py:284
  23.6 4.6 %collective-permute-done.1.refs_3_.refs_0_ = bf16[784,128]{1,0:T(8,128)(2,1)S(1)} collective-permute-done((bf16[784,128]{1,0:T(8,128)(2,1)S(1)}, bf16[784,128]{1,0:T(8,128)(2,1)S(1)}, u32[]{:S(2)}, u32[]{:S(2)}) %collective-permute-start.1) | collective-permute-done | bytes 200736 | tf_op jit(solution)/shard_map/ppermute | solution.py:290
  28.2 0.1 shard_map.39
  28.2 0.1 collective-permute-start.3
  28.3 0.0 collective-permute-done.7.refs_6_
  28.3 0.0 collective-permute-done.8.refs_9_.refs_3_
  28.4 0.1 collective-permute-start.9
  28.4 1.7 %collective-permute-start.11 = (bf16[1,784,128]{2,1,0:T(8,128)(2,1)S(1)}, bf16[1,784,128]{2,1,0:T(8,128)(2,1)S(1)}, u32[]{:S(2)}, u32[]{:S(2)}) collective-permute-start(bf16[1,784,128]{2,1,0:T(8,128)(2,1)S(1)} %shard_map.41), channel_id=1, source_target_pairs={{8,0},{24,8},{16,24},{4,16},{12,4},{28,12},{20,28},{0,20},{9,1},{2... | collective-permute-start | bytes 602120 | tf_op jit(solution)/shard_map/ppermute | solution.py:284
  30.2 0.4 collective-permute-done.3.refs_4_
  30.6 1.6 %shard_map.42.refs_11_ = f32[4,8,512]{2,1,0:T(8,128)S(1)} custom-call(bf16[784,128]{1,0:T(8,128)(2,1)S(1)} %collective-permute-done.1.refs_3_.refs_0_, bf16[784,128]{1,0:T(8,128)(2,1)S(1)} %collective-permute-done.refs_2_.refs_0_.refs_1_, bf16[784,128]{1,0:T(8,128)(2,1)S(1)} %collective-permute-done.2.refs_1_.refs_2_, ...), custom_call_target="tpu_custom_call" | custom-call | flops 805306368 | bytes 1572864 | tf_op jit(solution)/shard_map/pallas_call | solution.py:212
  32.2 0.0 collective-permute-done.10.refs_8_.refs_2_
  32.2 0.0 collective-permute-done.6.refs_5_
  32.2 1.6 %shard_map.43.refs_9_ = f32[4,8,512]{2,1,0:T(8,128)S(1)} custom-call(bf16[784,128]{1,0:T(8,128)(2,1)S(1)} %collective-permute-done.1.refs_3_.refs_0_, bf16[784,128]{1,0:T(8,128)(2,1)S(1)} %collective-permute-done.refs_2_.refs_0_.refs_1_, bf16[784,128]{1,0:T(8,128)(2,1)S(1)} %collective-permute-done.2.refs_1_.refs_2_, ...), custom_call_target="tpu_custom_call" | custom-call | flops 830472192 | bytes 2752512 | tf_op jit(solution)/shard_map/pallas_call | solution.py:212
  33.8 1.3 %collective-permute-done.9.refs_8_.refs_1_ = bf16[1,784,128]{2,1,0:T(8,128)(2,1)S(1)} collective-permute-done((bf16[1,784,128]{2,1,0:T(8,128)(2,1)S(1)}, bf16[1,784,128]{2,1,0:T(8,128)(2,1)S(1)}, u32[]{:S(2)}, u32[]{:S(2)}) %collective-permute-start.9) | collective-permute-done | bytes 200736 | tf_op jit(solution)/shard_map/ppermute | solution.py:284
  35.1 1.0 %shard_map.44 = (f32[4,8,512]{2,1,0:T(8,128)S(1)}, f32[1,512]{1,0:T(1,128)S(1)}, f32[1,512]{1,0:T(1,128)S(1)}) custom-call(bf16[784,128]{1,0:T(8,128)(2,1)S(1)} %collective-permute-done.1.refs_3_.refs_0_, bf16[784,128]{1,0:T(8,128)(2,1)S(1)} %collective-permute-done.refs_2_.refs_0_.refs_1_, bf16[784,128]{1,0:T(8,128)(2,1)S(1)} %collective-permute-done.2.refs_1_.refs_2_, ...), custom_call_target="tpu_custom_call" | custom-call | flops 276824064 | bytes 2359296 | tf_op jit(solution)/shard_map/pallas_call | solution.py:212
  36.1 0.0 collective-permute-done.11.refs_0_
  36.1 1.1 %shard_map.45 = (f32[4,8,512]{2,1,0:T(8,128)}, f32[1,512]{1,0:T(1,128)S(1)}, f32[1,512]{1,0:T(1,128)S(1)}) custom-call(bf16[1,784,128]{2,1,0:T(8,128)(2,1)S(1)} %collective-permute-done.11.refs_0_, bf16[1,784,128]{2,1,0:T(8,128)(2,1)S(1)} %collective-permute-done.9.refs_8_.refs_1_, bf16[1,784,128]{2,1,0:T(8,128)(2,1)S(1)} %collective-permute-done.10.refs_8_.refs_2_, ...), custom_call_target="tpu_custom_call" | custom-call | flops 100663296 | bytes 983040 | tf_op jit(solution)/shard_map/pallas_call | solution.py:212
  37.3 10.8 %all_to_all.5.refs_0_ = f32[32,1,128]{2,1,0:T(1,128)S(1)} all-to-all(f32[32,1,128]{2,1,0:T(1,128)S(1)} %shard_map.46), channel_id=1, replica_groups={{31,30,29,28,27,26,25,24,23,22,21,20,19,18,17,16,15,14,13,12,11,10,9,8,..., dimensions={0} | all-to-all | bytes 32768 | tf_op jit(solution)/shard_map/all_to_all | solution.py:370
  48.0 0.8 %shard_map.47 = f32[1,512]{1,0:T(1,128)} custom-call(f32[32,1,128]{2,1,0:T(1,128)S(1)} %all_to_all.5.refs_0_, s32[1,512]{1,0:T(1,128)S(1)} %get-tuple-element.36.refs_1_), custom_call_target="tpu_custom_call" | custom-call | flops 262144 | bytes 2048 | tf_op jit(solution)/shard_map/pallas_call | solution.py:212
  (3 shorter events, 0.1 us)
Async XLA Ops:
  0.0 1.5 %copy-start = (s32[512,1]{0,1:T(1,128)S(1)}, s32[512,1]{0,1:T(1,128)}, u32[]{:S(2)}) copy-start(s32[512,1]{0,1:T(1,128)} %param.4) | copy-start | bytes 6148
  0.0 1.5 %copy-start.1 = (s32[512]{0:T(512)S(1)}, s32[512]{0:T(512)}, u32[]{:S(2)}) copy-start(s32[512]{0:T(512)} %param.5) | copy-start | bytes 6148
  2.5 8.1 %collective-permute-start.2 = (bf16[784,128]{1,0:T(8,128)(2,1)S(1)}, bf16[784,128]{1,0:T(8,128)(2,1)S(1)}, u32[]{:S(2)}, u32[]{:S(2)}) collective-permute-start(bf16[784,128]{1,0:T(8,128)(2,1)S(1)} %get-tuple-element.26), channel_id=1, source_target_pairs={{0,1},{1,0},{2,3},{3,2},{4,5},{5,4},{6,7},{7,6},{8,9},{9,8},{10,11... | collective-permute-start | bytes 602120 | tf_op jit(solution)/shard_map/ppermute | solution.py:290
  5.6 6.5 %collective-permute-start.4 = (bf16[784,128]{1,0:T(8,128)(2,1)S(1)}, bf16[784,128]{1,0:T(8,128)(2,1)S(1)}, u32[]{:S(2)}, u32[]{:S(2)}) collective-permute-start(bf16[784,128]{1,0:T(8,128)(2,1)S(1)} %get-tuple-element.27.refs_0_.refs_3_), channel_id=1, source_target_pairs={{8,0},{24,8},{16,24},{4,16},{12,4},{28,12},{20,28},{0,20},{9,1},{2... | collective-permute-start | bytes 602120 | tf_op jit(solution)/shard_map/ppermute | solution.py:284
  6.2 13.1 %collective-permute-start = (bf16[784,128]{1,0:T(8,128)(2,1)S(1)}, bf16[784,128]{1,0:T(8,128)(2,1)S(1)}, u32[]{:S(2)}, u32[]{:S(2)}) collective-permute-start(bf16[784,128]{1,0:T(8,128)(2,1)S(1)} %get-tuple-element.24), channel_id=1, source_target_pairs={{0,2},{1,3},{2,0},{3,1},{4,6},{5,7},{6,4},{7,5},{8,10},{9,11},{10,... | collective-permute-start | bytes 602120 | tf_op jit(solution)/shard_map/ppermute | solution.py:290
  8.8 13.0 %collective-permute-start.5 = (bf16[784,128]{1,0:T(8,128)(2,1)S(1)}, bf16[784,128]{1,0:T(8,128)(2,1)S(1)}, u32[]{:S(2)}, u32[]{:S(2)}) collective-permute-start(bf16[784,128]{1,0:T(8,128)(2,1)S(1)} %get-tuple-element.27.refs_0_.refs_3_), channel_id=1, source_target_pairs={{20,0},{0,8},{8,24},{24,16},{16,4},{4,12},{12,28},{28,20},{21,1},{... | collective-permute-start | bytes 602120 | tf_op jit(solution)/shard_map/ppermute | solution.py:284
  12.0 16.3 %collective-permute-start.7 = (bf16[784,128]{1,0:T(8,128)(2,1)S(1)}, bf16[784,128]{1,0:T(8,128)(2,1)S(1)}, u32[]{:S(2)}, u32[]{:S(2)}) collective-permute-start(bf16[784,128]{1,0:T(8,128)(2,1)S(1)} %collective-permute-done.2.refs_1_.refs_2_), channel_id=1, source_target_pairs={{8,0},{24,8},{16,24},{4,16},{12,4},{28,12},{20,28},{0,20},{9,1},{2... | collective-permute-start | bytes 602120 | tf_op jit(solution)/shard_map/ppermute | solution.py:284
  13.6 14.8 %collective-permute-start.8 = (bf16[784,128]{1,0:T(8,128)(2,1)S(1)}, bf16[784,128]{1,0:T(8,128)(2,1)S(1)}, u32[]{:S(2)}, u32[]{:S(2)}) collective-permute-start(bf16[784,128]{1,0:T(8,128)(2,1)S(1)} %collective-permute-done.2.refs_1_.refs_2_), channel_id=1, source_target_pairs={{20,0},{0,8},{8,24},{24,16},{16,4},{4,12},{12,28},{28,20},{21,1},{... | collective-permute-start | bytes 602120 | tf_op jit(solution)/shard_map/ppermute | solution.py:284
  19.3 8.9 %collective-permute-start.1 = (bf16[784,128]{1,0:T(8,128)(2,1)S(1)}, bf16[784,128]{1,0:T(8,128)(2,1)S(1)}, u32[]{:S(2)}, u32[]{:S(2)}) collective-permute-start(bf16[784,128]{1,0:T(8,128)(2,1)S(1)} %get-tuple-element.25), channel_id=1, source_target_pairs={{0,3},{1,2},{2,1},{3,0},{4,7},{5,6},{6,5},{7,4},{8,11},{9,10},{10,... | collective-permute-start | bytes 602120 | tf_op jit(solution)/shard_map/ppermute | solution.py:290
  21.8 10.4 %collective-permute-start.10 = (bf16[1,784,128]{2,1,0:T(8,128)(2,1)S(1)}, bf16[1,784,128]{2,1,0:T(8,128)(2,1)S(1)}, u32[]{:S(2)}, u32[]{:S(2)}) collective-permute-start(bf16[1,784,128]{2,1,0:T(8,128)(2,1)S(1)} %shard_map.40), channel_id=1, source_target_pairs={{20,0},{0,8},{8,24},{24,16},{16,4},{4,12},{12,28},{28,20},{21,1},{... | collective-permute-start | bytes 602120 | tf_op jit(solution)/shard_map/ppermute | solution.py:284
  21.9 10.3 %collective-permute-start.6 = (bf16[1,784,128]{2,1,0:T(8,128)(2,1)S(1)}, bf16[1,784,128]{2,1,0:T(8,128)(2,1)S(1)}, u32[]{:S(2)}, u32[]{:S(2)}) collective-permute-start(bf16[1,784,128]{2,1,0:T(8,128)(2,1)S(1)} %shard_map.40), channel_id=1, source_target_pairs={{8,0},{24,8},{16,24},{4,16},{12,4},{28,12},{20,28},{0,20},{9,1},{2... | collective-permute-start | bytes 602120 | tf_op jit(solution)/shard_map/ppermute | solution.py:284
  28.2 2.4 %collective-permute-start.3 = (bf16[4,784,128]{2,1,0:T(8,128)(2,1)S(1)}, bf16[4,784,128]{2,1,0:T(8,128)(2,1)S(1)}, u32[]{:S(2)}, u32[]{:S(2)}) collective-permute-start(bf16[4,784,128]{2,1,0:T(8,128)(2,1)S(1)} %shard_map.39), channel_id=1, source_target_pairs={{4,0},{12,8},{28,24},{20,16},{0,4},{8,12},{24,28},{16,20},{5,1},{1... | collective-permute-start | bytes 2408456 | tf_op jit(solution)/shard_map/ppermute | solution.py:284
  28.4 6.7 %collective-permute-start.9 = (bf16[1,784,128]{2,1,0:T(8,128)(2,1)S(1)}, bf16[1,784,128]{2,1,0:T(8,128)(2,1)S(1)}, u32[]{:S(2)}, u32[]{:S(2)}) collective-permute-start(bf16[1,784,128]{2,1,0:T(8,128)(2,1)S(1)} %shard_map.41), channel_id=1, source_target_pairs={{20,0},{0,8},{8,24},{24,16},{16,4},{4,12},{12,28},{28,20},{21,1},{... | collective-permute-start | bytes 602120 | tf_op jit(solution)/shard_map/ppermute | solution.py:284
  28.4 7.6 %collective-permute-start.11 = (bf16[1,784,128]{2,1,0:T(8,128)(2,1)S(1)}, bf16[1,784,128]{2,1,0:T(8,128)(2,1)S(1)}, u32[]{:S(2)}, u32[]{:S(2)}) collective-permute-start(bf16[1,784,128]{2,1,0:T(8,128)(2,1)S(1)} %shard_map.41), channel_id=1, source_target_pairs={{8,0},{24,8},{16,24},{4,16},{12,4},{28,12},{20,28},{0,20},{9,1},{2... | collective-permute-start | bytes 602120 | tf_op jit(solution)/shard_map/ppermute | solution.py:284

commit v13 on v11

--- a/solution.py
+++ b/solution.py
@@ -115,10 +115,14 @@
         refs[-1][k] = ref[...]
 
 
-def score_kernel(sources, tasks, done, *refs):
+def score_kernel(sources, tasks, done, last, *refs):
     *refs, flat_ref, side_ref, row_ref = refs
-    outs = 1 + len(done)
-    inputs, (best_ref, *out_refs) = refs[:-outs], refs[-outs:]
+    if last:
+        *refs, best_ref = refs
+        inputs, out_refs = refs[: -len(done)], refs[-len(done) :]
+    else:
+        outs = 1 + len(done)
+        inputs, (best_ref, *out_refs) = refs[:-outs], refs[-outs:]
     capacity = LANES
     low = jnp.float32(LOW)
     arrays = 1 + max(index for index, _ in sources.values())
@@ -237,7 +241,7 @@
     )[0]
 
 
-def score(held, tasks, acc, done, slots, width):
+def score(held, tasks, acc, done, last, slots, width):
     roles = len(held)
     used = sorted(
         {(left, k) for left, ks, _, _, _ in tasks for k in ks}
@@ -253,19 +257,21 @@
         sources[role, k] = (index, part)
     ends = [jax.ShapeDtypeStruct((1, slots), jnp.float32)] * len(done)
     tiles = sum(len(task[1]) * len(task[3]) for task in tasks)
-    best, *ends = call(
-        lambda *refs: score_kernel(sources, tasks, done, *refs),
-        [jax.ShapeDtypeStruct((roles, 8, slots), jnp.float32)] + ends,
-        [
+    best = [] if last else [jax.ShapeDtypeStruct((roles, 8, slots), jnp.float32)]
+    got = call(
+        lambda *refs: score_kernel(sources, tasks, done, last, *refs),
+        best + ends,
+        ([pltpu.VMEM((roles, 8, slots), jnp.float32)] if last else [])
+        + [
             pltpu.VMEM((roles, slots, width), jnp.bfloat16),
             pltpu.VMEM((roles, slots, LANES), jnp.float32),
             pltpu.VMEM((roles, slots, LANES), jnp.float32),
         ],
-        arrays + acc,
+        arrays + list(acc),
         2 * tiles * LANES * LANES * width,
         2 * len(used) * LANES * width,
     )
-    return [best], ends
+    return got[: len(best)], got[len(best) :]
 
 
 def per_device(embeddings, row_group, row_cluster):
@@ -346,7 +352,7 @@
                         if role in near:
                             step = max(step, 1 if ks is early else 3 if role == near[0] else 2)
                     task = (left, left_ks, right, right_ks, both)
-                    if both and right_ks is late:
+                    if both and right_ks is late and left_ks is early:
                         task = (right, right_ks, left, left_ks, both)
                     steps[step].append(task)
                     final[right] = max(final[right], step)
@@ -356,7 +362,8 @@
     for step, tasks in enumerate(steps):
         if tasks:
             done = [r for r in range(roles) if final[r] == step]
-            acc, ends = score(held, tasks, acc, done, slots, width)
+            last = not any(steps[step + 1 :])
+            acc, ends = score(held, tasks, acc, done, last, slots, width)
             for r, end in zip(done, ends):
                 partial[r] = end
     (best,) = call(

time: 47.9 us -> 47.2 us (0.985)
  Pallas kernels: 8.58 us -> 7.97 us
    pallas_call x11, Pallas kernels: 8.58 us -> 7.97 us  [call(): pl.pallas_call(kernel, out_shape=out_shape, in_specs=in_specs or in_vmem(...]
where the time goes in v13:
time: 47.2 us; the launch traced here: 47.1 us
  starting transfers between devices  18.3 us (39%)
  blocking collectives  12.6 us (27%)
  waiting for transfers between devices  8.05 us (17%)
  Pallas kernels  7.97 us (17%)
    all_to_all x1, blocking collectives, per_device(): lax.all_to_all(best, ('shard', 'group'), split_axis=0, concat_axis=0, til...  12.6 us
    ppermute x9, starting transfers between devices, from_offset(): return lax.ppermute(x, 'shard', perm)  10.2 us
    ppermute x3, starting transfers between devices, exchange(): got[k] = lax.ppermute(block, 'group', [(z, z ^ k) for z in range(groups)])  8.15 us
    pallas_call x11, Pallas kernels, call(): pl.pallas_call(kernel, out_shape=out_shape, in_specs=in_specs or in_vmem(...  7.97 us
    ppermute x9, waiting for transfers between devices, from_offset(): return lax.ppermute(x, 'shard', perm)  4.4 us
    ppermute x3, waiting for transfers between devices, exchange(): got[k] = lax.ppermute(block, 'group', [(z, z ^ k) for z in range(groups)])  3.65 us
  transfers between devices with their start and end apart: 12, of which 7 were waited for; matrix products, arithmetic and copies ran while one was open for 0% of the time, Pallas kernels for 9%

profile of v13, /device:TPU:0, one launch (start us, length us, event | category | flops | bytes accessed | tf_op | source)
XLA Modules:
  0.0 47.1 jit_solution(10509002409647877483)
XLA Ops:
  0.0 0.0 copy-start
  0.0 0.0 copy-start.1
  0.0 1.5 %shard_map.37.refs_0_ = bf16[512,768]{1,0:T(8,128)(2,1)S(1)} custom-call(bf16[512,768]{1,0:T(8,128)(2,1)} %far_ref.1), custom_call_target="tpu_custom_call" | custom-call | flops 1572864 | bytes 1572864 | tf_op jit(solution)/shard_map/pallas_call | solution.py:216
  1.5 0.0 copy-done
  1.5 0.0 copy-done.1
  1.5 0.9 %shard_map.38 = (bf16[784,128]{1,0:T(8,128)(2,1)S(1)}, bf16[784,128]{1,0:T(8,128)(2,1)S(1)}, bf16[784,128]{1,0:T(8,128)(2,1)S(1)}, bf16[784,128]{1,0:T(8,128)(2,1)S(1)}, s32[1,512]{1,0:T(1,128)S(1)}) custom-call(bf16[512,768]{1,0:T(8,128)(2,1)S(1)} %shard_map.37.refs_0_, s32[1,512]{1,0:T(1,128)S(1)} %bitcast.3, s32[1,512]{1,0:T(1,128)S(1)} %bitcast.4), custom_call_target="tpu_custom_call" | custom-call | flops 402653184 | bytes 1572864 | tf_op jit(solution)/shard_map/pallas_call | solution.py:216
  2.5 3.1 %collective-permute-start = (bf16[784,128]{1,0:T(8,128)(2,1)S(1)}, bf16[784,128]{1,0:T(8,128)(2,1)S(1)}, u32[]{:S(2)}, u32[]{:S(2)}) collective-permute-start(bf16[784,128]{1,0:T(8,128)(2,1)S(1)} %get-tuple-element.24), channel_id=1, source_target_pairs={{0,1},{1,0},{2,3},{3,2},{4,5},{5,4},{6,7},{7,6},{8,9},{9,8},{10,11... | collective-permute-start | bytes 602120 | tf_op jit(solution)/shard_map/ppermute | solution.py:296
  5.6 0.7 %collective-permute-start.4 = (bf16[784,128]{1,0:T(8,128)(2,1)S(1)}, bf16[784,128]{1,0:T(8,128)(2,1)S(1)}, u32[]{:S(2)}, u32[]{:S(2)}) collective-permute-start(bf16[784,128]{1,0:T(8,128)(2,1)S(1)} %get-tuple-element.27.refs_0_.refs_3_), channel_id=1, source_target_pairs={{8,0},{24,8},{16,24},{4,16},{12,4},{28,12},{20,28},{0,20},{9,1},{2... | collective-permute-start | bytes 602120 | tf_op jit(solution)/shard_map/ppermute | solution.py:290
  6.2 2.6 %collective-permute-start.2 = (bf16[784,128]{1,0:T(8,128)(2,1)S(1)}, bf16[784,128]{1,0:T(8,128)(2,1)S(1)}, u32[]{:S(2)}, u32[]{:S(2)}) collective-permute-start(bf16[784,128]{1,0:T(8,128)(2,1)S(1)} %get-tuple-element.26), channel_id=1, source_target_pairs={{0,2},{1,3},{2,0},{3,1},{4,6},{5,7},{6,4},{7,5},{8,10},{9,11},{10,... | collective-permute-start | bytes 602120 | tf_op jit(solution)/shard_map/ppermute | solution.py:296
  8.8 1.3 %collective-permute-start.5 = (bf16[784,128]{1,0:T(8,128)(2,1)S(1)}, bf16[784,128]{1,0:T(8,128)(2,1)S(1)}, u32[]{:S(2)}, u32[]{:S(2)}) collective-permute-start(bf16[784,128]{1,0:T(8,128)(2,1)S(1)} %get-tuple-element.27.refs_0_.refs_3_), channel_id=1, source_target_pairs={{20,0},{0,8},{8,24},{24,16},{16,4},{4,12},{12,28},{28,20},{21,1},{... | collective-permute-start | bytes 602120 | tf_op jit(solution)/shard_map/ppermute | solution.py:290
  10.2 0.4 collective-permute-done.refs_1_.refs_2_
  10.5 1.5 %collective-permute-done.4.refs_7_ = bf16[784,128]{1,0:T(8,128)(2,1)S(1)} collective-permute-done((bf16[784,128]{1,0:T(8,128)(2,1)S(1)}, bf16[784,128]{1,0:T(8,128)(2,1)S(1)}, u32[]{:S(2)}, u32[]{:S(2)}) %collective-permute-start.4) | collective-permute-done | bytes 200736 | tf_op jit(solution)/shard_map/ppermute | solution.py:290
  12.0 1.5 %collective-permute-start.7 = (bf16[784,128]{1,0:T(8,128)(2,1)S(1)}, bf16[784,128]{1,0:T(8,128)(2,1)S(1)}, u32[]{:S(2)}, u32[]{:S(2)}) collective-permute-start(bf16[784,128]{1,0:T(8,128)(2,1)S(1)} %collective-permute-done.refs_1_.refs_2_), channel_id=1, source_target_pairs={{8,0},{24,8},{16,24},{4,16},{12,4},{28,12},{20,28},{0,20},{9,1},{2... | collective-permute-start | bytes 602120 | tf_op jit(solution)/shard_map/ppermute | solution.py:290
  13.6 2.6 %collective-permute-start.8 = (bf16[784,128]{1,0:T(8,128)(2,1)S(1)}, bf16[784,128]{1,0:T(8,128)(2,1)S(1)}, u32[]{:S(2)}, u32[]{:S(2)}) collective-permute-start(bf16[784,128]{1,0:T(8,128)(2,1)S(1)} %collective-permute-done.refs_1_.refs_2_), channel_id=1, source_target_pairs={{20,0},{0,8},{8,24},{24,16},{16,4},{4,12},{12,28},{28,20},{21,1},{... | collective-permute-start | bytes 602120 | tf_op jit(solution)/shard_map/ppermute | solution.py:290
  16.1 2.5 %collective-permute-start.1 = (bf16[784,128]{1,0:T(8,128)(2,1)S(1)}, bf16[784,128]{1,0:T(8,128)(2,1)S(1)}, u32[]{:S(2)}, u32[]{:S(2)}) collective-permute-start(bf16[784,128]{1,0:T(8,128)(2,1)S(1)} %get-tuple-element.25), channel_id=1, source_target_pairs={{0,3},{1,2},{2,1},{3,0},{4,7},{5,6},{6,5},{7,4},{8,11},{9,10},{10,... | collective-permute-start | bytes 602120 | tf_op jit(solution)/shard_map/ppermute | solution.py:296
  18.6 0.7 %collective-permute-done.2.refs_2_.refs_0_.refs_1_ = bf16[784,128]{1,0:T(8,128)(2,1)S(1)} collective-permute-done((bf16[784,128]{1,0:T(8,128)(2,1)S(1)}, bf16[784,128]{1,0:T(8,128)(2,1)S(1)}, u32[]{:S(2)}, u32[]{:S(2)}) %collective-permute-start.2) | collective-permute-done | bytes 200736 | tf_op jit(solution)/shard_map/ppermute | solution.py:296
  19.3 0.0 collective-permute-done.5.refs_10_.refs_4_
  19.3 1.4 %collective-permute-start.10 = (bf16[1,784,128]{2,1,0:T(8,128)(2,1)S(1)}, bf16[1,784,128]{2,1,0:T(8,128)(2,1)S(1)}, u32[]{:S(2)}, u32[]{:S(2)}) collective-permute-start(bf16[1,784,128]{2,1,0:T(8,128)(2,1)S(1)} %shard_map.40), channel_id=1, source_target_pairs={{20,0},{0,8},{8,24},{24,16},{16,4},{4,12},{12,28},{28,20},{21,1},{... | collective-permute-start | bytes 602120 | tf_op jit(solution)/shard_map/ppermute | solution.py:290
  20.7 0.4 collective-permute-start.6
  21.1 2.6 %collective-permute-done.1.refs_3_.refs_0_ = bf16[784,128]{1,0:T(8,128)(2,1)S(1)} collective-permute-done((bf16[784,128]{1,0:T(8,128)(2,1)S(1)}, bf16[784,128]{1,0:T(8,128)(2,1)S(1)}, u32[]{:S(2)}, u32[]{:S(2)}) %collective-permute-start.1) | collective-permute-done | bytes 200736 | tf_op jit(solution)/shard_map/ppermute | solution.py:296
  23.7 0.1 shard_map.39
  23.8 0.1 collective-permute-start.3
  23.9 0.0 collective-permute-done.7.refs_6_
  23.9 0.0 collective-permute-done.8.refs_9_.refs_3_
  23.9 2.1 %collective-permute-start.9 = (bf16[1,784,128]{2,1,0:T(8,128)(2,1)S(1)}, bf16[1,784,128]{2,1,0:T(8,128)(2,1)S(1)}, u32[]{:S(2)}, u32[]{:S(2)}) collective-permute-start(bf16[1,784,128]{2,1,0:T(8,128)(2,1)S(1)} %shard_map.41), channel_id=1, source_target_pairs={{20,0},{0,8},{8,24},{24,16},{16,4},{4,12},{12,28},{28,20},{21,1},{... | collective-permute-start | bytes 602120 | tf_op jit(solution)/shard_map/ppermute | solution.py:290
  26.0 0.0 collective-permute-start.11
  26.0 0.1 collective-permute-done.3.refs_4_
  26.2 1.6 %shard_map.42.refs_11_ = f32[4,8,512]{2,1,0:T(8,128)S(1)} custom-call(bf16[784,128]{1,0:T(8,128)(2,1)S(1)} %collective-permute-done.1.refs_3_.refs_0_, bf16[784,128]{1,0:T(8,128)(2,1)S(1)} %collective-permute-done.2.refs_2_.refs_0_.refs_1_, bf16[784,128]{1,0:T(8,128)(2,1)S(1)} %collective-permute-done.refs_1_.refs_2_, ...), custom_call_target="tpu_custom_call" | custom-call | flops 805306368 | bytes 1572864 | tf_op jit(solution)/shard_map/pallas_call | solution.py:216
  27.7 0.0 collective-permute-done.10.refs_8_.refs_2_
  27.7 0.0 collective-permute-done.6.refs_5_
  27.7 1.6 %shard_map.43.refs_9_ = f32[4,8,512]{2,1,0:T(8,128)S(1)} custom-call(bf16[784,128]{1,0:T(8,128)(2,1)S(1)} %collective-permute-done.1.refs_3_.refs_0_, bf16[784,128]{1,0:T(8,128)(2,1)S(1)} %collective-permute-done.2.refs_2_.refs_0_.refs_1_, bf16[784,128]{1,0:T(8,128)(2,1)S(1)} %collective-permute-done.refs_1_.refs_2_, ...), custom_call_target="tpu_custom_call" | custom-call | flops 830472192 | bytes 2752512 | tf_op jit(solution)/shard_map/pallas_call | solution.py:216
  29.3 1.6 %collective-permute-done.9.refs_8_.refs_1_ = bf16[1,784,128]{2,1,0:T(8,128)(2,1)S(1)} collective-permute-done((bf16[1,784,128]{2,1,0:T(8,128)(2,1)S(1)}, bf16[1,784,128]{2,1,0:T(8,128)(2,1)S(1)}, u32[]{:S(2)}, u32[]{:S(2)}) %collective-permute-start.9) | collective-permute-done | bytes 200736 | tf_op jit(solution)/shard_map/ppermute | solution.py:290
  30.9 1.0 %shard_map.44 = (f32[4,8,512]{2,1,0:T(8,128)S(1)}, f32[1,512]{1,0:T(1,128)S(1)}, f32[1,512]{1,0:T(1,128)S(1)}) custom-call(bf16[784,128]{1,0:T(8,128)(2,1)S(1)} %collective-permute-done.1.refs_3_.refs_0_, bf16[784,128]{1,0:T(8,128)(2,1)S(1)} %collective-permute-done.2.refs_2_.refs_0_.refs_1_, bf16[784,128]{1,0:T(8,128)(2,1)S(1)} %collective-permute-done.refs_1_.refs_2_, ...), custom_call_target="tpu_custom_call" | custom-call | flops 276824064 | bytes 2359296 | tf_op jit(solution)/shard_map/pallas_call | solution.py:216
  31.9 1.2 %collective-permute-done.11.refs_0_ = bf16[1,784,128]{2,1,0:T(8,128)(2,1)S(1)} collective-permute-done((bf16[1,784,128]{2,1,0:T(8,128)(2,1)S(1)}, bf16[1,784,128]{2,1,0:T(8,128)(2,1)S(1)}, u32[]{:S(2)}, u32[]{:S(2)}) %collective-permute-start.11) | collective-permute-done | bytes 200736 | tf_op jit(solution)/shard_map/ppermute | solution.py:290
  33.1 0.5 %shard_map.45 = (f32[1,512]{1,0:T(1,128)S(1)}, f32[1,512]{1,0:T(1,128)S(1)}) custom-call(bf16[1,784,128]{2,1,0:T(8,128)(2,1)S(1)} %collective-permute-done.11.refs_0_, bf16[1,784,128]{2,1,0:T(8,128)(2,1)S(1)} %collective-permute-done.9.refs_8_.refs_1_, bf16[1,784,128]{2,1,0:T(8,128)(2,1)S(1)} %collective-permute-done.10.refs_8_.refs_2_, ...), custom_call_target="tpu_custom_call" | custom-call | flops 100663296 | bytes 983040 | tf_op jit(solution)/shard_map/pallas_call | solution.py:216
  33.6 0.1 shard_map.46
  33.7 12.6 %all_to_all.5.refs_0_ = f32[32,1,128]{2,1,0:T(1,128)S(1)} all-to-all(f32[32,1,128]{2,1,0:T(1,128)S(1)} %shard_map.46), channel_id=1, replica_groups=mesh['shard'=8,'group'=4] {'shard','group'}, dimensions={0} | all-to-all | bytes 32768 | tf_op jit(solution)/shard_map/all_to_all | solution.py:377
  46.3 0.8 %shard_map.47 = f32[1,512]{1,0:T(1,128)} custom-call(f32[32,1,128]{2,1,0:T(1,128)S(1)} %all_to_all.5.refs_0_, s32[1,512]{1,0:T(1,128)S(1)} %get-tuple-element.36.refs_1_), custom_call_target="tpu_custom_call" | custom-call | flops 262144 | bytes 2048 | tf_op jit(solution)/shard_map/pallas_call | solution.py:216
  (2 shorter events, 0.0 us)
Async XLA Ops:
  0.0 1.5 %copy-start = (s32[512,1]{0,1:T(1,128)S(1)}, s32[512,1]{0,1:T(1,128)}, u32[]{:S(2)}) copy-start(s32[512,1]{0,1:T(1,128)} %param.4) | copy-start | bytes 6148
  0.0 1.5 %copy-start.1 = (s32[512]{0:T(512)S(1)}, s32[512]{0:T(512)}, u32[]{:S(2)}) copy-start(s32[512]{0:T(512)} %param.5) | copy-start | bytes 6148
  2.5 8.1 %collective-permute-start = (bf16[784,128]{1,0:T(8,128)(2,1)S(1)}, bf16[784,128]{1,0:T(8,128)(2,1)S(1)}, u32[]{:S(2)}, u32[]{:S(2)}) collective-permute-start(bf16[784,128]{1,0:T(8,128)(2,1)S(1)} %get-tuple-element.24), channel_id=1, source_target_pairs={{0,1},{1,0},{2,3},{3,2},{4,5},{5,4},{6,7},{7,6},{8,9},{9,8},{10,11... | collective-permute-start | bytes 602120 | tf_op jit(solution)/shard_map/ppermute | solution.py:296
  5.6 6.5 %collective-permute-start.4 = (bf16[784,128]{1,0:T(8,128)(2,1)S(1)}, bf16[784,128]{1,0:T(8,128)(2,1)S(1)}, u32[]{:S(2)}, u32[]{:S(2)}) collective-permute-start(bf16[784,128]{1,0:T(8,128)(2,1)S(1)} %get-tuple-element.27.refs_0_.refs_3_), channel_id=1, source_target_pairs={{8,0},{24,8},{16,24},{4,16},{12,4},{28,12},{20,28},{0,20},{9,1},{2... | collective-permute-start | bytes 602120 | tf_op jit(solution)/shard_map/ppermute | solution.py:290
  6.2 13.1 %collective-permute-start.2 = (bf16[784,128]{1,0:T(8,128)(2,1)S(1)}, bf16[784,128]{1,0:T(8,128)(2,1)S(1)}, u32[]{:S(2)}, u32[]{:S(2)}) collective-permute-start(bf16[784,128]{1,0:T(8,128)(2,1)S(1)} %get-tuple-element.26), channel_id=1, source_target_pairs={{0,2},{1,3},{2,0},{3,1},{4,6},{5,7},{6,4},{7,5},{8,10},{9,11},{10,... | collective-permute-start | bytes 602120 | tf_op jit(solution)/shard_map/ppermute | solution.py:296
  8.8 10.5 %collective-permute-start.5 = (bf16[784,128]{1,0:T(8,128)(2,1)S(1)}, bf16[784,128]{1,0:T(8,128)(2,1)S(1)}, u32[]{:S(2)}, u32[]{:S(2)}) collective-permute-start(bf16[784,128]{1,0:T(8,128)(2,1)S(1)} %get-tuple-element.27.refs_0_.refs_3_), channel_id=1, source_target_pairs={{20,0},{0,8},{8,24},{24,16},{16,4},{4,12},{12,28},{28,20},{21,1},{... | collective-permute-start | bytes 602120 | tf_op jit(solution)/shard_map/ppermute | solution.py:290
  12.0 11.9 %collective-permute-start.7 = (bf16[784,128]{1,0:T(8,128)(2,1)S(1)}, bf16[784,128]{1,0:T(8,128)(2,1)S(1)}, u32[]{:S(2)}, u32[]{:S(2)}) collective-permute-start(bf16[784,128]{1,0:T(8,128)(2,1)S(1)} %collective-permute-done.refs_1_.refs_2_), channel_id=1, source_target_pairs={{8,0},{24,8},{16,24},{4,16},{12,4},{28,12},{20,28},{0,20},{9,1},{2... | collective-permute-start | bytes 602120 | tf_op jit(solution)/shard_map/ppermute | solution.py:290
  13.6 10.3 %collective-permute-start.8 = (bf16[784,128]{1,0:T(8,128)(2,1)S(1)}, bf16[784,128]{1,0:T(8,128)(2,1)S(1)}, u32[]{:S(2)}, u32[]{:S(2)}) collective-permute-start(bf16[784,128]{1,0:T(8,128)(2,1)S(1)} %collective-permute-done.refs_1_.refs_2_), channel_id=1, source_target_pairs={{20,0},{0,8},{8,24},{24,16},{16,4},{4,12},{12,28},{28,20},{21,1},{... | collective-permute-start | bytes 602120 | tf_op jit(solution)/shard_map/ppermute | solution.py:290
  16.1 7.6 %collective-permute-start.1 = (bf16[784,128]{1,0:T(8,128)(2,1)S(1)}, bf16[784,128]{1,0:T(8,128)(2,1)S(1)}, u32[]{:S(2)}, u32[]{:S(2)}) collective-permute-start(bf16[784,128]{1,0:T(8,128)(2,1)S(1)} %get-tuple-element.25), channel_id=1, source_target_pairs={{0,3},{1,2},{2,1},{3,0},{4,7},{5,6},{6,5},{7,4},{8,11},{9,10},{10,... | collective-permute-start | bytes 602120 | tf_op jit(solution)/shard_map/ppermute | solution.py:296
  19.3 8.4 %collective-permute-start.10 = (bf16[1,784,128]{2,1,0:T(8,128)(2,1)S(1)}, bf16[1,784,128]{2,1,0:T(8,128)(2,1)S(1)}, u32[]{:S(2)}, u32[]{:S(2)}) collective-permute-start(bf16[1,784,128]{2,1,0:T(8,128)(2,1)S(1)} %shard_map.40), channel_id=1, source_target_pairs={{20,0},{0,8},{8,24},{24,16},{16,4},{4,12},{12,28},{28,20},{21,1},{... | collective-permute-start | bytes 602120 | tf_op jit(solution)/shard_map/ppermute | solution.py:290
  20.7 7.0 %collective-permute-start.6 = (bf16[1,784,128]{2,1,0:T(8,128)(2,1)S(1)}, bf16[1,784,128]{2,1,0:T(8,128)(2,1)S(1)}, u32[]{:S(2)}, u32[]{:S(2)}) collective-permute-start(bf16[1,784,128]{2,1,0:T(8,128)(2,1)S(1)} %shard_map.40), channel_id=1, source_target_pairs={{8,0},{24,8},{16,24},{4,16},{12,4},{28,12},{20,28},{0,20},{9,1},{2... | collective-permute-start | bytes 602120 | tf_op jit(solution)/shard_map/ppermute | solution.py:290
  23.8 2.4 %collective-permute-start.3 = (bf16[4,784,128]{2,1,0:T(8,128)(2,1)S(1)}, bf16[4,784,128]{2,1,0:T(8,128)(2,1)S(1)}, u32[]{:S(2)}, u32[]{:S(2)}) collective-permute-start(bf16[4,784,128]{2,1,0:T(8,128)(2,1)S(1)} %shard_map.39), channel_id=1, source_target_pairs={{4,0},{12,8},{28,24},{20,16},{0,4},{8,12},{24,28},{16,20},{5,1},{1... | collective-permute-start | bytes 2408456 | tf_op jit(solution)/shard_map/ppermute | solution.py:290
  23.9 7.0 %collective-permute-start.9 = (bf16[1,784,128]{2,1,0:T(8,128)(2,1)S(1)}, bf16[1,784,128]{2,1,0:T(8,128)(2,1)S(1)}, u32[]{:S(2)}, u32[]{:S(2)}) collective-permute-start(bf16[1,784,128]{2,1,0:T(8,128)(2,1)S(1)} %shard_map.41), channel_id=1, source_target_pairs={{20,0},{0,8},{8,24},{24,16},{16,4},{4,12},{12,28},{28,20},{21,1},{... | collective-permute-start | bytes 602120 | tf_op jit(solution)/shard_map/ppermute | solution.py:290
  26.0 7.1 %collective-permute-start.11 = (bf16[1,784,128]{2,1,0:T(8,128)(2,1)S(1)}, bf16[1,784,128]{2,1,0:T(8,128)(2,1)S(1)}, u32[]{:S(2)}, u32[]{:S(2)}) collective-permute-start(bf16[1,784,128]{2,1,0:T(8,128)(2,1)S(1)} %shard_map.41), channel_id=1, source_target_pairs={{8,0},{24,8},{16,24},{4,16},{12,4},{28,12},{20,28},{0,20},{9,1},{2... | collective-permute-start | bytes 602120 | tf_op jit(solution)/shard_map/ppermute | solution.py:290

commit v14 on v13

--- a/solution.py
+++ b/solution.py
@@ -292,7 +292,7 @@
     def exchange(blocks):
         got = list(blocks)
         for k in range(1, groups):
-            block = after(blocks[k], got[1]) if k > 2 else blocks[k]
+            block = after(blocks[k], got[2]) if k > 2 else blocks[k]
             got[k] = lax.ppermute(block, "group", [(z, z ^ k) for z in range(groups)])
         return got
 
@@ -333,7 +333,7 @@
             block = after(own[k], first[near[0]]) if near else own[k]
         else:
             passed = [held[r][k - 2][0] for r in near]
-            block = stack([after(own[k], *passed)], WAIT)
+            block = stack([after(own[k], *passed)], WAIT if k in late else WAIT // 20)
         for r in near:
             held[r][k] = (from_offset(block, offsets[r]), 0 if k > 1 else None)
     got = {r: from_offset(stack(own, 0), offsets[r]) for r in far}

time: 47.2 us -> 47.5 us (level)
  waiting for transfers between devices: 8.05 us -> 12.3 us
  blocking collectives: 12.6 us -> 9.84 us
  starting transfers between devices: 18.3 us -> 17.1 us
    ppermute x3, waiting for transfers between devices: 3.65 us -> 7.21 us  [exchange(): got[k] = lax.ppermute(block, 'group', [(z, z ^ k) for z in range(groups)])]
    all_to_all x1, blocking collectives: 12.6 us -> 9.84 us  [per_device(): lax.all_to_all(best, ('shard', 'group'), split_axis=0, concat_axis=0, til...]
    ppermute x9, starting transfers between devices: 10.2 us -> 7.99 us  [from_offset(): return lax.ppermute(x, 'shard', perm)]
    ppermute x3, starting transfers between devices: 8.15 us -> 9.11 us  [exchange(): got[k] = lax.ppermute(block, 'group', [(z, z ^ k) for z in range(groups)])]
    ppermute x9, waiting for transfers between devices: 4.4 us -> 5.13 us  [from_offset(): return lax.ppermute(x, 'shard', perm)]
  transfers between devices with their start and end apart: 12 -> 12, of which waited for: 7 -> 4; matrix products, arithmetic and copies ran while one was open for 0% -> 0% of each run, Pallas kernels for 9% -> 9%
where the time goes in v14:
time: 47.5 us; the launch traced here: 47.4 us
  starting transfers between devices  17.1 us (36%)
  waiting for transfers between devices  12.3 us (26%)
  blocking collectives  9.84 us (21%)
  Pallas kernels  7.98 us (17%)
    all_to_all x1, blocking collectives, per_device(): lax.all_to_all(best, ('shard', 'group'), split_axis=0, concat_axis=0, til...  9.84 us
    ppermute x3, starting transfers between devices, exchange(): got[k] = lax.ppermute(block, 'group', [(z, z ^ k) for z in range(groups)])  9.11 us
    ppermute x9, starting transfers between devices, from_offset(): return lax.ppermute(x, 'shard', perm)  7.99 us
    pallas_call x11, Pallas kernels, call(): pl.pallas_call(kernel, out_shape=out_shape, in_specs=in_specs or in_vmem(...  7.98 us
    ppermute x3, waiting for transfers between devices, exchange(): got[k] = lax.ppermute(block, 'group', [(z, z ^ k) for z in range(groups)])  7.21 us
    ppermute x9, waiting for transfers between devices, from_offset(): return lax.ppermute(x, 'shard', perm)  5.13 us
  transfers between devices with their start and end apart: 12, of which 4 were waited for; matrix products, arithmetic and copies ran while one was open for 0% of the time, Pallas kernels for 9%

profile of v14, /device:TPU:0, one launch (start us, length us, event | category | flops | bytes accessed | tf_op | source)
XLA Modules:
  0.0 47.4 jit_solution(9856724655628075866)
XLA Ops:
  0.0 0.0 copy-start
  0.0 0.0 copy-start.1
  0.0 1.5 %shard_map.37.refs_0_ = bf16[512,768]{1,0:T(8,128)(2,1)S(1)} custom-call(bf16[512,768]{1,0:T(8,128)(2,1)} %far_ref.1), custom_call_target="tpu_custom_call" | custom-call | flops 1572864 | bytes 1572864 | tf_op jit(solution)/shard_map/pallas_call | solution.py:216
  1.5 0.0 copy-done
  1.5 0.0 copy-done.1
  1.5 0.9 %shard_map.38 = (bf16[784,128]{1,0:T(8,128)(2,1)S(1)}, bf16[784,128]{1,0:T(8,128)(2,1)S(1)}, bf16[784,128]{1,0:T(8,128)(2,1)S(1)}, bf16[784,128]{1,0:T(8,128)(2,1)S(1)}, s32[1,512]{1,0:T(1,128)S(1)}) custom-call(bf16[512,768]{1,0:T(8,128)(2,1)S(1)} %shard_map.37.refs_0_, s32[1,512]{1,0:T(1,128)S(1)} %bitcast.3, s32[1,512]{1,0:T(1,128)S(1)} %bitcast.4), custom_call_target="tpu_custom_call" | custom-call | flops 402653184 | bytes 1572864 | tf_op jit(solution)/shard_map/pallas_call | solution.py:216
  2.5 4.1 %collective-permute-start = (bf16[784,128]{1,0:T(8,128)(2,1)S(1)}, bf16[784,128]{1,0:T(8,128)(2,1)S(1)}, u32[]{:S(2)}, u32[]{:S(2)}) collective-permute-start(bf16[784,128]{1,0:T(8,128)(2,1)S(1)} %get-tuple-element.24), channel_id=1, source_target_pairs={{0,2},{1,3},{2,0},{3,1},{4,6},{5,7},{6,4},{7,5},{8,10},{9,11},{10,... | collective-permute-start | bytes 602120 | tf_op jit(solution)/shard_map/ppermute | solution.py:296
  6.6 1.6 %collective-permute-start.2 = (bf16[784,128]{1,0:T(8,128)(2,1)S(1)}, bf16[784,128]{1,0:T(8,128)(2,1)S(1)}, u32[]{:S(2)}, u32[]{:S(2)}) collective-permute-start(bf16[784,128]{1,0:T(8,128)(2,1)S(1)} %get-tuple-element.26), channel_id=1, source_target_pairs={{0,1},{1,0},{2,3},{3,2},{4,5},{5,4},{6,7},{7,6},{8,9},{9,8},{10,11... | collective-permute-start | bytes 602120 | tf_op jit(solution)/shard_map/ppermute | solution.py:296
  8.1 0.4 collective-permute-start.4
  8.5 1.6 %collective-permute-start.5 = (bf16[784,128]{1,0:T(8,128)(2,1)S(1)}, bf16[784,128]{1,0:T(8,128)(2,1)S(1)}, u32[]{:S(2)}, u32[]{:S(2)}) collective-permute-start(bf16[784,128]{1,0:T(8,128)(2,1)S(1)} %get-tuple-element.27.refs_0_.refs_3_), channel_id=1, source_target_pairs={{20,0},{0,8},{8,24},{24,16},{16,4},{4,12},{12,28},{28,20},{21,1},{... | collective-permute-start | bytes 602120 | tf_op jit(solution)/shard_map/ppermute | solution.py:290
  10.2 5.8 %collective-permute-done.refs_2_.refs_0_.refs_1_ = bf16[784,128]{1,0:T(8,128)(2,1)S(1)} collective-permute-done((bf16[784,128]{1,0:T(8,128)(2,1)S(1)}, bf16[784,128]{1,0:T(8,128)(2,1)S(1)}, u32[]{:S(2)}, u32[]{:S(2)}) %collective-permute-start) | collective-permute-done | bytes 200736 | tf_op jit(solution)/shard_map/ppermute | solution.py:296
  16.0 3.4 %collective-permute-start.1 = (bf16[784,128]{1,0:T(8,128)(2,1)S(1)}, bf16[784,128]{1,0:T(8,128)(2,1)S(1)}, u32[]{:S(2)}, u32[]{:S(2)}) collective-permute-start(bf16[784,128]{1,0:T(8,128)(2,1)S(1)} %get-tuple-element.25), channel_id=1, source_target_pairs={{0,3},{1,2},{2,1},{3,0},{4,7},{5,6},{6,5},{7,4},{8,11},{9,10},{10,... | collective-permute-start | bytes 602120 | tf_op jit(solution)/shard_map/ppermute | solution.py:296
  19.4 0.0 collective-permute-done.2.refs_1_.refs_2_
  19.4 0.0 collective-permute-done.4.refs_7_
  19.4 0.9 %collective-permute-start.7 = (bf16[784,128]{1,0:T(8,128)(2,1)S(1)}, bf16[784,128]{1,0:T(8,128)(2,1)S(1)}, u32[]{:S(2)}, u32[]{:S(2)}) collective-permute-start(bf16[784,128]{1,0:T(8,128)(2,1)S(1)} %collective-permute-done.2.refs_1_.refs_2_), channel_id=1, source_target_pairs={{8,0},{24,8},{16,24},{4,16},{12,4},{28,12},{20,28},{0,20},{9,1},{2... | collective-permute-start | bytes 602120 | tf_op jit(solution)/shard_map/ppermute | solution.py:290
  20.3 1.2 %collective-permute-start.8 = (bf16[784,128]{1,0:T(8,128)(2,1)S(1)}, bf16[784,128]{1,0:T(8,128)(2,1)S(1)}, u32[]{:S(2)}, u32[]{:S(2)}) collective-permute-start(bf16[784,128]{1,0:T(8,128)(2,1)S(1)} %collective-permute-done.2.refs_1_.refs_2_), channel_id=1, source_target_pairs={{20,0},{0,8},{8,24},{24,16},{16,4},{4,12},{12,28},{28,20},{21,1},{... | collective-permute-start | bytes 602120 | tf_op jit(solution)/shard_map/ppermute | solution.py:290
  21.4 0.0 collective-permute-done.5.refs_10_.refs_4_
  21.5 1.6 %collective-permute-start.10 = (bf16[1,784,128]{2,1,0:T(8,128)(2,1)S(1)}, bf16[1,784,128]{2,1,0:T(8,128)(2,1)S(1)}, u32[]{:S(2)}, u32[]{:S(2)}) collective-permute-start(bf16[1,784,128]{2,1,0:T(8,128)(2,1)S(1)} %shard_map.40), channel_id=1, source_target_pairs={{20,0},{0,8},{8,24},{24,16},{16,4},{4,12},{12,28},{28,20},{21,1},{... | collective-permute-start | bytes 602120 | tf_op jit(solution)/shard_map/ppermute | solution.py:290
  23.0 0.3 collective-permute-start.6
  23.3 1.4 %collective-permute-done.1.refs_3_.refs_0_ = bf16[784,128]{1,0:T(8,128)(2,1)S(1)} collective-permute-done((bf16[784,128]{1,0:T(8,128)(2,1)S(1)}, bf16[784,128]{1,0:T(8,128)(2,1)S(1)}, u32[]{:S(2)}, u32[]{:S(2)}) %collective-permute-start.1) | collective-permute-done | bytes 200736 | tf_op jit(solution)/shard_map/ppermute | solution.py:296
  24.7 0.1 shard_map.39
  24.7 0.1 collective-permute-start.3
  24.8 2.5 %collective-permute-done.7.refs_6_ = bf16[784,128]{1,0:T(8,128)(2,1)S(1)} collective-permute-done((bf16[784,128]{1,0:T(8,128)(2,1)S(1)}, bf16[784,128]{1,0:T(8,128)(2,1)S(1)}, u32[]{:S(2)}, u32[]{:S(2)}) %collective-permute-start.7) | collective-permute-done | bytes 200736 | tf_op jit(solution)/shard_map/ppermute | solution.py:290
  27.3 0.0 collective-permute-done.8.refs_9_.refs_3_
  27.3 2.1 %collective-permute-start.9 = (bf16[1,784,128]{2,1,0:T(8,128)(2,1)S(1)}, bf16[1,784,128]{2,1,0:T(8,128)(2,1)S(1)}, u32[]{:S(2)}, u32[]{:S(2)}) collective-permute-start(bf16[1,784,128]{2,1,0:T(8,128)(2,1)S(1)} %shard_map.41), channel_id=1, source_target_pairs={{20,0},{0,8},{8,24},{24,16},{16,4},{4,12},{12,28},{28,20},{21,1},{... | collective-permute-start | bytes 602120 | tf_op jit(solution)/shard_map/ppermute | solution.py:290
  29.4 0.0 collective-permute-start.11
  29.4 0.0 collective-permute-done.3.refs_4_
  29.4 1.6 %shard_map.42.refs_11_ = f32[4,8,512]{2,1,0:T(8,128)S(1)} custom-call(bf16[784,128]{1,0:T(8,128)(2,1)S(1)} %collective-permute-done.1.refs_3_.refs_0_, bf16[784,128]{1,0:T(8,128)(2,1)S(1)} %collective-permute-done.refs_2_.refs_0_.refs_1_, bf16[784,128]{1,0:T(8,128)(2,1)S(1)} %collective-permute-done.2.refs_1_.refs_2_, ...), custom_call_target="tpu_custom_call" | custom-call | flops 805306368 | bytes 1572864 | tf_op jit(solution)/shard_map/pallas_call | solution.py:216
  31.0 0.0 collective-permute-done.10.refs_8_.refs_2_
  31.0 0.0 collective-permute-done.6.refs_5_
  31.0 1.6 %shard_map.43.refs_9_ = f32[4,8,512]{2,1,0:T(8,128)S(1)} custom-call(bf16[784,128]{1,0:T(8,128)(2,1)S(1)} %collective-permute-done.1.refs_3_.refs_0_, bf16[784,128]{1,0:T(8,128)(2,1)S(1)} %collective-permute-done.refs_2_.refs_0_.refs_1_, bf16[784,128]{1,0:T(8,128)(2,1)S(1)} %collective-permute-done.2.refs_1_.refs_2_, ...), custom_call_target="tpu_custom_call" | custom-call | flops 830472192 | bytes 2752512 | tf_op jit(solution)/shard_map/pallas_call | solution.py:216
  32.6 2.6 %collective-permute-done.9.refs_8_.refs_1_ = bf16[1,784,128]{2,1,0:T(8,128)(2,1)S(1)} collective-permute-done((bf16[1,784,128]{2,1,0:T(8,128)(2,1)S(1)}, bf16[1,784,128]{2,1,0:T(8,128)(2,1)S(1)}, u32[]{:S(2)}, u32[]{:S(2)}) %collective-permute-start.9) | collective-permute-done | bytes 200736 | tf_op jit(solution)/shard_map/ppermute | solution.py:290
  35.2 1.0 %shard_map.44 = (f32[4,8,512]{2,1,0:T(8,128)S(1)}, f32[1,512]{1,0:T(1,128)S(1)}, f32[1,512]{1,0:T(1,128)S(1)}) custom-call(bf16[784,128]{1,0:T(8,128)(2,1)S(1)} %collective-permute-done.1.refs_3_.refs_0_, bf16[784,128]{1,0:T(8,128)(2,1)S(1)} %collective-permute-done.refs_2_.refs_0_.refs_1_, bf16[784,128]{1,0:T(8,128)(2,1)S(1)} %collective-permute-done.2.refs_1_.refs_2_, ...), custom_call_target="tpu_custom_call" | custom-call | flops 276824064 | bytes 2359296 | tf_op jit(solution)/shard_map/pallas_call | solution.py:216
  36.2 0.0 collective-permute-done.11.refs_0_
  36.2 0.5 %shard_map.45 = (f32[1,512]{1,0:T(1,128)S(1)}, f32[1,512]{1,0:T(1,128)S(1)}) custom-call(bf16[1,784,128]{2,1,0:T(8,128)(2,1)S(1)} %collective-permute-done.11.refs_0_, bf16[1,784,128]{2,1,0:T(8,128)(2,1)S(1)} %collective-permute-done.9.refs_8_.refs_1_, bf16[1,784,128]{2,1,0:T(8,128)(2,1)S(1)} %collective-permute-done.10.refs_8_.refs_2_, ...), custom_call_target="tpu_custom_call" | custom-call | flops 100663296 | bytes 983040 | tf_op jit(solution)/shard_map/pallas_call | solution.py:216
  36.7 0.1 shard_map.46
  36.8 9.8 %all_to_all.5.refs_0_ = f32[32,1,128]{2,1,0:T(1,128)S(1)} all-to-all(f32[32,1,128]{2,1,0:T(1,128)S(1)} %shard_map.46), channel_id=1, replica_groups=mesh['shard'=8,'group'=4] {'shard','group'}, dimensions={0} | all-to-all | bytes 32768 | tf_op jit(solution)/shard_map/all_to_all | solution.py:377
  46.6 0.8 %shard_map.47 = f32[1,512]{1,0:T(1,128)} custom-call(f32[32,1,128]{2,1,0:T(1,128)S(1)} %all_to_all.5.refs_0_, s32[1,512]{1,0:T(1,128)S(1)} %get-tuple-element.36.refs_1_), custom_call_target="tpu_custom_call" | custom-call | flops 262144 | bytes 2048 | tf_op jit(solution)/shard_map/pallas_call | solution.py:216
  (2 shorter events, 0.0 us)
Async XLA Ops:
  0.0 1.5 %copy-start = (s32[512,1]{0,1:T(1,128)S(1)}, s32[512,1]{0,1:T(1,128)}, u32[]{:S(2)}) copy-start(s32[512,1]{0,1:T(1,128)} %param.4) | copy-start | bytes 6148
  0.0 1.5 %copy-start.1 = (s32[512]{0:T(512)S(1)}, s32[512]{0:T(512)}, u32[]{:S(2)}) copy-start(s32[512]{0:T(512)} %param.5) | copy-start | bytes 6148
  2.5 13.5 %collective-permute-start = (bf16[784,128]{1,0:T(8,128)(2,1)S(1)}, bf16[784,128]{1,0:T(8,128)(2,1)S(1)}, u32[]{:S(2)}, u32[]{:S(2)}) collective-permute-start(bf16[784,128]{1,0:T(8,128)(2,1)S(1)} %get-tuple-element.24), channel_id=1, source_target_pairs={{0,2},{1,3},{2,0},{3,1},{4,6},{5,7},{6,4},{7,5},{8,10},{9,11},{10,... | collective-permute-start | bytes 602120 | tf_op jit(solution)/shard_map/ppermute | solution.py:296
  6.6 12.8 %collective-permute-start.2 = (bf16[784,128]{1,0:T(8,128)(2,1)S(1)}, bf16[784,128]{1,0:T(8,128)(2,1)S(1)}, u32[]{:S(2)}, u32[]{:S(2)}) collective-permute-start(bf16[784,128]{1,0:T(8,128)(2,1)S(1)} %get-tuple-element.26), channel_id=1, source_target_pairs={{0,1},{1,0},{2,3},{3,2},{4,5},{5,4},{6,7},{7,6},{8,9},{9,8},{10,11... | collective-permute-start | bytes 602120 | tf_op jit(solution)/shard_map/ppermute | solution.py:296
  8.1 11.3 %collective-permute-start.4 = (bf16[784,128]{1,0:T(8,128)(2,1)S(1)}, bf16[784,128]{1,0:T(8,128)(2,1)S(1)}, u32[]{:S(2)}, u32[]{:S(2)}) collective-permute-start(bf16[784,128]{1,0:T(8,128)(2,1)S(1)} %get-tuple-element.27.refs_0_.refs_3_), channel_id=1, source_target_pairs={{8,0},{24,8},{16,24},{4,16},{12,4},{28,12},{20,28},{0,20},{9,1},{2... | collective-permute-start | bytes 602120 | tf_op jit(solution)/shard_map/ppermute | solution.py:290
  8.5 12.9 %collective-permute-start.5 = (bf16[784,128]{1,0:T(8,128)(2,1)S(1)}, bf16[784,128]{1,0:T(8,128)(2,1)S(1)}, u32[]{:S(2)}, u32[]{:S(2)}) collective-permute-start(bf16[784,128]{1,0:T(8,128)(2,1)S(1)} %get-tuple-element.27.refs_0_.refs_3_), channel_id=1, source_target_pairs={{20,0},{0,8},{8,24},{24,16},{16,4},{4,12},{12,28},{28,20},{21,1},{... | collective-permute-start | bytes 602120 | tf_op jit(solution)/shard_map/ppermute | solution.py:290
  16.0 8.7 %collective-permute-start.1 = (bf16[784,128]{1,0:T(8,128)(2,1)S(1)}, bf16[784,128]{1,0:T(8,128)(2,1)S(1)}, u32[]{:S(2)}, u32[]{:S(2)}) collective-permute-start(bf16[784,128]{1,0:T(8,128)(2,1)S(1)} %get-tuple-element.25), channel_id=1, source_target_pairs={{0,3},{1,2},{2,1},{3,0},{4,7},{5,6},{6,5},{7,4},{8,11},{9,10},{10,... | collective-permute-start | bytes 602120 | tf_op jit(solution)/shard_map/ppermute | solution.py:296
  19.4 7.9 %collective-permute-start.7 = (bf16[784,128]{1,0:T(8,128)(2,1)S(1)}, bf16[784,128]{1,0:T(8,128)(2,1)S(1)}, u32[]{:S(2)}, u32[]{:S(2)}) collective-permute-start(bf16[784,128]{1,0:T(8,128)(2,1)S(1)} %collective-permute-done.2.refs_1_.refs_2_), channel_id=1, source_target_pairs={{8,0},{24,8},{16,24},{4,16},{12,4},{28,12},{20,28},{0,20},{9,1},{2... | collective-permute-start | bytes 602120 | tf_op jit(solution)/shard_map/ppermute | solution.py:290
  20.3 7.0 %collective-permute-start.8 = (bf16[784,128]{1,0:T(8,128)(2,1)S(1)}, bf16[784,128]{1,0:T(8,128)(2,1)S(1)}, u32[]{:S(2)}, u32[]{:S(2)}) collective-permute-start(bf16[784,128]{1,0:T(8,128)(2,1)S(1)} %collective-permute-done.2.refs_1_.refs_2_), channel_id=1, source_target_pairs={{20,0},{0,8},{8,24},{24,16},{16,4},{4,12},{12,28},{28,20},{21,1},{... | collective-permute-start | bytes 602120 | tf_op jit(solution)/shard_map/ppermute | solution.py:290
  21.5 9.5 %collective-permute-start.10 = (bf16[1,784,128]{2,1,0:T(8,128)(2,1)S(1)}, bf16[1,784,128]{2,1,0:T(8,128)(2,1)S(1)}, u32[]{:S(2)}, u32[]{:S(2)}) collective-permute-start(bf16[1,784,128]{2,1,0:T(8,128)(2,1)S(1)} %shard_map.40), channel_id=1, source_target_pairs={{20,0},{0,8},{8,24},{24,16},{16,4},{4,12},{12,28},{28,20},{21,1},{... | collective-permute-start | bytes 602120 | tf_op jit(solution)/shard_map/ppermute | solution.py:290
  23.0 8.0 %collective-permute-start.6 = (bf16[1,784,128]{2,1,0:T(8,128)(2,1)S(1)}, bf16[1,784,128]{2,1,0:T(8,128)(2,1)S(1)}, u32[]{:S(2)}, u32[]{:S(2)}) collective-permute-start(bf16[1,784,128]{2,1,0:T(8,128)(2,1)S(1)} %shard_map.40), channel_id=1, source_target_pairs={{8,0},{24,8},{16,24},{4,16},{12,4},{28,12},{20,28},{0,20},{9,1},{2... | collective-permute-start | bytes 602120 | tf_op jit(solution)/shard_map/ppermute | solution.py:290
  24.7 4.7 %collective-permute-start.3 = (bf16[4,784,128]{2,1,0:T(8,128)(2,1)S(1)}, bf16[4,784,128]{2,1,0:T(8,128)(2,1)S(1)}, u32[]{:S(2)}, u32[]{:S(2)}) collective-permute-start(bf16[4,784,128]{2,1,0:T(8,128)(2,1)S(1)} %shard_map.39), channel_id=1, source_target_pairs={{4,0},{12,8},{28,24},{20,16},{0,4},{8,12},{24,28},{16,20},{5,1},{1... | collective-permute-start | bytes 2408456 | tf_op jit(solution)/shard_map/ppermute | solution.py:290
  27.3 7.9 %collective-permute-start.9 = (bf16[1,784,128]{2,1,0:T(8,128)(2,1)S(1)}, bf16[1,784,128]{2,1,0:T(8,128)(2,1)S(1)}, u32[]{:S(2)}, u32[]{:S(2)}) collective-permute-start(bf16[1,784,128]{2,1,0:T(8,128)(2,1)S(1)} %shard_map.41), channel_id=1, source_target_pairs={{20,0},{0,8},{8,24},{24,16},{16,4},{4,12},{12,28},{28,20},{21,1},{... | collective-permute-start | bytes 602120 | tf_op jit(solution)/shard_map/ppermute | solution.py:290
  29.4 6.8 %collective-permute-start.11 = (bf16[1,784,128]{2,1,0:T(8,128)(2,1)S(1)}, bf16[1,784,128]{2,1,0:T(8,128)(2,1)S(1)}, u32[]{:S(2)}, u32[]{:S(2)}) collective-permute-start(bf16[1,784,128]{2,1,0:T(8,128)(2,1)S(1)} %shard_map.41), channel_id=1, source_target_pairs={{8,0},{24,8},{16,24},{4,16},{12,4},{28,12},{20,28},{0,20},{9,1},{2... | collective-permute-start | bytes 602120 | tf_op jit(solution)/shard_map/ppermute | solution.py:290

commit v15 on v13

--- a/solution.py
+++ b/solution.py
@@ -330,7 +330,7 @@
         held[r][0] = (first[r], None)
     for k in range(1, groups):
         if k == 1:
-            block = after(own[k], first[near[0]]) if near else own[k]
+            block = after(own[k], *first.values())
         else:
             passed = [held[r][k - 2][0] for r in near]
             block = stack([after(own[k], *passed)], WAIT)

time: 47.2 us -> 48.8 us (1.034)
  waiting for transfers between devices: 8.05 us -> 12.8 us
  blocking collectives: 12.6 us -> 10.8 us
  starting transfers between devices: 18.3 us -> 17.1 us
    ppermute x3, waiting for transfers between devices: 3.65 us -> 7.17 us  [exchange(): got[k] = lax.ppermute(block, 'group', [(z, z ^ k) for z in range(groups)])]
    all_to_all x1, blocking collectives: 12.6 us -> 10.8 us  [per_device(): lax.all_to_all(best, ('shard', 'group'), split_axis=0, concat_axis=0, til...]
    ppermute x9, starting transfers between devices: 10.2 us -> 8.34 us  [from_offset(): return lax.ppermute(x, 'shard', perm)]
    ppermute x9, waiting for transfers between devices: 4.4 us -> 5.59 us  [from_offset(): return lax.ppermute(x, 'shard', perm)]
    ppermute x3, starting transfers between devices: 8.15 us -> 8.75 us  [exchange(): got[k] = lax.ppermute(block, 'group', [(z, z ^ k) for z in range(groups)])]
where the time goes in v15:
time: 48.8 us; the launch traced here: 48.7 us
  starting transfers between devices  17.1 us (35%)
  waiting for transfers between devices  12.8 us (26%)
  blocking collectives  10.8 us (22%)
  Pallas kernels  7.96 us (16%)
    all_to_all x1, blocking collectives, per_device(): lax.all_to_all(best, ('shard', 'group'), split_axis=0, concat_axis=0, til...  10.8 us
    ppermute x3, starting transfers between devices, exchange(): got[k] = lax.ppermute(block, 'group', [(z, z ^ k) for z in range(groups)])  8.75 us
    ppermute x9, starting transfers between devices, from_offset(): return lax.ppermute(x, 'shard', perm)  8.34 us
    pallas_call x11, Pallas kernels, call(): pl.pallas_call(kernel, out_shape=out_shape, in_specs=in_specs or in_vmem(...  7.96 us
    ppermute x3, waiting for transfers between devices, exchange(): got[k] = lax.ppermute(block, 'group', [(z, z ^ k) for z in range(groups)])  7.17 us
    ppermute x9, waiting for transfers between devices, from_offset(): return lax.ppermute(x, 'shard', perm)  5.59 us
  transfers between devices with their start and end apart: 12, of which 7 were waited for; matrix products, arithmetic and copies ran while one was open for 0% of the time, Pallas kernels for 9%

profile of v15, /device:TPU:0, one launch (start us, length us, event | category | flops | bytes accessed | tf_op | source)
XLA Modules:
  0.0 48.7 jit_solution(4076966219917068087)
XLA Ops:
  0.0 0.0 copy-start
  0.0 0.0 copy-start.1
  0.0 1.5 %shard_map.37.refs_0_ = bf16[512,768]{1,0:T(8,128)(2,1)S(1)} custom-call(bf16[512,768]{1,0:T(8,128)(2,1)} %far_ref.1), custom_call_target="tpu_custom_call" | custom-call | flops 1572864 | bytes 1572864 | tf_op jit(solution)/shard_map/pallas_call | solution.py:216
  1.5 0.0 copy-done
  1.5 0.0 copy-done.1
  1.5 0.9 %shard_map.38 = (bf16[784,128]{1,0:T(8,128)(2,1)S(1)}, bf16[784,128]{1,0:T(8,128)(2,1)S(1)}, bf16[784,128]{1,0:T(8,128)(2,1)S(1)}, bf16[784,128]{1,0:T(8,128)(2,1)S(1)}, s32[1,512]{1,0:T(1,128)S(1)}) custom-call(bf16[512,768]{1,0:T(8,128)(2,1)S(1)} %shard_map.37.refs_0_, s32[1,512]{1,0:T(1,128)S(1)} %bitcast.3, s32[1,512]{1,0:T(1,128)S(1)} %bitcast.4), custom_call_target="tpu_custom_call" | custom-call | flops 402653184 | bytes 1572864 | tf_op jit(solution)/shard_map/pallas_call | solution.py:216
  2.5 3.1 %collective-permute-start = (bf16[784,128]{1,0:T(8,128)(2,1)S(1)}, bf16[784,128]{1,0:T(8,128)(2,1)S(1)}, u32[]{:S(2)}, u32[]{:S(2)}) collective-permute-start(bf16[784,128]{1,0:T(8,128)(2,1)S(1)} %get-tuple-element.24), channel_id=1, source_target_pairs={{0,1},{1,0},{2,3},{3,2},{4,5},{5,4},{6,7},{7,6},{8,9},{9,8},{10,11... | collective-permute-start | bytes 602120 | tf_op jit(solution)/shard_map/ppermute | solution.py:296
  5.6 0.7 %collective-permute-start.4 = (bf16[784,128]{1,0:T(8,128)(2,1)S(1)}, bf16[784,128]{1,0:T(8,128)(2,1)S(1)}, u32[]{:S(2)}, u32[]{:S(2)}) collective-permute-start(bf16[784,128]{1,0:T(8,128)(2,1)S(1)} %get-tuple-element.27.refs_0_.refs_3_), channel_id=1, source_target_pairs={{8,0},{24,8},{16,24},{4,16},{12,4},{28,12},{20,28},{0,20},{9,1},{2... | collective-permute-start | bytes 602120 | tf_op jit(solution)/shard_map/ppermute | solution.py:290
  6.2 1.3 %collective-permute-start.5 = (bf16[784,128]{1,0:T(8,128)(2,1)S(1)}, bf16[784,128]{1,0:T(8,128)(2,1)S(1)}, u32[]{:S(2)}, u32[]{:S(2)}) collective-permute-start(bf16[784,128]{1,0:T(8,128)(2,1)S(1)} %get-tuple-element.27.refs_0_.refs_3_), channel_id=1, source_target_pairs={{20,0},{0,8},{8,24},{24,16},{16,4},{4,12},{12,28},{28,20},{21,1},{... | collective-permute-start | bytes 602120 | tf_op jit(solution)/shard_map/ppermute | solution.py:290
  7.6 2.6 %collective-permute-start.2 = (bf16[784,128]{1,0:T(8,128)(2,1)S(1)}, bf16[784,128]{1,0:T(8,128)(2,1)S(1)}, u32[]{:S(2)}, u32[]{:S(2)}) collective-permute-start(bf16[784,128]{1,0:T(8,128)(2,1)S(1)} %get-tuple-element.26), channel_id=1, source_target_pairs={{0,2},{1,3},{2,0},{3,1},{4,6},{5,7},{6,4},{7,5},{8,10},{9,11},{10,... | collective-permute-start | bytes 602120 | tf_op jit(solution)/shard_map/ppermute | solution.py:296
  10.2 0.4 collective-permute-done.refs_1_.refs_2_
  10.5 1.5 %collective-permute-done.4.refs_7_ = bf16[784,128]{1,0:T(8,128)(2,1)S(1)} collective-permute-done((bf16[784,128]{1,0:T(8,128)(2,1)S(1)}, bf16[784,128]{1,0:T(8,128)(2,1)S(1)}, u32[]{:S(2)}, u32[]{:S(2)}) %collective-permute-start.4) | collective-permute-done | bytes 200736 | tf_op jit(solution)/shard_map/ppermute | solution.py:290
  12.0 0.4 collective-permute-done.5.refs_10_.refs_4_
  12.4 1.2 %collective-permute-start.7 = (bf16[784,128]{1,0:T(8,128)(2,1)S(1)}, bf16[784,128]{1,0:T(8,128)(2,1)S(1)}, u32[]{:S(2)}, u32[]{:S(2)}) collective-permute-start(bf16[784,128]{1,0:T(8,128)(2,1)S(1)} %collective-permute-done.refs_1_.refs_2_), channel_id=1, source_target_pairs={{8,0},{24,8},{16,24},{4,16},{12,4},{28,12},{20,28},{0,20},{9,1},{2... | collective-permute-start | bytes 602120 | tf_op jit(solution)/shard_map/ppermute | solution.py:290
  13.6 0.8 %collective-permute-start.8 = (bf16[784,128]{1,0:T(8,128)(2,1)S(1)}, bf16[784,128]{1,0:T(8,128)(2,1)S(1)}, u32[]{:S(2)}, u32[]{:S(2)}) collective-permute-start(bf16[784,128]{1,0:T(8,128)(2,1)S(1)} %collective-permute-done.refs_1_.refs_2_), channel_id=1, source_target_pairs={{20,0},{0,8},{8,24},{24,16},{16,4},{4,12},{12,28},{28,20},{21,1},{... | collective-permute-start | bytes 602120 | tf_op jit(solution)/shard_map/ppermute | solution.py:290
  14.4 3.1 %collective-permute-start.1 = (bf16[784,128]{1,0:T(8,128)(2,1)S(1)}, bf16[784,128]{1,0:T(8,128)(2,1)S(1)}, u32[]{:S(2)}, u32[]{:S(2)}) collective-permute-start(bf16[784,128]{1,0:T(8,128)(2,1)S(1)} %get-tuple-element.25), channel_id=1, source_target_pairs={{0,3},{1,2},{2,1},{3,0},{4,7},{5,6},{6,5},{7,4},{8,11},{9,10},{10,... | collective-permute-start | bytes 602120 | tf_op jit(solution)/shard_map/ppermute | solution.py:296
  17.5 6.8 %collective-permute-done.2.refs_2_.refs_0_.refs_1_ = bf16[784,128]{1,0:T(8,128)(2,1)S(1)} collective-permute-done((bf16[784,128]{1,0:T(8,128)(2,1)S(1)}, bf16[784,128]{1,0:T(8,128)(2,1)S(1)}, u32[]{:S(2)}, u32[]{:S(2)}) %collective-permute-start.2) | collective-permute-done | bytes 200736 | tf_op jit(solution)/shard_map/ppermute | solution.py:296
  24.3 1.6 %collective-permute-start.10 = (bf16[1,784,128]{2,1,0:T(8,128)(2,1)S(1)}, bf16[1,784,128]{2,1,0:T(8,128)(2,1)S(1)}, u32[]{:S(2)}, u32[]{:S(2)}) collective-permute-start(bf16[1,784,128]{2,1,0:T(8,128)(2,1)S(1)} %shard_map.40), channel_id=1, source_target_pairs={{20,0},{0,8},{8,24},{24,16},{16,4},{4,12},{12,28},{28,20},{21,1},{... | collective-permute-start | bytes 602120 | tf_op jit(solution)/shard_map/ppermute | solution.py:290
  25.9 0.2 collective-permute-start.6
  26.1 0.0 collective-permute-done.1.refs_3_.refs_0_
  26.1 0.1 shard_map.39
  26.2 0.4 collective-permute-start.3
  26.5 0.0 collective-permute-done.7.refs_6_
  26.6 0.0 collective-permute-done.8.refs_9_.refs_3_
  26.6 1.6 %collective-permute-start.9 = (bf16[1,784,128]{2,1,0:T(8,128)(2,1)S(1)}, bf16[1,784,128]{2,1,0:T(8,128)(2,1)S(1)}, u32[]{:S(2)}, u32[]{:S(2)}) collective-permute-start(bf16[1,784,128]{2,1,0:T(8,128)(2,1)S(1)} %shard_map.41), channel_id=1, source_target_pairs={{20,0},{0,8},{8,24},{24,16},{16,4},{4,12},{12,28},{28,20},{21,1},{... | collective-permute-start | bytes 602120 | tf_op jit(solution)/shard_map/ppermute | solution.py:290
  28.2 0.5 collective-permute-start.11
  28.7 0.0 collective-permute-done.3.refs_4_
  28.7 1.6 %shard_map.42.refs_11_ = f32[4,8,512]{2,1,0:T(8,128)S(1)} custom-call(bf16[784,128]{1,0:T(8,128)(2,1)S(1)} %collective-permute-done.1.refs_3_.refs_0_, bf16[784,128]{1,0:T(8,128)(2,1)S(1)} %collective-permute-done.2.refs_2_.refs_0_.refs_1_, bf16[784,128]{1,0:T(8,128)(2,1)S(1)} %collective-permute-done.refs_1_.refs_2_, ...), custom_call_target="tpu_custom_call" | custom-call | flops 805306368 | bytes 1572864 | tf_op jit(solution)/shard_map/pallas_call | solution.py:216
  30.2 1.1 %collective-permute-done.10.refs_8_.refs_2_ = bf16[1,784,128]{2,1,0:T(8,128)(2,1)S(1)} collective-permute-done((bf16[1,784,128]{2,1,0:T(8,128)(2,1)S(1)}, bf16[1,784,128]{2,1,0:T(8,128)(2,1)S(1)}, u32[]{:S(2)}, u32[]{:S(2)}) %collective-permute-start.10) | collective-permute-done | bytes 200736 | tf_op jit(solution)/shard_map/ppermute | solution.py:290
  31.3 0.9 %collective-permute-done.6.refs_5_ = bf16[1,784,128]{2,1,0:T(8,128)(2,1)S(1)} collective-permute-done((bf16[1,784,128]{2,1,0:T(8,128)(2,1)S(1)}, bf16[1,784,128]{2,1,0:T(8,128)(2,1)S(1)}, u32[]{:S(2)}, u32[]{:S(2)}) %collective-permute-start.6) | collective-permute-done | bytes 200736 | tf_op jit(solution)/shard_map/ppermute | solution.py:290
  32.2 1.6 %shard_map.43.refs_9_ = f32[4,8,512]{2,1,0:T(8,128)S(1)} custom-call(bf16[784,128]{1,0:T(8,128)(2,1)S(1)} %collective-permute-done.1.refs_3_.refs_0_, bf16[784,128]{1,0:T(8,128)(2,1)S(1)} %collective-permute-done.2.refs_2_.refs_0_.refs_1_, bf16[784,128]{1,0:T(8,128)(2,1)S(1)} %collective-permute-done.refs_1_.refs_2_, ...), custom_call_target="tpu_custom_call" | custom-call | flops 830472192 | bytes 2752512 | tf_op jit(solution)/shard_map/pallas_call | solution.py:216
  33.8 1.8 %collective-permute-done.9.refs_8_.refs_1_ = bf16[1,784,128]{2,1,0:T(8,128)(2,1)S(1)} collective-permute-done((bf16[1,784,128]{2,1,0:T(8,128)(2,1)S(1)}, bf16[1,784,128]{2,1,0:T(8,128)(2,1)S(1)}, u32[]{:S(2)}, u32[]{:S(2)}) %collective-permute-start.9) | collective-permute-done | bytes 200736 | tf_op jit(solution)/shard_map/ppermute | solution.py:290
  35.6 1.0 %shard_map.44 = (f32[4,8,512]{2,1,0:T(8,128)S(1)}, f32[1,512]{1,0:T(1,128)S(1)}, f32[1,512]{1,0:T(1,128)S(1)}) custom-call(bf16[784,128]{1,0:T(8,128)(2,1)S(1)} %collective-permute-done.1.refs_3_.refs_0_, bf16[784,128]{1,0:T(8,128)(2,1)S(1)} %collective-permute-done.2.refs_2_.refs_0_.refs_1_, bf16[784,128]{1,0:T(8,128)(2,1)S(1)} %collective-permute-done.refs_1_.refs_2_, ...), custom_call_target="tpu_custom_call" | custom-call | flops 276824064 | bytes 2359296 | tf_op jit(solution)/shard_map/pallas_call | solution.py:216
  36.5 0.0 collective-permute-done.11.refs_0_
  36.6 0.5 %shard_map.45 = (f32[1,512]{1,0:T(1,128)S(1)}, f32[1,512]{1,0:T(1,128)S(1)}) custom-call(bf16[1,784,128]{2,1,0:T(8,128)(2,1)S(1)} %collective-permute-done.11.refs_0_, bf16[1,784,128]{2,1,0:T(8,128)(2,1)S(1)} %collective-permute-done.9.refs_8_.refs_1_, bf16[1,784,128]{2,1,0:T(8,128)(2,1)S(1)} %collective-permute-done.10.refs_8_.refs_2_, ...), custom_call_target="tpu_custom_call" | custom-call | flops 100663296 | bytes 983040 | tf_op jit(solution)/shard_map/pallas_call | solution.py:216
  37.1 0.1 shard_map.46
  37.1 10.8 %all_to_all.5.refs_0_ = f32[32,1,128]{2,1,0:T(1,128)S(1)} all-to-all(f32[32,1,128]{2,1,0:T(1,128)S(1)} %shard_map.46), channel_id=1, replica_groups=mesh['shard'=8,'group'=4] {'shard','group'}, dimensions={0} | all-to-all | bytes 32768 | tf_op jit(solution)/shard_map/all_to_all | solution.py:377
  47.9 0.8 %shard_map.47 = f32[1,512]{1,0:T(1,128)} custom-call(f32[32,1,128]{2,1,0:T(1,128)S(1)} %all_to_all.5.refs_0_, s32[1,512]{1,0:T(1,128)S(1)} %get-tuple-element.36.refs_1_), custom_call_target="tpu_custom_call" | custom-call | flops 262144 | bytes 2048 | tf_op jit(solution)/shard_map/pallas_call | solution.py:216
  (2 shorter events, 0.0 us)
Async XLA Ops:
  0.0 1.5 %copy-start = (s32[512,1]{0,1:T(1,128)S(1)}, s32[512,1]{0,1:T(1,128)}, u32[]{:S(2)}) copy-start(s32[512,1]{0,1:T(1,128)} %param.4) | copy-start | bytes 6148
  0.0 1.5 %copy-start.1 = (s32[512]{0:T(512)S(1)}, s32[512]{0:T(512)}, u32[]{:S(2)}) copy-start(s32[512]{0:T(512)} %param.5) | copy-start | bytes 6148
  2.5 8.1 %collective-permute-start = (bf16[784,128]{1,0:T(8,128)(2,1)S(1)}, bf16[784,128]{1,0:T(8,128)(2,1)S(1)}, u32[]{:S(2)}, u32[]{:S(2)}) collective-permute-start(bf16[784,128]{1,0:T(8,128)(2,1)S(1)} %get-tuple-element.24), channel_id=1, source_target_pairs={{0,1},{1,0},{2,3},{3,2},{4,5},{5,4},{6,7},{7,6},{8,9},{9,8},{10,11... | collective-permute-start | bytes 602120 | tf_op jit(solution)/shard_map/ppermute | solution.py:296
  5.6 6.5 %collective-permute-start.4 = (bf16[784,128]{1,0:T(8,128)(2,1)S(1)}, bf16[784,128]{1,0:T(8,128)(2,1)S(1)}, u32[]{:S(2)}, u32[]{:S(2)}) collective-permute-start(bf16[784,128]{1,0:T(8,128)(2,1)S(1)} %get-tuple-element.27.refs_0_.refs_3_), channel_id=1, source_target_pairs={{8,0},{24,8},{16,24},{4,16},{12,4},{28,12},{20,28},{0,20},{9,1},{2... | collective-permute-start | bytes 602120 | tf_op jit(solution)/shard_map/ppermute | solution.py:290
  6.2 6.1 %collective-permute-start.5 = (bf16[784,128]{1,0:T(8,128)(2,1)S(1)}, bf16[784,128]{1,0:T(8,128)(2,1)S(1)}, u32[]{:S(2)}, u32[]{:S(2)}) collective-permute-start(bf16[784,128]{1,0:T(8,128)(2,1)S(1)} %get-tuple-element.27.refs_0_.refs_3_), channel_id=1, source_target_pairs={{20,0},{0,8},{8,24},{24,16},{16,4},{4,12},{12,28},{28,20},{21,1},{... | collective-permute-start | bytes 602120 | tf_op jit(solution)/shard_map/ppermute | solution.py:290
  7.6 16.7 %collective-permute-start.2 = (bf16[784,128]{1,0:T(8,128)(2,1)S(1)}, bf16[784,128]{1,0:T(8,128)(2,1)S(1)}, u32[]{:S(2)}, u32[]{:S(2)}) collective-permute-start(bf16[784,128]{1,0:T(8,128)(2,1)S(1)} %get-tuple-element.26), channel_id=1, source_target_pairs={{0,2},{1,3},{2,0},{3,1},{4,6},{5,7},{6,4},{7,5},{8,10},{9,11},{10,... | collective-permute-start | bytes 602120 | tf_op jit(solution)/shard_map/ppermute | solution.py:296
  12.4 14.2 %collective-permute-start.7 = (bf16[784,128]{1,0:T(8,128)(2,1)S(1)}, bf16[784,128]{1,0:T(8,128)(2,1)S(1)}, u32[]{:S(2)}, u32[]{:S(2)}) collective-permute-start(bf16[784,128]{1,0:T(8,128)(2,1)S(1)} %collective-permute-done.refs_1_.refs_2_), channel_id=1, source_target_pairs={{8,0},{24,8},{16,24},{4,16},{12,4},{28,12},{20,28},{0,20},{9,1},{2... | collective-permute-start | bytes 602120 | tf_op jit(solution)/shard_map/ppermute | solution.py:290
  13.6 13.0 %collective-permute-start.8 = (bf16[784,128]{1,0:T(8,128)(2,1)S(1)}, bf16[784,128]{1,0:T(8,128)(2,1)S(1)}, u32[]{:S(2)}, u32[]{:S(2)}) collective-permute-start(bf16[784,128]{1,0:T(8,128)(2,1)S(1)} %collective-permute-done.refs_1_.refs_2_), channel_id=1, source_target_pairs={{20,0},{0,8},{8,24},{24,16},{16,4},{4,12},{12,28},{28,20},{21,1},{... | collective-permute-start | bytes 602120 | tf_op jit(solution)/shard_map/ppermute | solution.py:290
  14.4 11.7 %collective-permute-start.1 = (bf16[784,128]{1,0:T(8,128)(2,1)S(1)}, bf16[784,128]{1,0:T(8,128)(2,1)S(1)}, u32[]{:S(2)}, u32[]{:S(2)}) collective-permute-start(bf16[784,128]{1,0:T(8,128)(2,1)S(1)} %get-tuple-element.25), channel_id=1, source_target_pairs={{0,3},{1,2},{2,1},{3,0},{4,7},{5,6},{6,5},{7,4},{8,11},{9,10},{10,... | collective-permute-start | bytes 602120 | tf_op jit(solution)/shard_map/ppermute | solution.py:296
  24.3 7.0 %collective-permute-start.10 = (bf16[1,784,128]{2,1,0:T(8,128)(2,1)S(1)}, bf16[1,784,128]{2,1,0:T(8,128)(2,1)S(1)}, u32[]{:S(2)}, u32[]{:S(2)}) collective-permute-start(bf16[1,784,128]{2,1,0:T(8,128)(2,1)S(1)} %shard_map.40), channel_id=1, source_target_pairs={{20,0},{0,8},{8,24},{24,16},{16,4},{4,12},{12,28},{28,20},{21,1},{... | collective-permute-start | bytes 602120 | tf_op jit(solution)/shard_map/ppermute | solution.py:290
  25.9 6.3 %collective-permute-start.6 = (bf16[1,784,128]{2,1,0:T(8,128)(2,1)S(1)}, bf16[1,784,128]{2,1,0:T(8,128)(2,1)S(1)}, u32[]{:S(2)}, u32[]{:S(2)}) collective-permute-start(bf16[1,784,128]{2,1,0:T(8,128)(2,1)S(1)} %shard_map.40), channel_id=1, source_target_pairs={{8,0},{24,8},{16,24},{4,16},{12,4},{28,12},{20,28},{0,20},{9,1},{2... | collective-permute-start | bytes 602120 | tf_op jit(solution)/shard_map/ppermute | solution.py:290
  26.2 2.5 %collective-permute-start.3 = (bf16[4,784,128]{2,1,0:T(8,128)(2,1)S(1)}, bf16[4,784,128]{2,1,0:T(8,128)(2,1)S(1)}, u32[]{:S(2)}, u32[]{:S(2)}) collective-permute-start(bf16[4,784,128]{2,1,0:T(8,128)(2,1)S(1)} %shard_map.39), channel_id=1, source_target_pairs={{4,0},{12,8},{28,24},{20,16},{0,4},{8,12},{24,28},{16,20},{5,1},{1... | collective-permute-start | bytes 2408456 | tf_op jit(solution)/shard_map/ppermute | solution.py:290
  26.6 9.0 %collective-permute-start.9 = (bf16[1,784,128]{2,1,0:T(8,128)(2,1)S(1)}, bf16[1,784,128]{2,1,0:T(8,128)(2,1)S(1)}, u32[]{:S(2)}, u32[]{:S(2)}) collective-permute-start(bf16[1,784,128]{2,1,0:T(8,128)(2,1)S(1)} %shard_map.41), channel_id=1, source_target_pairs={{20,0},{0,8},{8,24},{24,16},{16,4},{4,12},{12,28},{28,20},{21,1},{... | collective-permute-start | bytes 602120 | tf_op jit(solution)/shard_map/ppermute | solution.py:290
  28.2 8.4 %collective-permute-start.11 = (bf16[1,784,128]{2,1,0:T(8,128)(2,1)S(1)}, bf16[1,784,128]{2,1,0:T(8,128)(2,1)S(1)}, u32[]{:S(2)}, u32[]{:S(2)}) collective-permute-start(bf16[1,784,128]{2,1,0:T(8,128)(2,1)S(1)} %shard_map.41), channel_id=1, source_target_pairs={{8,0},{24,8},{16,24},{4,16},{12,4},{28,12},{20,28},{0,20},{9,1},{2... | collective-permute-start | bytes 602120 | tf_op jit(solution)/shard_map/ppermute | solution.py:290

commit v16 on v13

--- a/solution.py
+++ b/solution.py
@@ -115,25 +115,36 @@
         refs[-1][k] = ref[...]
 
 
-def score_kernel(sources, tasks, done, last, *refs):
-    *refs, flat_ref, side_ref, row_ref = refs
+def score_kernel(sources, flats, layout, tasks, done, last, *refs):
+    *refs, side_ref, row_ref = refs
     if last:
-        *refs, best_ref = refs
+        *refs, best_ref, flat_ref = refs
         inputs, out_refs = refs[: -len(done)], refs[-len(done) :]
     else:
-        outs = 1 + len(done)
-        inputs, (best_ref, *out_refs) = refs[:-outs], refs[-outs:]
+        outs = 2 + len(done)
+        inputs, (best_ref, flat_ref, *out_refs) = refs[:-outs], refs[-outs:]
     capacity = LANES
     low = jnp.float32(LOW)
     arrays = 1 + max(index for index, _ in sources.values())
     best_ref[...] = inputs[arrays][...] if len(inputs) > arrays else jnp.full(best_ref.shape, low)
+
+    def units(role, ks):
+        rows = pl.ds(ks[0] * capacity, len(ks) * capacity)
+        if (role, ks[0]) in flats:
+            index, place = flats[role, ks[0]]
+            return inputs[arrays + 1 + index][place, rows, :]
+        return flat_ref[layout.index(role), rows, :]
+
     tops = {}
     for (role, k), (index, part) in sources.items():
         ref = inputs[index] if part is None else inputs[index].at[part]
         height = ref.shape[0] - TAIL
         rows = pl.ds(k * capacity, capacity)
-        for c in range(height // capacity):
-            flat_ref[role, rows, pl.ds(c * LANES, LANES)] = ref[pl.ds(c * capacity, capacity), :]
+        if (role, k) not in flats:
+            for c in range(height // capacity):
+                flat_ref[layout.index(role), rows, pl.ds(c * LANES, LANES)] = ref[
+                    pl.ds(c * capacity, capacity), :
+                ]
         tops[role, k] = ref[pl.ds(height, TAIL), :][0:1].astype(jnp.float32)
     for role, k in sorted({(left, k) for left, ks, _, _, _ in tasks for k in ks}):
         side_ref[role, pl.ds(k * capacity, capacity), :] = column_of(tops[role, k])
@@ -148,8 +159,8 @@
             width = len(some) * capacity
             columns = pl.ds(some[0] * capacity, width)
             scores = lax.dot_general(
-                flat_ref[left, rows, :],
-                flat_ref[right, columns, :],
+                units(left, left_ks),
+                units(right, some),
                 (((1,), (1,)), ((), ())),
                 preferred_element_type=jnp.float32,
             )
@@ -211,7 +222,7 @@
 
 
 def call(
-    kernel, out_shape, scratch, args, flops, bytes_accessed, in_specs=None, limit=48 * MIB
+    kernel, out_shape, scratch, args, flops, bytes_accessed, in_specs=None, limit=24 * MIB
 ):
     return pl.pallas_call(
         kernel,
@@ -241,7 +252,7 @@
     )[0]
 
 
-def score(held, tasks, acc, done, last, slots, width):
+def score(held, tasks, acc, flats, done, last, slots, width):
     roles = len(held)
     used = sorted(
         {(left, k) for left, ks, _, _, _ in tasks for k in ks}
@@ -255,23 +266,31 @@
         if index == len(arrays):
             arrays.append(array)
         sources[role, k] = (index, part)
-    ends = [jax.ShapeDtypeStruct((1, slots), jnp.float32)] * len(done)
+    layout = sorted({role for role, k in used if (role, k) not in flats})
     tiles = sum(len(task[1]) * len(task[3]) for task in tasks)
-    best = [] if last else [jax.ShapeDtypeStruct((roles, 8, slots), jnp.float32)]
+    kept = [
+        jax.ShapeDtypeStruct((roles, 8, slots), jnp.float32),
+        jax.ShapeDtypeStruct((len(layout), slots, width), jnp.bfloat16),
+    ]
+    scratch = [pltpu.VMEM((roles, slots, LANES), jnp.float32)] * 2
+    if last:
+        scratch = [pltpu.VMEM(x.shape, x.dtype) for x in kept] + scratch
+        kept = []
+    known = dict(flats)
     got = call(
-        lambda *refs: score_kernel(sources, tasks, done, last, *refs),
-        best + ends,
-        ([pltpu.VMEM((roles, 8, slots), jnp.float32)] if last else [])
-        + [
-            pltpu.VMEM((roles, slots, width), jnp.bfloat16),
-            pltpu.VMEM((roles, slots, LANES), jnp.float32),
-            pltpu.VMEM((roles, slots, LANES), jnp.float32),
-        ],
+        lambda *refs: score_kernel(sources, known, layout, tasks, done, last, *refs),
+        kept + [jax.ShapeDtypeStruct((1, slots), jnp.float32)] * len(done),
+        scratch,
         arrays + list(acc),
         2 * tiles * LANES * LANES * width,
         2 * len(used) * LANES * width,
     )
-    return got[: len(best)], got[len(best) :]
+    if last:
+        return acc, got
+    for role, k in used:
+        if (role, k) not in flats:
+            flats[role, k] = (max(len(acc) - 1, 0), layout.index(role))
+    return [got[0], *acc[1:], got[1]], got[2:]
 
 
 def per_device(embeddings, row_group, row_cluster):
@@ -341,7 +360,7 @@
         held[r] = [(got[r], k) for k in range(groups)]
     everything = [(0, 0, False)]
     everything += [(offsets.index(a), offsets.index(b), both) for a, b, both in pairs]
-    steps = [[] for _ in range(4)]
+    steps = [[] for _ in range(3)]
     final = [0] * roles
     for left, right, both in everything:
         for left_ks in (early, late):
@@ -350,7 +369,7 @@
                     step = 0
                     for role, ks in ((left, left_ks), (right, right_ks)):
                         if role in near:
-                            step = max(step, 1 if ks is early else 3 if role == near[0] else 2)
+                            step = max(step, 1 if ks is early else 2)
                     task = (left, left_ks, right, right_ks, both)
                     if both and right_ks is late and left_ks is early:
                         task = (right, right_ks, left, left_ks, both)
@@ -358,12 +377,12 @@
                     final[right] = max(final[right], step)
                     if both:
                         final[left] = max(final[left], step)
-    acc, partial = [], [None] * roles
+    acc, flats, partial = [], {}, [None] * roles
     for step, tasks in enumerate(steps):
         if tasks:
             done = [r for r in range(roles) if final[r] == step]
             last = not any(steps[step + 1 :])
-            acc, ends = score(held, tasks, acc, done, last, slots, width)
+            acc, ends = score(held, tasks, acc, flats, done, last, slots, width)
             for r, end in zip(done, ends):
                 partial[r] = end
     (best,) = call(

time: 47.2 us -> 47.8 us (1.013)
  starting transfers between devices: 18.3 us -> 20.2 us
  waiting for transfers between devices: 8.05 us -> 7.42 us
    ppermute x9, starting transfers between devices: 10.2 us -> 12 us  [from_offset(): return lax.ppermute(x, 'shard', perm)]
    ppermute x9, waiting for transfers between devices: 4.4 us -> 3.77 us  [from_offset(): return lax.ppermute(x, 'shard', perm)]
    pallas_call x11 -> x10, Pallas kernels: 7.97 us -> 7.52 us  [call(): pl.pallas_call(kernel, out_shape=out_shape, in_specs=in_specs or in_vmem(...]
  transfers between devices with their start and end apart: 12 -> 12, of which waited for: 7 -> 5; matrix products, arithmetic and copies ran while one was open for 0% -> 0% of each run, Pallas kernels for 9% -> 7%
where the time goes in v16:
time: 47.8 us; the launch traced here: 47.6 us
  starting transfers between devices  20.2 us (42%)
  blocking collectives  12.4 us (26%)
  Pallas kernels  7.52 us (16%)
  waiting for transfers between devices  7.42 us (16%)
    all_to_all x1, blocking collectives, per_device(): lax.all_to_all(best, ('shard', 'group'), split_axis=0, concat_axis=0, til...  12.4 us
    ppermute x9, starting transfers between devices, from_offset(): return lax.ppermute(x, 'shard', perm)  12 us
    ppermute x3, starting transfers between devices, exchange(): got[k] = lax.ppermute(block, 'group', [(z, z ^ k) for z in range(groups)])  8.15 us
    pallas_call x10, Pallas kernels, call(): pl.pallas_call(kernel, out_shape=out_shape, in_specs=in_specs or in_vmem(...  7.52 us
    ppermute x9, waiting for transfers between devices, from_offset(): return lax.ppermute(x, 'shard', perm)  3.77 us
    ppermute x3, waiting for transfers between devices, exchange(): got[k] = lax.ppermute(block, 'group', [(z, z ^ k) for z in range(groups)])  3.65 us
  transfers between devices with their start and end apart: 12, of which 5 were waited for; matrix products, arithmetic and copies ran while one was open for 0% of the time, Pallas kernels for 7%

profile of v16, /device:TPU:0, one launch (start us, length us, event | category | flops | bytes accessed | tf_op | source)
XLA Modules:
  0.0 47.6 jit_solution(4945438408247913017)
XLA Ops:
  0.0 0.0 copy-start.1
  0.0 0.0 copy-start
  0.0 1.5 %shard_map.37.refs_0_ = bf16[512,768]{1,0:T(8,128)(2,1)S(1)} custom-call(bf16[512,768]{1,0:T(8,128)(2,1)} %far_ref.1), custom_call_target="tpu_custom_call" | custom-call | flops 1572864 | bytes 1572864 | tf_op jit(solution)/shard_map/pallas_call | solution.py:227
  1.5 0.0 copy-done.1
  1.5 0.0 copy-done
  1.5 0.9 %shard_map.38 = (bf16[784,128]{1,0:T(8,128)(2,1)S(1)}, bf16[784,128]{1,0:T(8,128)(2,1)S(1)}, bf16[784,128]{1,0:T(8,128)(2,1)S(1)}, bf16[784,128]{1,0:T(8,128)(2,1)S(1)}, s32[1,512]{1,0:T(1,128)S(1)}) custom-call(bf16[512,768]{1,0:T(8,128)(2,1)S(1)} %shard_map.37.refs_0_, s32[1,512]{1,0:T(1,128)S(1)} %bitcast.3, s32[1,512]{1,0:T(1,128)S(1)} %bitcast.4), custom_call_target="tpu_custom_call" | custom-call | flops 402653184 | bytes 1572864 | tf_op jit(solution)/shard_map/pallas_call | solution.py:227
  2.5 3.1 %collective-permute-start = (bf16[784,128]{1,0:T(8,128)(2,1)S(1)}, bf16[784,128]{1,0:T(8,128)(2,1)S(1)}, u32[]{:S(2)}, u32[]{:S(2)}) collective-permute-start(bf16[784,128]{1,0:T(8,128)(2,1)S(1)} %get-tuple-element.27), channel_id=1, source_target_pairs={{0,1},{1,0},{2,3},{3,2},{4,5},{5,4},{6,7},{7,6},{8,9},{9,8},{10,11... | collective-permute-start | bytes 602120 | tf_op jit(solution)/shard_map/ppermute | solution.py:315
  5.6 0.7 %collective-permute-start.4 = (bf16[784,128]{1,0:T(8,128)(2,1)S(1)}, bf16[784,128]{1,0:T(8,128)(2,1)S(1)}, u32[]{:S(2)}, u32[]{:S(2)}) collective-permute-start(bf16[784,128]{1,0:T(8,128)(2,1)S(1)} %get-tuple-element.30.refs_0_.refs_3_), channel_id=1, source_target_pairs={{8,0},{24,8},{16,24},{4,16},{12,4},{28,12},{20,28},{0,20},{9,1},{2... | collective-permute-start | bytes 602120 | tf_op jit(solution)/shard_map/ppermute | solution.py:309
  6.2 2.6 %collective-permute-start.2 = (bf16[784,128]{1,0:T(8,128)(2,1)S(1)}, bf16[784,128]{1,0:T(8,128)(2,1)S(1)}, u32[]{:S(2)}, u32[]{:S(2)}) collective-permute-start(bf16[784,128]{1,0:T(8,128)(2,1)S(1)} %get-tuple-element.29), channel_id=1, source_target_pairs={{0,2},{1,3},{2,0},{3,1},{4,6},{5,7},{6,4},{7,5},{8,10},{9,11},{10,... | collective-permute-start | bytes 602120 | tf_op jit(solution)/shard_map/ppermute | solution.py:315
  8.8 1.3 %collective-permute-start.8 = (bf16[784,128]{1,0:T(8,128)(2,1)S(1)}, bf16[784,128]{1,0:T(8,128)(2,1)S(1)}, u32[]{:S(2)}, u32[]{:S(2)}) collective-permute-start(bf16[784,128]{1,0:T(8,128)(2,1)S(1)} %get-tuple-element.30.refs_0_.refs_3_), channel_id=1, source_target_pairs={{20,0},{0,8},{8,24},{24,16},{16,4},{4,12},{12,28},{28,20},{21,1},{... | collective-permute-start | bytes 602120 | tf_op jit(solution)/shard_map/ppermute | solution.py:309
  10.2 0.4 collective-permute-done.refs_1_.refs_2_
  10.5 1.5 %collective-permute-done.4.refs_7_.refs_8_ = bf16[784,128]{1,0:T(8,128)(2,1)S(1)} collective-permute-done((bf16[784,128]{1,0:T(8,128)(2,1)S(1)}, bf16[784,128]{1,0:T(8,128)(2,1)S(1)}, u32[]{:S(2)}, u32[]{:S(2)}) %collective-permute-start.4) | collective-permute-done | bytes 200736 | tf_op jit(solution)/shard_map/ppermute | solution.py:309
  12.0 4.1 %collective-permute-start.6 = (bf16[784,128]{1,0:T(8,128)(2,1)S(1)}, bf16[784,128]{1,0:T(8,128)(2,1)S(1)}, u32[]{:S(2)}, u32[]{:S(2)}) collective-permute-start(bf16[784,128]{1,0:T(8,128)(2,1)S(1)} %collective-permute-done.refs_1_.refs_2_), channel_id=1, source_target_pairs={{20,0},{0,8},{8,24},{24,16},{16,4},{4,12},{12,28},{28,20},{21,1},{... | collective-permute-start | bytes 602120 | tf_op jit(solution)/shard_map/ppermute | solution.py:309
  16.1 0.0 collective-permute-start.5
  16.1 2.5 %collective-permute-start.1 = (bf16[784,128]{1,0:T(8,128)(2,1)S(1)}, bf16[784,128]{1,0:T(8,128)(2,1)S(1)}, u32[]{:S(2)}, u32[]{:S(2)}) collective-permute-start(bf16[784,128]{1,0:T(8,128)(2,1)S(1)} %get-tuple-element.28), channel_id=1, source_target_pairs={{0,3},{1,2},{2,1},{3,0},{4,7},{5,6},{6,5},{7,4},{8,11},{9,10},{10,... | collective-permute-start | bytes 602120 | tf_op jit(solution)/shard_map/ppermute | solution.py:315
  18.6 0.7 %collective-permute-done.2.refs_2_.refs_0_.refs_1_ = bf16[784,128]{1,0:T(8,128)(2,1)S(1)} collective-permute-done((bf16[784,128]{1,0:T(8,128)(2,1)S(1)}, bf16[784,128]{1,0:T(8,128)(2,1)S(1)}, u32[]{:S(2)}, u32[]{:S(2)}) %collective-permute-start.2) | collective-permute-done | bytes 200736 | tf_op jit(solution)/shard_map/ppermute | solution.py:315
  19.3 0.0 collective-permute-done.8.refs_10_.refs_12_
  19.3 1.4 %collective-permute-start.11 = (bf16[1,784,128]{2,1,0:T(8,128)(2,1)S(1)}, bf16[1,784,128]{2,1,0:T(8,128)(2,1)S(1)}, u32[]{:S(2)}, u32[]{:S(2)}) collective-permute-start(bf16[1,784,128]{2,1,0:T(8,128)(2,1)S(1)} %shard_map.41), channel_id=1, source_target_pairs={{20,0},{0,8},{8,24},{24,16},{16,4},{4,12},{12,28},{28,20},{21,1},{... | collective-permute-start | bytes 602120 | tf_op jit(solution)/shard_map/ppermute | solution.py:309
  20.7 0.4 collective-permute-start.9
  21.1 2.6 %collective-permute-done.1.refs_3_.refs_0_ = bf16[784,128]{1,0:T(8,128)(2,1)S(1)} collective-permute-done((bf16[784,128]{1,0:T(8,128)(2,1)S(1)}, bf16[784,128]{1,0:T(8,128)(2,1)S(1)}, u32[]{:S(2)}, u32[]{:S(2)}) %collective-permute-start.1) | collective-permute-done | bytes 200736 | tf_op jit(solution)/shard_map/ppermute | solution.py:315
  23.7 0.0 collective-permute-done.6.refs_9_.refs_11_
  23.7 0.0 collective-permute-done.5.refs_6_.refs_7_
  23.7 0.1 shard_map.39
  23.8 2.0 %collective-permute-start.3 = (bf16[4,784,128]{2,1,0:T(8,128)(2,1)S(1)}, bf16[4,784,128]{2,1,0:T(8,128)(2,1)S(1)}, u32[]{:S(2)}, u32[]{:S(2)}) collective-permute-start(bf16[4,784,128]{2,1,0:T(8,128)(2,1)S(1)} %shard_map.39), channel_id=1, source_target_pairs={{4,0},{12,8},{28,24},{20,16},{0,4},{8,12},{24,28},{16,20},{5,1},{1... | collective-permute-start | bytes 2408456 | tf_op jit(solution)/shard_map/ppermute | solution.py:309
  25.8 0.2 collective-permute-start.10
  26.0 1.9 %collective-permute-start.7 = (bf16[1,784,128]{2,1,0:T(8,128)(2,1)S(1)}, bf16[1,784,128]{2,1,0:T(8,128)(2,1)S(1)}, u32[]{:S(2)}, u32[]{:S(2)}) collective-permute-start(bf16[1,784,128]{2,1,0:T(8,128)(2,1)S(1)} %shard_map.40), channel_id=1, source_target_pairs={{8,0},{24,8},{16,24},{4,16},{12,4},{28,12},{20,28},{0,20},{9,1},{2... | collective-permute-start | bytes 602120 | tf_op jit(solution)/shard_map/ppermute | solution.py:309
  27.9 0.0 collective-permute-done.3.refs_4_
  27.9 1.5 %shard_map.42 = (f32[4,8,512]{2,1,0:T(8,128)S(1)}, bf16[2,512,768]{2,1,0:T(8,128)(2,1)S(1)}) custom-call(bf16[784,128]{1,0:T(8,128)(2,1)S(1)} %collective-permute-done.1.refs_3_.refs_0_, bf16[784,128]{1,0:T(8,128)(2,1)S(1)} %collective-permute-done.2.refs_2_.refs_0_.refs_1_, bf16[784,128]{1,0:T(8,128)(2,1)S(1)} %collective-permute-done.refs_1_.refs_2_, ...), custom_call_target="tpu_custom_call" | custom-call | flops 805306368 | bytes 1572864 | tf_op jit(solution)/shard_map/pallas_call | solution.py:227
  29.4 0.0 collective-permute-done.11.refs_8_.refs_10_
  29.4 0.0 collective-permute-done.9.refs_5_.refs_6_
  29.4 1.6 %shard_map.43 = (f32[4,8,512]{2,1,0:T(8,128)S(1)}, bf16[2,512,768]{2,1,0:T(8,128)(2,1)S(1)}) custom-call(bf16[784,128]{1,0:T(8,128)(2,1)S(1)} %collective-permute-done.1.refs_3_.refs_0_, bf16[784,128]{1,0:T(8,128)(2,1)S(1)} %collective-permute-done.2.refs_2_.refs_0_.refs_1_, bf16[784,128]{1,0:T(8,128)(2,1)S(1)} %collective-permute-done.refs_1_.refs_2_, ...), custom_call_target="tpu_custom_call" | custom-call | flops 830472192 | bytes 2752512 | tf_op jit(solution)/shard_map/pallas_call | solution.py:227
  31.0 2.3 %collective-permute-done.10.refs_9_ = bf16[1,784,128]{2,1,0:T(8,128)(2,1)S(1)} collective-permute-done((bf16[1,784,128]{2,1,0:T(8,128)(2,1)S(1)}, bf16[1,784,128]{2,1,0:T(8,128)(2,1)S(1)}, u32[]{:S(2)}, u32[]{:S(2)}) %collective-permute-start.10) | collective-permute-done | bytes 200736 | tf_op jit(solution)/shard_map/ppermute | solution.py:309
  33.3 0.0 collective-permute-done.7.refs_5_
  33.3 1.1 %shard_map.44 = (f32[1,512]{1,0:T(1,128)S(1)}, f32[1,512]{1,0:T(1,128)S(1)}, f32[1,512]{1,0:T(1,128)S(1)}, f32[1,512]{1,0:T(1,128)S(1)}) custom-call(bf16[784,128]{1,0:T(8,128)(2,1)S(1)} %collective-permute-done.1.refs_3_.refs_0_, bf16[784,128]{1,0:T(8,128)(2,1)S(1)} %collective-permute-done.2.refs_2_.refs_0_.refs_1_, ...), custom_call_target="tpu_custom_call" | custom-call | flops 377487360 | bytes 3145728 | tf_op jit(solution)/shard_map/pallas_call | solution.py:227
  34.4 0.1 shard_map.45
  34.4 12.4 %all_to_all.5.refs_0_ = f32[32,1,128]{2,1,0:T(1,128)S(1)} all-to-all(f32[32,1,128]{2,1,0:T(1,128)S(1)} %shard_map.45), channel_id=1, replica_groups=mesh['shard'=8,'group'=4] {'shard','group'}, dimensions={0} | all-to-all | bytes 32768 | tf_op jit(solution)/shard_map/all_to_all | solution.py:396
  46.9 0.8 %shard_map.46 = f32[1,512]{1,0:T(1,128)} custom-call(f32[32,1,128]{2,1,0:T(1,128)S(1)} %all_to_all.5.refs_0_, s32[1,512]{1,0:T(1,128)S(1)} %get-tuple-element.42.refs_1_), custom_call_target="tpu_custom_call" | custom-call | flops 262144 | bytes 2048 | tf_op jit(solution)/shard_map/pallas_call | solution.py:227
  (2 shorter events, 0.0 us)
Async XLA Ops:
  0.0 1.5 %copy-start.1 = (s32[512]{0:T(512)S(1)}, s32[512]{0:T(512)}, u32[]{:S(2)}) copy-start(s32[512]{0:T(512)} %param.5) | copy-start | bytes 6148
  0.0 1.5 %copy-start = (s32[512,1]{0,1:T(1,128)S(1)}, s32[512,1]{0,1:T(1,128)}, u32[]{:S(2)}) copy-start(s32[512,1]{0,1:T(1,128)} %param.4) | copy-start | bytes 6148
  2.5 8.1 %collective-permute-start = (bf16[784,128]{1,0:T(8,128)(2,1)S(1)}, bf16[784,128]{1,0:T(8,128)(2,1)S(1)}, u32[]{:S(2)}, u32[]{:S(2)}) collective-permute-start(bf16[784,128]{1,0:T(8,128)(2,1)S(1)} %get-tuple-element.27), channel_id=1, source_target_pairs={{0,1},{1,0},{2,3},{3,2},{4,5},{5,4},{6,7},{7,6},{8,9},{9,8},{10,11... | collective-permute-start | bytes 602120 | tf_op jit(solution)/shard_map/ppermute | solution.py:315
  5.6 6.5 %collective-permute-start.4 = (bf16[784,128]{1,0:T(8,128)(2,1)S(1)}, bf16[784,128]{1,0:T(8,128)(2,1)S(1)}, u32[]{:S(2)}, u32[]{:S(2)}) collective-permute-start(bf16[784,128]{1,0:T(8,128)(2,1)S(1)} %get-tuple-element.30.refs_0_.refs_3_), channel_id=1, source_target_pairs={{8,0},{24,8},{16,24},{4,16},{12,4},{28,12},{20,28},{0,20},{9,1},{2... | collective-permute-start | bytes 602120 | tf_op jit(solution)/shard_map/ppermute | solution.py:309
  6.2 13.1 %collective-permute-start.2 = (bf16[784,128]{1,0:T(8,128)(2,1)S(1)}, bf16[784,128]{1,0:T(8,128)(2,1)S(1)}, u32[]{:S(2)}, u32[]{:S(2)}) collective-permute-start(bf16[784,128]{1,0:T(8,128)(2,1)S(1)} %get-tuple-element.29), channel_id=1, source_target_pairs={{0,2},{1,3},{2,0},{3,1},{4,6},{5,7},{6,4},{7,5},{8,10},{9,11},{10,... | collective-permute-start | bytes 602120 | tf_op jit(solution)/shard_map/ppermute | solution.py:315
  8.8 10.5 %collective-permute-start.8 = (bf16[784,128]{1,0:T(8,128)(2,1)S(1)}, bf16[784,128]{1,0:T(8,128)(2,1)S(1)}, u32[]{:S(2)}, u32[]{:S(2)}) collective-permute-start(bf16[784,128]{1,0:T(8,128)(2,1)S(1)} %get-tuple-element.30.refs_0_.refs_3_), channel_id=1, source_target_pairs={{20,0},{0,8},{8,24},{24,16},{16,4},{4,12},{12,28},{28,20},{21,1},{... | collective-permute-start | bytes 602120 | tf_op jit(solution)/shard_map/ppermute | solution.py:309
  12.0 11.7 %collective-permute-start.6 = (bf16[784,128]{1,0:T(8,128)(2,1)S(1)}, bf16[784,128]{1,0:T(8,128)(2,1)S(1)}, u32[]{:S(2)}, u32[]{:S(2)}) collective-permute-start(bf16[784,128]{1,0:T(8,128)(2,1)S(1)} %collective-permute-done.refs_1_.refs_2_), channel_id=1, source_target_pairs={{20,0},{0,8},{8,24},{24,16},{16,4},{4,12},{12,28},{28,20},{21,1},{... | collective-permute-start | bytes 602120 | tf_op jit(solution)/shard_map/ppermute | solution.py:309
  16.1 7.6 %collective-permute-start.5 = (bf16[784,128]{1,0:T(8,128)(2,1)S(1)}, bf16[784,128]{1,0:T(8,128)(2,1)S(1)}, u32[]{:S(2)}, u32[]{:S(2)}) collective-permute-start(bf16[784,128]{1,0:T(8,128)(2,1)S(1)} %collective-permute-done.refs_1_.refs_2_), channel_id=1, source_target_pairs={{8,0},{24,8},{16,24},{4,16},{12,4},{28,12},{20,28},{0,20},{9,1},{2... | collective-permute-start | bytes 602120 | tf_op jit(solution)/shard_map/ppermute | solution.py:309
  16.1 7.6 %collective-permute-start.1 = (bf16[784,128]{1,0:T(8,128)(2,1)S(1)}, bf16[784,128]{1,0:T(8,128)(2,1)S(1)}, u32[]{:S(2)}, u32[]{:S(2)}) collective-permute-start(bf16[784,128]{1,0:T(8,128)(2,1)S(1)} %get-tuple-element.28), channel_id=1, source_target_pairs={{0,3},{1,2},{2,1},{3,0},{4,7},{5,6},{6,5},{7,4},{8,11},{9,10},{10,... | collective-permute-start | bytes 602120 | tf_op jit(solution)/shard_map/ppermute | solution.py:315
  19.3 10.1 %collective-permute-start.11 = (bf16[1,784,128]{2,1,0:T(8,128)(2,1)S(1)}, bf16[1,784,128]{2,1,0:T(8,128)(2,1)S(1)}, u32[]{:S(2)}, u32[]{:S(2)}) collective-permute-start(bf16[1,784,128]{2,1,0:T(8,128)(2,1)S(1)} %shard_map.41), channel_id=1, source_target_pairs={{20,0},{0,8},{8,24},{24,16},{16,4},{4,12},{12,28},{28,20},{21,1},{... | collective-permute-start | bytes 602120 | tf_op jit(solution)/shard_map/ppermute | solution.py:309
  20.7 8.7 %collective-permute-start.9 = (bf16[1,784,128]{2,1,0:T(8,128)(2,1)S(1)}, bf16[1,784,128]{2,1,0:T(8,128)(2,1)S(1)}, u32[]{:S(2)}, u32[]{:S(2)}) collective-permute-start(bf16[1,784,128]{2,1,0:T(8,128)(2,1)S(1)} %shard_map.41), channel_id=1, source_target_pairs={{8,0},{24,8},{16,24},{4,16},{12,4},{28,12},{20,28},{0,20},{9,1},{2... | collective-permute-start | bytes 602120 | tf_op jit(solution)/shard_map/ppermute | solution.py:309
  23.8 4.1 %collective-permute-start.3 = (bf16[4,784,128]{2,1,0:T(8,128)(2,1)S(1)}, bf16[4,784,128]{2,1,0:T(8,128)(2,1)S(1)}, u32[]{:S(2)}, u32[]{:S(2)}) collective-permute-start(bf16[4,784,128]{2,1,0:T(8,128)(2,1)S(1)} %shard_map.39), channel_id=1, source_target_pairs={{4,0},{12,8},{28,24},{20,16},{0,4},{8,12},{24,28},{16,20},{5,1},{1... | collective-permute-start | bytes 2408456 | tf_op jit(solution)/shard_map/ppermute | solution.py:309
  25.8 7.5 %collective-permute-start.10 = (bf16[1,784,128]{2,1,0:T(8,128)(2,1)S(1)}, bf16[1,784,128]{2,1,0:T(8,128)(2,1)S(1)}, u32[]{:S(2)}, u32[]{:S(2)}) collective-permute-start(bf16[1,784,128]{2,1,0:T(8,128)(2,1)S(1)} %shard_map.40), channel_id=1, source_target_pairs={{20,0},{0,8},{8,24},{24,16},{16,4},{4,12},{12,28},{28,20},{21,1},{... | collective-permute-start | bytes 602120 | tf_op jit(solution)/shard_map/ppermute | solution.py:309
  26.0 7.3 %collective-permute-start.7 = (bf16[1,784,128]{2,1,0:T(8,128)(2,1)S(1)}, bf16[1,784,128]{2,1,0:T(8,128)(2,1)S(1)}, u32[]{:S(2)}, u32[]{:S(2)}) collective-permute-start(bf16[1,784,128]{2,1,0:T(8,128)(2,1)S(1)} %shard_map.40), channel_id=1, source_target_pairs={{8,0},{24,8},{16,24},{4,16},{12,4},{28,12},{20,28},{0,20},{9,1},{2... | collective-permute-start | bytes 602120 | tf_op jit(solution)/shard_map/ppermute | solution.py:309

commit v17 on v16

--- a/solution.py
+++ b/solution.py
@@ -360,7 +360,7 @@
         held[r] = [(got[r], k) for k in range(groups)]
     everything = [(0, 0, False)]
     everything += [(offsets.index(a), offsets.index(b), both) for a, b, both in pairs]
-    steps = [[] for _ in range(3)]
+    steps = [[] for _ in range(4)]
     final = [0] * roles
     for left, right, both in everything:
         for left_ks in (early, late):
@@ -369,7 +369,7 @@
                     step = 0
                     for role, ks in ((left, left_ks), (right, right_ks)):
                         if role in near:
-                            step = max(step, 1 if ks is early else 2)
+                            step = max(step, 1 if ks is early else 3 if role == near[0] else 2)
                     task = (left, left_ks, right, right_ks, both)
                     if both and right_ks is late and left_ks is early:
                         task = (right, right_ks, left, left_ks, both)

time: 47.8 us -> 47.2 us (0.987)
  blocking collectives: 12.4 us -> 11.6 us
    all_to_all x1, blocking collectives: 12.4 us -> 11.6 us  [per_device(): lax.all_to_all(best, ('shard', 'group'), split_axis=0, concat_axis=0, til...]
    pallas_call x10 -> x11, Pallas kernels: 7.52 us -> 7.77 us  [call(): pl.pallas_call(kernel, out_shape=out_shape, in_specs=in_specs or in_vmem(...]
  transfers between devices with their start and end apart: 12 -> 12, of which waited for: 5 -> 5; matrix products, arithmetic and copies ran while one was open for 0% -> 0% of each run, Pallas kernels for 7% -> 9%
where the time goes in v17:
time: 47.2 us; the launch traced here: 47 us
  starting transfers between devices  20.2 us (43%)
  blocking collectives  11.6 us (25%)
  Pallas kernels  7.77 us (16%)
  waiting for transfers between devices  7.41 us (16%)
    ppermute x9, starting transfers between devices, from_offset(): return lax.ppermute(x, 'shard', perm)  12 us
    all_to_all x1, blocking collectives, per_device(): lax.all_to_all(best, ('shard', 'group'), split_axis=0, concat_axis=0, til...  11.6 us
    ppermute x3, starting transfers between devices, exchange(): got[k] = lax.ppermute(block, 'group', [(z, z ^ k) for z in range(groups)])  8.15 us
    pallas_call x11, Pallas kernels, call(): pl.pallas_call(kernel, out_shape=out_shape, in_specs=in_specs or in_vmem(...  7.77 us
    ppermute x9, waiting for transfers between devices, from_offset(): return lax.ppermute(x, 'shard', perm)  3.77 us
    ppermute x3, waiting for transfers between devices, exchange(): got[k] = lax.ppermute(block, 'group', [(z, z ^ k) for z in range(groups)])  3.65 us
  transfers between devices with their start and end apart: 12, of which 5 were waited for; matrix products, arithmetic and copies ran while one was open for 0% of the time, Pallas kernels for 9%

profile of v17, /device:TPU:0, one launch (start us, length us, event | category | flops | bytes accessed | tf_op | source)
XLA Modules:
  0.0 47.0 jit_solution(2186435705485406297)
XLA Ops:
  0.0 0.0 copy-start.1
  0.0 0.0 copy-start
  0.0 1.5 %shard_map.37.refs_0_ = bf16[512,768]{1,0:T(8,128)(2,1)S(1)} custom-call(bf16[512,768]{1,0:T(8,128)(2,1)} %far_ref.1), custom_call_target="tpu_custom_call" | custom-call | flops 1572864 | bytes 1572864 | tf_op jit(solution)/shard_map/pallas_call | solution.py:227
  1.5 0.0 copy-done.1
  1.5 0.0 copy-done
  1.5 0.9 %shard_map.38 = (bf16[784,128]{1,0:T(8,128)(2,1)S(1)}, bf16[784,128]{1,0:T(8,128)(2,1)S(1)}, bf16[784,128]{1,0:T(8,128)(2,1)S(1)}, bf16[784,128]{1,0:T(8,128)(2,1)S(1)}, s32[1,512]{1,0:T(1,128)S(1)}) custom-call(bf16[512,768]{1,0:T(8,128)(2,1)S(1)} %shard_map.37.refs_0_, s32[1,512]{1,0:T(1,128)S(1)} %bitcast.3, s32[1,512]{1,0:T(1,128)S(1)} %bitcast.4), custom_call_target="tpu_custom_call" | custom-call | flops 402653184 | bytes 1572864 | tf_op jit(solution)/shard_map/pallas_call | solution.py:227
  2.5 3.1 %collective-permute-start = (bf16[784,128]{1,0:T(8,128)(2,1)S(1)}, bf16[784,128]{1,0:T(8,128)(2,1)S(1)}, u32[]{:S(2)}, u32[]{:S(2)}) collective-permute-start(bf16[784,128]{1,0:T(8,128)(2,1)S(1)} %get-tuple-element.29), channel_id=1, source_target_pairs={{0,1},{1,0},{2,3},{3,2},{4,5},{5,4},{6,7},{7,6},{8,9},{9,8},{10,11... | collective-permute-start | bytes 602120 | tf_op jit(solution)/shard_map/ppermute | solution.py:315
  5.6 0.7 %collective-permute-start.4 = (bf16[784,128]{1,0:T(8,128)(2,1)S(1)}, bf16[784,128]{1,0:T(8,128)(2,1)S(1)}, u32[]{:S(2)}, u32[]{:S(2)}) collective-permute-start(bf16[784,128]{1,0:T(8,128)(2,1)S(1)} %get-tuple-element.32.refs_0_.refs_3_), channel_id=1, source_target_pairs={{8,0},{24,8},{16,24},{4,16},{12,4},{28,12},{20,28},{0,20},{9,1},{2... | collective-permute-start | bytes 602120 | tf_op jit(solution)/shard_map/ppermute | solution.py:309
  6.2 2.6 %collective-permute-start.2 = (bf16[784,128]{1,0:T(8,128)(2,1)S(1)}, bf16[784,128]{1,0:T(8,128)(2,1)S(1)}, u32[]{:S(2)}, u32[]{:S(2)}) collective-permute-start(bf16[784,128]{1,0:T(8,128)(2,1)S(1)} %get-tuple-element.31), channel_id=1, source_target_pairs={{0,2},{1,3},{2,0},{3,1},{4,6},{5,7},{6,4},{7,5},{8,10},{9,11},{10,... | collective-permute-start | bytes 602120 | tf_op jit(solution)/shard_map/ppermute | solution.py:315
  8.8 1.3 %collective-permute-start.5 = (bf16[784,128]{1,0:T(8,128)(2,1)S(1)}, bf16[784,128]{1,0:T(8,128)(2,1)S(1)}, u32[]{:S(2)}, u32[]{:S(2)}) collective-permute-start(bf16[784,128]{1,0:T(8,128)(2,1)S(1)} %get-tuple-element.32.refs_0_.refs_3_), channel_id=1, source_target_pairs={{20,0},{0,8},{8,24},{24,16},{16,4},{4,12},{12,28},{28,20},{21,1},{... | collective-permute-start | bytes 602120 | tf_op jit(solution)/shard_map/ppermute | solution.py:309
  10.2 0.4 collective-permute-done.refs_1_.refs_2_
  10.5 1.5 %collective-permute-done.4.refs_7_ = bf16[784,128]{1,0:T(8,128)(2,1)S(1)} collective-permute-done((bf16[784,128]{1,0:T(8,128)(2,1)S(1)}, bf16[784,128]{1,0:T(8,128)(2,1)S(1)}, u32[]{:S(2)}, u32[]{:S(2)}) %collective-permute-start.4) | collective-permute-done | bytes 200736 | tf_op jit(solution)/shard_map/ppermute | solution.py:309
  12.0 4.1 %collective-permute-start.8 = (bf16[784,128]{1,0:T(8,128)(2,1)S(1)}, bf16[784,128]{1,0:T(8,128)(2,1)S(1)}, u32[]{:S(2)}, u32[]{:S(2)}) collective-permute-start(bf16[784,128]{1,0:T(8,128)(2,1)S(1)} %collective-permute-done.refs_1_.refs_2_), channel_id=1, source_target_pairs={{20,0},{0,8},{8,24},{24,16},{16,4},{4,12},{12,28},{28,20},{21,1},{... | collective-permute-start | bytes 602120 | tf_op jit(solution)/shard_map/ppermute | solution.py:309
  16.1 0.0 collective-permute-start.7
  16.1 2.5 %collective-permute-start.1 = (bf16[784,128]{1,0:T(8,128)(2,1)S(1)}, bf16[784,128]{1,0:T(8,128)(2,1)S(1)}, u32[]{:S(2)}, u32[]{:S(2)}) collective-permute-start(bf16[784,128]{1,0:T(8,128)(2,1)S(1)} %get-tuple-element.30), channel_id=1, source_target_pairs={{0,3},{1,2},{2,1},{3,0},{4,7},{5,6},{6,5},{7,4},{8,11},{9,10},{10,... | collective-permute-start | bytes 602120 | tf_op jit(solution)/shard_map/ppermute | solution.py:315
  18.6 0.7 %collective-permute-done.2.refs_2_.refs_0_.refs_1_ = bf16[784,128]{1,0:T(8,128)(2,1)S(1)} collective-permute-done((bf16[784,128]{1,0:T(8,128)(2,1)S(1)}, bf16[784,128]{1,0:T(8,128)(2,1)S(1)}, u32[]{:S(2)}, u32[]{:S(2)}) %collective-permute-start.2) | collective-permute-done | bytes 200736 | tf_op jit(solution)/shard_map/ppermute | solution.py:315
  19.3 0.0 collective-permute-done.5.refs_10_.refs_4_
  19.3 1.4 %collective-permute-start.10 = (bf16[1,784,128]{2,1,0:T(8,128)(2,1)S(1)}, bf16[1,784,128]{2,1,0:T(8,128)(2,1)S(1)}, u32[]{:S(2)}, u32[]{:S(2)}) collective-permute-start(bf16[1,784,128]{2,1,0:T(8,128)(2,1)S(1)} %shard_map.40), channel_id=1, source_target_pairs={{20,0},{0,8},{8,24},{24,16},{16,4},{4,12},{12,28},{28,20},{21,1},{... | collective-permute-start | bytes 602120 | tf_op jit(solution)/shard_map/ppermute | solution.py:309
  20.7 0.4 collective-permute-start.6
  21.1 2.6 %collective-permute-done.1.refs_3_.refs_0_ = bf16[784,128]{1,0:T(8,128)(2,1)S(1)} collective-permute-done((bf16[784,128]{1,0:T(8,128)(2,1)S(1)}, bf16[784,128]{1,0:T(8,128)(2,1)S(1)}, u32[]{:S(2)}, u32[]{:S(2)}) %collective-permute-start.1) | collective-permute-done | bytes 200736 | tf_op jit(solution)/shard_map/ppermute | solution.py:315
  23.7 0.0 collective-permute-done.8.refs_9_.refs_3_
  23.7 0.0 collective-permute-done.7.refs_6_
  23.7 0.1 shard_map.39
  23.8 2.0 %collective-permute-start.3 = (bf16[4,784,128]{2,1,0:T(8,128)(2,1)S(1)}, bf16[4,784,128]{2,1,0:T(8,128)(2,1)S(1)}, u32[]{:S(2)}, u32[]{:S(2)}) collective-permute-start(bf16[4,784,128]{2,1,0:T(8,128)(2,1)S(1)} %shard_map.39), channel_id=1, source_target_pairs={{4,0},{12,8},{28,24},{20,16},{0,4},{8,12},{24,28},{16,20},{5,1},{1... | collective-permute-start | bytes 2408456 | tf_op jit(solution)/shard_map/ppermute | solution.py:309
  25.8 0.2 collective-permute-start.9
  26.0 1.9 %collective-permute-start.11 = (bf16[1,784,128]{2,1,0:T(8,128)(2,1)S(1)}, bf16[1,784,128]{2,1,0:T(8,128)(2,1)S(1)}, u32[]{:S(2)}, u32[]{:S(2)}) collective-permute-start(bf16[1,784,128]{2,1,0:T(8,128)(2,1)S(1)} %shard_map.41), channel_id=1, source_target_pairs={{8,0},{24,8},{16,24},{4,16},{12,4},{28,12},{20,28},{0,20},{9,1},{2... | collective-permute-start | bytes 602120 | tf_op jit(solution)/shard_map/ppermute | solution.py:309
  27.9 0.0 collective-permute-done.3.refs_4_
  27.9 1.5 %shard_map.42 = (f32[4,8,512]{2,1,0:T(8,128)S(1)}, bf16[2,512,768]{2,1,0:T(8,128)(2,1)S(1)}) custom-call(bf16[784,128]{1,0:T(8,128)(2,1)S(1)} %collective-permute-done.1.refs_3_.refs_0_, bf16[784,128]{1,0:T(8,128)(2,1)S(1)} %collective-permute-done.2.refs_2_.refs_0_.refs_1_, bf16[784,128]{1,0:T(8,128)(2,1)S(1)} %collective-permute-done.refs_1_.refs_2_, ...), custom_call_target="tpu_custom_call" | custom-call | flops 805306368 | bytes 1572864 | tf_op jit(solution)/shard_map/pallas_call | solution.py:227
  29.4 0.0 collective-permute-done.10.refs_8_.refs_2_
  29.4 0.0 collective-permute-done.6.refs_5_
  29.4 1.6 %shard_map.43 = (f32[4,8,512]{2,1,0:T(8,128)S(1)}, bf16[2,512,768]{2,1,0:T(8,128)(2,1)S(1)}) custom-call(bf16[784,128]{1,0:T(8,128)(2,1)S(1)} %collective-permute-done.1.refs_3_.refs_0_, bf16[784,128]{1,0:T(8,128)(2,1)S(1)} %collective-permute-done.2.refs_2_.refs_0_.refs_1_, bf16[784,128]{1,0:T(8,128)(2,1)S(1)} %collective-permute-done.refs_1_.refs_2_, ...), custom_call_target="tpu_custom_call" | custom-call | flops 830472192 | bytes 2752512 | tf_op jit(solution)/shard_map/pallas_call | solution.py:227
  31.0 2.3 %collective-permute-done.9.refs_8_.refs_1_ = bf16[1,784,128]{2,1,0:T(8,128)(2,1)S(1)} collective-permute-done((bf16[1,784,128]{2,1,0:T(8,128)(2,1)S(1)}, bf16[1,784,128]{2,1,0:T(8,128)(2,1)S(1)}, u32[]{:S(2)}, u32[]{:S(2)}) %collective-permute-start.9) | collective-permute-done | bytes 200736 | tf_op jit(solution)/shard_map/ppermute | solution.py:309
  33.3 0.8 %shard_map.44 = (f32[4,8,512]{2,1,0:T(8,128)S(1)}, bf16[1,512,768]{2,1,0:T(8,128)(2,1)S(1)}, f32[1,512]{1,0:T(1,128)S(1)}, f32[1,512]{1,0:T(1,128)S(1)}) custom-call(bf16[784,128]{1,0:T(8,128)(2,1)S(1)} %collective-permute-done.1.refs_3_.refs_0_, bf16[784,128]{1,0:T(8,128)(2,1)S(1)} %collective-permute-done.2.refs_2_.refs_0_.refs_1_, ...), custom_call_target="tpu_custom_call" | custom-call | flops 276824064 | bytes 2359296 | tf_op jit(solution)/shard_map/pallas_call | solution.py:227
  34.2 0.0 collective-permute-done.11.refs_0_
  34.2 0.4 shard_map.45
  34.6 0.1 shard_map.46
  34.7 11.6 %all_to_all.5.refs_0_ = f32[32,1,128]{2,1,0:T(1,128)S(1)} all-to-all(f32[32,1,128]{2,1,0:T(1,128)S(1)} %shard_map.46), channel_id=1, replica_groups=mesh['shard'=8,'group'=4] {'shard','group'}, dimensions={0} | all-to-all | bytes 32768 | tf_op jit(solution)/shard_map/all_to_all | solution.py:396
  46.3 0.8 %shard_map.47 = f32[1,512]{1,0:T(1,128)} custom-call(f32[32,1,128]{2,1,0:T(1,128)S(1)} %all_to_all.5.refs_0_, s32[1,512]{1,0:T(1,128)S(1)} %get-tuple-element.46.refs_1_), custom_call_target="tpu_custom_call" | custom-call | flops 262144 | bytes 2048 | tf_op jit(solution)/shard_map/pallas_call | solution.py:227
  (2 shorter events, 0.0 us)
Async XLA Ops:
  0.0 1.5 %copy-start.1 = (s32[512]{0:T(512)S(1)}, s32[512]{0:T(512)}, u32[]{:S(2)}) copy-start(s32[512]{0:T(512)} %param.5) | copy-start | bytes 6148
  0.0 1.5 %copy-start = (s32[512,1]{0,1:T(1,128)S(1)}, s32[512,1]{0,1:T(1,128)}, u32[]{:S(2)}) copy-start(s32[512,1]{0,1:T(1,128)} %param.4) | copy-start | bytes 6148
  2.5 8.1 %collective-permute-start = (bf16[784,128]{1,0:T(8,128)(2,1)S(1)}, bf16[784,128]{1,0:T(8,128)(2,1)S(1)}, u32[]{:S(2)}, u32[]{:S(2)}) collective-permute-start(bf16[784,128]{1,0:T(8,128)(2,1)S(1)} %get-tuple-element.29), channel_id=1, source_target_pairs={{0,1},{1,0},{2,3},{3,2},{4,5},{5,4},{6,7},{7,6},{8,9},{9,8},{10,11... | collective-permute-start | bytes 602120 | tf_op jit(solution)/shard_map/ppermute | solution.py:315
  5.6 6.5 %collective-permute-start.4 = (bf16[784,128]{1,0:T(8,128)(2,1)S(1)}, bf16[784,128]{1,0:T(8,128)(2,1)S(1)}, u32[]{:S(2)}, u32[]{:S(2)}) collective-permute-start(bf16[784,128]{1,0:T(8,128)(2,1)S(1)} %get-tuple-element.32.refs_0_.refs_3_), channel_id=1, source_target_pairs={{8,0},{24,8},{16,24},{4,16},{12,4},{28,12},{20,28},{0,20},{9,1},{2... | collective-permute-start | bytes 602120 | tf_op jit(solution)/shard_map/ppermute | solution.py:309
  6.2 13.1 %collective-permute-start.2 = (bf16[784,128]{1,0:T(8,128)(2,1)S(1)}, bf16[784,128]{1,0:T(8,128)(2,1)S(1)}, u32[]{:S(2)}, u32[]{:S(2)}) collective-permute-start(bf16[784,128]{1,0:T(8,128)(2,1)S(1)} %get-tuple-element.31), channel_id=1, source_target_pairs={{0,2},{1,3},{2,0},{3,1},{4,6},{5,7},{6,4},{7,5},{8,10},{9,11},{10,... | collective-permute-start | bytes 602120 | tf_op jit(solution)/shard_map/ppermute | solution.py:315
  8.8 10.5 %collective-permute-start.5 = (bf16[784,128]{1,0:T(8,128)(2,1)S(1)}, bf16[784,128]{1,0:T(8,128)(2,1)S(1)}, u32[]{:S(2)}, u32[]{:S(2)}) collective-permute-start(bf16[784,128]{1,0:T(8,128)(2,1)S(1)} %get-tuple-element.32.refs_0_.refs_3_), channel_id=1, source_target_pairs={{20,0},{0,8},{8,24},{24,16},{16,4},{4,12},{12,28},{28,20},{21,1},{... | collective-permute-start | bytes 602120 | tf_op jit(solution)/shard_map/ppermute | solution.py:309
  12.0 11.7 %collective-permute-start.8 = (bf16[784,128]{1,0:T(8,128)(2,1)S(1)}, bf16[784,128]{1,0:T(8,128)(2,1)S(1)}, u32[]{:S(2)}, u32[]{:S(2)}) collective-permute-start(bf16[784,128]{1,0:T(8,128)(2,1)S(1)} %collective-permute-done.refs_1_.refs_2_), channel_id=1, source_target_pairs={{20,0},{0,8},{8,24},{24,16},{16,4},{4,12},{12,28},{28,20},{21,1},{... | collective-permute-start | bytes 602120 | tf_op jit(solution)/shard_map/ppermute | solution.py:309
  16.1 7.6 %collective-permute-start.7 = (bf16[784,128]{1,0:T(8,128)(2,1)S(1)}, bf16[784,128]{1,0:T(8,128)(2,1)S(1)}, u32[]{:S(2)}, u32[]{:S(2)}) collective-permute-start(bf16[784,128]{1,0:T(8,128)(2,1)S(1)} %collective-permute-done.refs_1_.refs_2_), channel_id=1, source_target_pairs={{8,0},{24,8},{16,24},{4,16},{12,4},{28,12},{20,28},{0,20},{9,1},{2... | collective-permute-start | bytes 602120 | tf_op jit(solution)/shard_map/ppermute | solution.py:309
  16.1 7.6 %collective-permute-start.1 = (bf16[784,128]{1,0:T(8,128)(2,1)S(1)}, bf16[784,128]{1,0:T(8,128)(2,1)S(1)}, u32[]{:S(2)}, u32[]{:S(2)}) collective-permute-start(bf16[784,128]{1,0:T(8,128)(2,1)S(1)} %get-tuple-element.30), channel_id=1, source_target_pairs={{0,3},{1,2},{2,1},{3,0},{4,7},{5,6},{6,5},{7,4},{8,11},{9,10},{10,... | collective-permute-start | bytes 602120 | tf_op jit(solution)/shard_map/ppermute | solution.py:315
  19.3 10.1 %collective-permute-start.10 = (bf16[1,784,128]{2,1,0:T(8,128)(2,1)S(1)}, bf16[1,784,128]{2,1,0:T(8,128)(2,1)S(1)}, u32[]{:S(2)}, u32[]{:S(2)}) collective-permute-start(bf16[1,784,128]{2,1,0:T(8,128)(2,1)S(1)} %shard_map.40), channel_id=1, source_target_pairs={{20,0},{0,8},{8,24},{24,16},{16,4},{4,12},{12,28},{28,20},{21,1},{... | collective-permute-start | bytes 602120 | tf_op jit(solution)/shard_map/ppermute | solution.py:309
  20.7 8.7 %collective-permute-start.6 = (bf16[1,784,128]{2,1,0:T(8,128)(2,1)S(1)}, bf16[1,784,128]{2,1,0:T(8,128)(2,1)S(1)}, u32[]{:S(2)}, u32[]{:S(2)}) collective-permute-start(bf16[1,784,128]{2,1,0:T(8,128)(2,1)S(1)} %shard_map.40), channel_id=1, source_target_pairs={{8,0},{24,8},{16,24},{4,16},{12,4},{28,12},{20,28},{0,20},{9,1},{2... | collective-permute-start | bytes 602120 | tf_op jit(solution)/shard_map/ppermute | solution.py:309
  23.8 4.1 %collective-permute-start.3 = (bf16[4,784,128]{2,1,0:T(8,128)(2,1)S(1)}, bf16[4,784,128]{2,1,0:T(8,128)(2,1)S(1)}, u32[]{:S(2)}, u32[]{:S(2)}) collective-permute-start(bf16[4,784,128]{2,1,0:T(8,128)(2,1)S(1)} %shard_map.39), channel_id=1, source_target_pairs={{4,0},{12,8},{28,24},{20,16},{0,4},{8,12},{24,28},{16,20},{5,1},{1... | collective-permute-start | bytes 2408456 | tf_op jit(solution)/shard_map/ppermute | solution.py:309
  25.8 7.5 %collective-permute-start.9 = (bf16[1,784,128]{2,1,0:T(8,128)(2,1)S(1)}, bf16[1,784,128]{2,1,0:T(8,128)(2,1)S(1)}, u32[]{:S(2)}, u32[]{:S(2)}) collective-permute-start(bf16[1,784,128]{2,1,0:T(8,128)(2,1)S(1)} %shard_map.41), channel_id=1, source_target_pairs={{20,0},{0,8},{8,24},{24,16},{16,4},{4,12},{12,28},{28,20},{21,1},{... | collective-permute-start | bytes 602120 | tf_op jit(solution)/shard_map/ppermute | solution.py:309
  26.0 8.1 %collective-permute-start.11 = (bf16[1,784,128]{2,1,0:T(8,128)(2,1)S(1)}, bf16[1,784,128]{2,1,0:T(8,128)(2,1)S(1)}, u32[]{:S(2)}, u32[]{:S(2)}) collective-permute-start(bf16[1,784,128]{2,1,0:T(8,128)(2,1)S(1)} %shard_map.41), channel_id=1, source_target_pairs={{8,0},{24,8},{16,24},{4,16},{12,4},{28,12},{20,28},{0,20},{9,1},{2... | collective-permute-start | bytes 602120 | tf_op jit(solution)/shard_map/ppermute | solution.py:309

commit v18 on v17

--- a/solution.py
+++ b/solution.py
@@ -311,14 +311,13 @@
     def exchange(blocks):
         got = list(blocks)
         for k in range(1, groups):
-            block = after(blocks[k], got[1]) if k > 2 else blocks[k]
-            got[k] = lax.ppermute(block, "group", [(z, z ^ k) for z in range(groups)])
+            got[k] = lax.ppermute(blocks[k], "group", [(z, z ^ k) for z in range(groups)])
         return got
 
     (units,) = call(
         unit_kernel,
         [jax.ShapeDtypeStruct((rows, width), jnp.bfloat16)],
-        [pltpu.VMEM((rows, width), embeddings.dtype), pltpu.SemaphoreType.DMA((4,))],
+        [pltpu.VMEM((rows, width), embeddings.dtype), pltpu.SemaphoreType.DMA((8,))],
         (embeddings,),
         4 * rows * width,
         4 * rows * width,

time: 47.2 us -> 48.3 us (1.023)
  waiting for transfers between devices: 7.41 us -> 12.7 us
  starting transfers between devices: 20.2 us -> 15.9 us
    ppermute x3, waiting for transfers between devices: 3.65 us -> 8.53 us  [exchange(): lax.ppermute(blocks[k], 'group', [(z, z ^ k) for z in range(groups)])]
    ppermute x3, starting transfers between devices: 8.15 us -> 5.68 us  [exchange(): lax.ppermute(blocks[k], 'group', [(z, z ^ k) for z in range(groups)])]
    ppermute x9, starting transfers between devices: 12 us -> 10.3 us  [from_offset(): return lax.ppermute(x, 'shard', perm)]
  transfers between devices with their start and end apart: 12 -> 12, of which waited for: 5 -> 5; matrix products, arithmetic and copies ran while one was open for 0% -> 0% of each run, Pallas kernels for 9% -> 8%
where the time goes in v18:
time: 48.3 us; the launch traced here: 48.2 us
  starting transfers between devices  15.9 us (33%)
  waiting for transfers between devices  12.7 us (26%)
  blocking collectives  11.3 us (23%)
  Pallas kernels  8.12 us (17%)
    all_to_all x1, blocking collectives, per_device(): lax.all_to_all(best, ('shard', 'group'), split_axis=0, concat_axis=0, til...  11.3 us
    ppermute x9, starting transfers between devices, from_offset(): return lax.ppermute(x, 'shard', perm)  10.3 us
    ppermute x3, waiting for transfers between devices, exchange(): lax.ppermute(blocks[k], 'group', [(z, z ^ k) for z in range(groups)])  8.53 us
    pallas_call x11, Pallas kernels, call(): pl.pallas_call(kernel, out_shape=out_shape, in_specs=in_specs or in_vmem(...  8.12 us
    ppermute x3, starting transfers between devices, exchange(): lax.ppermute(blocks[k], 'group', [(z, z ^ k) for z in range(groups)])  5.68 us
    ppermute x9, waiting for transfers between devices, from_offset(): return lax.ppermute(x, 'shard', perm)  4.16 us
  transfers between devices with their start and end apart: 12, of which 5 were waited for; matrix products, arithmetic and copies ran while one was open for 0% of the time, Pallas kernels for 8%

profile of v18, /device:TPU:0, one launch (start us, length us, event | category | flops | bytes accessed | tf_op | source)
XLA Modules:
  0.0 48.2 jit_solution(18405668366568834042)
XLA Ops:
  0.0 0.0 copy-start.1
  0.0 0.0 copy-start
  0.0 1.9 %shard_map.37.refs_0_ = bf16[512,768]{1,0:T(8,128)(2,1)S(1)} custom-call(bf16[512,768]{1,0:T(8,128)(2,1)} %far_ref.1), custom_call_target="tpu_custom_call" | custom-call | flops 1572864 | bytes 1572864 | tf_op jit(solution)/shard_map/pallas_call | solution.py:227
  1.9 0.0 copy-done.1
  1.9 0.0 copy-done
  1.9 0.9 %shard_map.38 = (bf16[784,128]{1,0:T(8,128)(2,1)S(1)}, bf16[784,128]{1,0:T(8,128)(2,1)S(1)}, bf16[784,128]{1,0:T(8,128)(2,1)S(1)}, bf16[784,128]{1,0:T(8,128)(2,1)S(1)}, s32[1,512]{1,0:T(1,128)S(1)}) custom-call(bf16[512,768]{1,0:T(8,128)(2,1)S(1)} %shard_map.37.refs_0_, s32[1,512]{1,0:T(1,128)S(1)} %bitcast.3, s32[1,512]{1,0:T(1,128)S(1)} %bitcast.4), custom_call_target="tpu_custom_call" | custom-call | flops 402653184 | bytes 1572864 | tf_op jit(solution)/shard_map/pallas_call | solution.py:227
  2.8 3.1 %collective-permute-start.2 = (bf16[784,128]{1,0:T(8,128)(2,1)S(1)}, bf16[784,128]{1,0:T(8,128)(2,1)S(1)}, u32[]{:S(2)}, u32[]{:S(2)}) collective-permute-start(bf16[784,128]{1,0:T(8,128)(2,1)S(1)} %get-tuple-element.29), channel_id=1, source_target_pairs={{0,1},{1,0},{2,3},{3,2},{4,5},{5,4},{6,7},{7,6},{8,9},{9,8},{10,11... | collective-permute-start | bytes 602120 | tf_op jit(solution)/shard_map/ppermute | solution.py:314
  5.9 0.7 %collective-permute-start.4 = (bf16[784,128]{1,0:T(8,128)(2,1)S(1)}, bf16[784,128]{1,0:T(8,128)(2,1)S(1)}, u32[]{:S(2)}, u32[]{:S(2)}) collective-permute-start(bf16[784,128]{1,0:T(8,128)(2,1)S(1)} %get-tuple-element.30.refs_0_.refs_3_), channel_id=1, source_target_pairs={{8,0},{24,8},{16,24},{4,16},{12,4},{28,12},{20,28},{0,20},{9,1},{2... | collective-permute-start | bytes 602120 | tf_op jit(solution)/shard_map/ppermute | solution.py:309
  6.6 2.6 %collective-permute-start.1 = (bf16[784,128]{1,0:T(8,128)(2,1)S(1)}, bf16[784,128]{1,0:T(8,128)(2,1)S(1)}, u32[]{:S(2)}, u32[]{:S(2)}) collective-permute-start(bf16[784,128]{1,0:T(8,128)(2,1)S(1)} %get-tuple-element.28), channel_id=1, source_target_pairs={{0,2},{1,3},{2,0},{3,1},{4,6},{5,7},{6,4},{7,5},{8,10},{9,11},{10,... | collective-permute-start | bytes 602120 | tf_op jit(solution)/shard_map/ppermute | solution.py:314
  9.2 1.3 %collective-permute-start.5 = (bf16[784,128]{1,0:T(8,128)(2,1)S(1)}, bf16[784,128]{1,0:T(8,128)(2,1)S(1)}, u32[]{:S(2)}, u32[]{:S(2)}) collective-permute-start(bf16[784,128]{1,0:T(8,128)(2,1)S(1)} %get-tuple-element.30.refs_0_.refs_3_), channel_id=1, source_target_pairs={{20,0},{0,8},{8,24},{24,16},{16,4},{4,12},{12,28},{28,20},{21,1},{... | collective-permute-start | bytes 602120 | tf_op jit(solution)/shard_map/ppermute | solution.py:309
  10.5 0.0 collective-permute-start
  10.5 0.4 collective-permute-done.2.refs_1_.refs_2_
  10.9 1.5 %collective-permute-done.4.refs_7_ = bf16[784,128]{1,0:T(8,128)(2,1)S(1)} collective-permute-done((bf16[784,128]{1,0:T(8,128)(2,1)S(1)}, bf16[784,128]{1,0:T(8,128)(2,1)S(1)}, u32[]{:S(2)}, u32[]{:S(2)}) %collective-permute-start.4) | collective-permute-done | bytes 200736 | tf_op jit(solution)/shard_map/ppermute | solution.py:309
  12.4 3.4 %collective-permute-start.8 = (bf16[784,128]{1,0:T(8,128)(2,1)S(1)}, bf16[784,128]{1,0:T(8,128)(2,1)S(1)}, u32[]{:S(2)}, u32[]{:S(2)}) collective-permute-start(bf16[784,128]{1,0:T(8,128)(2,1)S(1)} %collective-permute-done.2.refs_1_.refs_2_), channel_id=1, source_target_pairs={{20,0},{0,8},{8,24},{24,16},{16,4},{4,12},{12,28},{28,20},{21,1},{... | collective-permute-start | bytes 602120 | tf_op jit(solution)/shard_map/ppermute | solution.py:309
  15.8 0.0 collective-permute-start.7
  15.8 8.2 %collective-permute-done.1.refs_2_.refs_0_.refs_1_ = bf16[784,128]{1,0:T(8,128)(2,1)S(1)} collective-permute-done((bf16[784,128]{1,0:T(8,128)(2,1)S(1)}, bf16[784,128]{1,0:T(8,128)(2,1)S(1)}, u32[]{:S(2)}, u32[]{:S(2)}) %collective-permute-start.1) | collective-permute-done | bytes 200736 | tf_op jit(solution)/shard_map/ppermute | solution.py:314
  24.0 0.0 collective-permute-done.5.refs_10_.refs_4_
  24.0 1.5 %collective-permute-start.10 = (bf16[1,784,128]{2,1,0:T(8,128)(2,1)S(1)}, bf16[1,784,128]{2,1,0:T(8,128)(2,1)S(1)}, u32[]{:S(2)}, u32[]{:S(2)}) collective-permute-start(bf16[1,784,128]{2,1,0:T(8,128)(2,1)S(1)} %shard_map.40), channel_id=1, source_target_pairs={{20,0},{0,8},{8,24},{24,16},{16,4},{4,12},{12,28},{28,20},{21,1},{... | collective-permute-start | bytes 602120 | tf_op jit(solution)/shard_map/ppermute | solution.py:309
  25.5 0.3 collective-permute-start.6
  25.8 0.0 collective-permute-done.refs_3_.refs_0_
  25.8 0.1 shard_map.39
  25.9 0.9 %collective-permute-start.3 = (bf16[4,784,128]{2,1,0:T(8,128)(2,1)S(1)}, bf16[4,784,128]{2,1,0:T(8,128)(2,1)S(1)}, u32[]{:S(2)}, u32[]{:S(2)}) collective-permute-start(bf16[4,784,128]{2,1,0:T(8,128)(2,1)S(1)} %shard_map.39), channel_id=1, source_target_pairs={{4,0},{12,8},{28,24},{20,16},{0,4},{8,12},{24,28},{16,20},{5,1},{1... | collective-permute-start | bytes 2408456 | tf_op jit(solution)/shard_map/ppermute | solution.py:309
  26.8 0.0 collective-permute-done.8.refs_9_.refs_3_
  26.8 0.0 collective-permute-done.7.refs_6_
  26.8 0.9 %collective-permute-start.9 = (bf16[1,784,128]{2,1,0:T(8,128)(2,1)S(1)}, bf16[1,784,128]{2,1,0:T(8,128)(2,1)S(1)}, u32[]{:S(2)}, u32[]{:S(2)}) collective-permute-start(bf16[1,784,128]{2,1,0:T(8,128)(2,1)S(1)} %shard_map.41), channel_id=1, source_target_pairs={{20,0},{0,8},{8,24},{24,16},{16,4},{4,12},{12,28},{28,20},{21,1},{... | collective-permute-start | bytes 602120 | tf_op jit(solution)/shard_map/ppermute | solution.py:309
  27.7 1.1 %collective-permute-start.11 = (bf16[1,784,128]{2,1,0:T(8,128)(2,1)S(1)}, bf16[1,784,128]{2,1,0:T(8,128)(2,1)S(1)}, u32[]{:S(2)}, u32[]{:S(2)}) collective-permute-start(bf16[1,784,128]{2,1,0:T(8,128)(2,1)S(1)} %shard_map.41), channel_id=1, source_target_pairs={{8,0},{24,8},{16,24},{4,16},{12,4},{28,12},{20,28},{0,20},{9,1},{2... | collective-permute-start | bytes 602120 | tf_op jit(solution)/shard_map/ppermute | solution.py:309
  28.9 0.0 collective-permute-done.3.refs_4_
  28.9 1.5 %shard_map.42 = (f32[4,8,512]{2,1,0:T(8,128)S(1)}, bf16[2,512,768]{2,1,0:T(8,128)(2,1)S(1)}) custom-call(bf16[784,128]{1,0:T(8,128)(2,1)S(1)} %collective-permute-done.refs_3_.refs_0_, bf16[784,128]{1,0:T(8,128)(2,1)S(1)} %collective-permute-done.1.refs_2_.refs_0_.refs_1_, bf16[784,128]{1,0:T(8,128)(2,1)S(1)} %collective-permute-done.2.refs_1_.refs_2_, ...), custom_call_target="tpu_custom_call" | custom-call | flops 805306368 | bytes 1572864 | tf_op jit(solution)/shard_map/pallas_call | solution.py:227
  30.4 0.0 collective-permute-done.10.refs_8_.refs_2_
  30.4 1.3 %collective-permute-done.6.refs_5_ = bf16[1,784,128]{2,1,0:T(8,128)(2,1)S(1)} collective-permute-done((bf16[1,784,128]{2,1,0:T(8,128)(2,1)S(1)}, bf16[1,784,128]{2,1,0:T(8,128)(2,1)S(1)}, u32[]{:S(2)}, u32[]{:S(2)}) %collective-permute-start.6) | collective-permute-done | bytes 200736 | tf_op jit(solution)/shard_map/ppermute | solution.py:309
  31.8 1.6 %shard_map.43 = (f32[4,8,512]{2,1,0:T(8,128)S(1)}, bf16[2,512,768]{2,1,0:T(8,128)(2,1)S(1)}) custom-call(bf16[784,128]{1,0:T(8,128)(2,1)S(1)} %collective-permute-done.refs_3_.refs_0_, bf16[784,128]{1,0:T(8,128)(2,1)S(1)} %collective-permute-done.1.refs_2_.refs_0_.refs_1_, bf16[784,128]{1,0:T(8,128)(2,1)S(1)} %collective-permute-done.2.refs_1_.refs_2_, ...), custom_call_target="tpu_custom_call" | custom-call | flops 830472192 | bytes 2752512 | tf_op jit(solution)/shard_map/pallas_call | solution.py:227
  33.3 1.4 %collective-permute-done.9.refs_8_.refs_1_ = bf16[1,784,128]{2,1,0:T(8,128)(2,1)S(1)} collective-permute-done((bf16[1,784,128]{2,1,0:T(8,128)(2,1)S(1)}, bf16[1,784,128]{2,1,0:T(8,128)(2,1)S(1)}, u32[]{:S(2)}, u32[]{:S(2)}) %collective-permute-start.9) | collective-permute-done | bytes 200736 | tf_op jit(solution)/shard_map/ppermute | solution.py:309
  34.7 0.8 %shard_map.44 = (f32[4,8,512]{2,1,0:T(8,128)S(1)}, bf16[1,512,768]{2,1,0:T(8,128)(2,1)S(1)}, f32[1,512]{1,0:T(1,128)S(1)}, f32[1,512]{1,0:T(1,128)S(1)}) custom-call(bf16[784,128]{1,0:T(8,128)(2,1)S(1)} %collective-permute-done.refs_3_.refs_0_, bf16[784,128]{1,0:T(8,128)(2,1)S(1)} %collective-permute-done.1.refs_2_.refs_0_.refs_1_, ...), custom_call_target="tpu_custom_call" | custom-call | flops 276824064 | bytes 2359296 | tf_op jit(solution)/shard_map/pallas_call | solution.py:227
  35.5 0.0 collective-permute-done.11.refs_0_
  35.6 0.5 shard_map.45
  36.0 0.1 shard_map.46
  36.1 11.3 %all_to_all.5.refs_0_ = f32[32,1,128]{2,1,0:T(1,128)S(1)} all-to-all(f32[32,1,128]{2,1,0:T(1,128)S(1)} %shard_map.46), channel_id=1, replica_groups=mesh['shard'=8,'group'=4] {'shard','group'}, dimensions={0} | all-to-all | bytes 32768 | tf_op jit(solution)/shard_map/all_to_all | solution.py:395
  47.4 0.8 %shard_map.47 = f32[1,512]{1,0:T(1,128)} custom-call(f32[32,1,128]{2,1,0:T(1,128)S(1)} %all_to_all.5.refs_0_, s32[1,512]{1,0:T(1,128)S(1)} %get-tuple-element.44.refs_1_), custom_call_target="tpu_custom_call" | custom-call | flops 262144 | bytes 2048 | tf_op jit(solution)/shard_map/pallas_call | solution.py:227
  (2 shorter events, 0.0 us)
Async XLA Ops:
  0.0 1.9 %copy-start.1 = (s32[512]{0:T(512)S(1)}, s32[512]{0:T(512)}, u32[]{:S(2)}) copy-start(s32[512]{0:T(512)} %param.5) | copy-start | bytes 6148
  0.0 1.9 %copy-start = (s32[512,1]{0,1:T(1,128)S(1)}, s32[512,1]{0,1:T(1,128)}, u32[]{:S(2)}) copy-start(s32[512,1]{0,1:T(1,128)} %param.4) | copy-start | bytes 6148
  2.8 8.1 %collective-permute-start.2 = (bf16[784,128]{1,0:T(8,128)(2,1)S(1)}, bf16[784,128]{1,0:T(8,128)(2,1)S(1)}, u32[]{:S(2)}, u32[]{:S(2)}) collective-permute-start(bf16[784,128]{1,0:T(8,128)(2,1)S(1)} %get-tuple-element.29), channel_id=1, source_target_pairs={{0,1},{1,0},{2,3},{3,2},{4,5},{5,4},{6,7},{7,6},{8,9},{9,8},{10,11... | collective-permute-start | bytes 602120 | tf_op jit(solution)/shard_map/ppermute | solution.py:314
  5.9 6.4 %collective-permute-start.4 = (bf16[784,128]{1,0:T(8,128)(2,1)S(1)}, bf16[784,128]{1,0:T(8,128)(2,1)S(1)}, u32[]{:S(2)}, u32[]{:S(2)}) collective-permute-start(bf16[784,128]{1,0:T(8,128)(2,1)S(1)} %get-tuple-element.30.refs_0_.refs_3_), channel_id=1, source_target_pairs={{8,0},{24,8},{16,24},{4,16},{12,4},{28,12},{20,28},{0,20},{9,1},{2... | collective-permute-start | bytes 602120 | tf_op jit(solution)/shard_map/ppermute | solution.py:309
  6.6 17.4 %collective-permute-start.1 = (bf16[784,128]{1,0:T(8,128)(2,1)S(1)}, bf16[784,128]{1,0:T(8,128)(2,1)S(1)}, u32[]{:S(2)}, u32[]{:S(2)}) collective-permute-start(bf16[784,128]{1,0:T(8,128)(2,1)S(1)} %get-tuple-element.28), channel_id=1, source_target_pairs={{0,2},{1,3},{2,0},{3,1},{4,6},{5,7},{6,4},{7,5},{8,10},{9,11},{10,... | collective-permute-start | bytes 602120 | tf_op jit(solution)/shard_map/ppermute | solution.py:314
  9.2 14.8 %collective-permute-start.5 = (bf16[784,128]{1,0:T(8,128)(2,1)S(1)}, bf16[784,128]{1,0:T(8,128)(2,1)S(1)}, u32[]{:S(2)}, u32[]{:S(2)}) collective-permute-start(bf16[784,128]{1,0:T(8,128)(2,1)S(1)} %get-tuple-element.30.refs_0_.refs_3_), channel_id=1, source_target_pairs={{20,0},{0,8},{8,24},{24,16},{16,4},{4,12},{12,28},{28,20},{21,1},{... | collective-permute-start | bytes 602120 | tf_op jit(solution)/shard_map/ppermute | solution.py:309
  10.5 15.3 %collective-permute-start = (bf16[784,128]{1,0:T(8,128)(2,1)S(1)}, bf16[784,128]{1,0:T(8,128)(2,1)S(1)}, u32[]{:S(2)}, u32[]{:S(2)}) collective-permute-start(bf16[784,128]{1,0:T(8,128)(2,1)S(1)} %get-tuple-element.27), channel_id=1, source_target_pairs={{0,3},{1,2},{2,1},{3,0},{4,7},{5,6},{6,5},{7,4},{8,11},{9,10},{10,... | collective-permute-start | bytes 602120 | tf_op jit(solution)/shard_map/ppermute | solution.py:314
  12.4 14.4 %collective-permute-start.8 = (bf16[784,128]{1,0:T(8,128)(2,1)S(1)}, bf16[784,128]{1,0:T(8,128)(2,1)S(1)}, u32[]{:S(2)}, u32[]{:S(2)}) collective-permute-start(bf16[784,128]{1,0:T(8,128)(2,1)S(1)} %collective-permute-done.2.refs_1_.refs_2_), channel_id=1, source_target_pairs={{20,0},{0,8},{8,24},{24,16},{16,4},{4,12},{12,28},{28,20},{21,1},{... | collective-permute-start | bytes 602120 | tf_op jit(solution)/shard_map/ppermute | solution.py:309
  15.8 11.0 %collective-permute-start.7 = (bf16[784,128]{1,0:T(8,128)(2,1)S(1)}, bf16[784,128]{1,0:T(8,128)(2,1)S(1)}, u32[]{:S(2)}, u32[]{:S(2)}) collective-permute-start(bf16[784,128]{1,0:T(8,128)(2,1)S(1)} %collective-permute-done.2.refs_1_.refs_2_), channel_id=1, source_target_pairs={{8,0},{24,8},{16,24},{4,16},{12,4},{28,12},{20,28},{0,20},{9,1},{2... | collective-permute-start | bytes 602120 | tf_op jit(solution)/shard_map/ppermute | solution.py:309
  24.0 6.4 %collective-permute-start.10 = (bf16[1,784,128]{2,1,0:T(8,128)(2,1)S(1)}, bf16[1,784,128]{2,1,0:T(8,128)(2,1)S(1)}, u32[]{:S(2)}, u32[]{:S(2)}) collective-permute-start(bf16[1,784,128]{2,1,0:T(8,128)(2,1)S(1)} %shard_map.40), channel_id=1, source_target_pairs={{20,0},{0,8},{8,24},{24,16},{16,4},{4,12},{12,28},{28,20},{21,1},{... | collective-permute-start | bytes 602120 | tf_op jit(solution)/shard_map/ppermute | solution.py:309
  25.5 6.3 %collective-permute-start.6 = (bf16[1,784,128]{2,1,0:T(8,128)(2,1)S(1)}, bf16[1,784,128]{2,1,0:T(8,128)(2,1)S(1)}, u32[]{:S(2)}, u32[]{:S(2)}) collective-permute-start(bf16[1,784,128]{2,1,0:T(8,128)(2,1)S(1)} %shard_map.40), channel_id=1, source_target_pairs={{8,0},{24,8},{16,24},{4,16},{12,4},{28,12},{20,28},{0,20},{9,1},{2... | collective-permute-start | bytes 602120 | tf_op jit(solution)/shard_map/ppermute | solution.py:309
  25.9 3.0 %collective-permute-start.3 = (bf16[4,784,128]{2,1,0:T(8,128)(2,1)S(1)}, bf16[4,784,128]{2,1,0:T(8,128)(2,1)S(1)}, u32[]{:S(2)}, u32[]{:S(2)}) collective-permute-start(bf16[4,784,128]{2,1,0:T(8,128)(2,1)S(1)} %shard_map.39), channel_id=1, source_target_pairs={{4,0},{12,8},{28,24},{20,16},{0,4},{8,12},{24,28},{16,20},{5,1},{1... | collective-permute-start | bytes 2408456 | tf_op jit(solution)/shard_map/ppermute | solution.py:309
  26.8 7.9 %collective-permute-start.9 = (bf16[1,784,128]{2,1,0:T(8,128)(2,1)S(1)}, bf16[1,784,128]{2,1,0:T(8,128)(2,1)S(1)}, u32[]{:S(2)}, u32[]{:S(2)}) collective-permute-start(bf16[1,784,128]{2,1,0:T(8,128)(2,1)S(1)} %shard_map.41), channel_id=1, source_target_pairs={{20,0},{0,8},{8,24},{24,16},{16,4},{4,12},{12,28},{28,20},{21,1},{... | collective-permute-start | bytes 602120 | tf_op jit(solution)/shard_map/ppermute | solution.py:309
  27.7 7.8 %collective-permute-start.11 = (bf16[1,784,128]{2,1,0:T(8,128)(2,1)S(1)}, bf16[1,784,128]{2,1,0:T(8,128)(2,1)S(1)}, u32[]{:S(2)}, u32[]{:S(2)}) collective-permute-start(bf16[1,784,128]{2,1,0:T(8,128)(2,1)S(1)} %shard_map.41), channel_id=1, source_target_pairs={{8,0},{24,8},{16,24},{4,16},{12,4},{28,12},{20,28},{0,20},{9,1},{2... | collective-permute-start | bytes 602120 | tf_op jit(solution)/shard_map/ppermute | solution.py:309

commit v19 on v17

--- a/solution.py
+++ b/solution.py
@@ -318,7 +318,7 @@
     (units,) = call(
         unit_kernel,
         [jax.ShapeDtypeStruct((rows, width), jnp.bfloat16)],
-        [pltpu.VMEM((rows, width), embeddings.dtype), pltpu.SemaphoreType.DMA((4,))],
+        [pltpu.VMEM((rows, width), embeddings.dtype), pltpu.SemaphoreType.DMA((2,))],
         (embeddings,),
         4 * rows * width,
         4 * rows * width,
@@ -349,7 +349,7 @@
         held[r][0] = (first[r], None)
     for k in range(1, groups):
         if k == 1:
-            block = after(own[k], first[near[0]]) if near else own[k]
+            block = after(own[k], first[near[-1]]) if near else own[k]
         else:
             passed = [held[r][k - 2][0] for r in near]
             block = stack([after(own[k], *passed)], WAIT)

time: 47.2 us -> 47.2 us (level)
  blocking collectives: 11.6 us -> 10.2 us
  starting transfers between devices: 20.2 us -> 21.2 us
    all_to_all x1, blocking collectives: 11.6 us -> 10.2 us  [per_device(): lax.all_to_all(best, ('shard', 'group'), split_axis=0, concat_axis=0, til...]
    ppermute x3, starting transfers between devices: 8.15 us -> 8.87 us  [exchange(): got[k] = lax.ppermute(block, 'group', [(z, z ^ k) for z in range(groups)])]
where the time goes in v19:
time: 47.2 us; the launch traced here: 47.1 us
  starting transfers between devices  21.2 us (45%)
  blocking collectives  10.2 us (22%)
  waiting for transfers between devices  7.88 us (17%)
  Pallas kernels  7.64 us (16%)
    ppermute x9, starting transfers between devices, from_offset(): return lax.ppermute(x, 'shard', perm)  12.3 us
    all_to_all x1, blocking collectives, per_device(): lax.all_to_all(best, ('shard', 'group'), split_axis=0, concat_axis=0, til...  10.2 us
    ppermute x3, starting transfers between devices, exchange(): got[k] = lax.ppermute(block, 'group', [(z, z ^ k) for z in range(groups)])  8.87 us
    pallas_call x11, Pallas kernels, call(): pl.pallas_call(kernel, out_shape=out_shape, in_specs=in_specs or in_vmem(...  7.64 us
    ppermute x3, waiting for transfers between devices, exchange(): got[k] = lax.ppermute(block, 'group', [(z, z ^ k) for z in range(groups)])  4.12 us
    ppermute x9, waiting for transfers between devices, from_offset(): return lax.ppermute(x, 'shard', perm)  3.76 us
  transfers between devices with their start and end apart: 12, of which 5 were waited for; matrix products, arithmetic and copies ran while one was open for 0% of the time, Pallas kernels for 9%

profile of v19, /device:TPU:0, one launch (start us, length us, event | category | flops | bytes accessed | tf_op | source)
XLA Modules:
  0.0 47.1 jit_solution(18437841700332961400)
XLA Ops:
  0.0 0.0 copy-start.1
  0.0 0.0 copy-start
  0.0 1.4 %shard_map.37.refs_0_ = bf16[512,768]{1,0:T(8,128)(2,1)S(1)} custom-call(bf16[512,768]{1,0:T(8,128)(2,1)} %far_ref.1), custom_call_target="tpu_custom_call" | custom-call | flops 1572864 | bytes 1572864 | tf_op jit(solution)/shard_map/pallas_call | solution.py:227
  1.4 0.0 copy-done.1
  1.4 0.0 copy-done
  1.4 0.9 %shard_map.38 = (bf16[784,128]{1,0:T(8,128)(2,1)S(1)}, bf16[784,128]{1,0:T(8,128)(2,1)S(1)}, bf16[784,128]{1,0:T(8,128)(2,1)S(1)}, bf16[784,128]{1,0:T(8,128)(2,1)S(1)}, s32[1,512]{1,0:T(1,128)S(1)}) custom-call(bf16[512,768]{1,0:T(8,128)(2,1)S(1)} %shard_map.37.refs_0_, s32[1,512]{1,0:T(1,128)S(1)} %bitcast.3, s32[1,512]{1,0:T(1,128)S(1)} %bitcast.4), custom_call_target="tpu_custom_call" | custom-call | flops 402653184 | bytes 1572864 | tf_op jit(solution)/shard_map/pallas_call | solution.py:227
  2.3 3.1 %collective-permute-start = (bf16[784,128]{1,0:T(8,128)(2,1)S(1)}, bf16[784,128]{1,0:T(8,128)(2,1)S(1)}, u32[]{:S(2)}, u32[]{:S(2)}) collective-permute-start(bf16[784,128]{1,0:T(8,128)(2,1)S(1)} %get-tuple-element.29), channel_id=1, source_target_pairs={{0,1},{1,0},{2,3},{3,2},{4,5},{5,4},{6,7},{7,6},{8,9},{9,8},{10,11... | collective-permute-start | bytes 602120 | tf_op jit(solution)/shard_map/ppermute | solution.py:315
  5.4 1.5 %collective-permute-start.5 = (bf16[784,128]{1,0:T(8,128)(2,1)S(1)}, bf16[784,128]{1,0:T(8,128)(2,1)S(1)}, u32[]{:S(2)}, u32[]{:S(2)}) collective-permute-start(bf16[784,128]{1,0:T(8,128)(2,1)S(1)} %get-tuple-element.32.refs_0_.refs_3_), channel_id=1, source_target_pairs={{20,0},{0,8},{8,24},{24,16},{16,4},{4,12},{12,28},{28,20},{21,1},{... | collective-permute-start | bytes 602120 | tf_op jit(solution)/shard_map/ppermute | solution.py:309
  6.9 2.6 %collective-permute-start.2 = (bf16[784,128]{1,0:T(8,128)(2,1)S(1)}, bf16[784,128]{1,0:T(8,128)(2,1)S(1)}, u32[]{:S(2)}, u32[]{:S(2)}) collective-permute-start(bf16[784,128]{1,0:T(8,128)(2,1)S(1)} %get-tuple-element.31), channel_id=1, source_target_pairs={{0,2},{1,3},{2,0},{3,1},{4,6},{5,7},{6,4},{7,5},{8,10},{9,11},{10,... | collective-permute-start | bytes 602120 | tf_op jit(solution)/shard_map/ppermute | solution.py:315
  9.5 0.0 collective-permute-start.4
  9.5 3.3 %collective-permute-done.refs_1_.refs_2_ = bf16[784,128]{1,0:T(8,128)(2,1)S(1)} collective-permute-done((bf16[784,128]{1,0:T(8,128)(2,1)S(1)}, bf16[784,128]{1,0:T(8,128)(2,1)S(1)}, u32[]{:S(2)}, u32[]{:S(2)}) %collective-permute-start) | collective-permute-done | bytes 200736 | tf_op jit(solution)/shard_map/ppermute | solution.py:315
  12.8 0.0 collective-permute-done.5.refs_10_.refs_4_
  12.8 1.8 %collective-permute-start.8 = (bf16[784,128]{1,0:T(8,128)(2,1)S(1)}, bf16[784,128]{1,0:T(8,128)(2,1)S(1)}, u32[]{:S(2)}, u32[]{:S(2)}) collective-permute-start(bf16[784,128]{1,0:T(8,128)(2,1)S(1)} %collective-permute-done.refs_1_.refs_2_), channel_id=1, source_target_pairs={{20,0},{0,8},{8,24},{24,16},{16,4},{4,12},{12,28},{28,20},{21,1},{... | collective-permute-start | bytes 602120 | tf_op jit(solution)/shard_map/ppermute | solution.py:309
  14.6 0.0 collective-permute-start.7
  14.6 3.2 %collective-permute-start.1 = (bf16[784,128]{1,0:T(8,128)(2,1)S(1)}, bf16[784,128]{1,0:T(8,128)(2,1)S(1)}, u32[]{:S(2)}, u32[]{:S(2)}) collective-permute-start(bf16[784,128]{1,0:T(8,128)(2,1)S(1)} %get-tuple-element.30), channel_id=1, source_target_pairs={{0,3},{1,2},{2,1},{3,0},{4,7},{5,6},{6,5},{7,4},{8,11},{9,10},{10,... | collective-permute-start | bytes 602120 | tf_op jit(solution)/shard_map/ppermute | solution.py:315
  17.8 0.8 %collective-permute-done.2.refs_2_.refs_0_.refs_1_ = bf16[784,128]{1,0:T(8,128)(2,1)S(1)} collective-permute-done((bf16[784,128]{1,0:T(8,128)(2,1)S(1)}, bf16[784,128]{1,0:T(8,128)(2,1)S(1)}, u32[]{:S(2)}, u32[]{:S(2)}) %collective-permute-start.2) | collective-permute-done | bytes 200736 | tf_op jit(solution)/shard_map/ppermute | solution.py:315
  18.6 0.0 collective-permute-done.4.refs_7_
  18.6 6.9 %collective-permute-start.10 = (bf16[1,784,128]{2,1,0:T(8,128)(2,1)S(1)}, bf16[1,784,128]{2,1,0:T(8,128)(2,1)S(1)}, u32[]{:S(2)}, u32[]{:S(2)}) collective-permute-start(bf16[1,784,128]{2,1,0:T(8,128)(2,1)S(1)} %shard_map.40), channel_id=1, source_target_pairs={{20,0},{0,8},{8,24},{24,16},{16,4},{4,12},{12,28},{28,20},{21,1},{... | collective-permute-start | bytes 602120 | tf_op jit(solution)/shard_map/ppermute | solution.py:309
  25.5 0.0 collective-permute-start.6
  25.5 0.0 collective-permute-done.1.refs_3_.refs_0_
  25.5 0.0 collective-permute-done.8.refs_9_.refs_3_
  25.5 0.0 collective-permute-done.7.refs_6_
  25.6 0.1 shard_map.39
  25.6 0.1 collective-permute-start.3
  25.7 2.1 %collective-permute-start.9 = (bf16[1,784,128]{2,1,0:T(8,128)(2,1)S(1)}, bf16[1,784,128]{2,1,0:T(8,128)(2,1)S(1)}, u32[]{:S(2)}, u32[]{:S(2)}) collective-permute-start(bf16[1,784,128]{2,1,0:T(8,128)(2,1)S(1)} %shard_map.41), channel_id=1, source_target_pairs={{20,0},{0,8},{8,24},{24,16},{16,4},{4,12},{12,28},{28,20},{21,1},{... | collective-permute-start | bytes 602120 | tf_op jit(solution)/shard_map/ppermute | solution.py:309
  27.8 0.0 collective-permute-start.11
  27.8 0.2 collective-permute-done.3.refs_4_
  28.0 1.5 %shard_map.42 = (f32[4,8,512]{2,1,0:T(8,128)S(1)}, bf16[2,512,768]{2,1,0:T(8,128)(2,1)S(1)}) custom-call(bf16[784,128]{1,0:T(8,128)(2,1)S(1)} %collective-permute-done.1.refs_3_.refs_0_, bf16[784,128]{1,0:T(8,128)(2,1)S(1)} %collective-permute-done.2.refs_2_.refs_0_.refs_1_, bf16[784,128]{1,0:T(8,128)(2,1)S(1)} %collective-permute-done.refs_1_.refs_2_, ...), custom_call_target="tpu_custom_call" | custom-call | flops 805306368 | bytes 1572864 | tf_op jit(solution)/shard_map/pallas_call | solution.py:227
  29.5 0.0 collective-permute-done.10.refs_8_.refs_2_
  29.5 2.3 %collective-permute-done.6.refs_5_ = bf16[1,784,128]{2,1,0:T(8,128)(2,1)S(1)} collective-permute-done((bf16[1,784,128]{2,1,0:T(8,128)(2,1)S(1)}, bf16[1,784,128]{2,1,0:T(8,128)(2,1)S(1)}, u32[]{:S(2)}, u32[]{:S(2)}) %collective-permute-start.6) | collective-permute-done | bytes 200736 | tf_op jit(solution)/shard_map/ppermute | solution.py:309
  31.8 1.6 %shard_map.43 = (f32[4,8,512]{2,1,0:T(8,128)S(1)}, bf16[2,512,768]{2,1,0:T(8,128)(2,1)S(1)}) custom-call(bf16[784,128]{1,0:T(8,128)(2,1)S(1)} %collective-permute-done.1.refs_3_.refs_0_, bf16[784,128]{1,0:T(8,128)(2,1)S(1)} %collective-permute-done.2.refs_2_.refs_0_.refs_1_, bf16[784,128]{1,0:T(8,128)(2,1)S(1)} %collective-permute-done.refs_1_.refs_2_, ...), custom_call_target="tpu_custom_call" | custom-call | flops 830472192 | bytes 2752512 | tf_op jit(solution)/shard_map/pallas_call | solution.py:227
  33.4 0.0 collective-permute-done.9.refs_8_.refs_1_
  33.4 0.8 %shard_map.44 = (f32[4,8,512]{2,1,0:T(8,128)S(1)}, bf16[1,512,768]{2,1,0:T(8,128)(2,1)S(1)}, f32[1,512]{1,0:T(1,128)S(1)}, f32[1,512]{1,0:T(1,128)S(1)}) custom-call(bf16[784,128]{1,0:T(8,128)(2,1)S(1)} %collective-permute-done.1.refs_3_.refs_0_, bf16[784,128]{1,0:T(8,128)(2,1)S(1)} %collective-permute-done.2.refs_2_.refs_0_.refs_1_, ...), custom_call_target="tpu_custom_call" | custom-call | flops 276824064 | bytes 2359296 | tf_op jit(solution)/shard_map/pallas_call | solution.py:227
  34.3 1.3 %collective-permute-done.11.refs_0_ = bf16[1,784,128]{2,1,0:T(8,128)(2,1)S(1)} collective-permute-done((bf16[1,784,128]{2,1,0:T(8,128)(2,1)S(1)}, bf16[1,784,128]{2,1,0:T(8,128)(2,1)S(1)}, u32[]{:S(2)}, u32[]{:S(2)}) %collective-permute-start.11) | collective-permute-done | bytes 200736 | tf_op jit(solution)/shard_map/ppermute | solution.py:309
  35.5 0.4 shard_map.45
  36.0 0.1 shard_map.46
  36.1 10.2 %all_to_all.5.refs_0_ = f32[32,1,128]{2,1,0:T(1,128)S(1)} all-to-all(f32[32,1,128]{2,1,0:T(1,128)S(1)} %shard_map.46), channel_id=1, replica_groups=mesh['shard'=8,'group'=4] {'shard','group'}, dimensions={0} | all-to-all | bytes 32768 | tf_op jit(solution)/shard_map/all_to_all | solution.py:396
  46.3 0.8 %shard_map.47 = f32[1,512]{1,0:T(1,128)} custom-call(f32[32,1,128]{2,1,0:T(1,128)S(1)} %all_to_all.5.refs_0_, s32[1,512]{1,0:T(1,128)S(1)} %get-tuple-element.46.refs_1_), custom_call_target="tpu_custom_call" | custom-call | flops 262144 | bytes 2048 | tf_op jit(solution)/shard_map/pallas_call | solution.py:227
  (2 shorter events, 0.0 us)
Async XLA Ops:
  0.0 1.4 %copy-start.1 = (s32[512]{0:T(512)S(1)}, s32[512]{0:T(512)}, u32[]{:S(2)}) copy-start(s32[512]{0:T(512)} %param.5) | copy-start | bytes 6148
  0.0 1.4 %copy-start = (s32[512,1]{0,1:T(1,128)S(1)}, s32[512,1]{0,1:T(1,128)}, u32[]{:S(2)}) copy-start(s32[512,1]{0,1:T(1,128)} %param.4) | copy-start | bytes 6148
  2.3 10.5 %collective-permute-start = (bf16[784,128]{1,0:T(8,128)(2,1)S(1)}, bf16[784,128]{1,0:T(8,128)(2,1)S(1)}, u32[]{:S(2)}, u32[]{:S(2)}) collective-permute-start(bf16[784,128]{1,0:T(8,128)(2,1)S(1)} %get-tuple-element.29), channel_id=1, source_target_pairs={{0,1},{1,0},{2,3},{3,2},{4,5},{5,4},{6,7},{7,6},{8,9},{9,8},{10,11... | collective-permute-start | bytes 602120 | tf_op jit(solution)/shard_map/ppermute | solution.py:315
  5.4 7.4 %collective-permute-start.5 = (bf16[784,128]{1,0:T(8,128)(2,1)S(1)}, bf16[784,128]{1,0:T(8,128)(2,1)S(1)}, u32[]{:S(2)}, u32[]{:S(2)}) collective-permute-start(bf16[784,128]{1,0:T(8,128)(2,1)S(1)} %get-tuple-element.32.refs_0_.refs_3_), channel_id=1, source_target_pairs={{20,0},{0,8},{8,24},{24,16},{16,4},{4,12},{12,28},{28,20},{21,1},{... | collective-permute-start | bytes 602120 | tf_op jit(solution)/shard_map/ppermute | solution.py:309
  6.9 11.7 %collective-permute-start.2 = (bf16[784,128]{1,0:T(8,128)(2,1)S(1)}, bf16[784,128]{1,0:T(8,128)(2,1)S(1)}, u32[]{:S(2)}, u32[]{:S(2)}) collective-permute-start(bf16[784,128]{1,0:T(8,128)(2,1)S(1)} %get-tuple-element.31), channel_id=1, source_target_pairs={{0,2},{1,3},{2,0},{3,1},{4,6},{5,7},{6,4},{7,5},{8,10},{9,11},{10,... | collective-permute-start | bytes 602120 | tf_op jit(solution)/shard_map/ppermute | solution.py:315
  9.5 9.1 %collective-permute-start.4 = (bf16[784,128]{1,0:T(8,128)(2,1)S(1)}, bf16[784,128]{1,0:T(8,128)(2,1)S(1)}, u32[]{:S(2)}, u32[]{:S(2)}) collective-permute-start(bf16[784,128]{1,0:T(8,128)(2,1)S(1)} %get-tuple-element.32.refs_0_.refs_3_), channel_id=1, source_target_pairs={{8,0},{24,8},{16,24},{4,16},{12,4},{28,12},{20,28},{0,20},{9,1},{2... | collective-permute-start | bytes 602120 | tf_op jit(solution)/shard_map/ppermute | solution.py:309
  12.8 12.7 %collective-permute-start.8 = (bf16[784,128]{1,0:T(8,128)(2,1)S(1)}, bf16[784,128]{1,0:T(8,128)(2,1)S(1)}, u32[]{:S(2)}, u32[]{:S(2)}) collective-permute-start(bf16[784,128]{1,0:T(8,128)(2,1)S(1)} %collective-permute-done.refs_1_.refs_2_), channel_id=1, source_target_pairs={{20,0},{0,8},{8,24},{24,16},{16,4},{4,12},{12,28},{28,20},{21,1},{... | collective-permute-start | bytes 602120 | tf_op jit(solution)/shard_map/ppermute | solution.py:309
  14.6 11.0 %collective-permute-start.7 = (bf16[784,128]{1,0:T(8,128)(2,1)S(1)}, bf16[784,128]{1,0:T(8,128)(2,1)S(1)}, u32[]{:S(2)}, u32[]{:S(2)}) collective-permute-start(bf16[784,128]{1,0:T(8,128)(2,1)S(1)} %collective-permute-done.refs_1_.refs_2_), channel_id=1, source_target_pairs={{8,0},{24,8},{16,24},{4,16},{12,4},{28,12},{20,28},{0,20},{9,1},{2... | collective-permute-start | bytes 602120 | tf_op jit(solution)/shard_map/ppermute | solution.py:309
  14.6 10.9 %collective-permute-start.1 = (bf16[784,128]{1,0:T(8,128)(2,1)S(1)}, bf16[784,128]{1,0:T(8,128)(2,1)S(1)}, u32[]{:S(2)}, u32[]{:S(2)}) collective-permute-start(bf16[784,128]{1,0:T(8,128)(2,1)S(1)} %get-tuple-element.30), channel_id=1, source_target_pairs={{0,3},{1,2},{2,1},{3,0},{4,7},{5,6},{6,5},{7,4},{8,11},{9,10},{10,... | collective-permute-start | bytes 602120 | tf_op jit(solution)/shard_map/ppermute | solution.py:315
  18.6 10.9 %collective-permute-start.10 = (bf16[1,784,128]{2,1,0:T(8,128)(2,1)S(1)}, bf16[1,784,128]{2,1,0:T(8,128)(2,1)S(1)}, u32[]{:S(2)}, u32[]{:S(2)}) collective-permute-start(bf16[1,784,128]{2,1,0:T(8,128)(2,1)S(1)} %shard_map.40), channel_id=1, source_target_pairs={{20,0},{0,8},{8,24},{24,16},{16,4},{4,12},{12,28},{28,20},{21,1},{... | collective-permute-start | bytes 602120 | tf_op jit(solution)/shard_map/ppermute | solution.py:309
  25.5 6.3 %collective-permute-start.6 = (bf16[1,784,128]{2,1,0:T(8,128)(2,1)S(1)}, bf16[1,784,128]{2,1,0:T(8,128)(2,1)S(1)}, u32[]{:S(2)}, u32[]{:S(2)}) collective-permute-start(bf16[1,784,128]{2,1,0:T(8,128)(2,1)S(1)} %shard_map.40), channel_id=1, source_target_pairs={{8,0},{24,8},{16,24},{4,16},{12,4},{28,12},{20,28},{0,20},{9,1},{2... | collective-permute-start | bytes 602120 | tf_op jit(solution)/shard_map/ppermute | solution.py:309
  25.6 2.4 %collective-permute-start.3 = (bf16[4,784,128]{2,1,0:T(8,128)(2,1)S(1)}, bf16[4,784,128]{2,1,0:T(8,128)(2,1)S(1)}, u32[]{:S(2)}, u32[]{:S(2)}) collective-permute-start(bf16[4,784,128]{2,1,0:T(8,128)(2,1)S(1)} %shard_map.39), channel_id=1, source_target_pairs={{4,0},{12,8},{28,24},{20,16},{0,4},{8,12},{24,28},{16,20},{5,1},{1... | collective-permute-start | bytes 2408456 | tf_op jit(solution)/shard_map/ppermute | solution.py:309
  25.7 7.7 %collective-permute-start.9 = (bf16[1,784,128]{2,1,0:T(8,128)(2,1)S(1)}, bf16[1,784,128]{2,1,0:T(8,128)(2,1)S(1)}, u32[]{:S(2)}, u32[]{:S(2)}) collective-permute-start(bf16[1,784,128]{2,1,0:T(8,128)(2,1)S(1)} %shard_map.41), channel_id=1, source_target_pairs={{20,0},{0,8},{8,24},{24,16},{16,4},{4,12},{12,28},{28,20},{21,1},{... | collective-permute-start | bytes 602120 | tf_op jit(solution)/shard_map/ppermute | solution.py:309
  27.8 7.8 %collective-permute-start.11 = (bf16[1,784,128]{2,1,0:T(8,128)(2,1)S(1)}, bf16[1,784,128]{2,1,0:T(8,128)(2,1)S(1)}, u32[]{:S(2)}, u32[]{:S(2)}) collective-permute-start(bf16[1,784,128]{2,1,0:T(8,128)(2,1)S(1)} %shard_map.41), channel_id=1, source_target_pairs={{8,0},{24,8},{16,24},{4,16},{12,4},{28,12},{20,28},{0,20},{9,1},{2... | collective-permute-start | bytes 602120 | tf_op jit(solution)/shard_map/ppermute | solution.py:309

commit v20 on v19

--- a/solution.py
+++ b/solution.py
@@ -69,11 +69,10 @@
         unit_ref[pl.ds(i * size, size), :] = (feats * lax.rsqrt(squares)).astype(jnp.bfloat16)
 
 
-def sort_kernel(axis, unit_ref, group_ref, label_ref, *out_refs):
+def sort_kernel(axis, pieces, capacity, unit_ref, group_ref, label_ref, *out_refs):
     *block_refs, place_ref = out_refs
     rows, width = unit_ref.shape
-    groups = len(block_refs)
-    capacity = (block_refs[0].shape[0] - TAIL) * LANES // width
+    groups = len(pieces)
     slots = groups * capacity
     chunks = width // LANES
     owner = group_ref[...]
@@ -100,19 +99,26 @@
         )
         - 1.0
     ).astype(jnp.bfloat16)
-    for k, block_ref in enumerate(block_refs):
+    for k in range(groups):
         part = slice(k * capacity, (k + 1) * capacity)
         block = jnp.dot(
             move[part], unit_ref[...], preferred_element_type=jnp.float32
         ).astype(jnp.bfloat16)
-        for c in range(chunks):
-            block_ref[pl.ds(c * capacity, capacity), :] = block[:, c * LANES : (c + 1) * LANES]
-        block_ref[pl.ds(chunks * capacity, TAIL), :] = sorted_labels[:, part]
+        size = capacity // pieces[k]
+        for i in range(pieces[k]):
+            block_ref = block_refs[sum(pieces[:k]) + i]
+            for c in range(chunks):
+                block_ref[pl.ds(c * size, size), :] = block[
+                    i * size : (i + 1) * size, c * LANES : (c + 1) * LANES
+                ]
+            block_ref[pl.ds(chunks * size, TAIL), :] = sorted_labels[:, part]
 
 
 def stack_kernel(*refs):
-    for k, ref in enumerate(refs[:-1]):
-        refs[-1][k] = ref[...]
+    start = 0
+    for ref in refs[:-1]:
+        refs[-1][pl.ds(start, ref.shape[0]), :] = ref[...]
+        start += ref.shape[0]
 
 
 def score_kernel(sources, flats, layout, tasks, done, last, *refs):
@@ -125,7 +131,8 @@
         inputs, (best_ref, flat_ref, *out_refs) = refs[:-outs], refs[-outs:]
     capacity = LANES
     low = jnp.float32(LOW)
-    arrays = 1 + max(index for index, _ in sources.values())
+    arrays = 1 + max(index for found in sources.values() for index, _, _ in found)
+    chunks = flat_ref.shape[-1] // LANES
     best_ref[...] = inputs[arrays][...] if len(inputs) > arrays else jnp.full(best_ref.shape, low)
 
     def units(role, ks):
@@ -136,16 +143,18 @@
         return flat_ref[layout.index(role), rows, :]
 
     tops = {}
-    for (role, k), (index, part) in sources.items():
-        ref = inputs[index] if part is None else inputs[index].at[part]
-        height = ref.shape[0] - TAIL
-        rows = pl.ds(k * capacity, capacity)
-        if (role, k) not in flats:
-            for c in range(height // capacity):
-                flat_ref[layout.index(role), rows, pl.ds(c * LANES, LANES)] = ref[
-                    pl.ds(c * capacity, capacity), :
-                ]
-        tops[role, k] = ref[pl.ds(height, TAIL), :][0:1].astype(jnp.float32)
+    for (role, k), found in sources.items():
+        at = k * capacity
+        for index, start, size in found:
+            if (role, k) not in flats:
+                for c in range(chunks):
+                    flat_ref[
+                        layout.index(role), pl.ds(at, size), pl.ds(c * LANES, LANES)
+                    ] = inputs[index][pl.ds(start + c * size, size), :]
+            at += size
+        tops[role, k] = inputs[index][pl.ds(start + chunks * size, TAIL), :][0:1].astype(
+            jnp.float32
+        )
     for role, k in sorted({(left, k) for left, ks, _, _, _ in tasks for k in ks}):
         side_ref[role, pl.ds(k * capacity, capacity), :] = column_of(tops[role, k])
     turns = sorted({(left, k) for left, ks, _, _, both in tasks if both for k in ks})
@@ -242,14 +251,16 @@
 
 
 def stack(parts, wait):
-    return call(
+    starts = [sum(x.shape[0] for x in parts[:i]) for i in range(len(parts) + 1)]
+    (pack,) = call(
         stack_kernel,
-        [jax.ShapeDtypeStruct((len(parts), *parts[0].shape), parts[0].dtype)],
+        [jax.ShapeDtypeStruct((starts[-1], LANES), parts[0].dtype)],
         [],
         parts,
         wait,
-        4 * len(parts) * parts[0].size,
-    )[0]
+        4 * starts[-1] * LANES,
+    )
+    return pack, starts[:-1]
 
 
 def score(held, tasks, acc, flats, done, last, slots, width):
@@ -261,11 +272,12 @@
     )
     arrays, sources = [], {}
     for role, k in used:
-        array, part = held[role][k]
-        index = next((i for i, x in enumerate(arrays) if x is array), len(arrays))
-        if index == len(arrays):
-            arrays.append(array)
-        sources[role, k] = (index, part)
+        sources[role, k] = []
+        for array, start, size in held[role][k]:
+            index = next((i for i, x in enumerate(arrays) if x is array), len(arrays))
+            if index == len(arrays):
+                arrays.append(array)
+            sources[role, k].append((index, start, size))
     layout = sorted({role for role, k in used if (role, k) not in flats})
     tiles = sum(len(task[1]) * len(task[3]) for task in tasks)
     kept = [
@@ -302,18 +314,15 @@
     ring = ring_order(shards)
     offsets, pairs = offset_cover(shards)
     roles = len(offsets)
-    height = width * capacity // LANES + TAIL
+    pieces = [1] * (groups - 1) + [2 if groups > 2 else 1]
+    sizes = [capacity // n for n in pieces for _ in range(n)]
 
     def from_offset(x, offset):
         perm = [(ring[(e + offset) % shards], ring[e]) for e in range(shards)]
         return lax.ppermute(x, "shard", perm)
 
-    def exchange(blocks):
-        got = list(blocks)
-        for k in range(1, groups):
-            block = after(blocks[k], got[1]) if k > 2 else blocks[k]
-            got[k] = lax.ppermute(block, "group", [(z, z ^ k) for z in range(groups)])
-        return got
+    def across(x, k):
+        return lax.ppermute(x, "group", [(z, z ^ k) for z in range(groups)])
 
     (units,) = call(
         unit_kernel,
@@ -326,8 +335,11 @@
         53 * MIB,
     )
     *send, place = call(
-        lambda *refs: sort_kernel("group", *refs),
-        [jax.ShapeDtypeStruct((height, LANES), jnp.bfloat16)] * groups
+        lambda *refs: sort_kernel("group", pieces, capacity, *refs),
+        [
+            jax.ShapeDtypeStruct((width * size // LANES + TAIL, LANES), jnp.bfloat16)
+            for size in sizes
+        ]
         + [jax.ShapeDtypeStruct((1, rows), jnp.int32)],
         [],
         (units, *lax.optimization_barrier((row_group.reshape(1, rows), row_cluster.reshape(1, rows)))),
@@ -337,27 +349,45 @@
 
     late = [groups - 1] if groups > 1 else []
     early = list(range(groups - len(late)))
-    late = [groups - 1] if groups > 1 else []
-    early = list(range(groups - len(late)))
     near = [r for r in range(1, roles) if 2 * offsets[r] != shards]
     far = [r for r in range(1, roles) if r not in near]
     first = {r: from_offset(send[0], offsets[r]) for r in near}
-    own = exchange(send)
-    held = [[None] * groups for _ in offsets]
-    held[0] = [(x, None) for x in own]
+    own = []
+    for k in range(groups):
+        own.append([])
+        for i in range(pieces[k]):
+            piece = send[sum(pieces[:k]) + i]
+            if k > 2 and i == pieces[k] - 1:
+                piece = after(piece, own[1][0])
+            own[k].append(across(piece, k) if k else piece)
+    held = [[[] for _ in range(groups)] for _ in offsets]
+    held[0] = [[(x, 0, capacity // pieces[k]) for x in own[k]] for k in range(groups)]
     for r in near:
-        held[r][0] = (first[r], None)
+        held[r][0] = [(first[r], 0, capacity)]
     for k in range(1, groups):
         if k == 1:
-            block = after(own[k], first[near[-1]]) if near else own[k]
+            block, starts = own[k][0], [0]
+            if near:
+                block = after(block, first[near[-1]])
+            parts = [k]
         else:
-            passed = [held[r][k - 2][0] for r in near]
-            block = stack([after(own[k], *passed)], WAIT)
+            passed = [held[r][k - 2][0][0] for r in near]
+            parts = [k]
+            some = [own[k][-1]]
+            if k == groups - 2 and pieces[-1] == 2:
+                parts.append(k + 1)
+                some.append(own[k + 1][0])
+            block, starts = stack([after(x, *passed) for x in some], WAIT)
         for r in near:
-            held[r][k] = (from_offset(block, offsets[r]), 0 if k > 1 else None)
-    got = {r: from_offset(stack(own, 0), offsets[r]) for r in far}
+            moved = from_offset(block, offsets[r])
+            for j, start in zip(parts, starts):
+                held[r][j].append((moved, start, capacity // pieces[j]))
+    pack, starts = stack([x for found in own for x in found], 0)
     for r in far:
-        held[r] = [(got[r], k) for k in range(groups)]
+        got = from_offset(pack, offsets[r])
+        place_of = iter(zip(starts, sizes))
+        for k in range(groups):
+            held[r][k] = [(got, *next(place_of)) for _ in range(pieces[k])]
     everything = [(0, 0, False)]
     everything += [(offsets.index(a), offsets.index(b), both) for a, b, both in pairs]
     steps = [[] for _ in range(4)]

time: 47.2 us -> 50.8 us (1.076)
  starting transfers between devices: 21.2 us -> 14.6 us
  waiting for transfers between devices: 7.88 us -> 13.5 us
  blocking collectives: 10.2 us -> 14.7 us
    ppermute x9, starting transfers between devices: 12.3 us -> 7.45 us  [from_offset(): return lax.ppermute(x, 'shard', perm)]
    ppermute x3 -> x4, waiting for transfers between devices: 4.12 us -> 8.72 us  [across(): return lax.ppermute(x, 'group', [(z, z ^ k) for z in range(groups)])]
    all_to_all x1, blocking collectives: 10.2 us -> 14.7 us  [per_device(): lax.all_to_all(best, ('shard', 'group'), split_axis=0, concat_axis=0, til...]
    ppermute x3 -> x4, starting transfers between devices: 8.87 us -> 7.12 us  [across(): return lax.ppermute(x, 'group', [(z, z ^ k) for z in range(groups)])]
    ppermute x9, waiting for transfers between devices: 3.76 us -> 4.82 us  [from_offset(): return lax.ppermute(x, 'shard', perm)]
  transfers between devices with their start and end apart: 12 -> 13, of which waited for: 5 -> 8; matrix products, arithmetic and copies ran while one was open for 0% -> 0% of each run, Pallas kernels for 9% -> 8%
where the time goes in v20:
time: 50.8 us; the launch traced here: 50.6 us
  blocking collectives  14.7 us (29%)
  starting transfers between devices  14.6 us (29%)
  waiting for transfers between devices  13.5 us (27%)
  Pallas kernels  7.63 us (15%)
    all_to_all x1, blocking collectives, per_device(): lax.all_to_all(best, ('shard', 'group'), split_axis=0, concat_axis=0, til...  14.7 us
    ppermute x4, waiting for transfers between devices, across(): return lax.ppermute(x, 'group', [(z, z ^ k) for z in range(groups)])  8.72 us
    pallas_call x11, Pallas kernels, call(): pl.pallas_call(kernel, out_shape=out_shape, in_specs=in_specs or in_vmem(...  7.63 us
    ppermute x9, starting transfers between devices, from_offset(): return lax.ppermute(x, 'shard', perm)  7.45 us
    ppermute x4, starting transfers between devices, across(): return lax.ppermute(x, 'group', [(z, z ^ k) for z in range(groups)])  7.12 us
    ppermute x9, waiting for transfers between devices, from_offset(): return lax.ppermute(x, 'shard', perm)  4.82 us
  transfers between devices with their start and end apart: 13, of which 8 were waited for; matrix products, arithmetic and copies ran while one was open for 0% of the time, Pallas kernels for 8%

profile of v20, /device:TPU:0, one launch (start us, length us, event | category | flops | bytes accessed | tf_op | source)
XLA Modules:
  0.0 50.6 jit_solution(7023976838087444552)
XLA Ops:
  0.0 0.0 copy-start.1
  0.0 0.0 copy-start
  0.0 1.4 %shard_map.37.refs_0_ = bf16[512,768]{1,0:T(8,128)(2,1)S(1)} custom-call(bf16[512,768]{1,0:T(8,128)(2,1)} %far_ref.1), custom_call_target="tpu_custom_call" | custom-call | flops 1572864 | bytes 1572864 | tf_op jit(solution)/shard_map/pallas_call | solution.py:236
  1.4 0.0 copy-done.1
  1.4 0.0 copy-done
  1.4 0.9 %shard_map.38 = (bf16[784,128]{1,0:T(8,128)(2,1)S(1)}, bf16[784,128]{1,0:T(8,128)(2,1)S(1)}, bf16[784,128]{1,0:T(8,128)(2,1)S(1)}, bf16[400,128]{1,0:T(8,128)(2,...) custom-call(bf16[512,768]{1,0:T(8,128)(2,1)S(1)} %shard_map.37.refs_0_, s32[1,512]{1,0:T(1,128)S(1)} %bitcast.3, ...), custom_call_target="tpu_custom_call" | custom-call | flops 402653184 | bytes 1572864 | tf_op jit(solution)/shard_map/pallas_call | solution.py:236
  2.3 3.1 %collective-permute-start.1 = (bf16[784,128]{1,0:T(8,128)(2,1)S(1)}, bf16[784,128]{1,0:T(8,128)(2,1)S(1)}, u32[]{:S(2)}, u32[]{:S(2)}) collective-permute-start(bf16[784,128]{1,0:T(8,128)(2,1)S(1)} %get-tuple-element.32), channel_id=1, source_target_pairs={{0,1},{1,0},{2,3},{3,2},{4,5},{5,4},{6,7},{7,6},{8,9},{9,8},{10,11... | collective-permute-start | bytes 602120 | tf_op jit(solution)/shard_map/ppermute | solution.py:325
  5.4 1.5 %collective-permute-start.6 = (bf16[784,128]{1,0:T(8,128)(2,1)S(1)}, bf16[784,128]{1,0:T(8,128)(2,1)S(1)}, u32[]{:S(2)}, u32[]{:S(2)}) collective-permute-start(bf16[784,128]{1,0:T(8,128)(2,1)S(1)} %get-tuple-element.35.refs_0_.refs_4_), channel_id=1, source_target_pairs={{20,0},{0,8},{8,24},{24,16},{16,4},{4,12},{12,28},{28,20},{21,1},{... | collective-permute-start | bytes 602120 | tf_op jit(solution)/shard_map/ppermute | solution.py:322
  6.9 0.3 collective-permute-start.5
  7.2 2.6 %collective-permute-start.3 = (bf16[784,128]{1,0:T(8,128)(2,1)S(1)}, bf16[784,128]{1,0:T(8,128)(2,1)S(1)}, u32[]{:S(2)}, u32[]{:S(2)}) collective-permute-start(bf16[784,128]{1,0:T(8,128)(2,1)S(1)} %get-tuple-element.34), channel_id=1, source_target_pairs={{0,2},{1,3},{2,0},{3,1},{4,6},{5,7},{6,4},{7,5},{8,10},{9,11},{10,... | collective-permute-start | bytes 602120 | tf_op jit(solution)/shard_map/ppermute | solution.py:325
  9.8 0.0 collective-permute-start
  9.8 0.6 %collective-permute-done.1.refs_1_.refs_3_ = bf16[784,128]{1,0:T(8,128)(2,1)S(1)} collective-permute-done((bf16[784,128]{1,0:T(8,128)(2,1)S(1)}, bf16[784,128]{1,0:T(8,128)(2,1)S(1)}, u32[]{:S(2)}, u32[]{:S(2)}) %collective-permute-start.1) | collective-permute-done | bytes 200736 | tf_op jit(solution)/shard_map/ppermute | solution.py:325
  10.4 2.2 %collective-permute-done.6.refs_11_.refs_5_ = bf16[784,128]{1,0:T(8,128)(2,1)S(1)} collective-permute-done((bf16[784,128]{1,0:T(8,128)(2,1)S(1)}, bf16[784,128]{1,0:T(8,128)(2,1)S(1)}, u32[]{:S(2)}, u32[]{:S(2)}) %collective-permute-start.6) | collective-permute-done | bytes 200736 | tf_op jit(solution)/shard_map/ppermute | solution.py:322
  12.6 1.5 %collective-permute-start.10 = (bf16[784,128]{1,0:T(8,128)(2,1)S(1)}, bf16[784,128]{1,0:T(8,128)(2,1)S(1)}, u32[]{:S(2)}, u32[]{:S(2)}) collective-permute-start(bf16[784,128]{1,0:T(8,128)(2,1)S(1)} %collective-permute-done.1.refs_1_.refs_3_), channel_id=1, source_target_pairs={{20,0},{0,8},{8,24},{24,16},{16,4},{4,12},{12,28},{28,20},{21,1},{... | collective-permute-start | bytes 602120 | tf_op jit(solution)/shard_map/ppermute | solution.py:322
  14.1 0.3 collective-permute-start.8
  14.4 4.8 %collective-permute-done.refs_3_.refs_1_.refs_0_ = bf16[400,128]{1,0:T(8,128)(2,1)S(1)} collective-permute-done((bf16[400,128]{1,0:T(8,128)(2,1)S(1)}, bf16[400,128]{1,0:T(8,128)(2,1)S(1)}, u32[]{:S(2)}, u32[]{:S(2)}) %collective-permute-start) | collective-permute-done | bytes 102432 | tf_op jit(solution)/shard_map/ppermute | solution.py:325
  19.2 1.4 %collective-permute-start.2 = (bf16[400,128]{1,0:T(8,128)(2,1)S(1)}, bf16[400,128]{1,0:T(8,128)(2,1)S(1)}, u32[]{:S(2)}, u32[]{:S(2)}) collective-permute-start(bf16[400,128]{1,0:T(8,128)(2,1)S(1)} %get-tuple-element.33), channel_id=1, source_target_pairs={{0,3},{1,2},{2,1},{3,0},{4,7},{5,6},{6,5},{7,4},{8,11},{9,10},{10,... | collective-permute-start | bytes 307208 | tf_op jit(solution)/shard_map/ppermute | solution.py:325
  20.6 0.0 collective-permute-done.5.refs_8_
  20.6 1.7 %collective-permute-done.3.refs_2_.refs_0_ = bf16[784,128]{1,0:T(8,128)(2,1)S(1)} collective-permute-done((bf16[784,128]{1,0:T(8,128)(2,1)S(1)}, bf16[784,128]{1,0:T(8,128)(2,1)S(1)}, u32[]{:S(2)}, u32[]{:S(2)}) %collective-permute-start.3) | collective-permute-done | bytes 200736 | tf_op jit(solution)/shard_map/ppermute | solution.py:325
  22.4 1.1 %collective-permute-start.9 = (bf16[1184,128]{1,0:T(8,128)(2,1)S(1)}, bf16[1184,128]{1,0:T(8,128)(2,1)S(1)}, u32[]{:S(2)}, u32[]{:S(2)}) collective-permute-start(bf16[1184,128]{1,0:T(8,128)(2,1)S(1)} %shard_map.40), channel_id=1, source_target_pairs={{20,0},{0,8},{8,24},{24,16},{16,4},{4,12},{12,28},{28,20},{21,1},{... | collective-permute-start | bytes 909320 | tf_op jit(solution)/shard_map/ppermute | solution.py:322
  23.5 0.7 %collective-permute-start.7 = (bf16[1184,128]{1,0:T(8,128)(2,1)S(1)}, bf16[1184,128]{1,0:T(8,128)(2,1)S(1)}, u32[]{:S(2)}, u32[]{:S(2)}) collective-permute-start(bf16[1184,128]{1,0:T(8,128)(2,1)S(1)} %shard_map.40), channel_id=1, source_target_pairs={{8,0},{24,8},{16,24},{4,16},{12,4},{28,12},{20,28},{0,20},{9,1},{2... | collective-permute-start | bytes 909320 | tf_op jit(solution)/shard_map/ppermute | solution.py:322
  24.2 1.5 %collective-permute-done.2.refs_4_.refs_0_.refs_1_ = bf16[400,128]{1,0:T(8,128)(2,1)S(1)} collective-permute-done((bf16[400,128]{1,0:T(8,128)(2,1)S(1)}, bf16[400,128]{1,0:T(8,128)(2,1)S(1)}, u32[]{:S(2)}, u32[]{:S(2)}) %collective-permute-start.2) | collective-permute-done | bytes 102432 | tf_op jit(solution)/shard_map/ppermute | solution.py:325
  25.7 0.1 shard_map.39
  25.8 0.1 collective-permute-start.4
  25.9 0.0 collective-permute-done.10.refs_10_.refs_4_
  25.9 0.0 collective-permute-done.8.refs_7_
  25.9 1.7 %collective-permute-start.12 = (bf16[400,128]{1,0:T(8,128)(2,1)S(1)}, bf16[400,128]{1,0:T(8,128)(2,1)S(1)}, u32[]{:S(2)}, u32[]{:S(2)}) collective-permute-start(bf16[400,128]{1,0:T(8,128)(2,1)S(1)} %shard_map.41), channel_id=1, source_target_pairs={{8,0},{24,8},{16,24},{4,16},{12,4},{28,12},{20,28},{0,20},{9,1},{2... | collective-permute-start | bytes 307208 | tf_op jit(solution)/shard_map/ppermute | solution.py:322
  27.6 0.4 collective-permute-start.11
  28.0 0.2 collective-permute-done.4.refs_5_
  28.2 1.5 %shard_map.42 = (f32[4,8,512]{2,1,0:T(8,128)S(1)}, bf16[2,512,768]{2,1,0:T(8,128)(2,1)S(1)}) custom-call(bf16[400,128]{1,0:T(8,128)(2,1)S(1)} %collective-permute-done.refs_3_.refs_1_.refs_0_, bf16[400,128]{1,0:T(8,128)(2,1)S(1)} %collective-permute-done.2.refs_4_.refs_0_.refs_1_, bf16[784,128]{1,0:T(8,128)(2,1)S(1)} %collective-permute-done.3.refs_2_.refs_0_, ...), custom_call_target="tpu_custom_call" | custom-call | flops 805306368 | bytes 1572864 | tf_op jit(solution)/shard_map/pallas_call | solution.py:236
  29.7 2.1 %collective-permute-done.9.refs_9_.refs_2_ = bf16[1184,128]{1,0:T(8,128)(2,1)S(1)} collective-permute-done((bf16[1184,128]{1,0:T(8,128)(2,1)S(1)}, bf16[1184,128]{1,0:T(8,128)(2,1)S(1)}, u32[]{:S(2)}, u32[]{:S(2)}) %collective-permute-start.9) | collective-permute-done | bytes 303136 | tf_op jit(solution)/shard_map/ppermute | solution.py:322
  31.8 0.0 collective-permute-done.7.refs_6_.refs_0_
  31.9 1.6 %shard_map.43 = (f32[4,8,512]{2,1,0:T(8,128)S(1)}, bf16[2,512,768]{2,1,0:T(8,128)(2,1)S(1)}) custom-call(bf16[400,128]{1,0:T(8,128)(2,1)S(1)} %collective-permute-done.refs_3_.refs_1_.refs_0_, bf16[400,128]{1,0:T(8,128)(2,1)S(1)} %collective-permute-done.2.refs_4_.refs_0_.refs_1_, bf16[784,128]{1,0:T(8,128)(2,1)S(1)} %collective-permute-done.3.refs_2_.refs_0_, ...), custom_call_target="tpu_custom_call" | custom-call | flops 830472192 | bytes 2752512 | tf_op jit(solution)/shard_map/pallas_call | solution.py:236
  33.4 0.3 collective-permute-done.11.refs_10_.refs_3_
  33.7 0.8 %shard_map.44 = (f32[4,8,512]{2,1,0:T(8,128)S(1)}, bf16[1,512,768]{2,1,0:T(8,128)(2,1)S(1)}, f32[1,512]{1,0:T(1,128)S(1)}, f32[1,512]{1,0:T(1,128)S(1)}) custom-call(bf16[400,128]{1,0:T(8,128)(2,1)S(1)} %collective-permute-done.refs_3_.refs_1_.refs_0_, bf16[400,128]{1,0:T(8,128)(2,1)S(1)} %collective-permute-done.2.refs_4_.refs_0_.refs_1_, ...), custom_call_target="tpu_custom_call" | custom-call | flops 276824064 | bytes 2359296 | tf_op jit(solution)/shard_map/pallas_call | solution.py:236
  34.6 0.0 collective-permute-done.12.refs_1_
  34.6 0.4 shard_map.45
  35.0 0.1 shard_map.46
  35.1 14.7 %all_to_all.5.refs_0_ = f32[32,1,128]{2,1,0:T(1,128)S(1)} all-to-all(f32[32,1,128]{2,1,0:T(1,128)S(1)} %shard_map.46), channel_id=1, replica_groups=mesh['shard'=8,'group'=4] {'shard','group'}, dimensions={0} | all-to-all | bytes 32768 | tf_op jit(solution)/shard_map/all_to_all | solution.py:426
  49.8 0.8 %shard_map.47 = f32[1,512]{1,0:T(1,128)} custom-call(f32[32,1,128]{2,1,0:T(1,128)S(1)} %all_to_all.5.refs_0_, s32[1,512]{1,0:T(1,128)S(1)} %get-tuple-element.50.refs_1_), custom_call_target="tpu_custom_call" | custom-call | flops 262144 | bytes 2048 | tf_op jit(solution)/shard_map/pallas_call | solution.py:236
  (2 shorter events, 0.0 us)
Async XLA Ops:
  0.0 1.4 %copy-start.1 = (s32[512]{0:T(512)S(1)}, s32[512]{0:T(512)}, u32[]{:S(2)}) copy-start(s32[512]{0:T(512)} %param.5) | copy-start | bytes 6148
  0.0 1.4 %copy-start = (s32[512,1]{0,1:T(1,128)S(1)}, s32[512,1]{0,1:T(1,128)}, u32[]{:S(2)}) copy-start(s32[512,1]{0,1:T(1,128)} %param.4) | copy-start | bytes 6148
  2.3 8.1 %collective-permute-start.1 = (bf16[784,128]{1,0:T(8,128)(2,1)S(1)}, bf16[784,128]{1,0:T(8,128)(2,1)S(1)}, u32[]{:S(2)}, u32[]{:S(2)}) collective-permute-start(bf16[784,128]{1,0:T(8,128)(2,1)S(1)} %get-tuple-element.32), channel_id=1, source_target_pairs={{0,1},{1,0},{2,3},{3,2},{4,5},{5,4},{6,7},{7,6},{8,9},{9,8},{10,11... | collective-permute-start | bytes 602120 | tf_op jit(solution)/shard_map/ppermute | solution.py:325
  5.4 7.2 %collective-permute-start.6 = (bf16[784,128]{1,0:T(8,128)(2,1)S(1)}, bf16[784,128]{1,0:T(8,128)(2,1)S(1)}, u32[]{:S(2)}, u32[]{:S(2)}) collective-permute-start(bf16[784,128]{1,0:T(8,128)(2,1)S(1)} %get-tuple-element.35.refs_0_.refs_4_), channel_id=1, source_target_pairs={{20,0},{0,8},{8,24},{24,16},{16,4},{4,12},{12,28},{28,20},{21,1},{... | collective-permute-start | bytes 602120 | tf_op jit(solution)/shard_map/ppermute | solution.py:322
  6.9 13.7 %collective-permute-start.5 = (bf16[784,128]{1,0:T(8,128)(2,1)S(1)}, bf16[784,128]{1,0:T(8,128)(2,1)S(1)}, u32[]{:S(2)}, u32[]{:S(2)}) collective-permute-start(bf16[784,128]{1,0:T(8,128)(2,1)S(1)} %get-tuple-element.35.refs_0_.refs_4_), channel_id=1, source_target_pairs={{8,0},{24,8},{16,24},{4,16},{12,4},{28,12},{20,28},{0,20},{9,1},{2... | collective-permute-start | bytes 602120 | tf_op jit(solution)/shard_map/ppermute | solution.py:322
  7.2 15.2 %collective-permute-start.3 = (bf16[784,128]{1,0:T(8,128)(2,1)S(1)}, bf16[784,128]{1,0:T(8,128)(2,1)S(1)}, u32[]{:S(2)}, u32[]{:S(2)}) collective-permute-start(bf16[784,128]{1,0:T(8,128)(2,1)S(1)} %get-tuple-element.34), channel_id=1, source_target_pairs={{0,2},{1,3},{2,0},{3,1},{4,6},{5,7},{6,4},{7,5},{8,10},{9,11},{10,... | collective-permute-start | bytes 602120 | tf_op jit(solution)/shard_map/ppermute | solution.py:325
  9.8 9.4 %collective-permute-start = (bf16[400,128]{1,0:T(8,128)(2,1)S(1)}, bf16[400,128]{1,0:T(8,128)(2,1)S(1)}, u32[]{:S(2)}, u32[]{:S(2)}) collective-permute-start(bf16[400,128]{1,0:T(8,128)(2,1)S(1)} %get-tuple-element.30), channel_id=1, source_target_pairs={{0,3},{1,2},{2,1},{3,0},{4,7},{5,6},{6,5},{7,4},{8,11},{9,10},{10,... | collective-permute-start | bytes 307208 | tf_op jit(solution)/shard_map/ppermute | solution.py:325
  12.6 13.2 %collective-permute-start.10 = (bf16[784,128]{1,0:T(8,128)(2,1)S(1)}, bf16[784,128]{1,0:T(8,128)(2,1)S(1)}, u32[]{:S(2)}, u32[]{:S(2)}) collective-permute-start(bf16[784,128]{1,0:T(8,128)(2,1)S(1)} %collective-permute-done.1.refs_1_.refs_3_), channel_id=1, source_target_pairs={{20,0},{0,8},{8,24},{24,16},{16,4},{4,12},{12,28},{28,20},{21,1},{... | collective-permute-start | bytes 602120 | tf_op jit(solution)/shard_map/ppermute | solution.py:322
  14.1 11.8 %collective-permute-start.8 = (bf16[784,128]{1,0:T(8,128)(2,1)S(1)}, bf16[784,128]{1,0:T(8,128)(2,1)S(1)}, u32[]{:S(2)}, u32[]{:S(2)}) collective-permute-start(bf16[784,128]{1,0:T(8,128)(2,1)S(1)} %collective-permute-done.1.refs_1_.refs_3_), channel_id=1, source_target_pairs={{8,0},{24,8},{16,24},{4,16},{12,4},{28,12},{20,28},{0,20},{9,1},{2... | collective-permute-start | bytes 602120 | tf_op jit(solution)/shard_map/ppermute | solution.py:322
  19.2 6.5 %collective-permute-start.2 = (bf16[400,128]{1,0:T(8,128)(2,1)S(1)}, bf16[400,128]{1,0:T(8,128)(2,1)S(1)}, u32[]{:S(2)}, u32[]{:S(2)}) collective-permute-start(bf16[400,128]{1,0:T(8,128)(2,1)S(1)} %get-tuple-element.33), channel_id=1, source_target_pairs={{0,3},{1,2},{2,1},{3,0},{4,7},{5,6},{6,5},{7,4},{8,11},{9,10},{10,... | collective-permute-start | bytes 307208 | tf_op jit(solution)/shard_map/ppermute | solution.py:325
  22.4 9.5 %collective-permute-start.9 = (bf16[1184,128]{1,0:T(8,128)(2,1)S(1)}, bf16[1184,128]{1,0:T(8,128)(2,1)S(1)}, u32[]{:S(2)}, u32[]{:S(2)}) collective-permute-start(bf16[1184,128]{1,0:T(8,128)(2,1)S(1)} %shard_map.40), channel_id=1, source_target_pairs={{20,0},{0,8},{8,24},{24,16},{16,4},{4,12},{12,28},{28,20},{21,1},{... | collective-permute-start | bytes 909320 | tf_op jit(solution)/shard_map/ppermute | solution.py:322
  23.5 8.4 %collective-permute-start.7 = (bf16[1184,128]{1,0:T(8,128)(2,1)S(1)}, bf16[1184,128]{1,0:T(8,128)(2,1)S(1)}, u32[]{:S(2)}, u32[]{:S(2)}) collective-permute-start(bf16[1184,128]{1,0:T(8,128)(2,1)S(1)} %shard_map.40), channel_id=1, source_target_pairs={{8,0},{24,8},{16,24},{4,16},{12,4},{28,12},{20,28},{0,20},{9,1},{2... | collective-permute-start | bytes 909320 | tf_op jit(solution)/shard_map/ppermute | solution.py:322
  25.8 2.4 %collective-permute-start.4 = (bf16[3152,128]{1,0:T(8,128)(2,1)S(1)}, bf16[3152,128]{1,0:T(8,128)(2,1)S(1)}, u32[]{:S(2)}, u32[]{:S(2)}) collective-permute-start(bf16[3152,128]{1,0:T(8,128)(2,1)S(1)} %shard_map.39), channel_id=1, source_target_pairs={{4,0},{12,8},{28,24},{20,16},{0,4},{8,12},{24,28},{16,20},{5,1},{1... | collective-permute-start | bytes 2420744 | tf_op jit(solution)/shard_map/ppermute | solution.py:322
  25.9 8.6 %collective-permute-start.12 = (bf16[400,128]{1,0:T(8,128)(2,1)S(1)}, bf16[400,128]{1,0:T(8,128)(2,1)S(1)}, u32[]{:S(2)}, u32[]{:S(2)}) collective-permute-start(bf16[400,128]{1,0:T(8,128)(2,1)S(1)} %shard_map.41), channel_id=1, source_target_pairs={{8,0},{24,8},{16,24},{4,16},{12,4},{28,12},{20,28},{0,20},{9,1},{2... | collective-permute-start | bytes 307208 | tf_op jit(solution)/shard_map/ppermute | solution.py:322
  27.6 6.1 %collective-permute-start.11 = (bf16[400,128]{1,0:T(8,128)(2,1)S(1)}, bf16[400,128]{1,0:T(8,128)(2,1)S(1)}, u32[]{:S(2)}, u32[]{:S(2)}) collective-permute-start(bf16[400,128]{1,0:T(8,128)(2,1)S(1)} %shard_map.41), channel_id=1, source_target_pairs={{20,0},{0,8},{8,24},{24,16},{16,4},{4,12},{12,28},{28,20},{21,1},{... | collective-permute-start | bytes 307208 | tf_op jit(solution)/shard_map/ppermute | solution.py:322

commit v21 on v19

--- a/solution.py
+++ b/solution.py
@@ -77,7 +77,8 @@
     slots = groups * capacity
     chunks = width // LANES
     owner = group_ref[...]
-    rel = owner ^ lax.axis_index(axis)
+    shift = (owner - lax.axis_index(axis)) & (groups - 1)
+    rel = jnp.maximum(jnp.where(2 * shift > groups, 2 * (groups - shift), 2 * shift - 1), 0)
     lines = max(8, groups)
     onehot = lax.broadcasted_iota(jnp.int32, (lines, rows), 0) == rel
     before = lax.broadcasted_iota(jnp.int32, (rows, rows), 0) < lax.broadcasted_iota(
@@ -187,6 +188,10 @@
         out_ref[...] = jnp.max(best_ref[role], axis=0, keepdims=True)
 
 
+def slot_shift(k):
+    return (k + 1) // 2 if k % 2 else -(k // 2)
+
+
 def spread_kernel(ring, offsets, groups, *refs):
     *partial_refs, out_ref = refs
     shards = len(ring)
@@ -197,7 +202,7 @@
             jnp.where(shard == ring[e], ring[(e + offset) % shards], 0) for e in range(shards)
         )
         for k in range(groups):
-            row = target * groups + (group ^ k)
+            row = target * groups + ((group - slot_shift(k)) & (groups - 1))
             out_ref[pl.ds(row, 1)] = ref[:, k * LANES : (k + 1) * LANES].reshape(1, 1, LANES)
 
 
@@ -311,8 +316,9 @@
     def exchange(blocks):
         got = list(blocks)
         for k in range(1, groups):
+            shift = slot_shift(k)
             block = after(blocks[k], got[1]) if k > 2 else blocks[k]
-            got[k] = lax.ppermute(block, "group", [(z, z ^ k) for z in range(groups)])
+            got[k] = lax.ppermute(block, "group", [(z, (z + shift) % groups) for z in range(groups)])
         return got
 
     (units,) = call(
@@ -347,14 +353,13 @@
     held[0] = [(x, None) for x in own]
     for r in near:
         held[r][0] = (first[r], None)
-    for k in range(1, groups):
-        if k == 1:
-            block = after(own[k], first[near[-1]]) if near else own[k]
-        else:
-            passed = [held[r][k - 2][0] for r in near]
-            block = stack([after(own[k], *passed)], WAIT)
-        for r in near:
-            held[r][k] = (from_offset(block, offsets[r]), 0 if k > 1 else None)
+    for ks in (early[1:], late):
+        if ks:
+            block = stack([own[k] for k in ks], WAIT)
+            for r in near:
+                moved = from_offset(block, offsets[r])
+                for i, k in enumerate(ks):
+                    held[r][k] = (moved, i)
     got = {r: from_offset(stack(own, 0), offsets[r]) for r in far}
     for r in far:
         held[r] = [(got[r], k) for k in range(groups)]

time: 47.2 us -> 46.7 us (0.989)
  waiting for transfers between devices: 7.88 us -> 12 us
  starting transfers between devices: 21.2 us -> 17.9 us
  blocking collectives: 10.2 us -> 8.87 us
    ppermute x9 -> x7, starting transfers between devices: 12.3 us -> 6.44 us  [from_offset(): return lax.ppermute(x, 'shard', perm)]
    ppermute x3, waiting for transfers between devices: 4.12 us -> 7.93 us  [exchange(): lax.ppermute(block, 'group', [(z, (z + shift) % groups) for z in range(gr...]
    ppermute x3, starting transfers between devices: 8.87 us -> 11.5 us  [exchange(): lax.ppermute(block, 'group', [(z, (z + shift) % groups) for z in range(gr...]
    all_to_all x1, blocking collectives: 10.2 us -> 8.87 us  [per_device(): lax.all_to_all(best, ('shard', 'group'), split_axis=0, concat_axis=0, til...]
    ppermute x9 -> x7, waiting for transfers between devices: 3.76 us -> 4.08 us  [from_offset(): return lax.ppermute(x, 'shard', perm)]
  transfers between devices with their start and end apart: 12 -> 10, of which waited for: 5 -> 5; matrix products, arithmetic and copies ran while one was open for 0% -> 0% of each run, Pallas kernels for 9% -> 9%
where the time goes in v21:
time: 46.7 us; the launch traced here: 46.5 us
  starting transfers between devices  17.9 us (38%)
  waiting for transfers between devices  12 us (26%)
  blocking collectives  8.87 us (19%)
  Pallas kernels  7.63 us (16%)
    ppermute x3, starting transfers between devices, exchange(): lax.ppermute(block, 'group', [(z, (z + shift) % groups) for z in range(gr...  11.5 us
    all_to_all x1, blocking collectives, per_device(): lax.all_to_all(best, ('shard', 'group'), split_axis=0, concat_axis=0, til...  8.87 us
    ppermute x3, waiting for transfers between devices, exchange(): lax.ppermute(block, 'group', [(z, (z + shift) % groups) for z in range(gr...  7.93 us
    pallas_call x11, Pallas kernels, call(): pl.pallas_call(kernel, out_shape=out_shape, in_specs=in_specs or in_vmem(...  7.63 us
    ppermute x7, starting transfers between devices, from_offset(): return lax.ppermute(x, 'shard', perm)  6.44 us
    ppermute x7, waiting for transfers between devices, from_offset(): return lax.ppermute(x, 'shard', perm)  4.08 us
  transfers between devices with their start and end apart: 10, of which 5 were waited for; matrix products, arithmetic and copies ran while one was open for 0% of the time, Pallas kernels for 9%

profile of v21, /device:TPU:0, one launch (start us, length us, event | category | flops | bytes accessed | tf_op | source)
XLA Modules:
  0.0 46.5 jit_solution(12502354467021325347)
XLA Ops:
  0.0 0.0 copy-start.1
  0.0 0.0 copy-start
  0.0 1.4 %shard_map.37.refs_0_ = bf16[512,768]{1,0:T(8,128)(2,1)S(1)} custom-call(bf16[512,768]{1,0:T(8,128)(2,1)} %far_ref.1), custom_call_target="tpu_custom_call" | custom-call | flops 1572864 | bytes 1572864 | tf_op jit(solution)/shard_map/pallas_call | solution.py:232
  1.4 0.0 copy-done.1
  1.4 0.0 copy-done
  1.4 0.9 %shard_map.38 = (bf16[784,128]{1,0:T(8,128)(2,1)S(1)}, bf16[784,128]{1,0:T(8,128)(2,1)S(1)}, bf16[784,128]{1,0:T(8,128)(2,1)S(1)}, bf16[784,128]{1,0:T(8,128)(2,1)S(1)}, s32[1,512]{1,0:T(1,128)S(1)}) custom-call(bf16[512,768]{1,0:T(8,128)(2,1)S(1)} %shard_map.37.refs_0_, s32[1,512]{1,0:T(1,128)S(1)} %bitcast.3, s32[1,512]{1,0:T(1,128)S(1)} %bitcast.4), custom_call_target="tpu_custom_call" | custom-call | flops 402653184 | bytes 1572864 | tf_op jit(solution)/shard_map/pallas_call | solution.py:232
  2.3 3.1 %collective-permute-start = (bf16[784,128]{1,0:T(8,128)(2,1)S(1)}, bf16[784,128]{1,0:T(8,128)(2,1)S(1)}, u32[]{:S(2)}, u32[]{:S(2)}) collective-permute-start(bf16[784,128]{1,0:T(8,128)(2,1)S(1)} %get-tuple-element.26), channel_id=1, source_target_pairs={{0,1},{1,2},{2,3},{3,0},{4,5},{5,6},{6,7},{7,4},{8,9},{9,10},{10,1... | collective-permute-start | bytes 602120 | tf_op jit(solution)/shard_map/ppermute | solution.py:321
  5.4 2.1 %collective-permute-start.2 = (bf16[784,128]{1,0:T(8,128)(2,1)S(1)}, bf16[784,128]{1,0:T(8,128)(2,1)S(1)}, u32[]{:S(2)}, u32[]{:S(2)}) collective-permute-start(bf16[784,128]{1,0:T(8,128)(2,1)S(1)} %get-tuple-element.28), channel_id=1, source_target_pairs={{0,3},{1,0},{2,1},{3,2},{4,7},{5,4},{6,5},{7,6},{8,11},{9,8},{10,9... | collective-permute-start | bytes 602120 | tf_op jit(solution)/shard_map/ppermute | solution.py:321
  7.5 1.6 %collective-permute-start.8 = (bf16[784,128]{1,0:T(8,128)(2,1)S(1)}, bf16[784,128]{1,0:T(8,128)(2,1)S(1)}, u32[]{:S(2)}, u32[]{:S(2)}) collective-permute-start(bf16[784,128]{1,0:T(8,128)(2,1)S(1)} %get-tuple-element.29.refs_0_.refs_3_), channel_id=1, source_target_pairs={{20,0},{0,8},{8,24},{24,16},{16,4},{4,12},{12,28},{28,20},{21,1},{... | collective-permute-start | bytes 602120 | tf_op jit(solution)/shard_map/ppermute | solution.py:314
  9.2 0.1 collective-permute-start.5
  9.3 4.0 %collective-permute-done.refs_1_.refs_0_.refs_2_ = bf16[784,128]{1,0:T(8,128)(2,1)S(1)} collective-permute-done((bf16[784,128]{1,0:T(8,128)(2,1)S(1)}, bf16[784,128]{1,0:T(8,128)(2,1)S(1)}, u32[]{:S(2)}, u32[]{:S(2)}) %collective-permute-start) | collective-permute-done | bytes 200736 | tf_op jit(solution)/shard_map/ppermute | solution.py:321
  13.3 6.3 %collective-permute-start.1 = (bf16[784,128]{1,0:T(8,128)(2,1)S(1)}, bf16[784,128]{1,0:T(8,128)(2,1)S(1)}, u32[]{:S(2)}, u32[]{:S(2)}) collective-permute-start(bf16[784,128]{1,0:T(8,128)(2,1)S(1)} %get-tuple-element.27), channel_id=1, source_target_pairs={{0,2},{1,3},{2,0},{3,1},{4,6},{5,7},{6,4},{7,5},{8,10},{9,11},{10,... | collective-permute-start | bytes 602120 | tf_op jit(solution)/shard_map/ppermute | solution.py:321
  19.6 0.0 collective-permute-done.2.refs_2_.refs_1_
  19.6 1.6 %collective-permute-start.7 = (bf16[2,784,128]{2,1,0:T(8,128)(2,1)S(1)}, bf16[2,784,128]{2,1,0:T(8,128)(2,1)S(1)}, u32[]{:S(2)}, u32[]{:S(2)}) collective-permute-start(bf16[2,784,128]{2,1,0:T(8,128)(2,1)S(1)} %shard_map.40), channel_id=1, source_target_pairs={{20,0},{0,8},{8,24},{24,16},{16,4},{4,12},{12,28},{28,20},{21,1},{... | collective-permute-start | bytes 1204232 | tf_op jit(solution)/shard_map/ppermute | solution.py:314
  21.2 0.3 collective-permute-start.4
  21.5 3.9 %collective-permute-done.1.refs_3_.refs_0_ = bf16[784,128]{1,0:T(8,128)(2,1)S(1)} collective-permute-done((bf16[784,128]{1,0:T(8,128)(2,1)S(1)}, bf16[784,128]{1,0:T(8,128)(2,1)S(1)}, u32[]{:S(2)}, u32[]{:S(2)}) %collective-permute-start.1) | collective-permute-done | bytes 200736 | tf_op jit(solution)/shard_map/ppermute | solution.py:321
  25.3 0.1 shard_map.39
  25.4 0.1 collective-permute-start.3
  25.5 0.0 collective-permute-done.8.refs_8_.refs_3_
  25.5 1.6 %collective-permute-start.6 = (bf16[1,784,128]{2,1,0:T(8,128)(2,1)S(1)}, bf16[1,784,128]{2,1,0:T(8,128)(2,1)S(1)}, u32[]{:S(2)}, u32[]{:S(2)}) collective-permute-start(bf16[1,784,128]{2,1,0:T(8,128)(2,1)S(1)} %shard_map.41), channel_id=1, source_target_pairs={{20,0},{0,8},{8,24},{24,16},{16,4},{4,12},{12,28},{28,20},{21,1},{... | collective-permute-start | bytes 602120 | tf_op jit(solution)/shard_map/ppermute | solution.py:314
  27.1 0.7 %collective-permute-done.3.refs_4_ = bf16[4,784,128]{2,1,0:T(8,128)(2,1)S(1)} collective-permute-done((bf16[4,784,128]{2,1,0:T(8,128)(2,1)S(1)}, bf16[4,784,128]{2,1,0:T(8,128)(2,1)S(1)}, u32[]{:S(2)}, u32[]{:S(2)}) %collective-permute-start.3) | collective-permute-done | bytes 802848 | tf_op jit(solution)/shard_map/ppermute | solution.py:314
  27.8 1.3 %collective-permute-start.9 = (bf16[1,784,128]{2,1,0:T(8,128)(2,1)S(1)}, bf16[1,784,128]{2,1,0:T(8,128)(2,1)S(1)}, u32[]{:S(2)}, u32[]{:S(2)}) collective-permute-start(bf16[1,784,128]{2,1,0:T(8,128)(2,1)S(1)} %shard_map.41), channel_id=1, source_target_pairs={{8,0},{24,8},{16,24},{4,16},{12,4},{28,12},{20,28},{0,20},{9,1},{2... | collective-permute-start | bytes 602120 | tf_op jit(solution)/shard_map/ppermute | solution.py:314
  29.0 1.5 %shard_map.42 = (f32[4,8,512]{2,1,0:T(8,128)S(1)}, bf16[2,512,768]{2,1,0:T(8,128)(2,1)S(1)}) custom-call(bf16[784,128]{1,0:T(8,128)(2,1)S(1)} %collective-permute-done.1.refs_3_.refs_0_, bf16[784,128]{1,0:T(8,128)(2,1)S(1)} %collective-permute-done.2.refs_2_.refs_1_, bf16[784,128]{1,0:T(8,128)(2,1)S(1)} %collective-permute-done.refs_1_.refs_0_.refs_2_, ...), custom_call_target="tpu_custom_call" | custom-call | flops 805306368 | bytes 1572864 | tf_op jit(solution)/shard_map/pallas_call | solution.py:232
  30.6 0.0 collective-permute-done.5.refs_6_
  30.6 0.7 %collective-permute-done.7.refs_7_.refs_2_ = bf16[2,784,128]{2,1,0:T(8,128)(2,1)S(1)} collective-permute-done((bf16[2,784,128]{2,1,0:T(8,128)(2,1)S(1)}, bf16[2,784,128]{2,1,0:T(8,128)(2,1)S(1)}, u32[]{:S(2)}, u32[]{:S(2)}) %collective-permute-start.7) | collective-permute-done | bytes 401440 | tf_op jit(solution)/shard_map/ppermute | solution.py:314
  31.2 0.0 collective-permute-done.4.refs_5_
  31.2 1.6 %shard_map.43 = (f32[4,8,512]{2,1,0:T(8,128)S(1)}, bf16[2,512,768]{2,1,0:T(8,128)(2,1)S(1)}) custom-call(bf16[784,128]{1,0:T(8,128)(2,1)S(1)} %collective-permute-done.1.refs_3_.refs_0_, bf16[784,128]{1,0:T(8,128)(2,1)S(1)} %collective-permute-done.2.refs_2_.refs_1_, bf16[784,128]{1,0:T(8,128)(2,1)S(1)} %collective-permute-done.refs_1_.refs_0_.refs_2_, ...), custom_call_target="tpu_custom_call" | custom-call | flops 830472192 | bytes 2752512 | tf_op jit(solution)/shard_map/pallas_call | solution.py:232
  32.8 2.7 %collective-permute-done.6.refs_7_.refs_1_ = bf16[1,784,128]{2,1,0:T(8,128)(2,1)S(1)} collective-permute-done((bf16[1,784,128]{2,1,0:T(8,128)(2,1)S(1)}, bf16[1,784,128]{2,1,0:T(8,128)(2,1)S(1)}, u32[]{:S(2)}, u32[]{:S(2)}) %collective-permute-start.6) | collective-permute-done | bytes 200736 | tf_op jit(solution)/shard_map/ppermute | solution.py:314
  35.5 0.8 %shard_map.44 = (f32[4,8,512]{2,1,0:T(8,128)S(1)}, bf16[1,512,768]{2,1,0:T(8,128)(2,1)S(1)}, f32[1,512]{1,0:T(1,128)S(1)}, f32[1,512]{1,0:T(1,128)S(1)}) custom-call(bf16[784,128]{1,0:T(8,128)(2,1)S(1)} %collective-permute-done.1.refs_3_.refs_0_, bf16[784,128]{1,0:T(8,128)(2,1)S(1)} %collective-permute-done.2.refs_2_.refs_1_, ...), custom_call_target="tpu_custom_call" | custom-call | flops 276824064 | bytes 2359296 | tf_op jit(solution)/shard_map/pallas_call | solution.py:232
  36.4 0.0 collective-permute-done.9.refs_0_
  36.4 0.4 shard_map.45
  36.8 0.1 shard_map.46
  36.9 8.9 %all_to_all.5.refs_0_ = f32[32,1,128]{2,1,0:T(1,128)S(1)} all-to-all(f32[32,1,128]{2,1,0:T(1,128)S(1)} %shard_map.46), channel_id=1, replica_groups=mesh['shard'=8,'group'=4] {'shard','group'}, dimensions={0} | all-to-all | bytes 32768 | tf_op jit(solution)/shard_map/all_to_all | solution.py:401
  45.8 0.8 %shard_map.47 = f32[1,512]{1,0:T(1,128)} custom-call(f32[32,1,128]{2,1,0:T(1,128)S(1)} %all_to_all.5.refs_0_, s32[1,512]{1,0:T(1,128)S(1)} %get-tuple-element.40.refs_1_), custom_call_target="tpu_custom_call" | custom-call | flops 262144 | bytes 2048 | tf_op jit(solution)/shard_map/pallas_call | solution.py:232
  (2 shorter events, 0.0 us)
Async XLA Ops:
  0.0 1.4 %copy-start.1 = (s32[512]{0:T(512)S(1)}, s32[512]{0:T(512)}, u32[]{:S(2)}) copy-start(s32[512]{0:T(512)} %param.5) | copy-start | bytes 6148
  0.0 1.4 %copy-start = (s32[512,1]{0,1:T(1,128)S(1)}, s32[512,1]{0,1:T(1,128)}, u32[]{:S(2)}) copy-start(s32[512,1]{0,1:T(1,128)} %param.4) | copy-start | bytes 6148
  2.3 11.0 %collective-permute-start = (bf16[784,128]{1,0:T(8,128)(2,1)S(1)}, bf16[784,128]{1,0:T(8,128)(2,1)S(1)}, u32[]{:S(2)}, u32[]{:S(2)}) collective-permute-start(bf16[784,128]{1,0:T(8,128)(2,1)S(1)} %get-tuple-element.26), channel_id=1, source_target_pairs={{0,1},{1,2},{2,3},{3,0},{4,5},{5,6},{6,7},{7,4},{8,9},{9,10},{10,1... | collective-permute-start | bytes 602120 | tf_op jit(solution)/shard_map/ppermute | solution.py:321
  5.4 14.2 %collective-permute-start.2 = (bf16[784,128]{1,0:T(8,128)(2,1)S(1)}, bf16[784,128]{1,0:T(8,128)(2,1)S(1)}, u32[]{:S(2)}, u32[]{:S(2)}) collective-permute-start(bf16[784,128]{1,0:T(8,128)(2,1)S(1)} %get-tuple-element.28), channel_id=1, source_target_pairs={{0,3},{1,0},{2,1},{3,2},{4,7},{5,4},{6,5},{7,6},{8,11},{9,8},{10,9... | collective-permute-start | bytes 602120 | tf_op jit(solution)/shard_map/ppermute | solution.py:321
  7.5 18.0 %collective-permute-start.8 = (bf16[784,128]{1,0:T(8,128)(2,1)S(1)}, bf16[784,128]{1,0:T(8,128)(2,1)S(1)}, u32[]{:S(2)}, u32[]{:S(2)}) collective-permute-start(bf16[784,128]{1,0:T(8,128)(2,1)S(1)} %get-tuple-element.29.refs_0_.refs_3_), channel_id=1, source_target_pairs={{20,0},{0,8},{8,24},{24,16},{16,4},{4,12},{12,28},{28,20},{21,1},{... | collective-permute-start | bytes 602120 | tf_op jit(solution)/shard_map/ppermute | solution.py:314
  9.2 21.4 %collective-permute-start.5 = (bf16[784,128]{1,0:T(8,128)(2,1)S(1)}, bf16[784,128]{1,0:T(8,128)(2,1)S(1)}, u32[]{:S(2)}, u32[]{:S(2)}) collective-permute-start(bf16[784,128]{1,0:T(8,128)(2,1)S(1)} %get-tuple-element.29.refs_0_.refs_3_), channel_id=1, source_target_pairs={{8,0},{24,8},{16,24},{4,16},{12,4},{28,12},{20,28},{0,20},{9,1},{2... | collective-permute-start | bytes 602120 | tf_op jit(solution)/shard_map/ppermute | solution.py:314
  13.3 12.0 %collective-permute-start.1 = (bf16[784,128]{1,0:T(8,128)(2,1)S(1)}, bf16[784,128]{1,0:T(8,128)(2,1)S(1)}, u32[]{:S(2)}, u32[]{:S(2)}) collective-permute-start(bf16[784,128]{1,0:T(8,128)(2,1)S(1)} %get-tuple-element.27), channel_id=1, source_target_pairs={{0,2},{1,3},{2,0},{3,1},{4,6},{5,7},{6,4},{7,5},{8,10},{9,11},{10,... | collective-permute-start | bytes 602120 | tf_op jit(solution)/shard_map/ppermute | solution.py:321
  19.6 11.6 %collective-permute-start.7 = (bf16[2,784,128]{2,1,0:T(8,128)(2,1)S(1)}, bf16[2,784,128]{2,1,0:T(8,128)(2,1)S(1)}, u32[]{:S(2)}, u32[]{:S(2)}) collective-permute-start(bf16[2,784,128]{2,1,0:T(8,128)(2,1)S(1)} %shard_map.40), channel_id=1, source_target_pairs={{20,0},{0,8},{8,24},{24,16},{16,4},{4,12},{12,28},{28,20},{21,1},{... | collective-permute-start | bytes 1204232 | tf_op jit(solution)/shard_map/ppermute | solution.py:314
  21.2 10.0 %collective-permute-start.4 = (bf16[2,784,128]{2,1,0:T(8,128)(2,1)S(1)}, bf16[2,784,128]{2,1,0:T(8,128)(2,1)S(1)}, u32[]{:S(2)}, u32[]{:S(2)}) collective-permute-start(bf16[2,784,128]{2,1,0:T(8,128)(2,1)S(1)} %shard_map.40), channel_id=1, source_target_pairs={{8,0},{24,8},{16,24},{4,16},{12,4},{28,12},{20,28},{0,20},{9,1},{2... | collective-permute-start | bytes 1204232 | tf_op jit(solution)/shard_map/ppermute | solution.py:314
  25.4 2.4 %collective-permute-start.3 = (bf16[4,784,128]{2,1,0:T(8,128)(2,1)S(1)}, bf16[4,784,128]{2,1,0:T(8,128)(2,1)S(1)}, u32[]{:S(2)}, u32[]{:S(2)}) collective-permute-start(bf16[4,784,128]{2,1,0:T(8,128)(2,1)S(1)} %shard_map.39), channel_id=1, source_target_pairs={{4,0},{12,8},{28,24},{20,16},{0,4},{8,12},{24,28},{16,20},{5,1},{1... | collective-permute-start | bytes 2408456 | tf_op jit(solution)/shard_map/ppermute | solution.py:314
  25.5 10.0 %collective-permute-start.6 = (bf16[1,784,128]{2,1,0:T(8,128)(2,1)S(1)}, bf16[1,784,128]{2,1,0:T(8,128)(2,1)S(1)}, u32[]{:S(2)}, u32[]{:S(2)}) collective-permute-start(bf16[1,784,128]{2,1,0:T(8,128)(2,1)S(1)} %shard_map.41), channel_id=1, source_target_pairs={{20,0},{0,8},{8,24},{24,16},{16,4},{4,12},{12,28},{28,20},{21,1},{... | collective-permute-start | bytes 602120 | tf_op jit(solution)/shard_map/ppermute | solution.py:314
  27.8 8.6 %collective-permute-start.9 = (bf16[1,784,128]{2,1,0:T(8,128)(2,1)S(1)}, bf16[1,784,128]{2,1,0:T(8,128)(2,1)S(1)}, u32[]{:S(2)}, u32[]{:S(2)}) collective-permute-start(bf16[1,784,128]{2,1,0:T(8,128)(2,1)S(1)} %shard_map.41), channel_id=1, source_target_pairs={{8,0},{24,8},{16,24},{4,16},{12,4},{28,12},{20,28},{0,20},{9,1},{2... | collective-permute-start | bytes 602120 | tf_op jit(solution)/shard_map/ppermute | solution.py:314

commit v22 on v21

--- a/solution.py
+++ b/solution.py
@@ -317,7 +317,7 @@
         got = list(blocks)
         for k in range(1, groups):
             shift = slot_shift(k)
-            block = after(blocks[k], got[1]) if k > 2 else blocks[k]
+            block = after(blocks[k], got[1], got[2]) if k > 2 else blocks[k]
             got[k] = lax.ppermute(block, "group", [(z, (z + shift) % groups) for z in range(groups)])
         return got
 

time: 46.7 us -> 49.5 us (1.060)
  waiting for transfers between devices: 12 us -> 17.8 us
  starting transfers between devices: 17.9 us -> 12.9 us
  blocking collectives: 8.87 us -> 10.9 us
    ppermute x3, waiting for transfers between devices: 7.93 us -> 15.3 us  [exchange(): lax.ppermute(block, 'group', [(z, (z + shift) % groups) for z in range(gr...]
    ppermute x3, starting transfers between devices: 11.5 us -> 6.46 us  [exchange(): lax.ppermute(block, 'group', [(z, (z + shift) % groups) for z in range(gr...]
    all_to_all x1, blocking collectives: 8.87 us -> 10.9 us  [per_device(): lax.all_to_all(best, ('shard', 'group'), split_axis=0, concat_axis=0, til...]
    ppermute x7, waiting for transfers between devices: 4.08 us -> 2.5 us  [from_offset(): return lax.ppermute(x, 'shard', perm)]
  transfers between devices with their start and end apart: 10 -> 10, of which waited for: 5 -> 6; matrix products, arithmetic and copies ran while one was open for 0% -> 0% of each run, Pallas kernels for 9% -> 8%
where the time goes in v22:
time: 49.5 us; the launch traced here: 49.3 us
  waiting for transfers between devices  17.8 us (36%)
  starting transfers between devices  12.9 us (26%)
  blocking collectives  10.9 us (22%)
  Pallas kernels  7.63 us (15%)
    ppermute x3, waiting for transfers between devices, exchange(): lax.ppermute(block, 'group', [(z, (z + shift) % groups) for z in range(gr...  15.3 us
    all_to_all x1, blocking collectives, per_device(): lax.all_to_all(best, ('shard', 'group'), split_axis=0, concat_axis=0, til...  10.9 us
    pallas_call x11, Pallas kernels, call(): pl.pallas_call(kernel, out_shape=out_shape, in_specs=in_specs or in_vmem(...  7.63 us
    ppermute x3, starting transfers between devices, exchange(): lax.ppermute(block, 'group', [(z, (z + shift) % groups) for z in range(gr...  6.46 us
    ppermute x7, starting transfers between devices, from_offset(): return lax.ppermute(x, 'shard', perm)  6.43 us
    ppermute x7, waiting for transfers between devices, from_offset(): return lax.ppermute(x, 'shard', perm)  2.5 us
  transfers between devices with their start and end apart: 10, of which 6 were waited for; matrix products, arithmetic and copies ran while one was open for 0% of the time, Pallas kernels for 8%

profile of v22, /device:TPU:0, one launch (start us, length us, event | category | flops | bytes accessed | tf_op | source)
XLA Modules:
  0.0 49.3 jit_solution(10594412670035482570)
XLA Ops:
  0.0 0.0 copy-start.1
  0.0 0.0 copy-start
  0.0 1.4 %shard_map.37.refs_0_ = bf16[512,768]{1,0:T(8,128)(2,1)S(1)} custom-call(bf16[512,768]{1,0:T(8,128)(2,1)} %far_ref.1), custom_call_target="tpu_custom_call" | custom-call | flops 1572864 | bytes 1572864 | tf_op jit(solution)/shard_map/pallas_call | solution.py:232
  1.4 0.0 copy-done.1
  1.4 0.0 copy-done
  1.4 0.9 %shard_map.38 = (bf16[784,128]{1,0:T(8,128)(2,1)S(1)}, bf16[784,128]{1,0:T(8,128)(2,1)S(1)}, bf16[784,128]{1,0:T(8,128)(2,1)S(1)}, bf16[784,128]{1,0:T(8,128)(2,1)S(1)}, s32[1,512]{1,0:T(1,128)S(1)}) custom-call(bf16[512,768]{1,0:T(8,128)(2,1)S(1)} %shard_map.37.refs_0_, s32[1,512]{1,0:T(1,128)S(1)} %bitcast.3, s32[1,512]{1,0:T(1,128)S(1)} %bitcast.4), custom_call_target="tpu_custom_call" | custom-call | flops 402653184 | bytes 1572864 | tf_op jit(solution)/shard_map/pallas_call | solution.py:232
  2.3 3.1 %collective-permute-start = (bf16[784,128]{1,0:T(8,128)(2,1)S(1)}, bf16[784,128]{1,0:T(8,128)(2,1)S(1)}, u32[]{:S(2)}, u32[]{:S(2)}) collective-permute-start(bf16[784,128]{1,0:T(8,128)(2,1)S(1)} %get-tuple-element.26), channel_id=1, source_target_pairs={{0,1},{1,2},{2,3},{3,0},{4,5},{5,6},{6,7},{7,4},{8,9},{9,10},{10,1... | collective-permute-start | bytes 602120 | tf_op jit(solution)/shard_map/ppermute | solution.py:321
  5.4 2.1 %collective-permute-start.1 = (bf16[784,128]{1,0:T(8,128)(2,1)S(1)}, bf16[784,128]{1,0:T(8,128)(2,1)S(1)}, u32[]{:S(2)}, u32[]{:S(2)}) collective-permute-start(bf16[784,128]{1,0:T(8,128)(2,1)S(1)} %get-tuple-element.27), channel_id=1, source_target_pairs={{0,3},{1,0},{2,1},{3,2},{4,7},{5,4},{6,5},{7,6},{8,11},{9,8},{10,9... | collective-permute-start | bytes 602120 | tf_op jit(solution)/shard_map/ppermute | solution.py:321
  7.5 1.6 %collective-permute-start.8 = (bf16[784,128]{1,0:T(8,128)(2,1)S(1)}, bf16[784,128]{1,0:T(8,128)(2,1)S(1)}, u32[]{:S(2)}, u32[]{:S(2)}) collective-permute-start(bf16[784,128]{1,0:T(8,128)(2,1)S(1)} %get-tuple-element.29.refs_0_.refs_3_), channel_id=1, source_target_pairs={{20,0},{0,8},{8,24},{24,16},{16,4},{4,12},{12,28},{28,20},{21,1},{... | collective-permute-start | bytes 602120 | tf_op jit(solution)/shard_map/ppermute | solution.py:314
  9.2 0.1 collective-permute-start.5
  9.3 4.0 %collective-permute-done.refs_1_.refs_0_.refs_2_ = bf16[784,128]{1,0:T(8,128)(2,1)S(1)} collective-permute-done((bf16[784,128]{1,0:T(8,128)(2,1)S(1)}, bf16[784,128]{1,0:T(8,128)(2,1)S(1)}, u32[]{:S(2)}, u32[]{:S(2)}) %collective-permute-start) | collective-permute-done | bytes 200736 | tf_op jit(solution)/shard_map/ppermute | solution.py:321
  13.3 2.9 %collective-permute-done.1.refs_2_.refs_1_ = bf16[784,128]{1,0:T(8,128)(2,1)S(1)} collective-permute-done((bf16[784,128]{1,0:T(8,128)(2,1)S(1)}, bf16[784,128]{1,0:T(8,128)(2,1)S(1)}, u32[]{:S(2)}, u32[]{:S(2)}) %collective-permute-start.1) | collective-permute-done | bytes 200736 | tf_op jit(solution)/shard_map/ppermute | solution.py:321
  16.2 1.3 %collective-permute-start.2 = (bf16[784,128]{1,0:T(8,128)(2,1)S(1)}, bf16[784,128]{1,0:T(8,128)(2,1)S(1)}, u32[]{:S(2)}, u32[]{:S(2)}) collective-permute-start(bf16[784,128]{1,0:T(8,128)(2,1)S(1)} %get-tuple-element.28), channel_id=1, source_target_pairs={{0,2},{1,3},{2,0},{3,1},{4,6},{5,7},{6,4},{7,5},{8,10},{9,11},{10,... | collective-permute-start | bytes 602120 | tf_op jit(solution)/shard_map/ppermute | solution.py:321
  17.5 1.6 %collective-permute-start.7 = (bf16[2,784,128]{2,1,0:T(8,128)(2,1)S(1)}, bf16[2,784,128]{2,1,0:T(8,128)(2,1)S(1)}, u32[]{:S(2)}, u32[]{:S(2)}) collective-permute-start(bf16[2,784,128]{2,1,0:T(8,128)(2,1)S(1)} %shard_map.40), channel_id=1, source_target_pairs={{20,0},{0,8},{8,24},{24,16},{16,4},{4,12},{12,28},{28,20},{21,1},{... | collective-permute-start | bytes 1204232 | tf_op jit(solution)/shard_map/ppermute | solution.py:314
  19.0 0.3 collective-permute-start.4
  19.3 8.4 %collective-permute-done.2.refs_3_.refs_0_ = bf16[784,128]{1,0:T(8,128)(2,1)S(1)} collective-permute-done((bf16[784,128]{1,0:T(8,128)(2,1)S(1)}, bf16[784,128]{1,0:T(8,128)(2,1)S(1)}, u32[]{:S(2)}, u32[]{:S(2)}) %collective-permute-start.2) | collective-permute-done | bytes 200736 | tf_op jit(solution)/shard_map/ppermute | solution.py:321
  27.7 0.1 shard_map.39
  27.7 0.1 collective-permute-start.3
  27.8 0.0 collective-permute-done.8.refs_8_.refs_3_
  27.8 1.6 %collective-permute-start.6 = (bf16[1,784,128]{2,1,0:T(8,128)(2,1)S(1)}, bf16[1,784,128]{2,1,0:T(8,128)(2,1)S(1)}, u32[]{:S(2)}, u32[]{:S(2)}) collective-permute-start(bf16[1,784,128]{2,1,0:T(8,128)(2,1)S(1)} %shard_map.41), channel_id=1, source_target_pairs={{20,0},{0,8},{8,24},{24,16},{16,4},{4,12},{12,28},{28,20},{21,1},{... | collective-permute-start | bytes 602120 | tf_op jit(solution)/shard_map/ppermute | solution.py:314
  29.4 0.7 %collective-permute-done.3.refs_4_ = bf16[4,784,128]{2,1,0:T(8,128)(2,1)S(1)} collective-permute-done((bf16[4,784,128]{2,1,0:T(8,128)(2,1)S(1)}, bf16[4,784,128]{2,1,0:T(8,128)(2,1)S(1)}, u32[]{:S(2)}, u32[]{:S(2)}) %collective-permute-start.3) | collective-permute-done | bytes 802848 | tf_op jit(solution)/shard_map/ppermute | solution.py:314
  30.1 1.3 %collective-permute-start.9 = (bf16[1,784,128]{2,1,0:T(8,128)(2,1)S(1)}, bf16[1,784,128]{2,1,0:T(8,128)(2,1)S(1)}, u32[]{:S(2)}, u32[]{:S(2)}) collective-permute-start(bf16[1,784,128]{2,1,0:T(8,128)(2,1)S(1)} %shard_map.41), channel_id=1, source_target_pairs={{8,0},{24,8},{16,24},{4,16},{12,4},{28,12},{20,28},{0,20},{9,1},{2... | collective-permute-start | bytes 602120 | tf_op jit(solution)/shard_map/ppermute | solution.py:314
  31.3 1.5 %shard_map.42 = (f32[4,8,512]{2,1,0:T(8,128)S(1)}, bf16[2,512,768]{2,1,0:T(8,128)(2,1)S(1)}) custom-call(bf16[784,128]{1,0:T(8,128)(2,1)S(1)} %collective-permute-done.2.refs_3_.refs_0_, bf16[784,128]{1,0:T(8,128)(2,1)S(1)} %collective-permute-done.1.refs_2_.refs_1_, bf16[784,128]{1,0:T(8,128)(2,1)S(1)} %collective-permute-done.refs_1_.refs_0_.refs_2_, ...), custom_call_target="tpu_custom_call" | custom-call | flops 805306368 | bytes 1572864 | tf_op jit(solution)/shard_map/pallas_call | solution.py:232
  32.9 0.0 collective-permute-done.5.refs_6_
  32.9 0.0 collective-permute-done.7.refs_7_.refs_2_
  32.9 0.0 collective-permute-done.4.refs_5_
  32.9 1.6 %shard_map.43 = (f32[4,8,512]{2,1,0:T(8,128)S(1)}, bf16[2,512,768]{2,1,0:T(8,128)(2,1)S(1)}) custom-call(bf16[784,128]{1,0:T(8,128)(2,1)S(1)} %collective-permute-done.2.refs_3_.refs_0_, bf16[784,128]{1,0:T(8,128)(2,1)S(1)} %collective-permute-done.1.refs_2_.refs_1_, bf16[784,128]{1,0:T(8,128)(2,1)S(1)} %collective-permute-done.refs_1_.refs_0_.refs_2_, ...), custom_call_target="tpu_custom_call" | custom-call | flops 830472192 | bytes 2752512 | tf_op jit(solution)/shard_map/pallas_call | solution.py:232
  34.5 0.1 collective-permute-done.6.refs_7_.refs_1_
  34.6 0.8 %shard_map.44 = (f32[4,8,512]{2,1,0:T(8,128)S(1)}, bf16[1,512,768]{2,1,0:T(8,128)(2,1)S(1)}, f32[1,512]{1,0:T(1,128)S(1)}, f32[1,512]{1,0:T(1,128)S(1)}) custom-call(bf16[784,128]{1,0:T(8,128)(2,1)S(1)} %collective-permute-done.2.refs_3_.refs_0_, bf16[784,128]{1,0:T(8,128)(2,1)S(1)} %collective-permute-done.1.refs_2_.refs_1_, ...), custom_call_target="tpu_custom_call" | custom-call | flops 276824064 | bytes 2359296 | tf_op jit(solution)/shard_map/pallas_call | solution.py:232
  35.4 1.7 %collective-permute-done.9.refs_0_ = bf16[1,784,128]{2,1,0:T(8,128)(2,1)S(1)} collective-permute-done((bf16[1,784,128]{2,1,0:T(8,128)(2,1)S(1)}, bf16[1,784,128]{2,1,0:T(8,128)(2,1)S(1)}, u32[]{:S(2)}, u32[]{:S(2)}) %collective-permute-start.9) | collective-permute-done | bytes 200736 | tf_op jit(solution)/shard_map/ppermute | solution.py:314
  37.1 0.4 shard_map.45
  37.6 0.1 shard_map.46
  37.6 10.9 %all_to_all.5.refs_0_ = f32[32,1,128]{2,1,0:T(1,128)S(1)} all-to-all(f32[32,1,128]{2,1,0:T(1,128)S(1)} %shard_map.46), channel_id=1, replica_groups=mesh['shard'=8,'group'=4] {'shard','group'}, dimensions={0} | all-to-all | bytes 32768 | tf_op jit(solution)/shard_map/all_to_all | solution.py:401
  48.6 0.8 %shard_map.47 = f32[1,512]{1,0:T(1,128)} custom-call(f32[32,1,128]{2,1,0:T(1,128)S(1)} %all_to_all.5.refs_0_, s32[1,512]{1,0:T(1,128)S(1)} %get-tuple-element.40.refs_1_), custom_call_target="tpu_custom_call" | custom-call | flops 262144 | bytes 2048 | tf_op jit(solution)/shard_map/pallas_call | solution.py:232
  (2 shorter events, 0.0 us)
Async XLA Ops:
  0.0 1.4 %copy-start.1 = (s32[512]{0:T(512)S(1)}, s32[512]{0:T(512)}, u32[]{:S(2)}) copy-start(s32[512]{0:T(512)} %param.5) | copy-start | bytes 6148
  0.0 1.4 %copy-start = (s32[512,1]{0,1:T(1,128)S(1)}, s32[512,1]{0,1:T(1,128)}, u32[]{:S(2)}) copy-start(s32[512,1]{0,1:T(1,128)} %param.4) | copy-start | bytes 6148
  2.3 11.0 %collective-permute-start = (bf16[784,128]{1,0:T(8,128)(2,1)S(1)}, bf16[784,128]{1,0:T(8,128)(2,1)S(1)}, u32[]{:S(2)}, u32[]{:S(2)}) collective-permute-start(bf16[784,128]{1,0:T(8,128)(2,1)S(1)} %get-tuple-element.26), channel_id=1, source_target_pairs={{0,1},{1,2},{2,3},{3,0},{4,5},{5,6},{6,7},{7,4},{8,9},{9,10},{10,1... | collective-permute-start | bytes 602120 | tf_op jit(solution)/shard_map/ppermute | solution.py:321
  5.4 10.8 %collective-permute-start.1 = (bf16[784,128]{1,0:T(8,128)(2,1)S(1)}, bf16[784,128]{1,0:T(8,128)(2,1)S(1)}, u32[]{:S(2)}, u32[]{:S(2)}) collective-permute-start(bf16[784,128]{1,0:T(8,128)(2,1)S(1)} %get-tuple-element.27), channel_id=1, source_target_pairs={{0,3},{1,0},{2,1},{3,2},{4,7},{5,4},{6,5},{7,6},{8,11},{9,8},{10,9... | collective-permute-start | bytes 602120 | tf_op jit(solution)/shard_map/ppermute | solution.py:321
  7.5 20.3 %collective-permute-start.8 = (bf16[784,128]{1,0:T(8,128)(2,1)S(1)}, bf16[784,128]{1,0:T(8,128)(2,1)S(1)}, u32[]{:S(2)}, u32[]{:S(2)}) collective-permute-start(bf16[784,128]{1,0:T(8,128)(2,1)S(1)} %get-tuple-element.29.refs_0_.refs_3_), channel_id=1, source_target_pairs={{20,0},{0,8},{8,24},{24,16},{16,4},{4,12},{12,28},{28,20},{21,1},{... | collective-permute-start | bytes 602120 | tf_op jit(solution)/shard_map/ppermute | solution.py:314
  9.2 23.7 %collective-permute-start.5 = (bf16[784,128]{1,0:T(8,128)(2,1)S(1)}, bf16[784,128]{1,0:T(8,128)(2,1)S(1)}, u32[]{:S(2)}, u32[]{:S(2)}) collective-permute-start(bf16[784,128]{1,0:T(8,128)(2,1)S(1)} %get-tuple-element.29.refs_0_.refs_3_), channel_id=1, source_target_pairs={{8,0},{24,8},{16,24},{4,16},{12,4},{28,12},{20,28},{0,20},{9,1},{2... | collective-permute-start | bytes 602120 | tf_op jit(solution)/shard_map/ppermute | solution.py:314
  16.2 11.5 %collective-permute-start.2 = (bf16[784,128]{1,0:T(8,128)(2,1)S(1)}, bf16[784,128]{1,0:T(8,128)(2,1)S(1)}, u32[]{:S(2)}, u32[]{:S(2)}) collective-permute-start(bf16[784,128]{1,0:T(8,128)(2,1)S(1)} %get-tuple-element.28), channel_id=1, source_target_pairs={{0,2},{1,3},{2,0},{3,1},{4,6},{5,7},{6,4},{7,5},{8,10},{9,11},{10,... | collective-permute-start | bytes 602120 | tf_op jit(solution)/shard_map/ppermute | solution.py:321
  17.5 15.4 %collective-permute-start.7 = (bf16[2,784,128]{2,1,0:T(8,128)(2,1)S(1)}, bf16[2,784,128]{2,1,0:T(8,128)(2,1)S(1)}, u32[]{:S(2)}, u32[]{:S(2)}) collective-permute-start(bf16[2,784,128]{2,1,0:T(8,128)(2,1)S(1)} %shard_map.40), channel_id=1, source_target_pairs={{20,0},{0,8},{8,24},{24,16},{16,4},{4,12},{12,28},{28,20},{21,1},{... | collective-permute-start | bytes 1204232 | tf_op jit(solution)/shard_map/ppermute | solution.py:314
  19.0 13.9 %collective-permute-start.4 = (bf16[2,784,128]{2,1,0:T(8,128)(2,1)S(1)}, bf16[2,784,128]{2,1,0:T(8,128)(2,1)S(1)}, u32[]{:S(2)}, u32[]{:S(2)}) collective-permute-start(bf16[2,784,128]{2,1,0:T(8,128)(2,1)S(1)} %shard_map.40), channel_id=1, source_target_pairs={{8,0},{24,8},{16,24},{4,16},{12,4},{28,12},{20,28},{0,20},{9,1},{2... | collective-permute-start | bytes 1204232 | tf_op jit(solution)/shard_map/ppermute | solution.py:314
  27.7 2.4 %collective-permute-start.3 = (bf16[4,784,128]{2,1,0:T(8,128)(2,1)S(1)}, bf16[4,784,128]{2,1,0:T(8,128)(2,1)S(1)}, u32[]{:S(2)}, u32[]{:S(2)}) collective-permute-start(bf16[4,784,128]{2,1,0:T(8,128)(2,1)S(1)} %shard_map.39), channel_id=1, source_target_pairs={{4,0},{12,8},{28,24},{20,16},{0,4},{8,12},{24,28},{16,20},{5,1},{1... | collective-permute-start | bytes 2408456 | tf_op jit(solution)/shard_map/ppermute | solution.py:314
  27.8 6.7 %collective-permute-start.6 = (bf16[1,784,128]{2,1,0:T(8,128)(2,1)S(1)}, bf16[1,784,128]{2,1,0:T(8,128)(2,1)S(1)}, u32[]{:S(2)}, u32[]{:S(2)}) collective-permute-start(bf16[1,784,128]{2,1,0:T(8,128)(2,1)S(1)} %shard_map.41), channel_id=1, source_target_pairs={{20,0},{0,8},{8,24},{24,16},{16,4},{4,12},{12,28},{28,20},{21,1},{... | collective-permute-start | bytes 602120 | tf_op jit(solution)/shard_map/ppermute | solution.py:314
  30.1 7.0 %collective-permute-start.9 = (bf16[1,784,128]{2,1,0:T(8,128)(2,1)S(1)}, bf16[1,784,128]{2,1,0:T(8,128)(2,1)S(1)}, u32[]{:S(2)}, u32[]{:S(2)}) collective-permute-start(bf16[1,784,128]{2,1,0:T(8,128)(2,1)S(1)} %shard_map.41), channel_id=1, source_target_pairs={{8,0},{24,8},{16,24},{4,16},{12,4},{28,12},{20,28},{0,20},{9,1},{2... | collective-permute-start | bytes 602120 | tf_op jit(solution)/shard_map/ppermute | solution.py:314

commit v23 on v22

--- a/solution.py
+++ b/solution.py
@@ -317,7 +317,7 @@
         got = list(blocks)
         for k in range(1, groups):
             shift = slot_shift(k)
-            block = after(blocks[k], got[1], got[2]) if k > 2 else blocks[k]
+            block = after(blocks[k], got[2]) if k > 2 else blocks[k]
             got[k] = lax.ppermute(block, "group", [(z, (z + shift) % groups) for z in range(groups)])
         return got
 

time: 49.5 us -> 47.3 us (0.956)
  waiting for transfers between devices: 17.8 us -> 15.5 us
    ppermute x3, waiting for transfers between devices: 15.3 us -> 13 us  [exchange(): lax.ppermute(block, 'group', [(z, (z + shift) % groups) for z in range(gr...]
  transfers between devices with their start and end apart: 10 -> 10, of which waited for: 6 -> 6; matrix products, arithmetic and copies ran while one was open for 0% -> 0% of each run, Pallas kernels for 8% -> 9%
where the time goes in v23:
time: 47.3 us; the launch traced here: 47.1 us
  waiting for transfers between devices  15.5 us (33%)
  starting transfers between devices  13 us (27%)
  blocking collectives  10.9 us (23%)
  Pallas kernels  7.63 us (16%)
    ppermute x3, waiting for transfers between devices, exchange(): lax.ppermute(block, 'group', [(z, (z + shift) % groups) for z in range(gr...  13 us
    all_to_all x1, blocking collectives, per_device(): lax.all_to_all(best, ('shard', 'group'), split_axis=0, concat_axis=0, til...  10.9 us
    pallas_call x11, Pallas kernels, call(): pl.pallas_call(kernel, out_shape=out_shape, in_specs=in_specs or in_vmem(...  7.63 us
    ppermute x3, starting transfers between devices, exchange(): lax.ppermute(block, 'group', [(z, (z + shift) % groups) for z in range(gr...  6.57 us
    ppermute x7, starting transfers between devices, from_offset(): return lax.ppermute(x, 'shard', perm)  6.45 us
    ppermute x7, waiting for transfers between devices, from_offset(): return lax.ppermute(x, 'shard', perm)  2.49 us
  transfers between devices with their start and end apart: 10, of which 6 were waited for; matrix products, arithmetic and copies ran while one was open for 0% of the time, Pallas kernels for 9%

profile of v23, /device:TPU:0, one launch (start us, length us, event | category | flops | bytes accessed | tf_op | source)
XLA Modules:
  0.0 47.1 jit_solution(13604035551160130933)
XLA Ops:
  0.0 0.0 copy-start.1
  0.0 0.0 copy-start
  0.0 1.4 %shard_map.37.refs_0_ = bf16[512,768]{1,0:T(8,128)(2,1)S(1)} custom-call(bf16[512,768]{1,0:T(8,128)(2,1)} %far_ref.1), custom_call_target="tpu_custom_call" | custom-call | flops 1572864 | bytes 1572864 | tf_op jit(solution)/shard_map/pallas_call | solution.py:232
  1.4 0.0 copy-done.1
  1.4 0.0 copy-done
  1.4 0.9 %shard_map.38 = (bf16[784,128]{1,0:T(8,128)(2,1)S(1)}, bf16[784,128]{1,0:T(8,128)(2,1)S(1)}, bf16[784,128]{1,0:T(8,128)(2,1)S(1)}, bf16[784,128]{1,0:T(8,128)(2,1)S(1)}, s32[1,512]{1,0:T(1,128)S(1)}) custom-call(bf16[512,768]{1,0:T(8,128)(2,1)S(1)} %shard_map.37.refs_0_, s32[1,512]{1,0:T(1,128)S(1)} %bitcast.3, s32[1,512]{1,0:T(1,128)S(1)} %bitcast.4), custom_call_target="tpu_custom_call" | custom-call | flops 402653184 | bytes 1572864 | tf_op jit(solution)/shard_map/pallas_call | solution.py:232
  2.3 5.1 %collective-permute-start = (bf16[784,128]{1,0:T(8,128)(2,1)S(1)}, bf16[784,128]{1,0:T(8,128)(2,1)S(1)}, u32[]{:S(2)}, u32[]{:S(2)}) collective-permute-start(bf16[784,128]{1,0:T(8,128)(2,1)S(1)} %get-tuple-element.26), channel_id=1, source_target_pairs={{0,3},{1,0},{2,1},{3,2},{4,7},{5,4},{6,5},{7,6},{8,11},{9,8},{10,9... | collective-permute-start | bytes 602120 | tf_op jit(solution)/shard_map/ppermute | solution.py:321
  7.4 0.0 collective-permute-start.2
  7.4 1.5 %collective-permute-start.8 = (bf16[784,128]{1,0:T(8,128)(2,1)S(1)}, bf16[784,128]{1,0:T(8,128)(2,1)S(1)}, u32[]{:S(2)}, u32[]{:S(2)}) collective-permute-start(bf16[784,128]{1,0:T(8,128)(2,1)S(1)} %get-tuple-element.29.refs_0_.refs_3_), channel_id=1, source_target_pairs={{20,0},{0,8},{8,24},{24,16},{16,4},{4,12},{12,28},{28,20},{21,1},{... | collective-permute-start | bytes 602120 | tf_op jit(solution)/shard_map/ppermute | solution.py:314
  8.9 0.3 collective-permute-start.5
  9.2 3.6 %collective-permute-done.refs_2_.refs_1_ = bf16[784,128]{1,0:T(8,128)(2,1)S(1)} collective-permute-done((bf16[784,128]{1,0:T(8,128)(2,1)S(1)}, bf16[784,128]{1,0:T(8,128)(2,1)S(1)}, u32[]{:S(2)}, u32[]{:S(2)}) %collective-permute-start) | collective-permute-done | bytes 200736 | tf_op jit(solution)/shard_map/ppermute | solution.py:321
  12.8 1.5 %collective-permute-start.1 = (bf16[784,128]{1,0:T(8,128)(2,1)S(1)}, bf16[784,128]{1,0:T(8,128)(2,1)S(1)}, u32[]{:S(2)}, u32[]{:S(2)}) collective-permute-start(bf16[784,128]{1,0:T(8,128)(2,1)S(1)} %get-tuple-element.27), channel_id=1, source_target_pairs={{0,2},{1,3},{2,0},{3,1},{4,6},{5,7},{6,4},{7,5},{8,10},{9,11},{10,... | collective-permute-start | bytes 602120 | tf_op jit(solution)/shard_map/ppermute | solution.py:321
  14.3 3.7 %collective-permute-done.2.refs_1_.refs_0_.refs_2_ = bf16[784,128]{1,0:T(8,128)(2,1)S(1)} collective-permute-done((bf16[784,128]{1,0:T(8,128)(2,1)S(1)}, bf16[784,128]{1,0:T(8,128)(2,1)S(1)}, u32[]{:S(2)}, u32[]{:S(2)}) %collective-permute-start.2) | collective-permute-done | bytes 200736 | tf_op jit(solution)/shard_map/ppermute | solution.py:321
  18.0 1.6 %collective-permute-start.7 = (bf16[2,784,128]{2,1,0:T(8,128)(2,1)S(1)}, bf16[2,784,128]{2,1,0:T(8,128)(2,1)S(1)}, u32[]{:S(2)}, u32[]{:S(2)}) collective-permute-start(bf16[2,784,128]{2,1,0:T(8,128)(2,1)S(1)} %shard_map.40), channel_id=1, source_target_pairs={{20,0},{0,8},{8,24},{24,16},{16,4},{4,12},{12,28},{28,20},{21,1},{... | collective-permute-start | bytes 1204232 | tf_op jit(solution)/shard_map/ppermute | solution.py:314
  19.5 0.3 collective-permute-start.4
  19.8 5.7 %collective-permute-done.1.refs_3_.refs_0_ = bf16[784,128]{1,0:T(8,128)(2,1)S(1)} collective-permute-done((bf16[784,128]{1,0:T(8,128)(2,1)S(1)}, bf16[784,128]{1,0:T(8,128)(2,1)S(1)}, u32[]{:S(2)}, u32[]{:S(2)}) %collective-permute-start.1) | collective-permute-done | bytes 200736 | tf_op jit(solution)/shard_map/ppermute | solution.py:321
  25.5 0.1 shard_map.39
  25.6 0.1 collective-permute-start.3
  25.7 0.0 collective-permute-done.8.refs_8_.refs_3_
  25.7 1.6 %collective-permute-start.6 = (bf16[1,784,128]{2,1,0:T(8,128)(2,1)S(1)}, bf16[1,784,128]{2,1,0:T(8,128)(2,1)S(1)}, u32[]{:S(2)}, u32[]{:S(2)}) collective-permute-start(bf16[1,784,128]{2,1,0:T(8,128)(2,1)S(1)} %shard_map.41), channel_id=1, source_target_pairs={{20,0},{0,8},{8,24},{24,16},{16,4},{4,12},{12,28},{28,20},{21,1},{... | collective-permute-start | bytes 602120 | tf_op jit(solution)/shard_map/ppermute | solution.py:314
  27.2 0.7 %collective-permute-done.3.refs_4_ = bf16[4,784,128]{2,1,0:T(8,128)(2,1)S(1)} collective-permute-done((bf16[4,784,128]{2,1,0:T(8,128)(2,1)S(1)}, bf16[4,784,128]{2,1,0:T(8,128)(2,1)S(1)}, u32[]{:S(2)}, u32[]{:S(2)}) %collective-permute-start.3) | collective-permute-done | bytes 802848 | tf_op jit(solution)/shard_map/ppermute | solution.py:314
  27.9 1.3 %collective-permute-start.9 = (bf16[1,784,128]{2,1,0:T(8,128)(2,1)S(1)}, bf16[1,784,128]{2,1,0:T(8,128)(2,1)S(1)}, u32[]{:S(2)}, u32[]{:S(2)}) collective-permute-start(bf16[1,784,128]{2,1,0:T(8,128)(2,1)S(1)} %shard_map.41), channel_id=1, source_target_pairs={{8,0},{24,8},{16,24},{4,16},{12,4},{28,12},{20,28},{0,20},{9,1},{2... | collective-permute-start | bytes 602120 | tf_op jit(solution)/shard_map/ppermute | solution.py:314
  29.2 1.5 %shard_map.42 = (f32[4,8,512]{2,1,0:T(8,128)S(1)}, bf16[2,512,768]{2,1,0:T(8,128)(2,1)S(1)}) custom-call(bf16[784,128]{1,0:T(8,128)(2,1)S(1)} %collective-permute-done.1.refs_3_.refs_0_, bf16[784,128]{1,0:T(8,128)(2,1)S(1)} %collective-permute-done.refs_2_.refs_1_, bf16[784,128]{1,0:T(8,128)(2,1)S(1)} %collective-permute-done.2.refs_1_.refs_0_.refs_2_, ...), custom_call_target="tpu_custom_call" | custom-call | flops 805306368 | bytes 1572864 | tf_op jit(solution)/shard_map/pallas_call | solution.py:232
  30.7 0.0 collective-permute-done.5.refs_6_
  30.7 0.0 collective-permute-done.7.refs_7_.refs_2_
  30.7 0.0 collective-permute-done.4.refs_5_
  30.8 1.6 %shard_map.43 = (f32[4,8,512]{2,1,0:T(8,128)S(1)}, bf16[2,512,768]{2,1,0:T(8,128)(2,1)S(1)}) custom-call(bf16[784,128]{1,0:T(8,128)(2,1)S(1)} %collective-permute-done.1.refs_3_.refs_0_, bf16[784,128]{1,0:T(8,128)(2,1)S(1)} %collective-permute-done.refs_2_.refs_1_, bf16[784,128]{1,0:T(8,128)(2,1)S(1)} %collective-permute-done.2.refs_1_.refs_0_.refs_2_, ...), custom_call_target="tpu_custom_call" | custom-call | flops 830472192 | bytes 2752512 | tf_op jit(solution)/shard_map/pallas_call | solution.py:232
  32.3 1.5 %collective-permute-done.6.refs_7_.refs_1_ = bf16[1,784,128]{2,1,0:T(8,128)(2,1)S(1)} collective-permute-done((bf16[1,784,128]{2,1,0:T(8,128)(2,1)S(1)}, bf16[1,784,128]{2,1,0:T(8,128)(2,1)S(1)}, u32[]{:S(2)}, u32[]{:S(2)}) %collective-permute-start.6) | collective-permute-done | bytes 200736 | tf_op jit(solution)/shard_map/ppermute | solution.py:314
  33.9 0.8 %shard_map.44 = (f32[4,8,512]{2,1,0:T(8,128)S(1)}, bf16[1,512,768]{2,1,0:T(8,128)(2,1)S(1)}, f32[1,512]{1,0:T(1,128)S(1)}, f32[1,512]{1,0:T(1,128)S(1)}) custom-call(bf16[784,128]{1,0:T(8,128)(2,1)S(1)} %collective-permute-done.1.refs_3_.refs_0_, bf16[784,128]{1,0:T(8,128)(2,1)S(1)} %collective-permute-done.refs_2_.refs_1_, ...), custom_call_target="tpu_custom_call" | custom-call | flops 276824064 | bytes 2359296 | tf_op jit(solution)/shard_map/pallas_call | solution.py:232
  34.7 0.2 collective-permute-done.9.refs_0_
  35.0 0.4 shard_map.45
  35.4 0.1 shard_map.46
  35.5 10.9 %all_to_all.5.refs_0_ = f32[32,1,128]{2,1,0:T(1,128)S(1)} all-to-all(f32[32,1,128]{2,1,0:T(1,128)S(1)} %shard_map.46), channel_id=1, replica_groups=mesh['shard'=8,'group'=4] {'shard','group'}, dimensions={0} | all-to-all | bytes 32768 | tf_op jit(solution)/shard_map/all_to_all | solution.py:401
  46.3 0.8 %shard_map.47 = f32[1,512]{1,0:T(1,128)} custom-call(f32[32,1,128]{2,1,0:T(1,128)S(1)} %all_to_all.5.refs_0_, s32[1,512]{1,0:T(1,128)S(1)} %get-tuple-element.40.refs_1_), custom_call_target="tpu_custom_call" | custom-call | flops 262144 | bytes 2048 | tf_op jit(solution)/shard_map/pallas_call | solution.py:232
  (2 shorter events, 0.0 us)
Async XLA Ops:
  0.0 1.4 %copy-start.1 = (s32[512]{0:T(512)S(1)}, s32[512]{0:T(512)}, u32[]{:S(2)}) copy-start(s32[512]{0:T(512)} %param.5) | copy-start | bytes 6148
  0.0 1.4 %copy-start = (s32[512,1]{0,1:T(1,128)S(1)}, s32[512,1]{0,1:T(1,128)}, u32[]{:S(2)}) copy-start(s32[512,1]{0,1:T(1,128)} %param.4) | copy-start | bytes 6148
  2.3 10.5 %collective-permute-start = (bf16[784,128]{1,0:T(8,128)(2,1)S(1)}, bf16[784,128]{1,0:T(8,128)(2,1)S(1)}, u32[]{:S(2)}, u32[]{:S(2)}) collective-permute-start(bf16[784,128]{1,0:T(8,128)(2,1)S(1)} %get-tuple-element.26), channel_id=1, source_target_pairs={{0,3},{1,0},{2,1},{3,2},{4,7},{5,4},{6,5},{7,6},{8,11},{9,8},{10,9... | collective-permute-start | bytes 602120 | tf_op jit(solution)/shard_map/ppermute | solution.py:321
  7.4 10.5 %collective-permute-start.2 = (bf16[784,128]{1,0:T(8,128)(2,1)S(1)}, bf16[784,128]{1,0:T(8,128)(2,1)S(1)}, u32[]{:S(2)}, u32[]{:S(2)}) collective-permute-start(bf16[784,128]{1,0:T(8,128)(2,1)S(1)} %get-tuple-element.28), channel_id=1, source_target_pairs={{0,1},{1,2},{2,3},{3,0},{4,5},{5,6},{6,7},{7,4},{8,9},{9,10},{10,1... | collective-permute-start | bytes 602120 | tf_op jit(solution)/shard_map/ppermute | solution.py:321
  7.4 18.2 %collective-permute-start.8 = (bf16[784,128]{1,0:T(8,128)(2,1)S(1)}, bf16[784,128]{1,0:T(8,128)(2,1)S(1)}, u32[]{:S(2)}, u32[]{:S(2)}) collective-permute-start(bf16[784,128]{1,0:T(8,128)(2,1)S(1)} %get-tuple-element.29.refs_0_.refs_3_), channel_id=1, source_target_pairs={{20,0},{0,8},{8,24},{24,16},{16,4},{4,12},{12,28},{28,20},{21,1},{... | collective-permute-start | bytes 602120 | tf_op jit(solution)/shard_map/ppermute | solution.py:314
  8.9 21.8 %collective-permute-start.5 = (bf16[784,128]{1,0:T(8,128)(2,1)S(1)}, bf16[784,128]{1,0:T(8,128)(2,1)S(1)}, u32[]{:S(2)}, u32[]{:S(2)}) collective-permute-start(bf16[784,128]{1,0:T(8,128)(2,1)S(1)} %get-tuple-element.29.refs_0_.refs_3_), channel_id=1, source_target_pairs={{8,0},{24,8},{16,24},{4,16},{12,4},{28,12},{20,28},{0,20},{9,1},{2... | collective-permute-start | bytes 602120 | tf_op jit(solution)/shard_map/ppermute | solution.py:314
  12.8 12.7 %collective-permute-start.1 = (bf16[784,128]{1,0:T(8,128)(2,1)S(1)}, bf16[784,128]{1,0:T(8,128)(2,1)S(1)}, u32[]{:S(2)}, u32[]{:S(2)}) collective-permute-start(bf16[784,128]{1,0:T(8,128)(2,1)S(1)} %get-tuple-element.27), channel_id=1, source_target_pairs={{0,2},{1,3},{2,0},{3,1},{4,6},{5,7},{6,4},{7,5},{8,10},{9,11},{10,... | collective-permute-start | bytes 602120 | tf_op jit(solution)/shard_map/ppermute | solution.py:321
  18.0 12.7 %collective-permute-start.7 = (bf16[2,784,128]{2,1,0:T(8,128)(2,1)S(1)}, bf16[2,784,128]{2,1,0:T(8,128)(2,1)S(1)}, u32[]{:S(2)}, u32[]{:S(2)}) collective-permute-start(bf16[2,784,128]{2,1,0:T(8,128)(2,1)S(1)} %shard_map.40), channel_id=1, source_target_pairs={{20,0},{0,8},{8,24},{24,16},{16,4},{4,12},{12,28},{28,20},{21,1},{... | collective-permute-start | bytes 1204232 | tf_op jit(solution)/shard_map/ppermute | solution.py:314
  19.5 11.2 %collective-permute-start.4 = (bf16[2,784,128]{2,1,0:T(8,128)(2,1)S(1)}, bf16[2,784,128]{2,1,0:T(8,128)(2,1)S(1)}, u32[]{:S(2)}, u32[]{:S(2)}) collective-permute-start(bf16[2,784,128]{2,1,0:T(8,128)(2,1)S(1)} %shard_map.40), channel_id=1, source_target_pairs={{8,0},{24,8},{16,24},{4,16},{12,4},{28,12},{20,28},{0,20},{9,1},{2... | collective-permute-start | bytes 1204232 | tf_op jit(solution)/shard_map/ppermute | solution.py:314
  25.6 2.4 %collective-permute-start.3 = (bf16[4,784,128]{2,1,0:T(8,128)(2,1)S(1)}, bf16[4,784,128]{2,1,0:T(8,128)(2,1)S(1)}, u32[]{:S(2)}, u32[]{:S(2)}) collective-permute-start(bf16[4,784,128]{2,1,0:T(8,128)(2,1)S(1)} %shard_map.39), channel_id=1, source_target_pairs={{4,0},{12,8},{28,24},{20,16},{0,4},{8,12},{24,28},{16,20},{5,1},{1... | collective-permute-start | bytes 2408456 | tf_op jit(solution)/shard_map/ppermute | solution.py:314
  25.7 8.2 %collective-permute-start.6 = (bf16[1,784,128]{2,1,0:T(8,128)(2,1)S(1)}, bf16[1,784,128]{2,1,0:T(8,128)(2,1)S(1)}, u32[]{:S(2)}, u32[]{:S(2)}) collective-permute-start(bf16[1,784,128]{2,1,0:T(8,128)(2,1)S(1)} %shard_map.41), channel_id=1, source_target_pairs={{20,0},{0,8},{8,24},{24,16},{16,4},{4,12},{12,28},{28,20},{21,1},{... | collective-permute-start | bytes 602120 | tf_op jit(solution)/shard_map/ppermute | solution.py:314
  27.9 7.0 %collective-permute-start.9 = (bf16[1,784,128]{2,1,0:T(8,128)(2,1)S(1)}, bf16[1,784,128]{2,1,0:T(8,128)(2,1)S(1)}, u32[]{:S(2)}, u32[]{:S(2)}) collective-permute-start(bf16[1,784,128]{2,1,0:T(8,128)(2,1)S(1)} %shard_map.41), channel_id=1, source_target_pairs={{8,0},{24,8},{16,24},{4,16},{12,4},{28,12},{20,28},{0,20},{9,1},{2... | collective-permute-start | bytes 602120 | tf_op jit(solution)/shard_map/ppermute | solution.py:314

commit v24 on v21

--- a/solution.py
+++ b/solution.py
@@ -324,7 +324,7 @@
     (units,) = call(
         unit_kernel,
         [jax.ShapeDtypeStruct((rows, width), jnp.bfloat16)],
-        [pltpu.VMEM((rows, width), embeddings.dtype), pltpu.SemaphoreType.DMA((2,))],
+        [pltpu.VMEM((rows, width), embeddings.dtype), pltpu.SemaphoreType.DMA((1,))],
         (embeddings,),
         4 * rows * width,
         4 * rows * width,

time: 46.7 us -> 46.7 us (level)
  no operation moved by 1% of the time
where the time goes in v24:
time: 46.7 us; the launch traced here: 46.6 us
  starting transfers between devices  17.9 us (38%)
  waiting for transfers between devices  12 us (26%)
  blocking collectives  8.87 us (19%)
  Pallas kernels  7.68 us (16%)
    ppermute x3, starting transfers between devices, exchange(): lax.ppermute(block, 'group', [(z, (z + shift) % groups) for z in range(gr...  11.5 us
    all_to_all x1, blocking collectives, per_device(): lax.all_to_all(best, ('shard', 'group'), split_axis=0, concat_axis=0, til...  8.87 us
    ppermute x3, waiting for transfers between devices, exchange(): lax.ppermute(block, 'group', [(z, (z + shift) % groups) for z in range(gr...  7.93 us
    pallas_call x11, Pallas kernels, call(): pl.pallas_call(kernel, out_shape=out_shape, in_specs=in_specs or in_vmem(...  7.68 us
    ppermute x7, starting transfers between devices, from_offset(): return lax.ppermute(x, 'shard', perm)  6.44 us
    ppermute x7, waiting for transfers between devices, from_offset(): return lax.ppermute(x, 'shard', perm)  4.08 us
  transfers between devices with their start and end apart: 10, of which 5 were waited for; matrix products, arithmetic and copies ran while one was open for 0% of the time, Pallas kernels for 9%

profile of v24, /device:TPU:0, one launch (start us, length us, event | category | flops | bytes accessed | tf_op | source)
XLA Modules:
  0.0 46.6 jit_solution(5881447395517705556)
XLA Ops:
  0.0 0.0 copy-start.1
  0.0 0.0 copy-start
  0.0 1.4 %shard_map.37.refs_0_ = bf16[512,768]{1,0:T(8,128)(2,1)S(1)} custom-call(bf16[512,768]{1,0:T(8,128)(2,1)} %far_ref.1), custom_call_target="tpu_custom_call" | custom-call | flops 1572864 | bytes 1572864 | tf_op jit(solution)/shard_map/pallas_call | solution.py:232
  1.4 0.0 copy-done.1
  1.4 0.0 copy-done
  1.4 0.9 %shard_map.38 = (bf16[784,128]{1,0:T(8,128)(2,1)S(1)}, bf16[784,128]{1,0:T(8,128)(2,1)S(1)}, bf16[784,128]{1,0:T(8,128)(2,1)S(1)}, bf16[784,128]{1,0:T(8,128)(2,1)S(1)}, s32[1,512]{1,0:T(1,128)S(1)}) custom-call(bf16[512,768]{1,0:T(8,128)(2,1)S(1)} %shard_map.37.refs_0_, s32[1,512]{1,0:T(1,128)S(1)} %bitcast.3, s32[1,512]{1,0:T(1,128)S(1)} %bitcast.4), custom_call_target="tpu_custom_call" | custom-call | flops 402653184 | bytes 1572864 | tf_op jit(solution)/shard_map/pallas_call | solution.py:232
  2.4 3.1 %collective-permute-start = (bf16[784,128]{1,0:T(8,128)(2,1)S(1)}, bf16[784,128]{1,0:T(8,128)(2,1)S(1)}, u32[]{:S(2)}, u32[]{:S(2)}) collective-permute-start(bf16[784,128]{1,0:T(8,128)(2,1)S(1)} %get-tuple-element.26), channel_id=1, source_target_pairs={{0,1},{1,2},{2,3},{3,0},{4,5},{5,6},{6,7},{7,4},{8,9},{9,10},{10,1... | collective-permute-start | bytes 602120 | tf_op jit(solution)/shard_map/ppermute | solution.py:321
  5.5 2.1 %collective-permute-start.2 = (bf16[784,128]{1,0:T(8,128)(2,1)S(1)}, bf16[784,128]{1,0:T(8,128)(2,1)S(1)}, u32[]{:S(2)}, u32[]{:S(2)}) collective-permute-start(bf16[784,128]{1,0:T(8,128)(2,1)S(1)} %get-tuple-element.28), channel_id=1, source_target_pairs={{0,3},{1,0},{2,1},{3,2},{4,7},{5,4},{6,5},{7,6},{8,11},{9,8},{10,9... | collective-permute-start | bytes 602120 | tf_op jit(solution)/shard_map/ppermute | solution.py:321
  7.6 1.6 %collective-permute-start.8 = (bf16[784,128]{1,0:T(8,128)(2,1)S(1)}, bf16[784,128]{1,0:T(8,128)(2,1)S(1)}, u32[]{:S(2)}, u32[]{:S(2)}) collective-permute-start(bf16[784,128]{1,0:T(8,128)(2,1)S(1)} %get-tuple-element.29.refs_0_.refs_3_), channel_id=1, source_target_pairs={{20,0},{0,8},{8,24},{24,16},{16,4},{4,12},{12,28},{28,20},{21,1},{... | collective-permute-start | bytes 602120 | tf_op jit(solution)/shard_map/ppermute | solution.py:314
  9.2 0.1 collective-permute-start.5
  9.3 4.0 %collective-permute-done.refs_1_.refs_0_.refs_2_ = bf16[784,128]{1,0:T(8,128)(2,1)S(1)} collective-permute-done((bf16[784,128]{1,0:T(8,128)(2,1)S(1)}, bf16[784,128]{1,0:T(8,128)(2,1)S(1)}, u32[]{:S(2)}, u32[]{:S(2)}) %collective-permute-start) | collective-permute-done | bytes 200736 | tf_op jit(solution)/shard_map/ppermute | solution.py:321
  13.3 6.3 %collective-permute-start.1 = (bf16[784,128]{1,0:T(8,128)(2,1)S(1)}, bf16[784,128]{1,0:T(8,128)(2,1)S(1)}, u32[]{:S(2)}, u32[]{:S(2)}) collective-permute-start(bf16[784,128]{1,0:T(8,128)(2,1)S(1)} %get-tuple-element.27), channel_id=1, source_target_pairs={{0,2},{1,3},{2,0},{3,1},{4,6},{5,7},{6,4},{7,5},{8,10},{9,11},{10,... | collective-permute-start | bytes 602120 | tf_op jit(solution)/shard_map/ppermute | solution.py:321
  19.7 0.0 collective-permute-done.2.refs_2_.refs_1_
  19.7 1.6 %collective-permute-start.7 = (bf16[2,784,128]{2,1,0:T(8,128)(2,1)S(1)}, bf16[2,784,128]{2,1,0:T(8,128)(2,1)S(1)}, u32[]{:S(2)}, u32[]{:S(2)}) collective-permute-start(bf16[2,784,128]{2,1,0:T(8,128)(2,1)S(1)} %shard_map.40), channel_id=1, source_target_pairs={{20,0},{0,8},{8,24},{24,16},{16,4},{4,12},{12,28},{28,20},{21,1},{... | collective-permute-start | bytes 1204232 | tf_op jit(solution)/shard_map/ppermute | solution.py:314
  21.2 0.3 collective-permute-start.4
  21.5 3.9 %collective-permute-done.1.refs_3_.refs_0_ = bf16[784,128]{1,0:T(8,128)(2,1)S(1)} collective-permute-done((bf16[784,128]{1,0:T(8,128)(2,1)S(1)}, bf16[784,128]{1,0:T(8,128)(2,1)S(1)}, u32[]{:S(2)}, u32[]{:S(2)}) %collective-permute-start.1) | collective-permute-done | bytes 200736 | tf_op jit(solution)/shard_map/ppermute | solution.py:321
  25.4 0.1 shard_map.39
  25.4 0.1 collective-permute-start.3
  25.5 0.0 collective-permute-done.8.refs_8_.refs_3_
  25.5 1.6 %collective-permute-start.6 = (bf16[1,784,128]{2,1,0:T(8,128)(2,1)S(1)}, bf16[1,784,128]{2,1,0:T(8,128)(2,1)S(1)}, u32[]{:S(2)}, u32[]{:S(2)}) collective-permute-start(bf16[1,784,128]{2,1,0:T(8,128)(2,1)S(1)} %shard_map.41), channel_id=1, source_target_pairs={{20,0},{0,8},{8,24},{24,16},{16,4},{4,12},{12,28},{28,20},{21,1},{... | collective-permute-start | bytes 602120 | tf_op jit(solution)/shard_map/ppermute | solution.py:314
  27.1 0.7 %collective-permute-done.3.refs_4_ = bf16[4,784,128]{2,1,0:T(8,128)(2,1)S(1)} collective-permute-done((bf16[4,784,128]{2,1,0:T(8,128)(2,1)S(1)}, bf16[4,784,128]{2,1,0:T(8,128)(2,1)S(1)}, u32[]{:S(2)}, u32[]{:S(2)}) %collective-permute-start.3) | collective-permute-done | bytes 802848 | tf_op jit(solution)/shard_map/ppermute | solution.py:314
  27.8 1.3 %collective-permute-start.9 = (bf16[1,784,128]{2,1,0:T(8,128)(2,1)S(1)}, bf16[1,784,128]{2,1,0:T(8,128)(2,1)S(1)}, u32[]{:S(2)}, u32[]{:S(2)}) collective-permute-start(bf16[1,784,128]{2,1,0:T(8,128)(2,1)S(1)} %shard_map.41), channel_id=1, source_target_pairs={{8,0},{24,8},{16,24},{4,16},{12,4},{28,12},{20,28},{0,20},{9,1},{2... | collective-permute-start | bytes 602120 | tf_op jit(solution)/shard_map/ppermute | solution.py:314
  29.1 1.5 %shard_map.42 = (f32[4,8,512]{2,1,0:T(8,128)S(1)}, bf16[2,512,768]{2,1,0:T(8,128)(2,1)S(1)}) custom-call(bf16[784,128]{1,0:T(8,128)(2,1)S(1)} %collective-permute-done.1.refs_3_.refs_0_, bf16[784,128]{1,0:T(8,128)(2,1)S(1)} %collective-permute-done.2.refs_2_.refs_1_, bf16[784,128]{1,0:T(8,128)(2,1)S(1)} %collective-permute-done.refs_1_.refs_0_.refs_2_, ...), custom_call_target="tpu_custom_call" | custom-call | flops 805306368 | bytes 1572864 | tf_op jit(solution)/shard_map/pallas_call | solution.py:232
  30.6 0.0 collective-permute-done.5.refs_6_
  30.6 0.7 %collective-permute-done.7.refs_7_.refs_2_ = bf16[2,784,128]{2,1,0:T(8,128)(2,1)S(1)} collective-permute-done((bf16[2,784,128]{2,1,0:T(8,128)(2,1)S(1)}, bf16[2,784,128]{2,1,0:T(8,128)(2,1)S(1)}, u32[]{:S(2)}, u32[]{:S(2)}) %collective-permute-start.7) | collective-permute-done | bytes 401440 | tf_op jit(solution)/shard_map/ppermute | solution.py:314
  31.3 0.0 collective-permute-done.4.refs_5_
  31.3 1.6 %shard_map.43 = (f32[4,8,512]{2,1,0:T(8,128)S(1)}, bf16[2,512,768]{2,1,0:T(8,128)(2,1)S(1)}) custom-call(bf16[784,128]{1,0:T(8,128)(2,1)S(1)} %collective-permute-done.1.refs_3_.refs_0_, bf16[784,128]{1,0:T(8,128)(2,1)S(1)} %collective-permute-done.2.refs_2_.refs_1_, bf16[784,128]{1,0:T(8,128)(2,1)S(1)} %collective-permute-done.refs_1_.refs_0_.refs_2_, ...), custom_call_target="tpu_custom_call" | custom-call | flops 830472192 | bytes 2752512 | tf_op jit(solution)/shard_map/pallas_call | solution.py:232
  32.9 2.7 %collective-permute-done.6.refs_7_.refs_1_ = bf16[1,784,128]{2,1,0:T(8,128)(2,1)S(1)} collective-permute-done((bf16[1,784,128]{2,1,0:T(8,128)(2,1)S(1)}, bf16[1,784,128]{2,1,0:T(8,128)(2,1)S(1)}, u32[]{:S(2)}, u32[]{:S(2)}) %collective-permute-start.6) | collective-permute-done | bytes 200736 | tf_op jit(solution)/shard_map/ppermute | solution.py:314
  35.6 0.8 %shard_map.44 = (f32[4,8,512]{2,1,0:T(8,128)S(1)}, bf16[1,512,768]{2,1,0:T(8,128)(2,1)S(1)}, f32[1,512]{1,0:T(1,128)S(1)}, f32[1,512]{1,0:T(1,128)S(1)}) custom-call(bf16[784,128]{1,0:T(8,128)(2,1)S(1)} %collective-permute-done.1.refs_3_.refs_0_, bf16[784,128]{1,0:T(8,128)(2,1)S(1)} %collective-permute-done.2.refs_2_.refs_1_, ...), custom_call_target="tpu_custom_call" | custom-call | flops 276824064 | bytes 2359296 | tf_op jit(solution)/shard_map/pallas_call | solution.py:232
  36.4 0.0 collective-permute-done.9.refs_0_
  36.4 0.4 shard_map.45
  36.9 0.1 shard_map.46
  36.9 8.9 %all_to_all.5.refs_0_ = f32[32,1,128]{2,1,0:T(1,128)S(1)} all-to-all(f32[32,1,128]{2,1,0:T(1,128)S(1)} %shard_map.46), channel_id=1, replica_groups=mesh['shard'=8,'group'=4] {'shard','group'}, dimensions={0} | all-to-all | bytes 32768 | tf_op jit(solution)/shard_map/all_to_all | solution.py:401
  45.8 0.8 %shard_map.47 = f32[1,512]{1,0:T(1,128)} custom-call(f32[32,1,128]{2,1,0:T(1,128)S(1)} %all_to_all.5.refs_0_, s32[1,512]{1,0:T(1,128)S(1)} %get-tuple-element.40.refs_1_), custom_call_target="tpu_custom_call" | custom-call | flops 262144 | bytes 2048 | tf_op jit(solution)/shard_map/pallas_call | solution.py:232
  (2 shorter events, 0.0 us)
Async XLA Ops:
  0.0 1.4 %copy-start.1 = (s32[512]{0:T(512)S(1)}, s32[512]{0:T(512)}, u32[]{:S(2)}) copy-start(s32[512]{0:T(512)} %param.5) | copy-start | bytes 6148
  0.0 1.4 %copy-start = (s32[512,1]{0,1:T(1,128)S(1)}, s32[512,1]{0,1:T(1,128)}, u32[]{:S(2)}) copy-start(s32[512,1]{0,1:T(1,128)} %param.4) | copy-start | bytes 6148
  2.4 11.0 %collective-permute-start = (bf16[784,128]{1,0:T(8,128)(2,1)S(1)}, bf16[784,128]{1,0:T(8,128)(2,1)S(1)}, u32[]{:S(2)}, u32[]{:S(2)}) collective-permute-start(bf16[784,128]{1,0:T(8,128)(2,1)S(1)} %get-tuple-element.26), channel_id=1, source_target_pairs={{0,1},{1,2},{2,3},{3,0},{4,5},{5,6},{6,7},{7,4},{8,9},{9,10},{10,1... | collective-permute-start | bytes 602120 | tf_op jit(solution)/shard_map/ppermute | solution.py:321
  5.5 14.2 %collective-permute-start.2 = (bf16[784,128]{1,0:T(8,128)(2,1)S(1)}, bf16[784,128]{1,0:T(8,128)(2,1)S(1)}, u32[]{:S(2)}, u32[]{:S(2)}) collective-permute-start(bf16[784,128]{1,0:T(8,128)(2,1)S(1)} %get-tuple-element.28), channel_id=1, source_target_pairs={{0,3},{1,0},{2,1},{3,2},{4,7},{5,4},{6,5},{7,6},{8,11},{9,8},{10,9... | collective-permute-start | bytes 602120 | tf_op jit(solution)/shard_map/ppermute | solution.py:321
  7.6 18.0 %collective-permute-start.8 = (bf16[784,128]{1,0:T(8,128)(2,1)S(1)}, bf16[784,128]{1,0:T(8,128)(2,1)S(1)}, u32[]{:S(2)}, u32[]{:S(2)}) collective-permute-start(bf16[784,128]{1,0:T(8,128)(2,1)S(1)} %get-tuple-element.29.refs_0_.refs_3_), channel_id=1, source_target_pairs={{20,0},{0,8},{8,24},{24,16},{16,4},{4,12},{12,28},{28,20},{21,1},{... | collective-permute-start | bytes 602120 | tf_op jit(solution)/shard_map/ppermute | solution.py:314
  9.2 21.4 %collective-permute-start.5 = (bf16[784,128]{1,0:T(8,128)(2,1)S(1)}, bf16[784,128]{1,0:T(8,128)(2,1)S(1)}, u32[]{:S(2)}, u32[]{:S(2)}) collective-permute-start(bf16[784,128]{1,0:T(8,128)(2,1)S(1)} %get-tuple-element.29.refs_0_.refs_3_), channel_id=1, source_target_pairs={{8,0},{24,8},{16,24},{4,16},{12,4},{28,12},{20,28},{0,20},{9,1},{2... | collective-permute-start | bytes 602120 | tf_op jit(solution)/shard_map/ppermute | solution.py:314
  13.3 12.0 %collective-permute-start.1 = (bf16[784,128]{1,0:T(8,128)(2,1)S(1)}, bf16[784,128]{1,0:T(8,128)(2,1)S(1)}, u32[]{:S(2)}, u32[]{:S(2)}) collective-permute-start(bf16[784,128]{1,0:T(8,128)(2,1)S(1)} %get-tuple-element.27), channel_id=1, source_target_pairs={{0,2},{1,3},{2,0},{3,1},{4,6},{5,7},{6,4},{7,5},{8,10},{9,11},{10,... | collective-permute-start | bytes 602120 | tf_op jit(solution)/shard_map/ppermute | solution.py:321
  19.7 11.6 %collective-permute-start.7 = (bf16[2,784,128]{2,1,0:T(8,128)(2,1)S(1)}, bf16[2,784,128]{2,1,0:T(8,128)(2,1)S(1)}, u32[]{:S(2)}, u32[]{:S(2)}) collective-permute-start(bf16[2,784,128]{2,1,0:T(8,128)(2,1)S(1)} %shard_map.40), channel_id=1, source_target_pairs={{20,0},{0,8},{8,24},{24,16},{16,4},{4,12},{12,28},{28,20},{21,1},{... | collective-permute-start | bytes 1204232 | tf_op jit(solution)/shard_map/ppermute | solution.py:314
  21.2 10.0 %collective-permute-start.4 = (bf16[2,784,128]{2,1,0:T(8,128)(2,1)S(1)}, bf16[2,784,128]{2,1,0:T(8,128)(2,1)S(1)}, u32[]{:S(2)}, u32[]{:S(2)}) collective-permute-start(bf16[2,784,128]{2,1,0:T(8,128)(2,1)S(1)} %shard_map.40), channel_id=1, source_target_pairs={{8,0},{24,8},{16,24},{4,16},{12,4},{28,12},{20,28},{0,20},{9,1},{2... | collective-permute-start | bytes 1204232 | tf_op jit(solution)/shard_map/ppermute | solution.py:314
  25.4 2.4 %collective-permute-start.3 = (bf16[4,784,128]{2,1,0:T(8,128)(2,1)S(1)}, bf16[4,784,128]{2,1,0:T(8,128)(2,1)S(1)}, u32[]{:S(2)}, u32[]{:S(2)}) collective-permute-start(bf16[4,784,128]{2,1,0:T(8,128)(2,1)S(1)} %shard_map.39), channel_id=1, source_target_pairs={{4,0},{12,8},{28,24},{20,16},{0,4},{8,12},{24,28},{16,20},{5,1},{1... | collective-permute-start | bytes 2408456 | tf_op jit(solution)/shard_map/ppermute | solution.py:314
  25.5 10.0 %collective-permute-start.6 = (bf16[1,784,128]{2,1,0:T(8,128)(2,1)S(1)}, bf16[1,784,128]{2,1,0:T(8,128)(2,1)S(1)}, u32[]{:S(2)}, u32[]{:S(2)}) collective-permute-start(bf16[1,784,128]{2,1,0:T(8,128)(2,1)S(1)} %shard_map.41), channel_id=1, source_target_pairs={{20,0},{0,8},{8,24},{24,16},{16,4},{4,12},{12,28},{28,20},{21,1},{... | collective-permute-start | bytes 602120 | tf_op jit(solution)/shard_map/ppermute | solution.py:314
  27.8 8.6 %collective-permute-start.9 = (bf16[1,784,128]{2,1,0:T(8,128)(2,1)S(1)}, bf16[1,784,128]{2,1,0:T(8,128)(2,1)S(1)}, u32[]{:S(2)}, u32[]{:S(2)}) collective-permute-start(bf16[1,784,128]{2,1,0:T(8,128)(2,1)S(1)} %shard_map.41), channel_id=1, source_target_pairs={{8,0},{24,8},{16,24},{4,16},{12,4},{28,12},{20,28},{0,20},{9,1},{2... | collective-permute-start | bytes 602120 | tf_op jit(solution)/shard_map/ppermute | solution.py:314
